TPU v7x, 128 devices: a whole 4x4x4 slice. The times are simulated.
128 devices in a mesh: section: 2 (over z_hi), dp: 16 (over z_lo, x, core), tensor: 4 (over y).
Axes of the slice: x: 4, y: 4, z: 4 (z_hi: 2, z_lo: 2; z = z_hi * 2 + z_lo), core: 2. Of those that a mesh axis runs over, the one named last changes fastest.
Arguments:
- tokens: bfloat16 [2, 8192, 1024], P(None, ('dp', 'tensor')), may hold values from -6 to 6
- cotangent: bfloat16 [2, 8192, 1024], P(None, ('dp', 'tensor')), may hold values from -6 to 6
- lengths: int32 [2, 16, 4], P(None, 'dp'), may hold values from 1 to 386, 512 in all within a row
- gains: float32 [2, 2, 1024], P('section'), may hold values from 0.25 to 1.75
- w_qkv: bfloat16 [2, 1024, 3, 1024], P('section', None, None, 'tensor'), may hold values from -0.1875 to 0.1875
- w_out: bfloat16 [2, 1024, 1024], P('section', 'tensor'), may hold values from -1.5 to 1.5
- w_up: bfloat16 [2, 1024, 2, 2624], P('section', None, None, 'tensor'), may hold values from -0.1875 to 0.1875
- w_down: bfloat16 [2, 2624, 1024], P('section', 'tensor'), may hold values from -0.125 to 0.125
Outputs:
- section_out: bfloat16 [2, 2, 8192, 1024], P('section', None, ('dp', 'tensor'))
- input_grads: bfloat16 [2, 2, 8192, 1024], P('section', None, ('dp', 'tensor'))
- grad_gains: float32 [2, 2, 1024], P('section')
- grad_qkv: float32 [2, 1024, 3, 1024], P('section', None, None, 'tensor')
- grad_out: float32 [2, 1024, 1024], P('section', 'tensor')
- grad_up: float32 [2, 1024, 2, 2624], P('section', None, None, 'tensor')
- grad_down: float32 [2, 2624, 1024], P('section', 'tensor')
Inputs may be any that keep to these rules, and one draw needn't show every extreme that they name: `lengths`: in each group's micro-batch the 4 documents fill all 512 rows; the longest has exactly 386 rows.
All inputs are finite; a program needn't handle non-finite values.
Results may differ from a plain program's by a relative error of at most 0.03.
Values may be sent and summed in bfloat16 or wider, within the bound.
No kernel may reach another device: no remote copies, remote signals or barrier semaphores. Data moves between devices by JAX's collectives and lax.ppermute only.
A program may use at most 192 MiB of HBM per device.

v0:
```python
import jax
import jax.numpy as jnp
from jax import lax
from jax.sharding import PartitionSpec as P

HEAD_DIM = 64
WINDOW = 128


epsilon = 1e-05


def shifted(block, axis, distance):
    devices = range(lax.axis_size(axis))
    route = [(i - distance, i) for i in devices if i - distance in devices]
    return lax.ppermute(block, axis, route)


def layer_norm(values, gain_scale):
    centered = values - jnp.mean(values, axis=-1, keepdims=True)
    variance = jnp.mean(centered * centered, axis=-1, keepdims=True)
    return centered * lax.rsqrt(variance + epsilon) * gain_scale


def doc_layout(doc_lengths, total_rows):
    indices = jnp.arange(total_rows, dtype=jnp.int32)
    doc_ends = jnp.cumsum(doc_lengths)
    passed = indices[:, None] >= doc_ends[None, :]
    doc_ids = jnp.sum(passed.astype(jnp.int32), axis=1)
    starts = jnp.sum(jnp.where(passed, doc_lengths[None, :], 0), axis=1)
    return (doc_ids, indices - starts)


def rope_tables(positions, rope_base):
    half_dim = HEAD_DIM // 2
    inverse = rope_base ** (-2.0 * jnp.arange(half_dim, dtype=jnp.float32) / HEAD_DIM)
    angles = positions.astype(jnp.float32)[..., None] * inverse
    angles = jnp.concatenate([angles, angles], axis=-1)
    return (jnp.cos(angles), jnp.sin(angles))


def rotate(values, cosine_table, sine_table):
    half_dim = values.shape[-1] // 2
    turned = jnp.concatenate([-values[..., half_dim:], values[..., :half_dim]], axis=-1)
    return values * cosine_table[..., None, :] + turned * sine_table[..., None, :]


def rotate_back(gradients, cosine_table, sine_table):
    half_dim = gradients.shape[-1] // 2
    scaled = gradients * sine_table[..., None, :]
    turned = jnp.concatenate([scaled[..., half_dim:], -scaled[..., :half_dim]], axis=-1)
    return gradients * cosine_table[..., None, :] + turned


def allowed_pairs(doc_ids, reach_rows):
    indices = jnp.arange(doc_ids.shape[0], dtype=jnp.int32)
    distance = jnp.abs(indices[:, None] - indices[None, :])
    return (doc_ids[:, None] == doc_ids[None, :]) & (distance <= reach_rows)


def masked_scores(queries, keys_rot, allowed):
    scores = jnp.einsum(
        "qhd,khd->hqk", queries, keys_rot, preferred_element_type=jnp.float32
    ) * HEAD_DIM ** (-0.5)
    return jnp.where(allowed[None], scores, -1e30)


def contract_rows(left_rows, right_rows):
    return lax.dot_general(
        left_rows, right_rows, (((0,), (0,)), ((), ())), preferred_element_type=jnp.float32
    )


def contract_last(left_rows, weight):
    return lax.dot_general(
        left_rows, weight, (((1,), (1,)), ((), ())), preferred_element_type=jnp.float32
    )


def gather_rows(normed):
    return lax.all_gather(normed, "tensor", axis=0, tiled=True)


def scatter_rows(source, weight, row_count):

    def row_term(first_row, row_span):
        return jnp.dot(source, weight, preferred_element_type=jnp.float32)

    return lax.psum_scatter(
        row_term(jnp.int32(0), lax.axis_size("tensor") * row_count).astype(jnp.bfloat16),
        "tensor",
        scatter_dimension=0,
        tiled=True,
    ).astype(jnp.float32)


def gather_grads(gradients):
    return lax.all_gather(gradients, "tensor", axis=0, tiled=True)


def scatter_grads(source, weight, row_count):

    def row_term(first_row, row_span):
        return contract_last(source, weight)

    return lax.psum_scatter(
        row_term(jnp.int32(0), lax.axis_size("tensor") * row_count).astype(jnp.bfloat16),
        "tensor",
        scatter_dimension=0,
        tiled=True,
    ).astype(jnp.float32)


def forward_layer(
    inputs, gain_pair, w_qkv, w_out, w_up, w_down, doc_ids, positions, reach_rows, rope_base
):
    row_count = inputs.shape[0]
    normed = layer_norm(inputs, gain_pair[0]).astype(jnp.bfloat16)
    normed_all = gather_rows(normed)
    full_rows = normed_all.shape[0]
    local_width = w_qkv.shape[2]
    local_heads = local_width // HEAD_DIM
    projected = jnp.dot(
        normed_all,
        w_qkv.reshape(w_qkv.shape[0], 3 * local_width),
        preferred_element_type=jnp.float32,
    )
    projected = projected.reshape(full_rows, 3, local_heads, HEAD_DIM)
    cosine_table, sine_table = rope_tables(positions, rope_base)
    queries = rotate(projected[:, 0], cosine_table, sine_table).astype(jnp.bfloat16)
    keys_rot = rotate(projected[:, 1], cosine_table, sine_table).astype(jnp.bfloat16)
    values_in = projected[:, 2].astype(jnp.bfloat16)
    scores = masked_scores(queries, keys_rot, allowed_pairs(doc_ids, reach_rows))
    largest = jnp.max(scores, axis=2, keepdims=True)
    exp_scores = jnp.exp(scores - largest)
    totals = jnp.sum(exp_scores, axis=2, keepdims=True)
    soft_weights = (exp_scores / totals).astype(jnp.bfloat16)
    log_totals = largest + jnp.log(totals)
    attended = jnp.einsum(
        "hqk,khd->qhd", soft_weights, values_in, preferred_element_type=jnp.float32
    )
    attended = attended.reshape(full_rows, local_width).astype(jnp.bfloat16)
    resid_mid = inputs + scatter_rows(attended, w_out, row_count)
    normed_mid = layer_norm(resid_mid, gain_pair[1]).astype(jnp.bfloat16)
    normed_mid_all = gather_rows(normed_mid)
    local_hidden = w_up.shape[2]
    hidden = jnp.dot(
        normed_mid_all,
        w_up.reshape(w_up.shape[0], 2 * local_hidden),
        preferred_element_type=jnp.float32,
    )
    hidden = hidden.reshape(full_rows, 2, local_hidden)
    gelu_in = hidden[:, 0]
    gate_mult = hidden[:, 1]
    mixed_rows = (jax.nn.gelu(gelu_in, approximate=False) * gate_mult).astype(jnp.bfloat16)
    result = resid_mid + scatter_rows(mixed_rows, w_down, row_count)
    kept_values = (
        inputs,
        resid_mid,
        normed_all,
        queries,
        keys_rot,
        values_in,
        log_totals,
        attended,
        normed_mid_all,
        gelu_in,
        gate_mult,
        mixed_rows,
    )
    return (result, kept_values)


def gelu_product(first_half, second_half):
    return jax.nn.gelu(first_half, approximate=False) * second_half


def backward_ffn(grad_result, kept_values, gain_pair, w_up, w_down):
    resid_mid = kept_values[1]
    normed_mid_all = kept_values[8]
    gelu_in = kept_values[9]
    gate_mult = kept_values[10]
    mixed_rows = kept_values[11]
    row_count = grad_result.shape[0]
    full_rows = normed_mid_all.shape[0]
    grad_ffn_all = gather_grads(grad_result.astype(jnp.bfloat16))
    grad_mixed = contract_last(grad_ffn_all, w_down)
    grad_w_down = contract_rows(mixed_rows, grad_ffn_all)
    unused, pull_gelu = jax.vjp(gelu_product, gelu_in, gate_mult)
    grad_gelu, grad_gate = pull_gelu(grad_mixed)
    grad_hidden = (
        jnp.stack([grad_gelu, grad_gate], axis=1).astype(jnp.bfloat16).reshape(full_rows, -1)
    )
    up_flat = w_up.reshape(w_up.shape[0], -1)
    grad_w_up = contract_rows(normed_mid_all, grad_hidden)
    grad_normed_mid = scatter_grads(grad_hidden, up_flat, row_count)
    unused, pull_norm = jax.vjp(layer_norm, resid_mid, gain_pair[1])
    grad_resid, grad_gain = pull_norm(grad_normed_mid)
    return (grad_result + grad_resid, (grad_w_up.reshape(w_up.shape), grad_w_down, grad_gain))


def backward_attn(
    grad_mid, kept_values, gain_pair, w_qkv, w_out, doc_ids, positions, reach_rows, rope_base
):
    inputs = kept_values[0]
    normed_all = kept_values[2]
    queries = kept_values[3]
    keys_rot = kept_values[4]
    values_in = kept_values[5]
    log_totals = kept_values[6]
    attended = kept_values[7]
    row_count = grad_mid.shape[0]
    full_rows = normed_all.shape[0]
    grad_att_all = gather_grads(grad_mid.astype(jnp.bfloat16))
    grad_w_out = contract_rows(attended, grad_att_all)
    grad_attended = contract_last(grad_att_all, w_out).astype(jnp.bfloat16).reshape(queries.shape)
    scores = masked_scores(queries, keys_rot, allowed_pairs(doc_ids, reach_rows))
    soft_exact = jnp.exp(scores - log_totals)
    soft_weights = soft_exact.astype(jnp.bfloat16)
    grad_values = jnp.einsum(
        "hqk,qhd->khd", soft_weights, grad_attended, preferred_element_type=jnp.float32
    )
    grad_soft = jnp.einsum(
        "qhd,khd->hqk", grad_attended, values_in, preferred_element_type=jnp.float32
    )
    row_dots = jnp.sum(soft_exact * grad_soft, axis=2, keepdims=True)
    grad_scores = (soft_exact * (grad_soft - row_dots)).astype(jnp.bfloat16)
    grad_queries = jnp.einsum(
        "hqk,khd->qhd", grad_scores, keys_rot, preferred_element_type=jnp.float32
    ) * HEAD_DIM ** (-0.5)
    grad_keys = jnp.einsum(
        "hqk,qhd->khd", grad_scores, queries, preferred_element_type=jnp.float32
    ) * HEAD_DIM ** (-0.5)
    cosine_table, sine_table = rope_tables(positions, rope_base)
    grad_projected = jnp.stack(
        [
            rotate_back(grad_queries, cosine_table, sine_table),
            rotate_back(grad_keys, cosine_table, sine_table),
            grad_values,
        ],
        axis=1,
    )
    grad_projected = grad_projected.astype(jnp.bfloat16).reshape(full_rows, -1)
    qkv_flat = w_qkv.reshape(w_qkv.shape[0], -1)
    grad_w_qkv = contract_rows(normed_all, grad_projected)
    grad_normed = scatter_grads(grad_projected, qkv_flat, row_count)
    unused, pull_norm = jax.vjp(layer_norm, inputs, gain_pair[0])
    grad_resid, grad_gain = pull_norm(grad_normed)
    return (grad_mid + grad_resid, (grad_w_qkv.reshape(w_qkv.shape), grad_w_out, grad_gain))


def local(tokens, cotangent, lengths, gains, w_qkv, w_out, w_up, w_down):
    section_index = lax.axis_index("section")
    is_first = section_index == 0
    micro_count = tokens.shape[0]
    row_count = tokens.shape[1]
    full_rows = row_count * lax.axis_size("tensor")
    reach_rows = jnp.where(is_first, WINDOW // 2, full_rows).astype(jnp.int32)
    rope_base = jnp.where(is_first, 10000.0, 160000.0).astype(jnp.float32)
    gain_pair = gains[0]
    qkv_local = w_qkv[0]
    out_local = w_out[0]
    up_local = w_up[0]
    down_local = w_down[0]
    layouts = [doc_layout(lengths[micro_index, 0], full_rows) for micro_index in range(micro_count)]
    doc_table = jnp.stack([layout_pair[0] for layout_pair in layouts])
    pos_table = jnp.stack([layout_pair[1] for layout_pair in layouts])
    received = jnp.zeros((row_count, tokens.shape[2]), jnp.bfloat16)
    section_outs = []
    kept_list = []
    for step_index in range(micro_count + 1):
        micro_pick = jnp.clip(step_index - section_index, 0, micro_count - 1)
        own_tokens = tokens[min(step_index, micro_count - 1)].astype(jnp.float32)
        inputs = jnp.where(is_first, own_tokens, received.astype(jnp.float32))
        result, kept_values = forward_layer(
            inputs,
            gain_pair,
            qkv_local,
            out_local,
            up_local,
            down_local,
            doc_table[micro_pick],
            pos_table[micro_pick],
            reach_rows,
            rope_base,
        )
        sent = result.astype(jnp.bfloat16)
        section_outs.append(sent)
        kept_list.append(kept_values)
        if step_index < micro_count:
            received = shifted(sent, "section", 1)
    kept_stack = tuple(
        (
            jnp.stack([kept_step[slot_index] for kept_step in kept_list])
            for slot_index in range(len(kept_list[0]))
        )
    )
    acc_qkv = jnp.zeros(qkv_local.shape, jnp.float32)
    acc_out = jnp.zeros(out_local.shape, jnp.float32)
    acc_up = jnp.zeros(up_local.shape, jnp.float32)
    acc_down = jnp.zeros(down_local.shape, jnp.float32)
    acc_gain_first = jnp.zeros(gain_pair.shape[1:], jnp.float32)
    acc_gain_mid = jnp.zeros(gain_pair.shape[1:], jnp.float32)
    received = jnp.zeros((row_count, tokens.shape[2]), jnp.bfloat16)
    grad_list = []
    ffn_sums = (acc_up, acc_down, acc_gain_mid)
    for step_index in range(micro_count + 1):
        micro_index = step_index - 1 + section_index
        valid = (micro_index >= 0) & (micro_index < micro_count)
        micro_pick = jnp.clip(micro_index, 0, micro_count - 1)
        saved_pick = jnp.clip(step_index - 1 + 2 * section_index, 0, micro_count)
        kept_values = tuple((saved[saved_pick] for saved in kept_stack))
        own_grad = cotangent[min(step_index, micro_count - 1)].astype(jnp.float32)
        grad_result = jnp.where(is_first, received.astype(jnp.float32), own_grad)
        grad_mid, ffn_terms = backward_ffn(
            grad_result, kept_values, gain_pair, up_local, down_local
        )
        acc_up = acc_up + jnp.where(valid, ffn_terms[0], 0.0)
        acc_down = acc_down + jnp.where(valid, ffn_terms[1], 0.0)
        acc_gain_mid = acc_gain_mid + jnp.where(valid, ffn_terms[2], 0.0)
        if step_index == micro_count:
            ffn_sums = (acc_up, acc_down, acc_gain_mid)
        grad_input, attn_terms = backward_attn(
            grad_mid,
            kept_values,
            gain_pair,
            qkv_local,
            out_local,
            doc_table[micro_pick],
            pos_table[micro_pick],
            reach_rows,
            rope_base,
        )
        acc_qkv = acc_qkv + jnp.where(valid, attn_terms[0], 0.0)
        acc_out = acc_out + jnp.where(valid, attn_terms[1], 0.0)
        acc_gain_first = acc_gain_first + jnp.where(valid, attn_terms[2], 0.0)
        grad_sent = grad_input.astype(jnp.bfloat16)
        grad_list.append(grad_sent)
        if step_index < micro_count:
            received = shifted(grad_sent, "section", -1)
    qkv_sum, out_sum, first_gain, up_sum, down_sum, mid_gain = (
        lax.psum(acc_qkv.astype(jnp.bfloat16), "dp").astype(jnp.float32),
        lax.psum(acc_out.astype(jnp.bfloat16), "dp").astype(jnp.float32),
        lax.psum(acc_gain_first.astype(jnp.bfloat16), "dp").astype(jnp.float32),
        lax.psum(ffn_sums[0].astype(jnp.bfloat16), "dp").astype(jnp.float32),
        lax.psum(ffn_sums[1].astype(jnp.bfloat16), "dp").astype(jnp.float32),
        lax.psum(ffn_sums[2].astype(jnp.bfloat16), "dp").astype(jnp.float32),
    )
    gain_total = lax.psum(jnp.stack([first_gain, mid_gain]), "tensor")
    section_out = jnp.stack(
        [
            jnp.where(is_first, section_outs[micro_index], section_outs[micro_index + 1])
            for micro_index in range(micro_count)
        ]
    )
    input_grads = jnp.stack(
        [
            jnp.where(is_first, grad_list[micro_index + 1], grad_list[micro_index])
            for micro_index in range(micro_count)
        ]
    )
    return (
        section_out[None],
        input_grads[None],
        gain_total[None],
        qkv_sum[None],
        out_sum[None],
        up_sum[None],
        down_sum[None],
    )


def solution(mesh):
    in_specs = (
        P(None, ("dp", "tensor"), None),
        P(None, ("dp", "tensor"), None),
        P(None, "dp", None),
        P("section", None, None),
        P("section", None, None, "tensor"),
        P("section", "tensor", None),
        P("section", None, None, "tensor"),
        P("section", "tensor", None),
    )
    out_specs = (
        P("section", None, ("dp", "tensor"), None),
        P("section", None, ("dp", "tensor"), None),
        P("section", None, None),
        P("section", None, None, "tensor"),
        P("section", "tensor", None),
        P("section", None, None, "tensor"),
        P("section", "tensor", None),
    )
    return jax.shard_map(local, mesh=mesh, in_specs=in_specs, out_specs=out_specs, check_vma=False)
```

profile of v0, /device:TPU:1, one launch (start us, length us, event | category | flops | bytes accessed | tf_op | source)
XLA Modules:
  0.0 957.0 jit_solution(2227648318309350329)
XLA Ops:
  18.3 21.1 %all-gather.13.cloned.1.call-done = bf16[512,1024]{1,0:T(8,128)(2,1)} async-done(((bf16[128,1024]{1,0:T(8,128)(2,1)}), bf16[512,1024]{1,0:T(8,128)(2,1)}) %all-gather.13.cloned.1.call-update) | async-done | bytes 1048592 | tf_op jit(solution)/shard_map/all_gather | solution.py:81
  49.1 23.5 %reduce-scatter.13.cloned.1.call-done = bf16[128,1024]{1,0:T(8,128)(2,1)} async-done(((bf16[512,1024]{1,0:T(8,128)(2,1)}), bf16[128,1024]{1,0:T(8,128)(2,1)}) %reduce-scatter.13.cloned.1.call-update) | async-done | bytes 262160 | tf_op jit(solution)/shard_map/reduce_scatter | solution.py:89
  76.6 24.3 %all-gather.15.cloned.1.call-done = bf16[512,1024]{1,0:T(8,128)(2,1)} async-done(((bf16[128,1024]{1,0:T(8,128)(2,1)}), bf16[512,1024]{1,0:T(8,128)(2,1)}) %all-gather.15.cloned.1.call-update) | async-done | bytes 1048592 | tf_op jit(solution)/shard_map/all_gather | solution.py:81
  105.3 4.6 convolution_convert_fusion.10
  110.0 22.8 %reduce-scatter.15.cloned.1.call-done = bf16[128,1024]{1,0:T(8,128)(2,1)} async-done(((bf16[512,1024]{1,0:T(8,128)(2,1)}), bf16[128,1024]{1,0:T(8,128)(2,1)}) %reduce-scatter.15.cloned.1.call-update) | async-done | bytes 262160 | tf_op jit(solution)/shard_map/reduce_scatter | solution.py:89
  133.9 5.5 collective-permute-start
  149.1 21.8 %all-gather.17.cloned.1.call-done = bf16[512,1024]{1,0:T(8,128)(2,1)} async-done(((bf16[128,1024]{1,0:T(8,128)(2,1)}), bf16[512,1024]{1,0:T(8,128)(2,1)}) %all-gather.17.cloned.1.call-update) | async-done | bytes 1048592 | tf_op jit(solution)/shard_map/all_gather | solution.py:81
  181.1 23.4 %reduce-scatter.17.cloned.1.call-done = bf16[128,1024]{1,0:T(8,128)(2,1)} async-done(((bf16[512,1024]{1,0:T(8,128)(2,1)}), bf16[128,1024]{1,0:T(8,128)(2,1)}) %reduce-scatter.17.cloned.1.call-update) | async-done | bytes 262160 | tf_op jit(solution)/shard_map/reduce_scatter | solution.py:89
  207.4 24.3 %all-gather.19.cloned.1.call-done = bf16[512,1024]{1,0:T(8,128)(2,1)} async-done(((bf16[128,1024]{1,0:T(8,128)(2,1)}), bf16[512,1024]{1,0:T(8,128)(2,1)}) %all-gather.19.cloned.1.call-update) | async-done | bytes 1048592 | tf_op jit(solution)/shard_map/all_gather | solution.py:81
  236.2 4.6 convolution_convert_fusion.8
  240.9 23.5 %reduce-scatter.19.cloned.1.call-done = bf16[128,1024]{1,0:T(8,128)(2,1)} async-done(((bf16[512,1024]{1,0:T(8,128)(2,1)}), bf16[128,1024]{1,0:T(8,128)(2,1)}) %reduce-scatter.19.cloned.1.call-update) | async-done | bytes 262160 | tf_op jit(solution)/shard_map/reduce_scatter | solution.py:89
  266.3 4.8 collective-permute-start.1
  281.2 21.5 %all-gather.21.cloned.1.call-done = bf16[512,1024]{1,0:T(8,128)(2,1)} async-done(((bf16[128,1024]{1,0:T(8,128)(2,1)}), bf16[512,1024]{1,0:T(8,128)(2,1)}) %all-gather.21.cloned.1.call-update) | async-done | bytes 1048592 | tf_op jit(solution)/shard_map/all_gather | solution.py:81
  314.6 21.7 %reduce-scatter.21.cloned.1.call-done = bf16[128,1024]{1,0:T(8,128)(2,1)} async-done(((bf16[512,1024]{1,0:T(8,128)(2,1)}), bf16[128,1024]{1,0:T(8,128)(2,1)}) %reduce-scatter.21.cloned.1.call-update) | async-done | bytes 262160 | tf_op jit(solution)/shard_map/reduce_scatter | solution.py:89
  342.4 20.4 %all-gather.25.cloned.1.call-done = bf16[512,1024]{1,0:T(8,128)(2,1)} async-done(((bf16[128,1024]{1,0:T(8,128)(2,1)}), bf16[512,1024]{1,0:T(8,128)(2,1)}) %all-gather.25.cloned.1.call-update) | async-done | bytes 1048592 | tf_op jit(solution)/shard_map/all_gather | solution.py:98
  362.9 3.8 fusion.95
  371.3 18.1 %all-gather.23.cloned.1.call-done = bf16[512,1024]{1,0:T(8,128)(2,1)} async-done(((bf16[128,1024]{1,0:T(8,128)(2,1)}), bf16[512,1024]{1,0:T(8,128)(2,1)}) %all-gather.23.cloned.1.call-update) | async-done | bytes 1048592 | tf_op jit(solution)/shard_map/all_gather | solution.py:81
  414.9 15.2 %reduce-scatter.25.cloned.1.call-done = bf16[128,1024]{1,0:T(8,128)(2,1)} async-done(((bf16[512,1024]{1,0:T(8,128)(2,1)}), bf16[128,1024]{1,0:T(8,128)(2,1)}) %reduce-scatter.25.cloned.1.call-update) | async-done | bytes 262160 | tf_op jit(solution)/shard_map/reduce_scatter | solution.py:106
  446.9 12.8 %all-gather.27.cloned.1.call-done = bf16[512,1024]{1,0:T(8,128)(2,1)} async-done(((bf16[128,1024]{1,0:T(8,128)(2,1)}), bf16[512,1024]{1,0:T(8,128)(2,1)}) %all-gather.27.cloned.1.call-update) | async-done | bytes 1048592 | tf_op jit(solution)/shard_map/all_gather | solution.py:98
  461.6 3.5 fusion.179
  480.3 20.2 %reduce-scatter.27.cloned.1.call-done = bf16[128,1024]{1,0:T(8,128)(2,1)} async-done(((bf16[512,1024]{1,0:T(8,128)(2,1)}), bf16[128,1024]{1,0:T(8,128)(2,1)}) %reduce-scatter.27.cloned.1.call-update) | async-done | bytes 262160 | tf_op jit(solution)/shard_map/reduce_scatter | solution.py:106
  506.7 7.8 collective-permute-done.2
  515.4 23.6 %all-gather.29.cloned.1.call-done = bf16[512,1024]{1,0:T(8,128)(2,1)} async-done(((bf16[128,1024]{1,0:T(8,128)(2,1)}), bf16[512,1024]{1,0:T(8,128)(2,1)}) %all-gather.29.cloned.1.call-update) | async-done | bytes 1048592 | tf_op jit(solution)/shard_map/all_gather | solution.py:98
  541.8 4.3 fusion.79
  551.6 22.3 %reduce-scatter.29.cloned.1.call-done = bf16[128,1024]{1,0:T(8,128)(2,1)} async-done(((bf16[512,1024]{1,0:T(8,128)(2,1)}), bf16[128,1024]{1,0:T(8,128)(2,1)}) %reduce-scatter.29.cloned.1.call-update) | async-done | bytes 262160 | tf_op jit(solution)/shard_map/reduce_scatter | solution.py:106
  584.0 3.8 fusion.325
  587.8 16.2 %all-gather.31.cloned.1.call-done = bf16[512,1024]{1,0:T(8,128)(2,1)} async-done(((bf16[128,1024]{1,0:T(8,128)(2,1)}), bf16[512,1024]{1,0:T(8,128)(2,1)}) %all-gather.31.cloned.1.call-update) | async-done | bytes 1048592 | tf_op jit(solution)/shard_map/all_gather | solution.py:98
  605.9 4.0 multiply_reduce_fusion.1
  621.7 22.3 %reduce-scatter.31.cloned.1.call-done = bf16[128,1024]{1,0:T(8,128)(2,1)} async-done(((bf16[512,1024]{1,0:T(8,128)(2,1)}), bf16[128,1024]{1,0:T(8,128)(2,1)}) %reduce-scatter.31.cloned.1.call-update) | async-done | bytes 262160 | tf_op jit(solution)/shard_map/reduce_scatter | solution.py:106
  651.0 7.8 collective-permute-done.3
  662.6 20.7 %all-gather.33.cloned.1.call-done = bf16[512,1024]{1,0:T(8,128)(2,1)} async-done(((bf16[128,1024]{1,0:T(8,128)(2,1)}), bf16[512,1024]{1,0:T(8,128)(2,1)}) %all-gather.33.cloned.1.call-update) | async-done | bytes 1048592 | tf_op jit(solution)/shard_map/all_gather | solution.py:98
  686.2 4.3 fusion.70
  694.8 5.2 fusion.50
  700.0 3.7 fusion.54
  707.3 3.9 fusion.318
  711.2 7.0 reduce-scatter.33.cloned.1.call-done
  722.8 5.2 fusion.58
  729.3 4.3 fusion.62
  734.5 4.6 convolution_convert_fusion.6
  747.7 5.3 fusion.60
  762.4 4.0 multiply_reduce_fusion
  777.3 4.4 fusion.29
  781.8 6.5 fusion.6
  792.1 3.7 fusion.28
  803.4 29.1 %all-reduce = (bf16[1,1024]{1,0:T(2,128)(2,1)S(1)}, bf16[1,1024]{1,0:T(2,128)(2,1)S(1)}) all-reduce(bf16[1,1024]{1,0:T(2,128)(2,1)S(1)} %stack.242, bf16[1,1024]{1,0:T(2,128)(2,1)S(1)} %stack.241), channel_id=1, replica_groups=mesh['section'=2,'dp'=16,'tensor'=4] {'dp'}, use_global_device_ids=true, to_apply=%region_70.71 | all-reduce | flops 2048 | bytes 8192 | tf_op jit(solution)/shard_map/psum | solution.py:347
  832.5 7.5 psum.51
  842.6 97.7 %all-reduce.4.cloned.1.call-done = (bf16[1,1024,3,256]{3,1,2,0:T(8,128)(2,1)}, bf16[1,256,1024]{2,1,0:T(8,128)(2,1)}, bf16[1,1024,2,656]{1,3,2,0:T(8,128)(2,1)}, bf16[1,656,1024]{2,1,0:T(8,128)(2,1)}) async-done(((bf16[1,1024,3,256]{3,1,2,0:T(8,128)(2,1)}, bf16[1,256,1024]{2,1,0:T(8,128)(2,1)}, bf16[1,1024,2,656]{1,3,2,0:T(8,128)(2,1)}, bf16[1,656,1024]{2,1,0:T(8,128)(2,1)}), ...) | async-done | bytes 6127632 | tf_op jit(solution)/shard_map/psum | solution.py:342
  940.2 5.0 broadcast_in_dim.293
  (626 shorter events, 264.9 us)
Async XLA Ops:
  7.2 93.7 %copy-start = (bf16[1,1024,2,656]{1,3,2,0:T(8,128)(2,1)S(1)}, bf16[1,1024,2,656]{1,3,2,0:T(8,128)(2,1)}, u32[]{:S(2)}) copy-start(bf16[1,1024,2,656]{1,3,2,0:T(8,128)(2,1)} %param.14) | copy-start | bytes 8060932
  7.2 32.2 %all-gather.13.cloned.1.call-start = ((), (), s32[]{:S(2)}) async-start(), calls=%async_computation.12 | async-start | bytes 1310720 | tf_op jit(solution)/shard_map/all_gather | solution.py:81
  13.0 59.6 %reduce-scatter.13.cloned.1.call-start = ((), (), s32[]{:S(2)}) async-start(), calls=%async_computation.13 | async-start | bytes 1310720 | tf_op jit(solution)/shard_map/reduce_scatter | solution.py:89
  16.1 26.0 %copy-start.150 = (s32[512]{0:T(512)}, s32[512]{0:T(512)S(1)}, u32[]{:S(2)}) copy-start(s32[512]{0:T(512)S(1)} %get-tuple-element.35) | copy-start | bytes 6148
  16.1 26.0 %copy-start.151 = (s32[512]{0:T(512)}, s32[512]{0:T(512)S(1)}, u32[]{:S(2)}) copy-start(s32[512]{0:T(512)S(1)} %get-tuple-element.198) | copy-start | bytes 6148
  17.9 25.6 %copy-start.79 = (f32[512,64]{0,1:T(8,128)}, f32[512,64]{0,1:T(8,128)S(1)}, u32[]{:S(2)}) copy-start(f32[512,64]{0,1:T(8,128)S(1)} %get-tuple-element.147) | copy-start | bytes 393220
  17.9 25.6 %copy-start.81 = (f32[512,64]{0,1:T(8,128)}, f32[512,64]{0,1:T(8,128)S(1)}, u32[]{:S(2)}) copy-start(f32[512,64]{0,1:T(8,128)S(1)} %get-tuple-element.148) | copy-start | bytes 393220
  47.6 25.0 %copy-start.9 = (bf16[2,128,1024]{2,1,0:T(8,128)(2,1)S(1)}, bf16[2,128,1024]{2,1,0:T(8,128)(2,1)}, u32[]{:S(2)}) copy-start(bf16[2,128,1024]{2,1,0:T(8,128)(2,1)} %param.8) | copy-start | bytes 1572868
  49.1 51.8 %all-gather.15.cloned.1.call-start = ((), (), s32[]{:S(2)}) async-start(), calls=%async_computation.14 | async-start | bytes 1310720 | tf_op jit(solution)/shard_map/all_gather | solution.py:81
  76.6 56.3 %reduce-scatter.15.cloned.1.call-start = ((), (), s32[]{:S(2)}) async-start(), calls=%async_computation.15 | async-start | bytes 1310720 | tf_op jit(solution)/shard_map/reduce_scatter | solution.py:89
  110.0 60.9 %all-gather.17.cloned.1.call-start = ((), (), s32[]{:S(2)}) async-start(), calls=%async_computation.16 | async-start | bytes 1310720 | tf_op jit(solution)/shard_map/all_gather | solution.py:81
  133.9 9.0 copy-start.121
  133.9 9.0 collective-permute-start
  144.8 59.7 %reduce-scatter.17.cloned.1.call-start = ((), (), s32[]{:S(2)}) async-start(), calls=%async_computation.17 | async-start | bytes 1310720 | tf_op jit(solution)/shard_map/reduce_scatter | solution.py:89
  181.1 50.7 %all-gather.19.cloned.1.call-start = ((), (), s32[]{:S(2)}) async-start(), calls=%async_computation.18 | async-start | bytes 1310720 | tf_op jit(solution)/shard_map/all_gather | solution.py:81
  207.4 57.0 %reduce-scatter.19.cloned.1.call-start = ((), (), s32[]{:S(2)}) async-start(), calls=%async_computation.19 | async-start | bytes 1310720 | tf_op jit(solution)/shard_map/reduce_scatter | solution.py:89
  236.2 28.2 %copy-start.122 = (bf16[128,1024]{1,0:T(8,128)(2,1)S(1)}, bf16[128,1024]{1,0:T(8,128)(2,1)}, u32[]{:S(2)}) copy-start(bf16[128,1024]{1,0:T(8,128)(2,1)} %copy-done.121) | copy-start | bytes 786436
  240.9 61.8 %all-gather.21.cloned.1.call-start = ((), (), s32[]{:S(2)}) async-start(), calls=%async_computation.20 | async-start | bytes 1310720 | tf_op jit(solution)/shard_map/all_gather | solution.py:81
  266.3 8.3 collective-permute-start.1
  276.6 59.7 %reduce-scatter.21.cloned.1.call-start = ((), (), s32[]{:S(2)}) async-start(), calls=%async_computation.21 | async-start | bytes 1310720 | tf_op jit(solution)/shard_map/reduce_scatter | solution.py:89
  312.8 50.1 %all-gather.25.cloned.1.call-start = ((), (), s32[]{:S(2)}) async-start(), calls=%async_computation.24 | async-start | bytes 1310720 | tf_op jit(solution)/shard_map/all_gather | solution.py:98
  314.6 74.8 %all-gather.23.cloned.1.call-start = ((), (), s32[]{:S(2)}) async-start(), calls=%async_computation.22 | async-start | bytes 1310720 | tf_op jit(solution)/shard_map/all_gather | solution.py:81
  339.1 90.9 %reduce-scatter.25.cloned.1.call-start = ((), (), s32[]{:S(2)}) async-start(), calls=%async_computation.25 | async-start | bytes 1310720 | tf_op jit(solution)/shard_map/reduce_scatter | solution.py:106
  406.4 53.4 %all-gather.27.cloned.1.call-start = ((), (), s32[]{:S(2)}) async-start(), calls=%async_computation.26 | async-start | bytes 1310720 | tf_op jit(solution)/shard_map/all_gather | solution.py:98
  414.8 15.2 %copy-start.156 = (f32[128]{0:T(128)}, f32[128]{0:T(128)S(1)}, u32[]{:S(2)}) copy-start(f32[128]{0:T(128)S(1)} %broadcast_multiply_fusion.13) | copy-start | bytes 1540
  414.9 15.2 %copy-start.158 = (f32[128]{0:T(128)}, f32[128]{0:T(128)S(1)}, u32[]{:S(2)}) copy-start(f32[128]{0:T(128)S(1)} %broadcast_multiply_fusion.15) | copy-start | bytes 1540
  435.6 64.9 %reduce-scatter.27.cloned.1.call-start = ((), (), s32[]{:S(2)}) async-start(), calls=%async_computation.27 | async-start | bytes 1310720 | tf_op jit(solution)/shard_map/reduce_scatter | solution.py:106
  477.0 62.0 %all-gather.29.cloned.1.call-start = ((), (), s32[]{:S(2)}) async-start(), calls=%async_computation.28 | async-start | bytes 1310720 | tf_op jit(solution)/shard_map/all_gather | solution.py:98
  479.6 24.4 %copy-start.163 = (f32[128]{0:T(128)S(1)}, f32[128]{0:T(128)}, u32[]{:S(2)}) copy-start(f32[128]{0:T(128)} %copy-done.162) | copy-start | bytes 1540
  505.4 9.1 copy-start.108
  505.4 9.1 collective-permute-start.2
  515.3 58.6 %reduce-scatter.29.cloned.1.call-start = ((), (), s32[]{:S(2)}) async-start(), calls=%async_computation.29 | async-start | bytes 1310720 | tf_op jit(solution)/shard_map/reduce_scatter | solution.py:106
  550.4 53.6 %all-gather.31.cloned.1.call-start = ((), (), s32[]{:S(2)}) async-start(), calls=%async_computation.30 | async-start | bytes 1310720 | tf_op jit(solution)/shard_map/all_gather | solution.py:98
  579.7 64.3 %reduce-scatter.31.cloned.1.call-start = ((), (), s32[]{:S(2)}) async-start(), calls=%async_computation.31 | async-start | bytes 1310720 | tf_op jit(solution)/shard_map/reduce_scatter | solution.py:106
  620.5 62.8 %all-gather.33.cloned.1.call-start = ((), (), s32[]{:S(2)}) async-start(), calls=%async_computation.32 | async-start | bytes 1310720 | tf_op jit(solution)/shard_map/all_gather | solution.py:98
  649.7 9.1 copy-start.120
  649.7 9.1 collective-permute-start.3
  658.8 62.3 %copy-start.76 = (bf16[128,1024]{1,0:T(8,128)(2,1)}, bf16[128,1024]{1,0:T(8,128)(2,1)S(1)}, u32[]{:S(2)}) copy-start(bf16[128,1024]{1,0:T(8,128)(2,1)S(1)} %collective-permute-done.3) | copy-start | bytes 786436
  659.6 58.6 %reduce-scatter.33.cloned.1.call-start = ((), (), s32[]{:S(2)}) async-start(), calls=%async_computation.33 | async-start | bytes 1310720 | tf_op jit(solution)/shard_map/reduce_scatter | solution.py:106
  694.7 65.8 %all-gather.35.cloned.1.call-start = ((), (), s32[]{:S(2)}) async-start(), calls=%async_computation.34 | async-start | bytes 1310720 | tf_op jit(solution)/shard_map/all_gather | solution.py:98
  707.3 10.9 %copy-start.157 = (f32[128]{0:T(128)S(1)}, f32[128]{0:T(128)}, u32[]{:S(2)}) copy-start(f32[128]{0:T(128)} %copy-done.156) | copy-start | bytes 1540
  722.7 73.7 %reduce-scatter.23.cloned.1.call-start = ((), (), s32[]{:S(2)}) async-start(), calls=%async_computation.23 | async-start | bytes 1310720 | tf_op jit(solution)/shard_map/reduce_scatter | solution.py:89
  739.1 61.3 %reduce-scatter.35.cloned.1.call-start = ((), (), s32[]{:S(2)}) async-start(), calls=%async_computation.35 | async-start | bytes 1310720 | tf_op jit(solution)/shard_map/reduce_scatter | solution.py:106
  741.2 11.8 %copy-start.50 = (bf16[3,512,656]{1,2,0:T(8,128)(2,1)}, bf16[3,512,656]{1,2,0:T(8,128)(2,1)S(1)}, u32[]{:S(2)}) copy-start(bf16[3,512,656]{1,2,0:T(8,128)(2,1)S(1)} %pad_maximum_fusion.4) | copy-start | bytes 6045700
  777.0 163.2 %all-reduce.4.cloned.1.call-start = ((), (), s32[]{:S(2)}) async-start(), calls=%async_computation.36 | async-start | bytes 12255232 | tf_op jit(solution)/shard_map/psum | solution.py:342
  781.8 9.3 copy-start.58
  797.8 42.2 %copy-start.27 = (bf16[2,128,1024]{2,1,0:T(8,128)(2,1)S(1)}, bf16[2,128,1024]{2,1,0:T(8,128)(2,1)}, u32[]{:S(2)}) copy-start(bf16[2,128,1024]{2,1,0:T(8,128)(2,1)} %param.9) | copy-start | bytes 1572868
  800.5 39.6 %copy-start.75 = (bf16[128,1024]{1,0:T(8,128)(2,1)S(1)}, bf16[128,1024]{1,0:T(8,128)(2,1)}, u32[]{:S(2)}) copy-start(bf16[128,1024]{1,0:T(8,128)(2,1)} %reduce-scatter.35.cloned.1.call-done) | copy-start | bytes 786436
  (158 other events, 415.7 us)
Sparse Core Ops, SparseCore 0:
  13.1 26.2 all-gather.12
  49.2 23.3 reduce-scatter.12
  76.7 24.1 all-gather.14
  110.1 22.6 reduce-scatter.14
  145.0 25.8 all-gather.16
  181.2 23.3 reduce-scatter.16
  207.5 24.2 all-gather.18
  241.0 23.3 reduce-scatter.18
  276.7 25.9 all-gather.20
  312.9 23.3 reduce-scatter.20
  338.7 24.1 all-gather.24
  365.1 24.2 all-gather.22
  406.5 23.5 reduce-scatter.24
  435.8 23.9 all-gather.26
  477.1 23.3 reduce-scatter.26
  515.4 23.4 all-gather.28
  550.5 23.3 reduce-scatter.28
  579.8 24.1 all-gather.30
  620.6 23.3 reduce-scatter.30
  659.8 23.5 all-gather.32
  694.8 23.3 reduce-scatter.32
  722.8 24.1 all-gather.34
  750.0 23.3 reduce-scatter.22
  777.1 23.2 reduce-scatter.34
  803.8 136.3 all-reduce.3
where the time goes:
time: 968 us; the launch traced here: 957 us
  waiting for transfers between devices  549 us (57%)
  matrix products  146 us (15%)
  other arithmetic  145 us (15%)
  local copies, waits for them, and re-layouts  47.5 us (5%)
  blocking collectives  36.6 us (4%)
  between operations  16.6 us (2%)
  starting transfers between devices  15.7 us (2%)
    all_gather x6, waiting for transfers between devices, gather_rows(): return lax.all_gather(normed, 'tensor', axis=0, tiled=True)  131 us
    reduce_scatter x6, waiting for transfers between devices, scatter_rows(): lax.psum_scatter(row_term(jnp.int32(0), lax.axis_size('tensor') * row_cou...  115 us
    psum x1, waiting for transfers between devices, local(): lax.psum(acc_qkv.astype(jnp.bfloat16), 'dp').astype(jnp.float32)  97.7 us
    all_gather x6, waiting for transfers between devices, gather_grads(): return lax.all_gather(gradients, 'tensor', axis=0, tiled=True)  93.7 us
    reduce_scatter x6, waiting for transfers between devices, scatter_grads(): lax.psum_scatter(row_term(jnp.int32(0), lax.axis_size('tensor') * row_cou...  88.8 us
    dot_general x12, matrix products, contract_rows(): lax.dot_general(left_rows, right_rows, (((0,), (0,)), ((), ())), preferre...  38.3 us
    unnamed x355, local copies, waits for them, and re-layouts  38 us
    dot_general x12, matrix products, contract_last(): lax.dot_general(left_rows, weight, (((1,), (1,)), ((), ())), preferred_el...  29.2 us
  transfers between devices with their start and end apart: 29, of which 27 were waited for; matrix products, arithmetic and copies ran while one was open for 15% of the time, Pallas kernels for 0%

commit v1 on v0

v1 whole, which is shorter than its diff:
```python
import jax
import jax.numpy as jnp
from jax import lax
from jax.sharding import Mesh
from jax.sharding import PartitionSpec as P

HEAD_DIM = 64
WINDOW = 128

epsilon = 1e-05
bf16 = jnp.bfloat16
f32 = jnp.float32

DP = ("zlo", "x", "core")


def around(block, axis, distance):
    count = lax.axis_size(axis)
    return lax.ppermute(block, axis, [(i, (i + distance) % count) for i in range(count)])


def swap_core(block):
    return lax.ppermute(block, "core", [(0, 1), (1, 0)])


def swap_section(block):
    return lax.ppermute(block, "section", [(0, 1), (1, 0)])


def swap_layer(block):
    return lax.ppermute(block, ("section", "zlo"), [(0, 3), (1, 2), (2, 1), (3, 0)])


def gather_rows(block):
    ahead2 = around(block, "tensor", 2)
    ahead1 = around(block, "tensor", -1)
    ahead3 = around(block, "tensor", 1)
    return jnp.concatenate([block, ahead1, ahead2, ahead3], axis=0)


def scatter_rows(terms, row_count):
    parts = [terms[k * row_count : (k + 1) * row_count] for k in range(4)]
    sent2 = around(parts[2].astype(bf16), "tensor", 2)
    sent1 = around(parts[1].astype(bf16), "tensor", 1)
    sent3 = around(parts[3].astype(bf16), "tensor", -1)
    return (
        parts[0].astype(f32) + sent2.astype(f32) + sent1.astype(f32) + sent3.astype(f32)
    )


def sum_tensor(block):
    return (
        block
        + around(block, "tensor", 2)
        + around(block, "tensor", 1)
        + around(block, "tensor", -1)
    )


def layer_norm(values, gain_scale):
    centered = values - jnp.mean(values, axis=-1, keepdims=True)
    variance = jnp.mean(centered * centered, axis=-1, keepdims=True)
    return centered * lax.rsqrt(variance + epsilon) * gain_scale


def doc_layout(doc_lengths, indices):
    doc_ends = jnp.cumsum(doc_lengths)
    passed = indices[:, None] >= doc_ends[None, :]
    doc_ids = jnp.sum(passed.astype(jnp.int32), axis=1)
    starts = jnp.sum(jnp.where(passed, doc_lengths[None, :], 0), axis=1)
    return (doc_ids, indices - starts)


def rope_tables(positions, rope_base):
    half_dim = HEAD_DIM // 2
    inverse = rope_base ** (-2.0 * jnp.arange(half_dim, dtype=f32) / HEAD_DIM)
    angles = positions.astype(f32)[..., None] * inverse
    angles = jnp.concatenate([angles, angles], axis=-1)
    return (jnp.cos(angles), jnp.sin(angles))


def rotate(values, cosine_table, sine_table):
    half_dim = values.shape[-1] // 2
    turned = jnp.concatenate([-values[..., half_dim:], values[..., :half_dim]], axis=-1)
    return values * cosine_table[..., None, :] + turned * sine_table[..., None, :]


def rotate_back(gradients, cosine_table, sine_table):
    half_dim = gradients.shape[-1] // 2
    scaled = gradients * sine_table[..., None, :]
    turned = jnp.concatenate([scaled[..., half_dim:], -scaled[..., :half_dim]], axis=-1)
    return gradients * cosine_table[..., None, :] + turned


def masked_scores(queries, keys_rot, allowed):
    scores = jnp.einsum(
        "qhd,khd->hqk", queries, keys_rot, preferred_element_type=f32
    ) * HEAD_DIM ** (-0.5)
    return jnp.where(allowed[None], scores, -1e30)


def contract_rows(left_rows, right_rows):
    return lax.dot_general(
        left_rows, right_rows, (((0,), (0,)), ((), ())), preferred_element_type=f32
    )


def contract_last(left_rows, weight):
    return lax.dot_general(
        left_rows, weight, (((1,), (1,)), ((), ())), preferred_element_type=f32
    )


def times(left_rows, weight):
    return jnp.dot(left_rows, weight, preferred_element_type=f32)


def forward_layer(inputs, gain_pair, weights, allowed, tables):
    w_qkv, w_out, w_up, w_down = weights
    row_count = inputs.shape[0]
    normed_all = gather_rows(layer_norm(inputs, gain_pair[0]).astype(bf16))
    full_rows = normed_all.shape[0]
    local_width = w_out.shape[0]
    projected = times(normed_all, w_qkv).reshape(full_rows, 3, -1, HEAD_DIM)
    queries = rotate(projected[:, 0], *tables).astype(bf16)
    keys_rot = rotate(projected[:, 1], *tables).astype(bf16)
    values_in = projected[:, 2].astype(bf16)
    scores = masked_scores(queries, keys_rot, allowed)
    largest = jnp.max(scores, axis=2, keepdims=True)
    exp_scores = jnp.exp(scores - largest)
    totals = jnp.sum(exp_scores, axis=2, keepdims=True)
    soft_weights = (exp_scores / totals).astype(bf16)
    log_totals = largest + jnp.log(totals)
    attended = jnp.einsum("hqk,khd->qhd", soft_weights, values_in, preferred_element_type=f32)
    attended = attended.reshape(full_rows, local_width).astype(bf16)
    resid_mid = inputs + scatter_rows(times(attended, w_out), row_count)
    normed_mid_all = gather_rows(layer_norm(resid_mid, gain_pair[1]).astype(bf16))
    hidden = times(normed_mid_all, w_up)
    local_hidden = hidden.shape[1] // 2
    gelu_in = hidden[:, :local_hidden]
    gate_mult = hidden[:, local_hidden:]
    mixed_rows = (jax.nn.gelu(gelu_in, approximate=False) * gate_mult).astype(bf16)
    result = resid_mid + scatter_rows(times(mixed_rows, w_down), row_count)
    kept = (
        inputs,
        resid_mid,
        normed_all,
        queries,
        keys_rot,
        values_in,
        log_totals,
        attended,
        normed_mid_all,
        gelu_in,
        gate_mult,
        mixed_rows,
    )
    return (result, kept)


def gelu_product(first_half, second_half):
    return jax.nn.gelu(first_half, approximate=False) * second_half


def backward_ffn(grad_result, kept, gain_pair, weights):
    w_up, w_down = weights[2], weights[3]
    resid_mid, normed_mid_all = kept[1], kept[8]
    gelu_in, gate_mult, mixed_rows = kept[9], kept[10], kept[11]
    row_count = grad_result.shape[0]
    grad_ffn_all = gather_rows(grad_result.astype(bf16))
    grad_mixed = contract_last(grad_ffn_all, w_down)
    unused, pull_gelu = jax.vjp(gelu_product, gelu_in, gate_mult)
    grad_gelu, grad_gate = pull_gelu(grad_mixed)
    grad_hidden = jnp.concatenate([grad_gelu, grad_gate], axis=1).astype(bf16)
    grad_normed_mid = scatter_rows(contract_last(grad_hidden, w_up), row_count)
    unused, pull_norm = jax.vjp(layer_norm, resid_mid, gain_pair[1])
    grad_resid, grad_gain = pull_norm(grad_normed_mid)
    grad_w_down = contract_rows(mixed_rows, grad_ffn_all).astype(bf16)
    grad_w_up = contract_rows(normed_mid_all, grad_hidden).astype(bf16)
    return (grad_result + grad_resid, grad_w_up, grad_w_down, grad_gain)


def backward_attn(grad_mid, kept, gain_pair, weights, allowed, tables):
    w_qkv, w_out = weights[0], weights[1]
    inputs, normed_all = kept[0], kept[2]
    queries, keys_rot, values_in, log_totals, attended = kept[3:8]
    row_count = grad_mid.shape[0]
    full_rows = normed_all.shape[0]
    grad_att_all = gather_rows(grad_mid.astype(bf16))
    grad_attended = contract_last(grad_att_all, w_out).astype(bf16).reshape(queries.shape)
    scores = masked_scores(queries, keys_rot, allowed)
    soft_exact = jnp.exp(scores - log_totals)
    soft_weights = soft_exact.astype(bf16)
    grad_values = jnp.einsum(
        "hqk,qhd->khd", soft_weights, grad_attended, preferred_element_type=f32
    )
    grad_soft = jnp.einsum("qhd,khd->hqk", grad_attended, values_in, preferred_element_type=f32)
    row_dots = jnp.sum(soft_exact * grad_soft, axis=2, keepdims=True)
    grad_scores = (soft_exact * (grad_soft - row_dots)).astype(bf16)
    grad_queries = jnp.einsum(
        "hqk,khd->qhd", grad_scores, keys_rot, preferred_element_type=f32
    ) * HEAD_DIM ** (-0.5)
    grad_keys = jnp.einsum(
        "hqk,qhd->khd", grad_scores, queries, preferred_element_type=f32
    ) * HEAD_DIM ** (-0.5)
    grad_projected = jnp.stack(
        [
            rotate_back(grad_queries, *tables),
            rotate_back(grad_keys, *tables),
            grad_values,
        ],
        axis=1,
    )
    grad_projected = grad_projected.astype(bf16).reshape(full_rows, -1)
    grad_normed = scatter_rows(contract_last(grad_projected, w_qkv), row_count)
    unused, pull_norm = jax.vjp(layer_norm, inputs, gain_pair[0])
    grad_resid, grad_gain = pull_norm(grad_normed)
    grad_w_out = contract_rows(attended, grad_att_all).astype(bf16)
    grad_w_qkv = contract_rows(normed_all, grad_projected).astype(bf16)
    return (grad_mid + grad_resid, grad_w_qkv, grad_w_out, grad_gain)


def other_layer(own, core_index):
    half = own.shape[0] // 2
    sent = jnp.where(core_index == 0, own[:half], own[half:])
    got = swap_layer(sent)
    beside = swap_core(got)
    low = jnp.where(core_index == 0, got, beside)
    high = jnp.where(core_index == 0, beside, got)
    return jnp.concatenate([low, high], axis=0)


def reduce_part(grads):
    core_index = lax.axis_index("core")
    half = grads.shape[0] // 2
    sent = jnp.where(core_index == 0, grads[half:], grads[:half])
    held = jnp.where(core_index == 0, grads[:half], grads[half:])
    both = (held.astype(f32) + swap_core(sent).astype(f32)).astype(bf16)
    return lax.psum_scatter(both, ("zlo", "x"), scatter_dimension=0, tiled=True)


def reduce_part_now(grads):
    core_index = lax.axis_index("core")
    half = grads.shape[0] // 2
    sent = jnp.where(core_index == 0, grads[half:], grads[:half])
    held = jnp.where(core_index == 0, grads[:half], grads[half:])
    both = (held.astype(f32) + swap_core(sent).astype(f32)).astype(bf16)
    pieces = lax.all_to_all(both, ("zlo", "x"), 0, 0, tiled=True)
    pieces = pieces.reshape(8, -1, pieces.shape[1])
    return jnp.sum(pieces.astype(f32), axis=0).astype(bf16)


def spread_part(part):
    core_index = lax.axis_index("core")
    half = lax.all_gather(part, ("zlo", "x"), axis=0, tiled=True)
    beside = swap_core(half)
    low = jnp.where(core_index == 0, half, beside)
    high = jnp.where(core_index == 0, beside, half)
    return jnp.concatenate([low, high], axis=0)


def pad_rows(block, rows):
    return jnp.concatenate([block, jnp.zeros((rows - block.shape[0], block.shape[1]), block.dtype)])


def join_sections(is_first, part_first, part_second):
    own = jnp.where(is_first, part_first, part_second)
    sent = jnp.where(is_first, part_second, part_first)
    return (own.astype(f32) + swap_section(sent).astype(f32)).astype(bf16)


def local(tokens, cotangent, lengths, gains, w_qkv, w_out, w_up, w_down):
    section_index = lax.axis_index("section")
    core_index = lax.axis_index("core")
    is_first = section_index == 0
    row_count = tokens.shape[1]
    full_rows = row_count * lax.axis_size("tensor")
    own = (
        w_qkv[0].reshape(w_qkv.shape[1], -1),
        w_out[0],
        w_up[0].reshape(w_up.shape[1], -1),
        w_down[0],
    )
    others = tuple(other_layer(weight, core_index) for weight in own)
    gains_other = swap_layer(gains[0])
    layer0 = tuple(jnp.where(is_first, a, b) for a, b in zip(own, others))
    layer1 = tuple(jnp.where(is_first, b, a) for a, b in zip(own, others))
    gains0 = jnp.where(is_first, gains[0], gains_other)
    gains1 = jnp.where(is_first, gains_other, gains[0])
    start_rows = jnp.where(is_first, tokens[0], tokens[1])
    end_grads = jnp.where(is_first, cotangent[0], cotangent[1])
    doc_lengths = jnp.where(is_first, lengths[0, 0], lengths[1, 0])
    indices = jnp.arange(full_rows, dtype=jnp.int32)
    indices = (indices + lax.axis_index("tensor") * row_count) % full_rows
    doc_ids, positions = doc_layout(doc_lengths, indices)
    same_doc = doc_ids[:, None] == doc_ids[None, :]
    near = jnp.abs(indices[:, None] - indices[None, :]) <= WINDOW // 2
    allowed0 = same_doc & near
    allowed1 = same_doc
    tables0 = rope_tables(positions, 10000.0)
    tables1 = rope_tables(positions, 160000.0)

    out0, kept0 = forward_layer(start_rows.astype(f32), gains0, layer0, allowed0, tables0)
    out0 = out0.astype(bf16)
    out1, kept1 = forward_layer(out0.astype(f32), gains1, layer1, allowed1, tables1)
    out1 = out1.astype(bf16)
    mid1, up1, down1, gain_mid1 = backward_ffn(end_grads.astype(f32), kept1, gains1, layer1)
    in1, qkv1, wout1, gain_first1 = backward_attn(mid1, kept1, gains1, layer1, allowed1, tables1)
    in1 = in1.astype(bf16)
    mid0, up0, down0, gain_mid0 = backward_ffn(in1.astype(f32), kept0, gains0, layer0)
    in0, qkv0, wout0, gain_first0 = backward_attn(mid0, kept0, gains0, layer0, allowed0, tables0)
    in0 = in0.astype(bf16)

    down_rows = down1.shape[0]
    padded = -(-down_rows // 256) * 256
    part_up1 = reduce_part(up1)
    part_down1 = reduce_part(pad_rows(down1, padded))
    part_qkv1 = reduce_part(qkv1)
    part_out1 = reduce_part(wout1)
    part_up0 = reduce_part(up0)
    part_down0 = reduce_part(pad_rows(down0, padded))
    up_sum = spread_part(join_sections(is_first, part_up0, part_up1))
    down_sum = spread_part(join_sections(is_first, part_down0, part_down1))[:down_rows]
    part_qkv0 = reduce_part_now(qkv0)
    part_out0 = reduce_part_now(wout0)
    qkv_sum = spread_part(join_sections(is_first, part_qkv0, part_qkv1))
    out_sum = spread_part(join_sections(is_first, part_out0, part_out1))

    gain0 = jnp.stack([gain_first0, gain_mid0])
    gain1 = jnp.stack([gain_first1, gain_mid1])
    gain_own = jnp.where(is_first, gain0, gain1)
    gain_sent = jnp.where(is_first, gain1, gain0)
    gain_total = gain_own + swap_section(gain_sent)
    gain_total = sum_tensor(gain_total)
    gain_total = gain_total + swap_core(gain_total)
    gain_total = (
        gain_total
        + around(gain_total, "x", 1)
        + around(gain_total, "x", 2)
        + around(gain_total, "x", 3)
    )
    gain_total = gain_total + around(gain_total, "zlo", 1)

    got_out = swap_section(jnp.where(is_first, out1, out0))
    section_out = jnp.stack(
        [jnp.where(is_first, out0, got_out), jnp.where(is_first, got_out, out1)]
    )
    got_in = swap_section(jnp.where(is_first, in1, in0))
    input_grads = jnp.stack(
        [jnp.where(is_first, in0, got_in), jnp.where(is_first, got_in, in1)]
    )
    return (
        section_out[None],
        input_grads[None],
        gain_total[None],
        qkv_sum.astype(f32).reshape(w_qkv.shape),
        out_sum.astype(f32)[None],
        up_sum.astype(f32).reshape(w_up.shape),
        down_sum.astype(f32)[None],
    )


def solution(mesh):
    sizes = dict(zip(mesh.axis_names, mesh.devices.shape))
    fine = Mesh(
        mesh.devices.reshape(sizes["section"], 2, sizes["dp"] // 4, 2, sizes["tensor"]),
        ("section", "zlo", "x", "core", "tensor"),
    )
    rows = ("zlo", "x", "core", "tensor")
    in_specs = (
        P(None, rows, None),
        P(None, rows, None),
        P(None, DP, None),
        P("section", None, None),
        P("section", None, None, "tensor"),
        P("section", "tensor", None),
        P("section", None, None, "tensor"),
        P("section", "tensor", None),
    )
    out_specs = (
        P("section", None, rows, None),
        P("section", None, rows, None),
        P("section", None, None),
        P("section", None, None, "tensor"),
        P("section", "tensor", None),
        P("section", None, None, "tensor"),
        P("section", "tensor", None),
    )
    return jax.shard_map(local, mesh=fine, in_specs=in_specs, out_specs=out_specs, check_vma=False)
```

time: 968 us -> 653 us (0.67)
  waiting for transfers between devices: 549 us -> 231 us
  starting transfers between devices: 15.7 us -> 134 us
  matrix products: 146 us -> 56.7 us
  other arithmetic: 145 us -> 84.3 us
  blocking collectives: 36.6 us -> 82.8 us
    all_gather x12 -> x1, waiting for transfers between devices: 225 us -> 0.01 us  [spread_part(): half = lax.all_gather(part, ('zlo', 'x'), axis=0, tiled=True)]
    ppermute x4 -> x84, waiting for transfers between devices: 22.7 us -> 218 us  [the longest x55 136 us: around(): lax.ppermute(block, axis, [(i, (i + distance) % count) for i in range(cou...]
    reduce_scatter x12 -> x6, waiting for transfers between devices: 204 us -> 13.6 us  [reduce_part(): return lax.psum_scatter(both, ('zlo', 'x'), scatter_dimension=0, tiled=True)]
    ppermute x4 -> x84, starting transfers between devices: 12.8 us -> 125 us  [the longest x55 69.1 us: around(): lax.ppermute(block, axis, [(i, (i + distance) % count) for i in range(cou...]
    psum x1 -> x0, waiting for transfers between devices: 97.7 us -> none  [local(): lax.psum(acc_qkv.astype(jnp.bfloat16), 'dp').astype(jnp.float32)]
    all_gather x0 -> x3, blocking collectives: none -> 82.8 us  [spread_part(): half = lax.all_gather(part, ('zlo', 'x'), axis=0, tiled=True)]
    psum x2 -> x0, blocking collectives: 36.6 us -> none  [the longest x1 29.1 us: local(): lax.psum(ffn_sums[2].astype(jnp.bfloat16), 'dp').astype(jnp.float32)]
    dot_general x21 -> x12, matrix products: 53.8 us -> 17.7 us  [the longest x8 14.3 us: times(): return jnp.dot(left_rows, weight, preferred_element_type=f32)]
  transfers between devices with their start and end apart: 29 -> 93, of which waited for: 27 -> 45; matrix products, arithmetic and copies ran while one was open for 15% -> 21% of each run, Pallas kernels for 0% -> 0%
where the time goes in v1:
time: 653 us; the launch traced here: 643 us
  waiting for transfers between devices  231 us (35%)
  starting transfers between devices  134 us (21%)
  other arithmetic  84.3 us (13%)
  blocking collectives  82.8 us (13%)
  matrix products  56.7 us (9%)
  local copies, waits for them, and re-layouts  38 us (6%)
  between operations  16.6 us (3%)
    ppermute x55, waiting for transfers between devices, around(): lax.ppermute(block, axis, [(i, (i + distance) % count) for i in range(cou...  136 us
    all_gather x3, blocking collectives, spread_part(): half = lax.all_gather(part, ('zlo', 'x'), axis=0, tiled=True)  82.8 us
    ppermute x55, starting transfers between devices, around(): lax.ppermute(block, axis, [(i, (i + distance) % count) for i in range(cou...  69.1 us
    ppermute x5, waiting for transfers between devices, swap_layer(): lax.ppermute(block, ('section', 'zlo'), [(0, 3), (1, 2), (2, 1), (3, 0)])  51 us
    ppermute x17, starting transfers between devices, swap_core(): return lax.ppermute(block, 'core', [(0, 1), (1, 0)])  40 us
    ppermute x7, waiting for transfers between devices, swap_section(): return lax.ppermute(block, 'section', [(0, 1), (1, 0)])  26.1 us
    unnamed x224, local copies, waits for them, and re-layouts  20.4 us
    dot_general x8, matrix products, contract_last(): lax.dot_general(left_rows, weight, (((1,), (1,)), ((), ())), preferred_el...  16.4 us
  transfers between devices with their start and end apart: 93, of which 45 were waited for; matrix products, arithmetic and copies ran while one was open for 21% of the time, Pallas kernels for 0%

profile of v1, /device:TPU:1, one launch (start us, length us, event | category | flops | bytes accessed | tf_op | source)
XLA Modules:
  0.0 643.2 jit_solution(14875652956671286253)
XLA Ops:
  7.2 4.7 collective-permute-start
  31.0 51.0 %collective-permute-done.4 = bf16[512,768]{1,0:T(8,128)(2,1)} collective-permute-done((bf16[512,768]{1,0:T(8,128)(2,1)S(1)}, bf16[512,768]{1,0:T(8,128)(2,1)}, u32[]{:S(2)}, u32[]{:S(2)}) %collective-permute-start.4) | collective-permute-done | bytes 786464 | tf_op jit(solution)/shard_map/ppermute | solution.py:31
  86.4 2.9 collective-permute-start.2
  119.3 7.1 %collective-permute-done.10 = bf16[128,1024]{1,0:T(8,128)(2,1)S(1)} collective-permute-done((bf16[128,1024]{1,0:T(8,128)(2,1)S(1)}, bf16[128,1024]{1,0:T(8,128)(2,1)S(1)}, u32[]{:S(2)}, u32[]{:S(2)}) %collective-permute-start.10) | collective-permute-done | bytes 262176 | tf_op jit(solution)/shard_map/ppermute | solution.py:19
  133.9 3.2 bitcast_select_fusion
  137.1 6.4 collective-permute-done.12
  145.2 3.8 multiply_convert_fusion.5
  151.1 2.8 collective-permute-start.20
  153.9 4.3 collective-permute-done.18
  158.2 6.9 %collective-permute-done.20 = bf16[128,1024]{1,0:T(8,128)(2,1)S(1)} collective-permute-done((bf16[128,1024]{1,0:T(8,128)(2,1)S(1)}, bf16[128,1024]{1,0:T(8,128)(2,1)S(1)}, u32[]{:S(2)}, u32[]{:S(2)}) %collective-permute-start.20) | collective-permute-done | bytes 262176 | tf_op jit(solution)/shard_map/ppermute | solution.py:19
  176.2 7.2 %collective-permute-done.22 = bf16[128,1024]{1,0:T(8,128)(2,1)} collective-permute-done((bf16[128,1024]{1,0:T(8,128)(2,1)}, bf16[128,1024]{1,0:T(8,128)(2,1)}, u32[]{:S(2)}, u32[]{:S(2)}) %collective-permute-start.22) | collective-permute-done | bytes 262176 | tf_op jit(solution)/shard_map/ppermute | solution.py:19
  206.3 3.5 collective-permute-done.26
  218.8 9.6 %collective-permute-done.29 = bf16[128,1024]{1,0:T(8,128)(2,1)S(1)} collective-permute-done((bf16[128,1024]{1,0:T(8,128)(2,1)S(1)}, bf16[128,1024]{1,0:T(8,128)(2,1)S(1)}, u32[]{:S(2)}, u32[]{:S(2)}) %collective-permute-start.29) | collective-permute-done | bytes 262176 | tf_op jit(solution)/shard_map/ppermute | solution.py:19
  232.7 3.0 collective-permute-done.34
  235.6 5.1 add_convert_fusion.7
  248.1 3.6 collective-permute-done.37
  251.7 5.2 collective-permute-done.39
  268.3 6.0 collective-permute-done.41
  284.2 2.8 collective-permute-start.45
  290.8 7.9 %collective-permute-done.45 = bf16[128,1024]{1,0:T(8,128)(2,1)S(1)} collective-permute-done((bf16[128,1024]{1,0:T(8,128)(2,1)S(1)}, bf16[128,1024]{1,0:T(8,128)(2,1)S(1)}, u32[]{:S(2)}, u32[]{:S(2)}) %collective-permute-start.45) | collective-permute-done | bytes 262176 | tf_op jit(solution)/shard_map/ppermute | solution.py:19
  301.6 3.2 collective-permute-start.47
  305.7 3.6 collective-permute-done.48
  309.2 7.2 %collective-permute-done.47 = bf16[128,1024]{1,0:T(8,128)(2,1)} collective-permute-done((bf16[128,1024]{1,0:T(8,128)(2,1)S(1)}, bf16[128,1024]{1,0:T(8,128)(2,1)}, u32[]{:S(2)}, u32[]{:S(2)}) %collective-permute-start.47) | collective-permute-done | bytes 262176 | tf_op jit(solution)/shard_map/ppermute | solution.py:19
  320.9 3.0 add_convert_fusion
  326.6 3.2 convolution_convert_fusion.1
  355.0 5.1 collective-permute-done.32
  363.0 16.7 %collective-permute-done.33 = bf16[128,1024]{1,0:T(8,128)(2,1)S(1)} collective-permute-done((bf16[128,1024]{1,0:T(8,128)(2,1)S(1)}, bf16[128,1024]{1,0:T(8,128)(2,1)S(1)}, u32[]{:S(2)}, u32[]{:S(2)}) %collective-permute-start.33) | collective-permute-done | bytes 262176 | tf_op jit(solution)/shard_map/ppermute | solution.py:27
  382.0 4.0 fusion.195
  391.3 3.7 collective-permute-done.49
  395.0 5.8 collective-permute-done.51
  402.5 3.0 collective-permute-start.53
  407.2 3.9 collective-permute-done.54
  411.0 5.8 collective-permute-done.53
  435.5 3.4 collective-permute-done.55
  440.1 4.2 collective-permute-done.57
  447.1 3.1 collective-permute-done.59
  455.0 4.0 all-to-all-start.1
  462.7 2.8 collective-permute-start.66
  479.2 3.7 all-to-all-start
  484.4 31.5 %all_gather.13 = bf16[128,1024]{1,0:T(8,128)(2,1)S(1)} all-gather(bf16[16,1024]{1,0:T(8,128)(2,1)S(1)} %add_convert_fusion.15), channel_id=1, replica_groups=mesh['section'=2,'zlo'=2,'x'=4,'core'=2,'tensor'=4] {'zlo','x'}, dimensions={0}, use_global_device_ids=true | all-gather | bytes 294912 | tf_op jit(solution)/shard_map/all_gather | solution.py:255
  515.9 6.2 collective-permute-start.75
  524.2 6.3 collective-permute-done.70
  530.6 13.5 %reduce-scatter.15.cloned.1.call-done = bf16[48,1024]{1,0:T(8,128)(2,1)} async-done(((bf16[384,1024]{1,0:T(8,128)(2,1)}), bf16[48,1024]{1,0:T(8,128)(2,1)}) %reduce-scatter.15.cloned.1.call-update) | async-done | bytes 98320 | tf_op jit(solution)/shard_map/reduce_scatter | solution.py:239
  547.6 25.8 %all_gather.12 = bf16[512,768]{1,0:T(8,128)(2,1)S(1)} all-gather(bf16[64,768]{1,0:T(8,128)(2,1)S(1)} %add_convert_fusion.14), channel_id=1, replica_groups=mesh['section'=2,'zlo'=2,'x'=4,'core'=2,'tensor'=4] {'zlo','x'}, dimensions={0}, use_global_device_ids=true | all-gather | bytes 884736 | tf_op jit(solution)/shard_map/all_gather | solution.py:255
  573.5 11.2 %collective-permute-start.71 = (bf16[512,768]{1,0:T(8,128)(2,1)S(1)}, bf16[512,768]{1,0:T(8,128)(2,1)S(1)}, u32[]{:S(2)}, u32[]{:S(2)}) collective-permute-start(bf16[512,768]{1,0:T(8,128)(2,1)S(1)} %all_gather.12), channel_id=1, source_target_pairs={{0,4},{4,0},{1,5},{5,1},{2,6},{6,2},{3,7},{7,3},{8,12},{12,8},{9,1... | collective-permute-start | bytes 2359304 | tf_op jit(solution)/shard_map/ppermute | solution.py:23
  585.6 25.5 %all_gather.15 = bf16[384,1024]{1,0:T(8,128)(2,1)} all-gather(bf16[48,1024]{1,0:T(8,128)(2,1)S(1)} %add_convert_fusion.13), channel_id=1, replica_groups=mesh['section'=2,'zlo'=2,'x'=4,'core'=2,'tensor'=4] {'zlo','x'}, dimensions={0}, use_global_device_ids=true | all-gather | bytes 884736 | tf_op jit(solution)/shard_map/all_gather | solution.py:255
  611.1 6.2 collective-permute-start.83
  632.8 3.2 maximum_convert_fusion
  (560 shorter events, 261.1 us)
Async XLA Ops:
  7.2 465.0 %reduce-scatter.13.cloned.1.call-start = ((), (), s32[]{:S(2)}) async-start(), calls=%async_computation.9 | async-start | bytes 294912 | tf_op jit(solution)/shard_map/reduce_scatter | solution.py:239
  7.2 76.7 %collective-permute-start = (f32[2,1024]{1,0:T(2,128)}, f32[2,1024]{1,0:T(2,128)S(1)}, u32[]{:S(2)}, u32[]{:S(2)}) collective-permute-start(f32[2,1024]{1,0:T(2,128)} %bitcast.299), channel_id=1, source_target_pairs={{0,96},{32,64},{64,32},{96,0},{1,97},{33,65},{65,33},{97,1},{2,98}... | collective-permute-start | bytes 24584 | tf_op jit(solution)/shard_map/ppermute | solution.py:31
  13.7 70.3 %collective-permute-start.6 = (bf16[128,1024]{1,0:T(8,128)(2,1)}, bf16[128,1024]{1,0:T(8,128)(2,1)}, u32[]{:S(2)}, u32[]{:S(2)}) collective-permute-start(bf16[128,1024]{1,0:T(8,128)(2,1)} %select_bitcast_fusion.10), channel_id=1, source_target_pairs={{0,96},{32,64},{64,32},{96,0},{1,97},{33,65},{65,33},{97,1},{2,98}... | collective-permute-start | bytes 786440 | tf_op jit(solution)/shard_map/ppermute | solution.py:31
  16.0 74.3 %collective-permute-start.16 = (bf16[328,1024]{1,0:T(8,128)(2,1)}, bf16[328,1024]{1,0:T(8,128)(2,1)}, u32[]{:S(2)}, u32[]{:S(2)}) collective-permute-start(bf16[328,1024]{1,0:T(8,128)(2,1)} %select_bitcast_fusion.2), channel_id=1, source_target_pairs={{0,96},{32,64},{64,32},{96,0},{1,97},{33,65},{65,33},{97,1},{2,98}... | collective-permute-start | bytes 2015240 | tf_op jit(solution)/shard_map/ppermute | solution.py:31
  19.7 71.5 %collective-permute-start.14 = (bf16[512,1312]{0,1:T(8,128)(2,1)}, bf16[512,1312]{0,1:T(8,128)(2,1)}, u32[]{:S(2)}, u32[]{:S(2)}) collective-permute-start(bf16[512,1312]{0,1:T(8,128)(2,1)} %bitcast.23), channel_id=1, source_target_pairs={{0,96},{32,64},{64,32},{96,0},{1,97},{33,65},{65,33},{97,1},{2,98}... | collective-permute-start | bytes 4030472 | tf_op jit(solution)/shard_map/ppermute | solution.py:31
  22.0 60.1 %collective-permute-start.4 = (bf16[512,768]{1,0:T(8,128)(2,1)S(1)}, bf16[512,768]{1,0:T(8,128)(2,1)}, u32[]{:S(2)}, u32[]{:S(2)}) collective-permute-start(bf16[512,768]{1,0:T(8,128)(2,1)S(1)} %copy.111), channel_id=1, source_target_pairs={{0,96},{32,64},{64,32},{96,0},{1,97},{33,65},{65,33},{97,1},{2,98}... | collective-permute-start | bytes 2359304 | tf_op jit(solution)/shard_map/ppermute | solution.py:31
  84.3 14.0 %collective-permute-start.3 = (bf16[128,1024]{1,0:T(8,128)(2,1)S(1)}, bf16[128,1024]{1,0:T(8,128)(2,1)}, u32[]{:S(2)}, u32[]{:S(2)}) collective-permute-start(bf16[128,1024]{1,0:T(8,128)(2,1)S(1)} %fusion.59), channel_id=1, source_target_pairs={{0,1},{1,2},{2,3},{3,0},{4,5},{5,6},{6,7},{7,4},{8,9},{9,10},{10,1... | collective-permute-start | bytes 786440 | tf_op jit(solution)/shard_map/ppermute | solution.py:19
  86.4 13.5 %collective-permute-start.2 = (bf16[128,1024]{1,0:T(8,128)(2,1)S(1)}, bf16[128,1024]{1,0:T(8,128)(2,1)}, u32[]{:S(2)}, u32[]{:S(2)}) collective-permute-start(bf16[128,1024]{1,0:T(8,128)(2,1)S(1)} %fusion.59), channel_id=1, source_target_pairs={{0,2},{1,3},{2,0},{3,1},{4,6},{5,7},{6,4},{7,5},{8,10},{9,11},{10,... | collective-permute-start | bytes 786440 | tf_op jit(solution)/shard_map/ppermute | solution.py:19
  91.2 23.9 %collective-permute-start.17 = (bf16[328,1024]{1,0:T(8,128)(2,1)}, bf16[328,1024]{1,0:T(8,128)(2,1)}, u32[]{:S(2)}, u32[]{:S(2)}) collective-permute-start(bf16[328,1024]{1,0:T(8,128)(2,1)} %collective-permute-done.16), channel_id=1, source_target_pairs={{0,4},{4,0},{1,5},{5,1},{2,6},{6,2},{3,7},{7,3},{8,12},{12,8},{9,1... | collective-permute-start | bytes 2015240 | tf_op jit(solution)/shard_map/ppermute | solution.py:23
  92.2 39.8 %collective-permute-start.15 = (bf16[512,1312]{0,1:T(8,128)(2,1)}, bf16[512,1312]{0,1:T(8,128)(2,1)}, u32[]{:S(2)}, u32[]{:S(2)}) collective-permute-start(bf16[512,1312]{0,1:T(8,128)(2,1)} %collective-permute-done.14), channel_id=1, source_target_pairs={{0,4},{4,0},{1,5},{5,1},{2,6},{6,2},{3,7},{7,3},{8,12},{12,8},{9,1... | collective-permute-start | bytes 4030472 | tf_op jit(solution)/shard_map/ppermute | solution.py:23
  112.7 13.7 %collective-permute-start.10 = (bf16[128,1024]{1,0:T(8,128)(2,1)S(1)}, bf16[128,1024]{1,0:T(8,128)(2,1)S(1)}, u32[]{:S(2)}, u32[]{:S(2)}) collective-permute-start(bf16[128,1024]{1,0:T(8,128)(2,1)S(1)} %get-tuple-element.123), channel_id=1, source_target_pairs={{0,3},{1,0},{2,1},{3,2},{4,7},{5,4},{6,5},{7,6},{8,11},{9,8},{10,9... | collective-permute-start | bytes 786440 | tf_op jit(solution)/shard_map/ppermute | solution.py:19
  129.4 14.2 %collective-permute-start.12 = (bf16[128,1024]{1,0:T(8,128)(2,1)S(1)}, bf16[128,1024]{1,0:T(8,128)(2,1)S(1)}, u32[]{:S(2)}, u32[]{:S(2)}) collective-permute-start(bf16[128,1024]{1,0:T(8,128)(2,1)S(1)} %multiply_convert_fusion.7), channel_id=1, source_target_pairs={{0,2},{1,3},{2,0},{3,1},{4,6},{5,7},{6,4},{7,5},{8,10},{9,11},{10,... | collective-permute-start | bytes 786440 | tf_op jit(solution)/shard_map/ppermute | solution.py:19
  151.1 14.0 %collective-permute-start.20 = (bf16[128,1024]{1,0:T(8,128)(2,1)S(1)}, bf16[128,1024]{1,0:T(8,128)(2,1)S(1)}, u32[]{:S(2)}, u32[]{:S(2)}) collective-permute-start(bf16[128,1024]{1,0:T(8,128)(2,1)S(1)} %get-tuple-element.120), channel_id=1, source_target_pairs={{0,3},{1,0},{2,1},{3,2},{4,7},{5,4},{6,5},{7,6},{8,11},{9,8},{10,9... | collective-permute-start | bytes 786440 | tf_op jit(solution)/shard_map/ppermute | solution.py:19
  168.8 14.5 %collective-permute-start.22 = (bf16[128,1024]{1,0:T(8,128)(2,1)}, bf16[128,1024]{1,0:T(8,128)(2,1)}, u32[]{:S(2)}, u32[]{:S(2)}) collective-permute-start(bf16[128,1024]{1,0:T(8,128)(2,1)} %fusion.57), channel_id=1, source_target_pairs={{0,2},{1,3},{2,0},{3,1},{4,6},{5,7},{6,4},{7,5},{8,10},{9,11},{10,... | collective-permute-start | bytes 786440 | tf_op jit(solution)/shard_map/ppermute | solution.py:19
  195.4 14.4 %collective-permute-start.26 = (bf16[128,1024]{1,0:T(8,128)(2,1)}, bf16[128,1024]{1,0:T(8,128)(2,1)}, u32[]{:S(2)}, u32[]{:S(2)}) collective-permute-start(bf16[128,1024]{1,0:T(8,128)(2,1)} %get-tuple-element.117), channel_id=1, source_target_pairs={{0,3},{1,0},{2,1},{3,2},{4,7},{5,4},{6,5},{7,6},{8,11},{9,8},{10,9... | collective-permute-start | bytes 786440 | tf_op jit(solution)/shard_map/ppermute | solution.py:19
  199.0 33.6 %collective-permute-start.36 = (bf16[128,1024]{1,0:T(8,128)(2,1)}, bf16[128,1024]{1,0:T(8,128)(2,1)}, u32[]{:S(2)}, u32[]{:S(2)}) collective-permute-start(bf16[128,1024]{1,0:T(8,128)(2,1)} %select_bitcast_fusion.7), channel_id=1, source_target_pairs={{0,1},{1,2},{2,3},{3,0},{4,5},{5,6},{6,7},{7,4},{8,9},{9,10},{10,1... | collective-permute-start | bytes 786440 | tf_op jit(solution)/shard_map/ppermute | solution.py:19
  200.1 32.5 %collective-permute-start.35 = (bf16[128,1024]{1,0:T(8,128)(2,1)}, bf16[128,1024]{1,0:T(8,128)(2,1)}, u32[]{:S(2)}, u32[]{:S(2)}) collective-permute-start(bf16[128,1024]{1,0:T(8,128)(2,1)} %select_bitcast_fusion.7), channel_id=1, source_target_pairs={{0,2},{1,3},{2,0},{3,1},{4,6},{5,7},{6,4},{7,5},{8,10},{9,11},{10,... | collective-permute-start | bytes 786440 | tf_op jit(solution)/shard_map/ppermute | solution.py:19
  211.9 16.5 %collective-permute-start.29 = (bf16[128,1024]{1,0:T(8,128)(2,1)S(1)}, bf16[128,1024]{1,0:T(8,128)(2,1)S(1)}, u32[]{:S(2)}, u32[]{:S(2)}) collective-permute-start(bf16[128,1024]{1,0:T(8,128)(2,1)S(1)} %multiply_convert_fusion.6), channel_id=1, source_target_pairs={{0,1},{1,2},{2,3},{3,0},{4,5},{5,6},{6,7},{7,4},{8,9},{9,10},{10,1... | collective-permute-start | bytes 786440 | tf_op jit(solution)/shard_map/ppermute | solution.py:19
  214.4 16.6 %collective-permute-start.28 = (bf16[128,1024]{1,0:T(8,128)(2,1)S(1)}, bf16[128,1024]{1,0:T(8,128)(2,1)S(1)}, u32[]{:S(2)}, u32[]{:S(2)}) collective-permute-start(bf16[128,1024]{1,0:T(8,128)(2,1)S(1)} %multiply_convert_fusion.6), channel_id=1, source_target_pairs={{0,2},{1,3},{2,0},{3,1},{4,6},{5,7},{6,4},{7,5},{8,10},{9,11},{10,... | collective-permute-start | bytes 786440 | tf_op jit(solution)/shard_map/ppermute | solution.py:19
  217.0 13.9 %collective-permute-start.27 = (bf16[128,1024]{1,0:T(8,128)(2,1)S(1)}, bf16[128,1024]{1,0:T(8,128)(2,1)S(1)}, u32[]{:S(2)}, u32[]{:S(2)}) collective-permute-start(bf16[128,1024]{1,0:T(8,128)(2,1)S(1)} %multiply_convert_fusion.6), channel_id=1, source_target_pairs={{0,3},{1,0},{2,1},{3,2},{4,7},{5,4},{6,5},{7,6},{8,11},{9,8},{10,9... | collective-permute-start | bytes 786440 | tf_op jit(solution)/shard_map/ppermute | solution.py:19
  260.4 13.9 %collective-permute-start.41 = (bf16[128,1024]{1,0:T(8,128)(2,1)S(1)}, bf16[128,1024]{1,0:T(8,128)(2,1)S(1)}, u32[]{:S(2)}, u32[]{:S(2)}) collective-permute-start(bf16[128,1024]{1,0:T(8,128)(2,1)S(1)} %fusion.107), channel_id=1, source_target_pairs={{0,2},{1,3},{2,0},{3,1},{4,6},{5,7},{6,4},{7,5},{8,10},{9,11},{10,... | collective-permute-start | bytes 786440 | tf_op jit(solution)/shard_map/ppermute | solution.py:19
  264.5 56.4 %collective-permute-start.77 = (bf16[512,1312]{0,1:T(8,128)(2,1)}, bf16[512,1312]{0,1:T(8,128)(2,1)}, u32[]{:S(2)}, u32[]{:S(2)}) collective-permute-start(bf16[512,1312]{0,1:T(8,128)(2,1)} %broadcast_select_fusion.4), channel_id=1, source_target_pairs={{0,4},{4,0},{1,5},{5,1},{2,6},{6,2},{3,7},{7,3},{8,12},{12,8},{9,1... | collective-permute-start | bytes 4030472 | tf_op jit(solution)/shard_map/ppermute | solution.py:23
  284.2 14.5 %collective-permute-start.45 = (bf16[128,1024]{1,0:T(8,128)(2,1)S(1)}, bf16[128,1024]{1,0:T(8,128)(2,1)S(1)}, u32[]{:S(2)}, u32[]{:S(2)}) collective-permute-start(bf16[128,1024]{1,0:T(8,128)(2,1)S(1)} %get-tuple-element.108), channel_id=1, source_target_pairs={{0,3},{1,0},{2,1},{3,2},{4,7},{5,4},{6,5},{7,6},{8,11},{9,8},{10,9... | collective-permute-start | bytes 786440 | tf_op jit(solution)/shard_map/ppermute | solution.py:19
  287.8 17.0 %collective-permute-start.73 = (bf16[128,1024]{1,0:T(8,128)(2,1)S(1)}, bf16[128,1024]{1,0:T(8,128)(2,1)S(1)}, u32[]{:S(2)}, u32[]{:S(2)}) collective-permute-start(bf16[128,1024]{1,0:T(8,128)(2,1)S(1)} %broadcast_select_fusion.20), channel_id=1, source_target_pairs={{0,4},{4,0},{1,5},{5,1},{2,6},{6,2},{3,7},{7,3},{8,12},{12,8},{9,1... | collective-permute-start | bytes 786440 | tf_op jit(solution)/shard_map/ppermute | solution.py:23
  301.6 14.8 %collective-permute-start.47 = (bf16[128,1024]{1,0:T(8,128)(2,1)S(1)}, bf16[128,1024]{1,0:T(8,128)(2,1)}, u32[]{:S(2)}, u32[]{:S(2)}) collective-permute-start(bf16[128,1024]{1,0:T(8,128)(2,1)S(1)} %add_convert_fusion.11), channel_id=1, source_target_pairs={{0,2},{1,3},{2,0},{3,1},{4,6},{5,7},{6,4},{7,5},{8,10},{9,11},{10,... | collective-permute-start | bytes 786440 | tf_op jit(solution)/shard_map/ppermute | solution.py:19
  305.6 168.1 %reduce-scatter.21.cloned.1.call-start = ((), (), s32[]{:S(2)}) async-start(), calls=%async_computation.14 | async-start | bytes 1622016 | tf_op jit(solution)/shard_map/reduce_scatter | solution.py:239
  326.4 147.4 %reduce-scatter.19.cloned.1.call-start = ((), (), s32[]{:S(2)}) async-start(), calls=%async_computation.13 | async-start | bytes 1622016 | tf_op jit(solution)/shard_map/reduce_scatter | solution.py:239
  338.3 184.0 %reduce-scatter.11.cloned.1.call-start = ((), (), s32[]{:S(2)}) async-start(), calls=%async_computation.8 | async-start | bytes 884736 | tf_op jit(solution)/shard_map/reduce_scatter | solution.py:239
  346.1 14.0 %collective-permute-start.32 = (bf16[128,1024]{1,0:T(8,128)(2,1)}, bf16[128,1024]{1,0:T(8,128)(2,1)}, u32[]{:S(2)}, u32[]{:S(2)}) collective-permute-start(bf16[128,1024]{1,0:T(8,128)(2,1)} %get-tuple-element.114), channel_id=1, source_target_pairs={{0,3},{1,0},{2,1},{3,2},{4,7},{5,4},{6,5},{7,6},{8,11},{9,8},{10,9... | collective-permute-start | bytes 786440 | tf_op jit(solution)/shard_map/ppermute | solution.py:19
  349.3 181.3 %reduce-scatter.17.cloned.1.call-start = ((), (), s32[]{:S(2)}) async-start(), calls=%async_computation.12 | async-start | bytes 884736 | tf_op jit(solution)/shard_map/reduce_scatter | solution.py:239
  351.9 28.7 %collective-permute-start.81 = (bf16[384,1024]{1,0:T(8,128)(2,1)S(1)}, bf16[384,1024]{1,0:T(8,128)(2,1)S(1)}, u32[]{:S(2)}, u32[]{:S(2)}) collective-permute-start(bf16[384,1024]{1,0:T(8,128)(2,1)S(1)} %broadcast_select_fusion.10), channel_id=1, source_target_pairs={{0,4},{4,0},{1,5},{5,1},{2,6},{6,2},{3,7},{7,3},{8,12},{12,8},{9,1... | collective-permute-start | bytes 2359304 | tf_op jit(solution)/shard_map/ppermute | solution.py:23
  362.8 16.8 %collective-permute-start.33 = (bf16[128,1024]{1,0:T(8,128)(2,1)S(1)}, bf16[128,1024]{1,0:T(8,128)(2,1)S(1)}, u32[]{:S(2)}, u32[]{:S(2)}) collective-permute-start(bf16[128,1024]{1,0:T(8,128)(2,1)S(1)} %get-tuple-element.59), channel_id=1, source_target_pairs={{0,64},{64,0},{1,65},{65,1},{2,66},{66,2},{3,67},{67,3},{4,68},{68... | collective-permute-start | bytes 786440 | tf_op jit(solution)/shard_map/ppermute | solution.py:27
  381.9 162.2 %reduce-scatter.15.cloned.1.call-start = ((), (), s32[]{:S(2)}) async-start(), calls=%async_computation.11 | async-start | bytes 884736 | tf_op jit(solution)/shard_map/reduce_scatter | solution.py:239
  386.1 14.7 %collective-permute-start.51 = (bf16[128,1024]{1,0:T(8,128)(2,1)S(1)}, bf16[128,1024]{1,0:T(8,128)(2,1)S(1)}, u32[]{:S(2)}, u32[]{:S(2)}) collective-permute-start(bf16[128,1024]{1,0:T(8,128)(2,1)S(1)} %get-tuple-element.105), channel_id=1, source_target_pairs={{0,3},{1,0},{2,1},{3,2},{4,7},{5,4},{6,5},{7,6},{8,11},{9,8},{10,9... | collective-permute-start | bytes 786440 | tf_op jit(solution)/shard_map/ppermute | solution.py:19
  402.5 14.3 %collective-permute-start.53 = (bf16[128,1024]{1,0:T(8,128)(2,1)S(1)}, bf16[128,1024]{1,0:T(8,128)(2,1)S(1)}, u32[]{:S(2)}, u32[]{:S(2)}) collective-permute-start(bf16[128,1024]{1,0:T(8,128)(2,1)S(1)} %fusion.108), channel_id=1, source_target_pairs={{0,2},{1,3},{2,0},{3,1},{4,6},{5,7},{6,4},{7,5},{8,10},{9,11},{10,... | collective-permute-start | bytes 786440 | tf_op jit(solution)/shard_map/ppermute | solution.py:19
  405.8 40.0 %collective-permute-start.80 = (bf16[384,1024]{1,0:T(8,128)(2,1)S(1)}, bf16[384,1024]{1,0:T(8,128)(2,1)S(1)}, u32[]{:S(2)}, u32[]{:S(2)}) collective-permute-start(bf16[384,1024]{1,0:T(8,128)(2,1)S(1)} %broadcast_select_fusion.11), channel_id=1, source_target_pairs={{0,4},{4,0},{1,5},{5,1},{2,6},{6,2},{3,7},{7,3},{8,12},{12,8},{9,1... | collective-permute-start | bytes 2359304 | tf_op jit(solution)/shard_map/ppermute | solution.py:23
  421.7 31.3 %collective-permute-start.72 = (bf16[128,1024]{1,0:T(8,128)(2,1)}, bf16[128,1024]{1,0:T(8,128)(2,1)}, u32[]{:S(2)}, u32[]{:S(2)}) collective-permute-start(bf16[128,1024]{1,0:T(8,128)(2,1)} %broadcast_select_fusion.21), channel_id=1, source_target_pairs={{0,4},{4,0},{1,5},{5,1},{2,6},{6,2},{3,7},{7,3},{8,12},{12,8},{9,1... | collective-permute-start | bytes 786440 | tf_op jit(solution)/shard_map/ppermute | solution.py:23
  430.0 14.3 %collective-permute-start.57 = (bf16[128,1024]{1,0:T(8,128)(2,1)S(1)}, bf16[128,1024]{1,0:T(8,128)(2,1)S(1)}, u32[]{:S(2)}, u32[]{:S(2)}) collective-permute-start(bf16[128,1024]{1,0:T(8,128)(2,1)S(1)} %get-tuple-element.102), channel_id=1, source_target_pairs={{0,3},{1,0},{2,1},{3,2},{4,7},{5,4},{6,5},{7,6},{8,11},{9,8},{10,9... | collective-permute-start | bytes 786440 | tf_op jit(solution)/shard_map/ppermute | solution.py:19
  438.8 38.1 %collective-permute-start.68 = (bf16[512,768]{1,0:T(8,128)(2,1)}, bf16[512,768]{1,0:T(8,128)(2,1)}, u32[]{:S(2)}, u32[]{:S(2)}) collective-permute-start(bf16[512,768]{1,0:T(8,128)(2,1)} %broadcast_select_fusion.15), channel_id=1, source_target_pairs={{0,4},{4,0},{1,5},{5,1},{2,6},{6,2},{3,7},{7,3},{8,12},{12,8},{9,1... | collective-permute-start | bytes 2359304 | tf_op jit(solution)/shard_map/ppermute | solution.py:23
  455.0 16.1 %all-to-all-start.1 = ((bf16[8,16,1024]{2,1,0:T(8,128)(2,1)}), bf16[8,16,1024]{2,1,0:T(8,128)(2,1)}, u32[]{:S(2)}, u32[]{:S(2)}) async-start(bf16[8,16,1024]{2,1,0:T(8,128)(2,1)} %bitcast.75), calls=%async_computation.2 | async-start | bytes 524288 | tf_op jit(solution)/shard_map/all_to_all | solution.py:248
  467.7 54.4 %collective-permute-start.58 = (bf16[128,1024]{1,0:T(8,128)(2,1)}, bf16[128,1024]{1,0:T(8,128)(2,1)S(1)}, u32[]{:S(2)}, u32[]{:S(2)}) collective-permute-start(bf16[128,1024]{1,0:T(8,128)(2,1)} %get-tuple-element.45), channel_id=1, source_target_pairs={{0,64},{64,0},{1,65},{65,1},{2,66},{66,2},{3,67},{67,3},{4,68},{68... | collective-permute-start | bytes 786440 | tf_op jit(solution)/shard_map/ppermute | solution.py:27
  469.8 13.9 %collective-permute-start.67 = (f32[2,1024]{1,0:T(2,128)S(1)}, f32[2,1024]{1,0:T(2,128)S(1)}, u32[]{:S(2)}, u32[]{:S(2)}) collective-permute-start(f32[2,1024]{1,0:T(2,128)S(1)} %add_add_fusion.6), channel_id=1, source_target_pairs={{0,32},{32,0},{1,33},{33,1},{2,34},{34,2},{3,35},{35,3},{4,36},{36... | collective-permute-start | bytes 24584 | tf_op jit(solution)/shard_map/ppermute | solution.py:19
  479.2 42.9 %all-to-all-start = ((bf16[8,64,768]{2,1,0:T(8,128)(2,1)}), bf16[8,64,768]{2,1,0:T(8,128)(2,1)S(1)}, u32[]{:S(2)}, u32[]{:S(2)}) async-start(bf16[8,64,768]{2,1,0:T(8,128)(2,1)} %bitcast.71), calls=%async_computation | async-start | bytes 1572864 | tf_op jit(solution)/shard_map/all_to_all | solution.py:248
  482.9 134.4 %all-gather.2.cloned.1.call-start = ((), (), s32[]{:S(2)}) async-start(), calls=%async_computation.10 | async-start | bytes 1622016 | tf_op jit(solution)/shard_map/all_gather | solution.py:255
  515.9 103.9 %collective-permute-start.75 = (bf16[128,1024]{1,0:T(8,128)(2,1)S(1)}, bf16[128,1024]{1,0:T(8,128)(2,1)S(1)}, u32[]{:S(2)}, u32[]{:S(2)}) collective-permute-start(bf16[128,1024]{1,0:T(8,128)(2,1)S(1)} %all_gather.13), channel_id=1, source_target_pairs={{0,4},{4,0},{1,5},{5,1},{2,6},{6,2},{3,7},{7,3},{8,12},{12,8},{9,1... | collective-permute-start | bytes 786440 | tf_op jit(solution)/shard_map/ppermute | solution.py:23
  545.0 39.7 %collective-permute-start.82 = (bf16[48,1024]{1,0:T(8,128)(2,1)S(1)}, bf16[48,1024]{1,0:T(8,128)(2,1)S(1)}, u32[]{:S(2)}, u32[]{:S(2)}) collective-permute-start(bf16[48,1024]{1,0:T(8,128)(2,1)S(1)} %broadcast_select_fusion.27), channel_id=1, source_target_pairs={{0,64},{64,0},{1,65},{65,1},{2,66},{66,2},{3,67},{67,3},{4,68},{68... | collective-permute-start | bytes 294920 | tf_op jit(solution)/shard_map/ppermute | solution.py:27
  573.5 47.5 %collective-permute-start.71 = (bf16[512,768]{1,0:T(8,128)(2,1)S(1)}, bf16[512,768]{1,0:T(8,128)(2,1)S(1)}, u32[]{:S(2)}, u32[]{:S(2)}) collective-permute-start(bf16[512,768]{1,0:T(8,128)(2,1)S(1)} %all_gather.12), channel_id=1, source_target_pairs={{0,4},{4,0},{1,5},{5,1},{2,6},{6,2},{3,7},{7,3},{8,12},{12,8},{9,1... | collective-permute-start | bytes 2359304 | tf_op jit(solution)/shard_map/ppermute | solution.py:23
  611.1 16.4 %collective-permute-start.83 = (bf16[384,1024]{1,0:T(8,128)(2,1)}, bf16[384,1024]{1,0:T(8,128)(2,1)}, u32[]{:S(2)}, u32[]{:S(2)}) collective-permute-start(bf16[384,1024]{1,0:T(8,128)(2,1)} %all_gather.15), channel_id=1, source_target_pairs={{0,4},{4,0},{1,5},{5,1},{2,6},{6,2},{3,7},{7,3},{8,12},{12,8},{9,1... | collective-permute-start | bytes 2359304 | tf_op jit(solution)/shard_map/ppermute | solution.py:23
  (155 other events, 1258.8 us)
Sparse Core Ops, SparseCore 0:
  305.7 30.3 reduce-scatter.12
  339.2 39.9 reduce-scatter.20
  381.8 38.4 reduce-scatter.18
  423.3 36.8 reduce-scatter.10
  462.4 40.7 reduce-scatter.16
  506.1 37.9 reduce-scatter.14
  546.3 40.1 all-gather.1

commit v2 on v1

--- a/solution.py
+++ b/solution.py
@@ -175,9 +175,10 @@
     grad_normed_mid = scatter_rows(contract_last(grad_hidden, w_up), row_count)
     unused, pull_norm = jax.vjp(layer_norm, resid_mid, gain_pair[1])
     grad_resid, grad_gain = pull_norm(grad_normed_mid)
-    grad_w_down = contract_rows(mixed_rows, grad_ffn_all).astype(bf16)
+    grad_w_down = contract_rows(grad_ffn_all, mixed_rows).astype(bf16)
     grad_w_up = contract_rows(normed_mid_all, grad_hidden).astype(bf16)
-    return (grad_result + grad_resid, grad_w_up, grad_w_down, grad_gain)
+    grad_w = jnp.concatenate([grad_w_up, grad_w_down], axis=1)
+    return (grad_result + grad_resid, grad_w, grad_gain)
 
 
 def backward_attn(grad_mid, kept, gain_pair, weights, allowed, tables):
@@ -215,52 +216,58 @@
     grad_normed = scatter_rows(contract_last(grad_projected, w_qkv), row_count)
     unused, pull_norm = jax.vjp(layer_norm, inputs, gain_pair[0])
     grad_resid, grad_gain = pull_norm(grad_normed)
-    grad_w_out = contract_rows(attended, grad_att_all).astype(bf16)
+    grad_w_out = contract_rows(grad_att_all, attended).astype(bf16)
     grad_w_qkv = contract_rows(normed_all, grad_projected).astype(bf16)
-    return (grad_mid + grad_resid, grad_w_qkv, grad_w_out, grad_gain)
-
-
-def other_layer(own, core_index):
-    half = own.shape[0] // 2
-    sent = jnp.where(core_index == 0, own[:half], own[half:])
-    got = swap_layer(sent)
-    beside = swap_core(got)
-    low = jnp.where(core_index == 0, got, beside)
-    high = jnp.where(core_index == 0, beside, got)
+    grad_w = jnp.concatenate([grad_w_qkv, grad_w_out], axis=1)
+    return (grad_mid + grad_resid, grad_w, grad_gain)
+
+
+def other_layer(own, after, pair_x):
+    core_index = lax.axis_index("core")
+    parity = lax.axis_index("x") % 2
+    own, unused = lax.optimization_barrier((own, after))
+    rows = own.shape[0]
+    if pair_x:
+        piece = rows // 4
+        sent = lax.dynamic_slice_in_dim(own, (core_index * 2 + parity) * piece, piece)
+        got = swap_layer(sent)
+        beside = lax.ppermute(got, "x", [(0, 1), (1, 0), (2, 3), (3, 2)])
+        half = in_order(parity, got, beside)
+    else:
+        piece = rows // 2
+        sent = lax.dynamic_slice_in_dim(own, core_index * piece, piece)
+        got = half = swap_layer(sent)
+    return in_order(core_index, half, swap_core(half)), got
+
+
+def in_order(index, mine, other):
+    low = jnp.where(index == 0, mine, other)
+    high = jnp.where(index == 0, other, mine)
     return jnp.concatenate([low, high], axis=0)
 
 
-def reduce_part(grads):
+def add_core(grads):
     core_index = lax.axis_index("core")
     half = grads.shape[0] // 2
-    sent = jnp.where(core_index == 0, grads[half:], grads[:half])
-    held = jnp.where(core_index == 0, grads[:half], grads[half:])
-    both = (held.astype(f32) + swap_core(sent).astype(f32)).astype(bf16)
-    return lax.psum_scatter(both, ("zlo", "x"), scatter_dimension=0, tiled=True)
+    sent = lax.dynamic_slice_in_dim(grads, (1 - core_index) * half, half)
+    held = lax.dynamic_slice_in_dim(grads, core_index * half, half)
+    return (held.astype(f32) + swap_core(sent).astype(f32)).astype(bf16)
+
+
+def reduce_part(grads):
+    return lax.psum_scatter(add_core(grads), ("zlo", "x"), scatter_dimension=0, tiled=True)
 
 
 def reduce_part_now(grads):
-    core_index = lax.axis_index("core")
-    half = grads.shape[0] // 2
-    sent = jnp.where(core_index == 0, grads[half:], grads[:half])
-    held = jnp.where(core_index == 0, grads[:half], grads[half:])
-    both = (held.astype(f32) + swap_core(sent).astype(f32)).astype(bf16)
-    pieces = lax.all_to_all(both, ("zlo", "x"), 0, 0, tiled=True)
+    pieces = lax.all_to_all(add_core(grads), ("zlo", "x"), 0, 0, tiled=True)
     pieces = pieces.reshape(8, -1, pieces.shape[1])
     return jnp.sum(pieces.astype(f32), axis=0).astype(bf16)
 
 
 def spread_part(part):
-    core_index = lax.axis_index("core")
-    half = lax.all_gather(part, ("zlo", "x"), axis=0, tiled=True)
-    beside = swap_core(half)
-    low = jnp.where(core_index == 0, half, beside)
-    high = jnp.where(core_index == 0, beside, half)
-    return jnp.concatenate([low, high], axis=0)
-
-
-def pad_rows(block, rows):
-    return jnp.concatenate([block, jnp.zeros((rows - block.shape[0], block.shape[1]), block.dtype)])
+    copies = jnp.broadcast_to(part[None], (8,) + part.shape).reshape(-1, part.shape[1])
+    half = lax.all_to_all(copies, ("zlo", "x"), 0, 0, tiled=True)
+    return in_order(lax.axis_index("core"), half, swap_core(half))
 
 
 def join_sections(is_first, part_first, part_second):
@@ -271,7 +278,6 @@
 
 def local(tokens, cotangent, lengths, gains, w_qkv, w_out, w_up, w_down):
     section_index = lax.axis_index("section")
-    core_index = lax.axis_index("core")
     is_first = section_index == 0
     row_count = tokens.shape[1]
     full_rows = row_count * lax.axis_size("tensor")
@@ -281,7 +287,11 @@
         w_up[0].reshape(w_up.shape[1], -1),
         w_down[0],
     )
-    others = tuple(other_layer(weight, core_index) for weight in own)
+    other_qkv, after = other_layer(own[0], tokens[0, 0, 0], False)
+    other_out, after = other_layer(own[1], after, False)
+    other_up, after = other_layer(own[2], after, True)
+    other_down, after = other_layer(own[3], after, True)
+    others = (other_qkv, other_out, other_up, other_down)
     gains_other = swap_layer(gains[0])
     layer0 = tuple(jnp.where(is_first, a, b) for a, b in zip(own, others))
     layer1 = tuple(jnp.where(is_first, b, a) for a, b in zip(own, others))
@@ -304,27 +314,21 @@
     out0 = out0.astype(bf16)
     out1, kept1 = forward_layer(out0.astype(f32), gains1, layer1, allowed1, tables1)
     out1 = out1.astype(bf16)
-    mid1, up1, down1, gain_mid1 = backward_ffn(end_grads.astype(f32), kept1, gains1, layer1)
-    in1, qkv1, wout1, gain_first1 = backward_attn(mid1, kept1, gains1, layer1, allowed1, tables1)
+    mid1, ffn1, gain_mid1 = backward_ffn(end_grads.astype(f32), kept1, gains1, layer1)
+    in1, attn1, gain_first1 = backward_attn(mid1, kept1, gains1, layer1, allowed1, tables1)
     in1 = in1.astype(bf16)
-    mid0, up0, down0, gain_mid0 = backward_ffn(in1.astype(f32), kept0, gains0, layer0)
-    in0, qkv0, wout0, gain_first0 = backward_attn(mid0, kept0, gains0, layer0, allowed0, tables0)
+    mid0, ffn0, gain_mid0 = backward_ffn(in1.astype(f32), kept0, gains0, layer0)
+    in0, attn0, gain_first0 = backward_attn(mid0, kept0, gains0, layer0, allowed0, tables0)
     in0 = in0.astype(bf16)
 
-    down_rows = down1.shape[0]
-    padded = -(-down_rows // 256) * 256
-    part_up1 = reduce_part(up1)
-    part_down1 = reduce_part(pad_rows(down1, padded))
-    part_qkv1 = reduce_part(qkv1)
-    part_out1 = reduce_part(wout1)
-    part_up0 = reduce_part(up0)
-    part_down0 = reduce_part(pad_rows(down0, padded))
-    up_sum = spread_part(join_sections(is_first, part_up0, part_up1))
-    down_sum = spread_part(join_sections(is_first, part_down0, part_down1))[:down_rows]
-    part_qkv0 = reduce_part_now(qkv0)
-    part_out0 = reduce_part_now(wout0)
-    qkv_sum = spread_part(join_sections(is_first, part_qkv0, part_qkv1))
-    out_sum = spread_part(join_sections(is_first, part_out0, part_out1))
+    both1 = reduce_part(jnp.concatenate([attn1, ffn1], axis=1))
+    attn_width = attn1.shape[1]
+    part_ffn0 = reduce_part(ffn0)
+    ffn_sum = spread_part(join_sections(is_first, part_ffn0, both1[:, attn_width:]))
+    part_attn0 = reduce_part_now(attn0)
+    attn_sum = spread_part(join_sections(is_first, part_attn0, both1[:, :attn_width]))
+    up_width = own[2].shape[1]
+    qkv_width = own[0].shape[1]
 
     gain0 = jnp.stack([gain_first0, gain_mid0])
     gain1 = jnp.stack([gain_first1, gain_mid1])
@@ -353,10 +357,10 @@
         section_out[None],
         input_grads[None],
         gain_total[None],
-        qkv_sum.astype(f32).reshape(w_qkv.shape),
-        out_sum.astype(f32)[None],
-        up_sum.astype(f32).reshape(w_up.shape),
-        down_sum.astype(f32)[None],
+        attn_sum[:, :qkv_width].astype(f32).reshape(w_qkv.shape),
+        attn_sum[:, qkv_width:].T.astype(f32)[None],
+        ffn_sum[:, :up_width].astype(f32).reshape(w_up.shape),
+        ffn_sum[:, up_width:].T.astype(f32)[None],
     )
 
 

time: 653 us -> 531 us (0.81)
  blocking collectives: 82.8 us -> 0 us
  waiting for transfers between devices: 231 us -> 212 us
  starting transfers between devices: 134 us -> 122 us
  other arithmetic: 84.3 us -> 73.9 us
  local copies, waits for them, and re-layouts: 38 us -> 48 us
  matrix products: 56.7 us -> 49.1 us
    all_gather x3 -> x0, blocking collectives: 82.8 us -> none  [spread_part(): half = lax.all_gather(part, ('zlo', 'x'), axis=0, tiled=True)]
    ppermute x5, waiting for transfers between devices: 51 us -> 20.1 us  [swap_layer(): lax.ppermute(block, ('section', 'zlo'), [(0, 3), (1, 2), (2, 1), (3, 0)])]
    ppermute x17 -> x10, starting transfers between devices: 40 us -> 16.8 us  [swap_core(): return lax.ppermute(block, 'core', [(0, 1), (1, 0)])]
    ppermute x55, waiting for transfers between devices: 136 us -> 157 us  [around(): lax.ppermute(block, axis, [(i, (i + distance) % count) for i in range(cou...]
    ppermute x7 -> x5, waiting for transfers between devices: 26.1 us -> 11.1 us  [swap_section(): return lax.ppermute(block, 'section', [(0, 1), (1, 0)])]
    convert_element_type x11 -> x3, other arithmetic: 19.5 us -> 6.41 us  [add_core(): return (held.astype(f32) + swap_core(sent).astype(f32)).astype(bf16)]
    select_n x19 -> x8, other arithmetic: 18 us -> 9.05 us  [the longest x6 4.89 us: in_order(): low = jnp.where(index == 0, mine, other)]
    ppermute x7 -> x5, starting transfers between devices: 6.19 us -> 13.5 us  [swap_section(): return lax.ppermute(block, 'section', [(0, 1), (1, 0)])]
  transfers between devices with their start and end apart: 93 -> 82, of which waited for: 45 -> 43; matrix products, arithmetic and copies ran while one was open for 21% -> 21% of each run, Pallas kernels for 0% -> 0%
where the time goes in v2:
time: 531 us; the launch traced here: 521 us
  waiting for transfers between devices  212 us (40%)
  starting transfers between devices  122 us (23%)
  other arithmetic  73.9 us (14%)
  matrix products  49.1 us (9%)
  local copies, waits for them, and re-layouts  48 us (9%)
  between operations  16.7 us (3%)
    ppermute x55, waiting for transfers between devices, around(): lax.ppermute(block, axis, [(i, (i + distance) % count) for i in range(cou...  157 us
    ppermute x55, starting transfers between devices, around(): lax.ppermute(block, axis, [(i, (i + distance) % count) for i in range(cou...  70.2 us
    unnamed x305, local copies, waits for them, and re-layouts  27.1 us
    ppermute x5, waiting for transfers between devices, swap_layer(): lax.ppermute(block, ('section', 'zlo'), [(0, 3), (1, 2), (2, 1), (3, 0)])  20.1 us
    dot_general x8, matrix products, contract_last(): lax.dot_general(left_rows, weight, (((1,), (1,)), ((), ())), preferred_el...  18.4 us
    reduce_scatter x2, waiting for transfers between devices, reduce_part(): lax.psum_scatter(add_core(grads), ('zlo', 'x'), scatter_dimension=0, tile...  18.2 us
    ppermute x10, starting transfers between devices, swap_core(): return lax.ppermute(block, 'core', [(0, 1), (1, 0)])  16.8 us
    ppermute x5, starting transfers between devices, swap_section(): return lax.ppermute(block, 'section', [(0, 1), (1, 0)])  13.5 us
  transfers between devices with their start and end apart: 82, of which 43 were waited for; matrix products, arithmetic and copies ran while one was open for 21% of the time, Pallas kernels for 0%

profile of v2, /device:TPU:1, one launch (start us, length us, event | category | flops | bytes accessed | tf_op | source)
XLA Modules:
  0.0 520.9 jit_solution(17475306967313295922)
XLA Ops:
  7.2 4.7 collective-permute-start
  18.4 15.9 %collective-permute-done.4 = bf16[512,768]{0,1:T(8,128)(2,1)} collective-permute-done((bf16[512,768]{0,1:T(8,128)(2,1)}, bf16[512,768]{0,1:T(8,128)(2,1)}, u32[]{:S(2)}, u32[]{:S(2)}) %collective-permute-start.4) | collective-permute-done | bytes 786464 | tf_op jit(solution)/shard_map/ppermute | solution.py:31
  37.2 4.3 collective-permute-done.6
  54.7 5.9 %collective-permute-done.2 = bf16[128,1024]{1,0:T(8,128)(2,1)S(1)} collective-permute-done((bf16[128,1024]{1,0:T(8,128)(2,1)S(1)}, bf16[128,1024]{1,0:T(8,128)(2,1)S(1)}, u32[]{:S(2)}, u32[]{:S(2)}) %collective-permute-start.2) | collective-permute-done | bytes 262176 | tf_op jit(solution)/shard_map/ppermute | solution.py:19
  77.7 6.9 %collective-permute-done.10 = bf16[128,1024]{1,0:T(8,128)(2,1)S(1)} collective-permute-done((bf16[128,1024]{1,0:T(8,128)(2,1)}, bf16[128,1024]{1,0:T(8,128)(2,1)S(1)}, u32[]{:S(2)}, u32[]{:S(2)}) %collective-permute-start.10) | collective-permute-done | bytes 262176 | tf_op jit(solution)/shard_map/ppermute | solution.py:19
  91.1 4.8 collective-permute-done.18
  105.6 4.4 collective-permute-done.13
  110.0 6.6 %collective-permute-done.12 = bf16[128,1024]{1,0:T(8,128)(2,1)S(1)} collective-permute-done((bf16[128,1024]{1,0:T(8,128)(2,1)S(1)}, bf16[128,1024]{1,0:T(8,128)(2,1)S(1)}, u32[]{:S(2)}, u32[]{:S(2)}) %collective-permute-start.12) | collective-permute-done | bytes 262176 | tf_op jit(solution)/shard_map/ppermute | solution.py:19
  119.1 3.8 multiply_convert_fusion.5
  127.3 5.3 %collective-permute-done.20 = bf16[128,1024]{1,0:T(8,128)(2,1)S(1)} collective-permute-done((bf16[128,1024]{1,0:T(8,128)(2,1)S(1)}, bf16[128,1024]{1,0:T(8,128)(2,1)S(1)}, u32[]{:S(2)}, u32[]{:S(2)}) %collective-permute-start.20) | collective-permute-done | bytes 262176 | tf_op jit(solution)/shard_map/ppermute | solution.py:19
  132.7 5.7 %collective-permute-done.22 = bf16[128,1024]{1,0:T(8,128)(2,1)S(1)} collective-permute-done((bf16[128,1024]{1,0:T(8,128)(2,1)S(1)}, bf16[128,1024]{1,0:T(8,128)(2,1)S(1)}, u32[]{:S(2)}, u32[]{:S(2)}) %collective-permute-start.22) | collective-permute-done | bytes 262176 | tf_op jit(solution)/shard_map/ppermute | solution.py:19
  144.0 4.9 collective-permute-done.25
  148.9 6.2 %collective-permute-done.24 = bf16[128,1024]{1,0:T(8,128)(2,1)S(1)} collective-permute-done((bf16[128,1024]{1,0:T(8,128)(2,1)S(1)}, bf16[128,1024]{1,0:T(8,128)(2,1)S(1)}, u32[]{:S(2)}, u32[]{:S(2)}) %collective-permute-start.24) | collective-permute-done | bytes 262176 | tf_op jit(solution)/shard_map/ppermute | solution.py:19
  164.5 4.1 collective-permute-done.26
  168.7 7.4 %collective-permute-done.28 = bf16[128,1024]{1,0:T(8,128)(2,1)S(1)} collective-permute-done((bf16[128,1024]{1,0:T(8,128)(2,1)S(1)}, bf16[128,1024]{1,0:T(8,128)(2,1)S(1)}, u32[]{:S(2)}, u32[]{:S(2)}) %collective-permute-start.28) | collective-permute-done | bytes 262176 | tf_op jit(solution)/shard_map/ppermute | solution.py:19
  178.2 3.0 collective-permute-start.30
  187.5 5.2 %collective-permute-done.30 = bf16[128,1024]{1,0:T(8,128)(2,1)S(1)} collective-permute-done((bf16[128,1024]{1,0:T(8,128)(2,1)S(1)}, bf16[128,1024]{1,0:T(8,128)(2,1)S(1)}, u32[]{:S(2)}, u32[]{:S(2)}) %collective-permute-start.30) | collective-permute-done | bytes 262176 | tf_op jit(solution)/shard_map/ppermute | solution.py:19
  196.8 7.2 %collective-permute-done.37 = bf16[128,1024]{1,0:T(8,128)(2,1)S(1)} collective-permute-done((bf16[128,1024]{1,0:T(8,128)(2,1)S(1)}, bf16[128,1024]{1,0:T(8,128)(2,1)S(1)}, u32[]{:S(2)}, u32[]{:S(2)}) %collective-permute-start.37) | collective-permute-done | bytes 262176 | tf_op jit(solution)/shard_map/ppermute | solution.py:19
  204.0 3.8 add_convert_fusion.4
  214.8 4.7 collective-permute-done.39
  219.5 6.6 %collective-permute-done.41 = bf16[128,1024]{1,0:T(8,128)(2,1)S(1)} collective-permute-done((bf16[128,1024]{1,0:T(8,128)(2,1)S(1)}, bf16[128,1024]{1,0:T(8,128)(2,1)S(1)}, u32[]{:S(2)}, u32[]{:S(2)}) %collective-permute-start.41) | collective-permute-done | bytes 262176 | tf_op jit(solution)/shard_map/ppermute | solution.py:19
  236.3 7.2 %collective-permute-done.43 = bf16[128,1024]{1,0:T(8,128)(2,1)S(1)} collective-permute-done((bf16[128,1024]{1,0:T(8,128)(2,1)S(1)}, bf16[128,1024]{1,0:T(8,128)(2,1)S(1)}, u32[]{:S(2)}, u32[]{:S(2)}) %collective-permute-start.43) | collective-permute-done | bytes 262176 | tf_op jit(solution)/shard_map/ppermute | solution.py:19
  254.4 4.6 collective-permute-done.45
  259.0 6.8 %collective-permute-done.47 = bf16[128,1024]{1,0:T(8,128)(2,1)S(1)} collective-permute-done((bf16[128,1024]{1,0:T(8,128)(2,1)S(1)}, bf16[128,1024]{1,0:T(8,128)(2,1)S(1)}, u32[]{:S(2)}, u32[]{:S(2)}) %collective-permute-start.47) | collective-permute-done | bytes 262176 | tf_op jit(solution)/shard_map/ppermute | solution.py:19
  272.2 4.0 collective-permute-done.50
  276.2 7.2 %collective-permute-done.49 = bf16[128,1024]{1,0:T(8,128)(2,1)} collective-permute-done((bf16[128,1024]{1,0:T(8,128)(2,1)S(1)}, bf16[128,1024]{1,0:T(8,128)(2,1)}, u32[]{:S(2)}, u32[]{:S(2)}) %collective-permute-start.49) | collective-permute-done | bytes 262176 | tf_op jit(solution)/shard_map/ppermute | solution.py:19
  298.3 3.5 pad_maximum_fusion
  303.9 3.8 copy.139
  311.3 4.4 fusion.208
  318.7 6.3 %collective-permute-done.51 = bf16[128,1024]{1,0:T(8,128)(2,1)S(1)} collective-permute-done((bf16[128,1024]{1,0:T(8,128)(2,1)S(1)}, bf16[128,1024]{1,0:T(8,128)(2,1)S(1)}, u32[]{:S(2)}, u32[]{:S(2)}) %collective-permute-start.51) | collective-permute-done | bytes 262176 | tf_op jit(solution)/shard_map/ppermute | solution.py:19
  325.0 5.2 %collective-permute-done.53 = bf16[128,1024]{1,0:T(8,128)(2,1)S(1)} collective-permute-done((bf16[128,1024]{1,0:T(8,128)(2,1)S(1)}, bf16[128,1024]{1,0:T(8,128)(2,1)S(1)}, u32[]{:S(2)}, u32[]{:S(2)}) %collective-permute-start.53) | collective-permute-done | bytes 262176 | tf_op jit(solution)/shard_map/ppermute | solution.py:19
  335.8 4.6 copy.137
  345.9 5.4 %collective-permute-done.56 = bf16[128,1024]{1,0:T(8,128)(2,1)S(1)} collective-permute-done((bf16[128,1024]{1,0:T(8,128)(2,1)S(1)}, bf16[128,1024]{1,0:T(8,128)(2,1)S(1)}, u32[]{:S(2)}, u32[]{:S(2)}) %collective-permute-start.56) | collective-permute-done | bytes 262176 | tf_op jit(solution)/shard_map/ppermute | solution.py:19
  351.3 6.1 %collective-permute-done.55 = bf16[128,1024]{1,0:T(8,128)(2,1)S(1)} collective-permute-done((bf16[128,1024]{1,0:T(8,128)(2,1)S(1)}, bf16[128,1024]{1,0:T(8,128)(2,1)S(1)}, u32[]{:S(2)}, u32[]{:S(2)}) %collective-permute-start.55) | collective-permute-done | bytes 262176 | tf_op jit(solution)/shard_map/ppermute | solution.py:19
  379.8 4.5 all-to-all-start
  384.3 18.2 %reduce-scatter.7.cloned.1.call-done = bf16[64,2992]{1,0:T(8,128)(2,1)} async-done(((bf16[512,2992]{1,0:T(8,128)(2,1)}), bf16[64,2992]{1,0:T(8,128)(2,1)}) %reduce-scatter.7.cloned.1.call-update) | async-done | bytes 382992 | tf_op jit(solution)/shard_map/reduce_scatter | solution.py:258
  403.4 5.7 %collective-permute-start.75 = (bf16[64,1968]{1,0:T(8,128)(2,1)S(1)}, bf16[64,1968]{1,0:T(8,128)(2,1)S(1)}, u32[]{:S(2)}, u32[]{:S(2)}) collective-permute-start(bf16[64,1968]{1,0:T(8,128)(2,1)S(1)} %broadcast_select_fusion.22), channel_id=1, source_target_pairs={{0,64},{64,0},{1,65},{65,1},{2,66},{66,2},{3,67},{67,3},{4,68},{68... | collective-permute-start | bytes 755720 | tf_op jit(solution)/shard_map/ppermute | solution.py:27
  409.1 3.9 fusion.209
  415.4 3.6 all-to-all-start.2
  426.3 3.3 collective-permute-start.35
  429.6 3.8 collective-permute-done.59
  438.0 3.2 collective-permute-start.72
  443.4 10.0 %collective-permute-done.72 = bf16[64,1024]{1,0:T(8,128)(2,1)S(1)} collective-permute-done((bf16[64,1024]{1,0:T(8,128)(2,1)S(1)}, bf16[64,1024]{1,0:T(8,128)(2,1)S(1)}, u32[]{:S(2)}, u32[]{:S(2)}) %collective-permute-start.72) | collective-permute-done | bytes 131104 | tf_op jit(solution)/shard_map/ppermute | solution.py:27
  457.0 5.4 %all-to-all-start.1 = ((bf16[8,64,1024]{2,1,0:T(8,128)(2,1)}), bf16[8,64,1024]{2,1,0:T(8,128)(2,1)}, u32[]{:S(2)}, u32[]{:S(2)}) async-start(bf16[8,64,1024]{2,1,0:T(8,128)(2,1)} %broadcast_in_dim.164), calls=%async_computation.1 | async-start | bytes 2097152 | tf_op jit(solution)/shard_map/all_to_all | solution.py:269
  475.8 3.0 collective-permute-start.68
  485.7 5.4 %collective-permute-done.69 = f32[2,1024]{1,0:T(2,128)S(1)} collective-permute-done((f32[2,1024]{1,0:T(2,128)S(1)}, f32[2,1024]{1,0:T(2,128)S(1)}, u32[]{:S(2)}, u32[]{:S(2)}) %collective-permute-start.69) | collective-permute-done | bytes 8224 | tf_op jit(solution)/shard_map/ppermute | solution.py:19
  502.7 3.7 copy.125
  510.5 3.1 convert.79
  (596 shorter events, 236.8 us)
Async XLA Ops:
  7.2 377.1 %reduce-scatter.9.cloned.1.call-start = ((), (), s32[]{:S(2)}) async-start(), calls=%async_computation.6 | async-start | bytes 2359296 | tf_op jit(solution)/shard_map/reduce_scatter | solution.py:258
  7.2 27.5 %collective-permute-start = (f32[2,1024]{1,0:T(2,128)}, f32[2,1024]{1,0:T(2,128)S(1)}, u32[]{:S(2)}, u32[]{:S(2)}) collective-permute-start(f32[2,1024]{1,0:T(2,128)} %bitcast.312), channel_id=1, source_target_pairs={{0,96},{32,64},{64,32},{96,0},{1,97},{33,65},{65,33},{97,1},{2,98}... | collective-permute-start | bytes 24584 | tf_op jit(solution)/shard_map/ppermute | solution.py:31
  14.6 19.6 %collective-permute-start.4 = (bf16[512,768]{0,1:T(8,128)(2,1)}, bf16[512,768]{0,1:T(8,128)(2,1)}, u32[]{:S(2)}, u32[]{:S(2)}) collective-permute-start(bf16[512,768]{0,1:T(8,128)(2,1)} %constant_dynamic-slice_fusion.4), channel_id=1, source_target_pairs={{0,96},{32,64},{64,32},{96,0},{1,97},{33,65},{65,33},{97,1},{2,98}... | collective-permute-start | bytes 2359304 | tf_op jit(solution)/shard_map/ppermute | solution.py:31
  34.7 16.5 %collective-permute-start.5 = (bf16[512,768]{0,1:T(8,128)(2,1)}, bf16[512,768]{0,1:T(8,128)(2,1)S(1)}, u32[]{:S(2)}, u32[]{:S(2)}) collective-permute-start(bf16[512,768]{0,1:T(8,128)(2,1)} %collective-permute-done.4), channel_id=1, source_target_pairs={{0,4},{4,0},{1,5},{5,1},{2,6},{6,2},{3,7},{7,3},{8,12},{12,8},{9,1... | collective-permute-start | bytes 2359304 | tf_op jit(solution)/shard_map/ppermute | solution.py:23
  45.9 14.7 %collective-permute-start.2 = (bf16[128,1024]{1,0:T(8,128)(2,1)S(1)}, bf16[128,1024]{1,0:T(8,128)(2,1)S(1)}, u32[]{:S(2)}, u32[]{:S(2)}) collective-permute-start(bf16[128,1024]{1,0:T(8,128)(2,1)S(1)} %fusion.64), channel_id=1, source_target_pairs={{0,2},{1,3},{2,0},{3,1},{4,6},{5,7},{6,4},{7,5},{8,10},{9,11},{10,... | collective-permute-start | bytes 786440 | tf_op jit(solution)/shard_map/ppermute | solution.py:19
  48.5 12.1 %collective-permute-start.1 = (bf16[128,1024]{1,0:T(8,128)(2,1)S(1)}, bf16[128,1024]{1,0:T(8,128)(2,1)S(1)}, u32[]{:S(2)}, u32[]{:S(2)}) collective-permute-start(bf16[128,1024]{1,0:T(8,128)(2,1)S(1)} %fusion.64), channel_id=1, source_target_pairs={{0,3},{1,0},{2,1},{3,2},{4,7},{5,4},{6,5},{7,6},{8,11},{9,8},{10,9... | collective-permute-start | bytes 786440 | tf_op jit(solution)/shard_map/ppermute | solution.py:19
  50.7 17.2 %collective-permute-start.14 = (bf16[256,1312]{0,1:T(8,128)(2,1)S(1)}, bf16[256,1312]{0,1:T(8,128)(2,1)}, u32[]{:S(2)}, u32[]{:S(2)}) collective-permute-start(bf16[256,1312]{0,1:T(8,128)(2,1)S(1)} %constant_dynamic-slice_fusion.2), channel_id=1, source_target_pairs={{0,96},{32,64},{64,32},{96,0},{1,97},{33,65},{65,33},{97,1},{2,98}... | collective-permute-start | bytes 2015240 | tf_op jit(solution)/shard_map/ppermute | solution.py:31
  68.0 19.8 %collective-permute-start.15 = (bf16[256,1312]{0,1:T(8,128)(2,1)}, bf16[256,1312]{0,1:T(8,128)(2,1)}, u32[]{:S(2)}, u32[]{:S(2)}) collective-permute-start(bf16[256,1312]{0,1:T(8,128)(2,1)} %collective-permute-done.14), channel_id=1, source_target_pairs={{0,8},{8,0},{16,24},{24,16},{1,9},{9,1},{17,25},{25,17},{2,10},{10... | collective-permute-start | bytes 2015240 | tf_op jit(solution)/shard_map/ppermute | solution.py:234
  72.2 12.5 %collective-permute-start.10 = (bf16[128,1024]{1,0:T(8,128)(2,1)}, bf16[128,1024]{1,0:T(8,128)(2,1)S(1)}, u32[]{:S(2)}, u32[]{:S(2)}) collective-permute-start(bf16[128,1024]{1,0:T(8,128)(2,1)} %get-tuple-element.134), channel_id=1, source_target_pairs={{0,3},{1,0},{2,1},{3,2},{4,7},{5,4},{6,5},{7,6},{8,11},{9,8},{10,9... | collective-permute-start | bytes 786440 | tf_op jit(solution)/shard_map/ppermute | solution.py:19
  75.5 12.0 %collective-permute-start.17 = (bf16[164,1024]{1,0:T(8,128)(2,1)}, bf16[164,1024]{1,0:T(8,128)(2,1)}, u32[]{:S(2)}, u32[]{:S(2)}) collective-permute-start(bf16[164,1024]{1,0:T(8,128)(2,1)} %constant_dynamic-slice_fusion.1), channel_id=1, source_target_pairs={{0,96},{32,64},{64,32},{96,0},{1,97},{33,65},{65,33},{97,1},{2,98}... | collective-permute-start | bytes 1007624 | tf_op jit(solution)/shard_map/ppermute | solution.py:31
  89.3 15.6 %collective-permute-start.16 = (bf16[512,1312]{0,1:T(8,128)(2,1)S(1)}, bf16[512,1312]{0,1:T(8,128)(2,1)S(1)}, u32[]{:S(2)}, u32[]{:S(2)}) collective-permute-start(bf16[512,1312]{0,1:T(8,128)(2,1)S(1)} %pad_maximum_fusion.5), channel_id=1, source_target_pairs={{0,4},{4,0},{1,5},{5,1},{2,6},{6,2},{3,7},{7,3},{8,12},{12,8},{9,1... | collective-permute-start | bytes 4030472 | tf_op jit(solution)/shard_map/ppermute | solution.py:23
  101.7 14.8 %collective-permute-start.12 = (bf16[128,1024]{1,0:T(8,128)(2,1)S(1)}, bf16[128,1024]{1,0:T(8,128)(2,1)S(1)}, u32[]{:S(2)}, u32[]{:S(2)}) collective-permute-start(bf16[128,1024]{1,0:T(8,128)(2,1)S(1)} %multiply_convert_fusion.7), channel_id=1, source_target_pairs={{0,2},{1,3},{2,0},{3,1},{4,6},{5,7},{6,4},{7,5},{8,10},{9,11},{10,... | collective-permute-start | bytes 786440 | tf_op jit(solution)/shard_map/ppermute | solution.py:19
  104.5 12.1 %collective-permute-start.11 = (bf16[128,1024]{1,0:T(8,128)(2,1)S(1)}, bf16[128,1024]{1,0:T(8,128)(2,1)S(1)}, u32[]{:S(2)}, u32[]{:S(2)}) collective-permute-start(bf16[128,1024]{1,0:T(8,128)(2,1)S(1)} %multiply_convert_fusion.7), channel_id=1, source_target_pairs={{0,3},{1,0},{2,1},{3,2},{4,7},{5,4},{6,5},{7,6},{8,11},{9,8},{10,9... | collective-permute-start | bytes 786440 | tf_op jit(solution)/shard_map/ppermute | solution.py:19
  124.9 13.5 %collective-permute-start.22 = (bf16[128,1024]{1,0:T(8,128)(2,1)S(1)}, bf16[128,1024]{1,0:T(8,128)(2,1)S(1)}, u32[]{:S(2)}, u32[]{:S(2)}) collective-permute-start(bf16[128,1024]{1,0:T(8,128)(2,1)S(1)} %get-tuple-element.131), channel_id=1, source_target_pairs={{0,3},{1,0},{2,1},{3,2},{4,7},{5,4},{6,5},{7,6},{8,11},{9,8},{10,9... | collective-permute-start | bytes 786440 | tf_op jit(solution)/shard_map/ppermute | solution.py:19
  127.3 12.2 %collective-permute-start.21 = (bf16[128,1024]{1,0:T(8,128)(2,1)S(1)}, bf16[128,1024]{1,0:T(8,128)(2,1)S(1)}, u32[]{:S(2)}, u32[]{:S(2)}) collective-permute-start(bf16[128,1024]{1,0:T(8,128)(2,1)S(1)} %get-tuple-element.132), channel_id=1, source_target_pairs={{0,1},{1,2},{2,3},{3,0},{4,5},{5,6},{6,7},{7,4},{8,9},{9,10},{10,1... | collective-permute-start | bytes 786440 | tf_op jit(solution)/shard_map/ppermute | solution.py:19
  141.1 14.0 %collective-permute-start.24 = (bf16[128,1024]{1,0:T(8,128)(2,1)S(1)}, bf16[128,1024]{1,0:T(8,128)(2,1)S(1)}, u32[]{:S(2)}, u32[]{:S(2)}) collective-permute-start(bf16[128,1024]{1,0:T(8,128)(2,1)S(1)} %fusion.62), channel_id=1, source_target_pairs={{0,2},{1,3},{2,0},{3,1},{4,6},{5,7},{6,4},{7,5},{8,10},{9,11},{10,... | collective-permute-start | bytes 786440 | tf_op jit(solution)/shard_map/ppermute | solution.py:19
  143.6 11.5 %collective-permute-start.23 = (bf16[128,1024]{1,0:T(8,128)(2,1)S(1)}, bf16[128,1024]{1,0:T(8,128)(2,1)S(1)}, u32[]{:S(2)}, u32[]{:S(2)}) collective-permute-start(bf16[128,1024]{1,0:T(8,128)(2,1)S(1)} %fusion.62), channel_id=1, source_target_pairs={{0,3},{1,0},{2,1},{3,2},{4,7},{5,4},{6,5},{7,6},{8,11},{9,8},{10,9... | collective-permute-start | bytes 786440 | tf_op jit(solution)/shard_map/ppermute | solution.py:19
  161.7 14.3 %collective-permute-start.28 = (bf16[128,1024]{1,0:T(8,128)(2,1)S(1)}, bf16[128,1024]{1,0:T(8,128)(2,1)S(1)}, u32[]{:S(2)}, u32[]{:S(2)}) collective-permute-start(bf16[128,1024]{1,0:T(8,128)(2,1)S(1)} %get-tuple-element.128), channel_id=1, source_target_pairs={{0,3},{1,0},{2,1},{3,2},{4,7},{5,4},{6,5},{7,6},{8,11},{9,8},{10,9... | collective-permute-start | bytes 786440 | tf_op jit(solution)/shard_map/ppermute | solution.py:19
  164.5 11.5 %collective-permute-start.27 = (bf16[128,1024]{1,0:T(8,128)(2,1)S(1)}, bf16[128,1024]{1,0:T(8,128)(2,1)S(1)}, u32[]{:S(2)}, u32[]{:S(2)}) collective-permute-start(bf16[128,1024]{1,0:T(8,128)(2,1)S(1)} %get-tuple-element.129), channel_id=1, source_target_pairs={{0,1},{1,2},{2,3},{3,0},{4,5},{5,6},{6,7},{7,4},{8,9},{9,10},{10,1... | collective-permute-start | bytes 786440 | tf_op jit(solution)/shard_map/ppermute | solution.py:19
  178.2 14.5 %collective-permute-start.30 = (bf16[128,1024]{1,0:T(8,128)(2,1)S(1)}, bf16[128,1024]{1,0:T(8,128)(2,1)S(1)}, u32[]{:S(2)}, u32[]{:S(2)}) collective-permute-start(bf16[128,1024]{1,0:T(8,128)(2,1)S(1)} %multiply_convert_fusion.6), channel_id=1, source_target_pairs={{0,2},{1,3},{2,0},{3,1},{4,6},{5,7},{6,4},{7,5},{8,10},{9,11},{10,... | collective-permute-start | bytes 786440 | tf_op jit(solution)/shard_map/ppermute | solution.py:19
  181.2 11.7 %collective-permute-start.29 = (bf16[128,1024]{1,0:T(8,128)(2,1)S(1)}, bf16[128,1024]{1,0:T(8,128)(2,1)S(1)}, u32[]{:S(2)}, u32[]{:S(2)}) collective-permute-start(bf16[128,1024]{1,0:T(8,128)(2,1)S(1)} %multiply_convert_fusion.6), channel_id=1, source_target_pairs={{0,3},{1,0},{2,1},{3,2},{4,7},{5,4},{6,5},{7,6},{8,11},{9,8},{10,9... | collective-permute-start | bytes 786440 | tf_op jit(solution)/shard_map/ppermute | solution.py:19
  181.2 15.6 %collective-permute-start.38 = (bf16[128,1024]{1,0:T(8,128)(2,1)S(1)}, bf16[128,1024]{1,0:T(8,128)(2,1)S(1)}, u32[]{:S(2)}, u32[]{:S(2)}) collective-permute-start(bf16[128,1024]{1,0:T(8,128)(2,1)S(1)} %select_bitcast_fusion.2), channel_id=1, source_target_pairs={{0,1},{1,2},{2,3},{3,0},{4,5},{5,6},{6,7},{7,4},{8,9},{9,10},{10,1... | collective-permute-start | bytes 786440 | tf_op jit(solution)/shard_map/ppermute | solution.py:19
  182.7 21.2 %collective-permute-start.37 = (bf16[128,1024]{1,0:T(8,128)(2,1)S(1)}, bf16[128,1024]{1,0:T(8,128)(2,1)S(1)}, u32[]{:S(2)}, u32[]{:S(2)}) collective-permute-start(bf16[128,1024]{1,0:T(8,128)(2,1)S(1)} %select_bitcast_fusion.2), channel_id=1, source_target_pairs={{0,2},{1,3},{2,0},{3,1},{4,6},{5,7},{6,4},{7,5},{8,10},{9,11},{10,... | collective-permute-start | bytes 786440 | tf_op jit(solution)/shard_map/ppermute | solution.py:19
  185.5 18.5 %collective-permute-start.36 = (bf16[128,1024]{1,0:T(8,128)(2,1)S(1)}, bf16[128,1024]{1,0:T(8,128)(2,1)S(1)}, u32[]{:S(2)}, u32[]{:S(2)}) collective-permute-start(bf16[128,1024]{1,0:T(8,128)(2,1)S(1)} %select_bitcast_fusion.2), channel_id=1, source_target_pairs={{0,3},{1,0},{2,1},{3,2},{4,7},{5,4},{6,5},{7,6},{8,11},{9,8},{10,9... | collective-permute-start | bytes 786440 | tf_op jit(solution)/shard_map/ppermute | solution.py:19
  212.0 14.1 %collective-permute-start.41 = (bf16[128,1024]{1,0:T(8,128)(2,1)S(1)}, bf16[128,1024]{1,0:T(8,128)(2,1)S(1)}, u32[]{:S(2)}, u32[]{:S(2)}) collective-permute-start(bf16[128,1024]{1,0:T(8,128)(2,1)S(1)} %get-tuple-element.122), channel_id=1, source_target_pairs={{0,3},{1,0},{2,1},{3,2},{4,7},{5,4},{6,5},{7,6},{8,11},{9,8},{10,9... | collective-permute-start | bytes 786440 | tf_op jit(solution)/shard_map/ppermute | solution.py:19
  214.8 11.7 %collective-permute-start.40 = (bf16[128,1024]{1,0:T(8,128)(2,1)S(1)}, bf16[128,1024]{1,0:T(8,128)(2,1)S(1)}, u32[]{:S(2)}, u32[]{:S(2)}) collective-permute-start(bf16[128,1024]{1,0:T(8,128)(2,1)S(1)} %get-tuple-element.123), channel_id=1, source_target_pairs={{0,1},{1,2},{2,3},{3,0},{4,5},{5,6},{6,7},{7,4},{8,9},{9,10},{10,1... | collective-permute-start | bytes 786440 | tf_op jit(solution)/shard_map/ppermute | solution.py:19
  229.1 14.4 %collective-permute-start.43 = (bf16[128,1024]{1,0:T(8,128)(2,1)S(1)}, bf16[128,1024]{1,0:T(8,128)(2,1)S(1)}, u32[]{:S(2)}, u32[]{:S(2)}) collective-permute-start(bf16[128,1024]{1,0:T(8,128)(2,1)S(1)} %fusion.114), channel_id=1, source_target_pairs={{0,2},{1,3},{2,0},{3,1},{4,6},{5,7},{6,4},{7,5},{8,10},{9,11},{10,... | collective-permute-start | bytes 786440 | tf_op jit(solution)/shard_map/ppermute | solution.py:19
  251.6 14.2 %collective-permute-start.47 = (bf16[128,1024]{1,0:T(8,128)(2,1)S(1)}, bf16[128,1024]{1,0:T(8,128)(2,1)S(1)}, u32[]{:S(2)}, u32[]{:S(2)}) collective-permute-start(bf16[128,1024]{1,0:T(8,128)(2,1)S(1)} %get-tuple-element.119), channel_id=1, source_target_pairs={{0,3},{1,0},{2,1},{3,2},{4,7},{5,4},{6,5},{7,6},{8,11},{9,8},{10,9... | collective-permute-start | bytes 786440 | tf_op jit(solution)/shard_map/ppermute | solution.py:19
  254.4 11.6 %collective-permute-start.46 = (bf16[128,1024]{1,0:T(8,128)(2,1)S(1)}, bf16[128,1024]{1,0:T(8,128)(2,1)S(1)}, u32[]{:S(2)}, u32[]{:S(2)}) collective-permute-start(bf16[128,1024]{1,0:T(8,128)(2,1)S(1)} %get-tuple-element.120), channel_id=1, source_target_pairs={{0,1},{1,2},{2,3},{3,0},{4,5},{5,6},{6,7},{7,4},{8,9},{9,10},{10,1... | collective-permute-start | bytes 786440 | tf_op jit(solution)/shard_map/ppermute | solution.py:19
  268.9 14.5 %collective-permute-start.49 = (bf16[128,1024]{1,0:T(8,128)(2,1)S(1)}, bf16[128,1024]{1,0:T(8,128)(2,1)}, u32[]{:S(2)}, u32[]{:S(2)}) collective-permute-start(bf16[128,1024]{1,0:T(8,128)(2,1)S(1)} %add_convert_fusion.7), channel_id=1, source_target_pairs={{0,2},{1,3},{2,0},{3,1},{4,6},{5,7},{6,4},{7,5},{8,10},{9,11},{10,... | collective-permute-start | bytes 786440 | tf_op jit(solution)/shard_map/ppermute | solution.py:19
  271.8 11.6 %collective-permute-start.48 = (bf16[128,1024]{1,0:T(8,128)(2,1)S(1)}, bf16[128,1024]{1,0:T(8,128)(2,1)}, u32[]{:S(2)}, u32[]{:S(2)}) collective-permute-start(bf16[128,1024]{1,0:T(8,128)(2,1)S(1)} %add_convert_fusion.7), channel_id=1, source_target_pairs={{0,3},{1,0},{2,1},{3,2},{4,7},{5,4},{6,5},{7,6},{8,11},{9,8},{10,9... | collective-permute-start | bytes 786440 | tf_op jit(solution)/shard_map/ppermute | solution.py:19
  307.8 94.7 %reduce-scatter.7.cloned.1.call-start = ((), (), s32[]{:S(2)}) async-start(), calls=%async_computation.5 | async-start | bytes 3538944 | tf_op jit(solution)/shard_map/reduce_scatter | solution.py:258
  310.1 22.8 %collective-permute-start.71 = (bf16[512,2992]{0,1:T(8,128)(2,1)S(1)}, bf16[512,2992]{0,1:T(8,128)(2,1)S(1)}, u32[]{:S(2)}, u32[]{:S(2)}) collective-permute-start(bf16[512,2992]{0,1:T(8,128)(2,1)S(1)} %constant_dynamic-slice_fusion), channel_id=1, source_target_pairs={{0,4},{4,0},{1,5},{5,1},{2,6},{6,2},{3,7},{7,3},{8,12},{12,8},{9,1... | collective-permute-start | bytes 9191432 | tf_op jit(solution)/shard_map/ppermute | solution.py:23
  316.7 13.6 %collective-permute-start.53 = (bf16[128,1024]{1,0:T(8,128)(2,1)S(1)}, bf16[128,1024]{1,0:T(8,128)(2,1)S(1)}, u32[]{:S(2)}, u32[]{:S(2)}) collective-permute-start(bf16[128,1024]{1,0:T(8,128)(2,1)S(1)} %get-tuple-element.116), channel_id=1, source_target_pairs={{0,3},{1,0},{2,1},{3,2},{4,7},{5,4},{6,5},{7,6},{8,11},{9,8},{10,9... | collective-permute-start | bytes 786440 | tf_op jit(solution)/shard_map/ppermute | solution.py:19
  318.6 12.7 %collective-permute-start.52 = (bf16[128,1024]{1,0:T(8,128)(2,1)S(1)}, bf16[128,1024]{1,0:T(8,128)(2,1)S(1)}, u32[]{:S(2)}, u32[]{:S(2)}) collective-permute-start(bf16[128,1024]{1,0:T(8,128)(2,1)S(1)} %get-tuple-element.117), channel_id=1, source_target_pairs={{0,1},{1,2},{2,3},{3,0},{4,5},{5,6},{6,7},{7,4},{8,9},{9,10},{10,1... | collective-permute-start | bytes 786440 | tf_op jit(solution)/shard_map/ppermute | solution.py:19
  343.0 14.4 %collective-permute-start.55 = (bf16[128,1024]{1,0:T(8,128)(2,1)S(1)}, bf16[128,1024]{1,0:T(8,128)(2,1)S(1)}, u32[]{:S(2)}, u32[]{:S(2)}) collective-permute-start(bf16[128,1024]{1,0:T(8,128)(2,1)S(1)} %fusion.115), channel_id=1, source_target_pairs={{0,2},{1,3},{2,0},{3,1},{4,6},{5,7},{6,4},{7,5},{8,10},{9,11},{10,... | collective-permute-start | bytes 786440 | tf_op jit(solution)/shard_map/ppermute | solution.py:19
  345.8 11.6 %collective-permute-start.54 = (bf16[128,1024]{1,0:T(8,128)(2,1)S(1)}, bf16[128,1024]{1,0:T(8,128)(2,1)S(1)}, u32[]{:S(2)}, u32[]{:S(2)}) collective-permute-start(bf16[128,1024]{1,0:T(8,128)(2,1)S(1)} %fusion.115), channel_id=1, source_target_pairs={{0,3},{1,0},{2,1},{3,2},{4,7},{5,4},{6,5},{7,6},{8,11},{9,8},{10,9... | collective-permute-start | bytes 786440 | tf_op jit(solution)/shard_map/ppermute | solution.py:19
  372.3 50.9 %collective-permute-start.32 = (bf16[128,1024]{1,0:T(8,128)(2,1)}, bf16[128,1024]{1,0:T(8,128)(2,1)}, u32[]{:S(2)}, u32[]{:S(2)}) collective-permute-start(bf16[128,1024]{1,0:T(8,128)(2,1)} %get-tuple-element.124), channel_id=1, source_target_pairs={{0,2},{1,3},{2,0},{3,1},{4,6},{5,7},{6,4},{7,5},{8,10},{9,11},{10,... | collective-permute-start | bytes 786440 | tf_op jit(solution)/shard_map/ppermute | solution.py:19
  373.0 50.9 %collective-permute-start.34 = (bf16[128,1024]{1,0:T(8,128)(2,1)}, bf16[128,1024]{1,0:T(8,128)(2,1)}, u32[]{:S(2)}, u32[]{:S(2)}) collective-permute-start(bf16[128,1024]{1,0:T(8,128)(2,1)} %get-tuple-element.125), channel_id=1, source_target_pairs={{0,3},{1,0},{2,1},{3,2},{4,7},{5,4},{6,5},{7,6},{8,11},{9,8},{10,9... | collective-permute-start | bytes 786440 | tf_op jit(solution)/shard_map/ppermute | solution.py:19
  375.6 48.4 %collective-permute-start.33 = (bf16[128,1024]{1,0:T(8,128)(2,1)}, bf16[128,1024]{1,0:T(8,128)(2,1)}, u32[]{:S(2)}, u32[]{:S(2)}) collective-permute-start(bf16[128,1024]{1,0:T(8,128)(2,1)} %get-tuple-element.126), channel_id=1, source_target_pairs={{0,1},{1,2},{2,3},{3,0},{4,5},{5,6},{6,7},{7,4},{8,9},{9,10},{10,1... | collective-permute-start | bytes 786440 | tf_op jit(solution)/shard_map/ppermute | solution.py:19
  379.8 34.1 %all-to-all-start = ((bf16[8,64,1024]{2,1,0:T(8,128)(2,1)}), bf16[8,64,1024]{2,1,0:T(8,128)(2,1)}, u32[]{:S(2)}, u32[]{:S(2)}) async-start(bf16[8,64,1024]{2,1,0:T(8,128)(2,1)} %bitcast.261), calls=%async_computation | async-start | bytes 2097152 | tf_op jit(solution)/shard_map/all_to_all | solution.py:262
  415.4 39.6 %all-to-all-start.2 = ((bf16[8,64,1968]{2,1,0:T(8,128)(2,1)}), bf16[8,64,1968]{2,1,0:T(8,128)(2,1)S(1)}, u32[]{:S(2)}, u32[]{:S(2)}) async-start(bf16[8,64,1968]{2,1,0:T(8,128)(2,1)} %broadcast_in_dim.167), calls=%async_computation.2 | async-start | bytes 4194304 | tf_op jit(solution)/shard_map/all_to_all | solution.py:269
  426.3 40.5 %collective-permute-start.35 = (bf16[128,1024]{1,0:T(8,128)(2,1)}, bf16[128,1024]{1,0:T(8,128)(2,1)}, u32[]{:S(2)}, u32[]{:S(2)}) collective-permute-start(bf16[128,1024]{1,0:T(8,128)(2,1)} %get-tuple-element.72), channel_id=1, source_target_pairs={{0,64},{64,0},{1,65},{65,1},{2,66},{66,2},{3,67},{67,3},{4,68},{68... | collective-permute-start | bytes 786440 | tf_op jit(solution)/shard_map/ppermute | solution.py:27
  438.0 15.4 %collective-permute-start.72 = (bf16[64,1024]{1,0:T(8,128)(2,1)S(1)}, bf16[64,1024]{1,0:T(8,128)(2,1)S(1)}, u32[]{:S(2)}, u32[]{:S(2)}) collective-permute-start(bf16[64,1024]{1,0:T(8,128)(2,1)S(1)} %broadcast_select_fusion.27), channel_id=1, source_target_pairs={{0,64},{64,0},{1,65},{65,1},{2,66},{66,2},{3,67},{67,3},{4,68},{68... | collective-permute-start | bytes 393224 | tf_op jit(solution)/shard_map/ppermute | solution.py:27
  443.4 19.0 %collective-permute-start.61 = (f32[2,1024]{1,0:T(2,128)}, f32[2,1024]{1,0:T(2,128)}, u32[]{:S(2)}, u32[]{:S(2)}) collective-permute-start(f32[2,1024]{1,0:T(2,128)} %broadcast_select_fusion.36), channel_id=1, source_target_pairs={{0,64},{64,0},{1,65},{65,1},{2,66},{66,2},{3,67},{67,3},{4,68},{68... | collective-permute-start | bytes 24584 | tf_op jit(solution)/shard_map/ppermute | solution.py:27
  457.0 22.9 %all-to-all-start.1 = ((bf16[8,64,1024]{2,1,0:T(8,128)(2,1)}), bf16[8,64,1024]{2,1,0:T(8,128)(2,1)}, u32[]{:S(2)}, u32[]{:S(2)}) async-start(bf16[8,64,1024]{2,1,0:T(8,128)(2,1)} %broadcast_in_dim.164), calls=%async_computation.1 | async-start | bytes 2097152 | tf_op jit(solution)/shard_map/all_to_all | solution.py:269
  475.7 30.7 %collective-permute-start.76 = (bf16[512,1968]{0,1:T(8,128)(2,1)}, bf16[512,1968]{0,1:T(8,128)(2,1)}, u32[]{:S(2)}, u32[]{:S(2)}) collective-permute-start(bf16[512,1968]{0,1:T(8,128)(2,1)} %copy.123), channel_id=1, source_target_pairs={{0,4},{4,0},{1,5},{5,1},{2,6},{6,2},{3,7},{7,3},{8,12},{12,8},{9,1... | collective-permute-start | bytes 6045704 | tf_op jit(solution)/shard_map/ppermute | solution.py:23
  480.0 13.1 %collective-permute-start.73 = (bf16[512,1024]{1,0:T(8,128)(2,1)}, bf16[512,1024]{1,0:T(8,128)(2,1)S(1)}, u32[]{:S(2)}, u32[]{:S(2)}) collective-permute-start(bf16[512,1024]{1,0:T(8,128)(2,1)} %bitcast.70), channel_id=1, source_target_pairs={{0,4},{4,0},{1,5},{5,1},{2,6},{6,2},{3,7},{7,3},{8,12},{12,8},{9,1... | collective-permute-start | bytes 3145736 | tf_op jit(solution)/shard_map/ppermute | solution.py:23
  (184 other events, 1928.6 us)
Sparse Core Ops, SparseCore 0:
  307.9 35.5 reduce-scatter.8
  346.6 55.8 reduce-scatter.6

commit v3 on v2

--- a/solution.py
+++ b/solution.py
@@ -31,21 +31,27 @@
     return lax.ppermute(block, ("section", "zlo"), [(0, 3), (1, 2), (2, 1), (3, 0)])
 
 
-def gather_rows(block):
+def gather_parts(block):
     ahead2 = around(block, "tensor", 2)
     ahead1 = around(block, "tensor", -1)
     ahead3 = around(block, "tensor", 1)
-    return jnp.concatenate([block, ahead1, ahead2, ahead3], axis=0)
-
-
-def scatter_rows(terms, row_count):
-    parts = [terms[k * row_count : (k + 1) * row_count] for k in range(4)]
-    sent2 = around(parts[2].astype(bf16), "tensor", 2)
-    sent1 = around(parts[1].astype(bf16), "tensor", 1)
-    sent3 = around(parts[3].astype(bf16), "tensor", -1)
-    return (
-        parts[0].astype(f32) + sent2.astype(f32) + sent1.astype(f32) + sent3.astype(f32)
-    )
+    return [block, ahead1, ahead2, ahead3]
+
+
+def scatter_parts(term_of):
+    sent2 = around(term_of(2).astype(bf16), "tensor", 2)
+    sent1 = around(term_of(1).astype(bf16), "tensor", 1)
+    sent3 = around(term_of(3).astype(bf16), "tensor", -1)
+    kept = term_of(0).astype(f32)
+    return kept + sent2.astype(f32) + sent1.astype(f32) + sent3.astype(f32)
+
+
+def joined(parts, axis=0):
+    return jnp.concatenate(parts, axis=axis)
+
+
+def after_all(values, *others):
+    return lax.optimization_barrier((values,) + others)[0]
 
 
 def sum_tensor(block):
@@ -115,82 +121,107 @@
     return jnp.dot(left_rows, weight, preferred_element_type=f32)
 
 
-def forward_layer(inputs, gain_pair, weights, allowed, tables):
+def gelu_product(first_half, second_half):
+    return jax.nn.gelu(first_half, approximate=False) * second_half
+
+
+def forward_layer(inputs, normed_parts, gain_mid, weights, allowed, tables):
     w_qkv, w_out, w_up, w_down = weights
     row_count = inputs.shape[0]
-    normed_all = gather_rows(layer_norm(inputs, gain_pair[0]).astype(bf16))
-    full_rows = normed_all.shape[0]
     local_width = w_out.shape[0]
-    projected = times(normed_all, w_qkv).reshape(full_rows, 3, -1, HEAD_DIM)
-    queries = rotate(projected[:, 0], *tables).astype(bf16)
-    keys_rot = rotate(projected[:, 1], *tables).astype(bf16)
-    values_in = projected[:, 2].astype(bf16)
+    queries, keys_rot, values_in = [], [], []
+    for k, part in enumerate(normed_parts):
+        projected = times(part, w_qkv).reshape(row_count, 3, -1, HEAD_DIM)
+        rows = slice(k * row_count, (k + 1) * row_count)
+        turns = (tables[0][rows], tables[1][rows])
+        queries.append(rotate(projected[:, 0], *turns).astype(bf16))
+        keys_rot.append(rotate(projected[:, 1], *turns).astype(bf16))
+        values_in.append(projected[:, 2].astype(bf16))
+    keys_all = joined(keys_rot)
+    values_all = joined(values_in)
+    attended = [None] * 4
+    log_totals = [None] * 4
+
+    def attend(k):
+        rows = slice(k * row_count, (k + 1) * row_count)
+        scores = masked_scores(queries[k], keys_all, allowed[rows])
+        largest = jnp.max(scores, axis=2, keepdims=True)
+        exp_scores = jnp.exp(scores - largest)
+        totals = jnp.sum(exp_scores, axis=2, keepdims=True)
+        soft_weights = (exp_scores / totals).astype(bf16)
+        log_totals[k] = largest + jnp.log(totals)
+        mixed = jnp.einsum("hqk,khd->qhd", soft_weights, values_all, preferred_element_type=f32)
+        attended[k] = mixed.reshape(row_count, local_width).astype(bf16)
+        return times(attended[k], w_out)
+
+    resid_mid = inputs + scatter_parts(attend)
+    mid_parts = gather_parts(layer_norm(resid_mid, gain_mid).astype(bf16))
+    gelu_in = [None] * 4
+    gate_mult = [None] * 4
+    mixed_rows = [None] * 4
+
+    def feed(k):
+        hidden = times(mid_parts[k], w_up)
+        local_hidden = hidden.shape[1] // 2
+        gelu_in[k] = hidden[:, :local_hidden]
+        gate_mult[k] = hidden[:, local_hidden:]
+        mixed_rows[k] = gelu_product(gelu_in[k], gate_mult[k]).astype(bf16)
+        return times(mixed_rows[k], w_down)
+
+    result = resid_mid + scatter_parts(feed)
+    kept = dict(
+        inputs=inputs,
+        resid_mid=resid_mid,
+        normed=normed_parts,
+        queries=joined(queries),
+        keys=keys_all,
+        values=values_all,
+        log_totals=joined(log_totals, 1),
+        attended=attended,
+        normed_mid=mid_parts,
+        gelu_in=gelu_in,
+        gate_mult=gate_mult,
+        mixed=mixed_rows,
+    )
+    return (result, kept)
+
+
+def backward_ffn(grad_result, kept, gain_mid, weights):
+    w_up, w_down = weights[2], weights[3]
+    grad_parts = gather_parts(grad_result.astype(bf16))
+    grad_hidden = [None] * 4
+
+    def feed_back(k):
+        grad_mixed = contract_last(grad_parts[k], w_down)
+        unused, pull_gelu = jax.vjp(gelu_product, kept["gelu_in"][k], kept["gate_mult"][k])
+        grad_hidden[k] = joined(pull_gelu(grad_mixed), 1).astype(bf16)
+        return contract_last(grad_hidden[k], w_up)
+
+    grad_normed_mid = scatter_parts(feed_back)
+    unused, pull_norm = jax.vjp(layer_norm, kept["resid_mid"], gain_mid)
+    grad_resid, grad_gain = pull_norm(grad_normed_mid)
+    grad_mid = grad_result + grad_resid
+
+    def weight_grads(gate):
+        outer, inner, left, right = after_all(
+            (grad_parts, kept["mixed"], kept["normed_mid"], grad_hidden), gate
+        )
+        grad_down = contract_rows(joined(outer), joined(inner)).astype(bf16)
+        grad_up = contract_rows(joined(left), joined(right)).astype(bf16)
+        return joined([grad_up, grad_down], 1)
+
+    return (grad_mid, weight_grads, grad_gain)
+
+
+def backward_attn(grad_mid, kept, gain_first, weights, allowed, tables):
+    w_qkv, w_out = weights[0], weights[1]
+    queries, keys_rot, values_in = kept["queries"], kept["keys"], kept["values"]
+    row_count = grad_mid.shape[0]
+    grad_parts = gather_parts(grad_mid.astype(bf16))
+    grad_attended = joined([contract_last(part, w_out).astype(bf16) for part in grad_parts])
+    grad_attended = grad_attended.reshape(queries.shape)
     scores = masked_scores(queries, keys_rot, allowed)
-    largest = jnp.max(scores, axis=2, keepdims=True)
-    exp_scores = jnp.exp(scores - largest)
-    totals = jnp.sum(exp_scores, axis=2, keepdims=True)
-    soft_weights = (exp_scores / totals).astype(bf16)
-    log_totals = largest + jnp.log(totals)
-    attended = jnp.einsum("hqk,khd->qhd", soft_weights, values_in, preferred_element_type=f32)
-    attended = attended.reshape(full_rows, local_width).astype(bf16)
-    resid_mid = inputs + scatter_rows(times(attended, w_out), row_count)
-    normed_mid_all = gather_rows(layer_norm(resid_mid, gain_pair[1]).astype(bf16))
-    hidden = times(normed_mid_all, w_up)
-    local_hidden = hidden.shape[1] // 2
-    gelu_in = hidden[:, :local_hidden]
-    gate_mult = hidden[:, local_hidden:]
-    mixed_rows = (jax.nn.gelu(gelu_in, approximate=False) * gate_mult).astype(bf16)
-    result = resid_mid + scatter_rows(times(mixed_rows, w_down), row_count)
-    kept = (
-        inputs,
-        resid_mid,
-        normed_all,
-        queries,
-        keys_rot,
-        values_in,
-        log_totals,
-        attended,
-        normed_mid_all,
-        gelu_in,
-        gate_mult,
-        mixed_rows,
-    )
-    return (result, kept)
-
-
-def gelu_product(first_half, second_half):
-    return jax.nn.gelu(first_half, approximate=False) * second_half
-
-
-def backward_ffn(grad_result, kept, gain_pair, weights):
-    w_up, w_down = weights[2], weights[3]
-    resid_mid, normed_mid_all = kept[1], kept[8]
-    gelu_in, gate_mult, mixed_rows = kept[9], kept[10], kept[11]
-    row_count = grad_result.shape[0]
-    grad_ffn_all = gather_rows(grad_result.astype(bf16))
-    grad_mixed = contract_last(grad_ffn_all, w_down)
-    unused, pull_gelu = jax.vjp(gelu_product, gelu_in, gate_mult)
-    grad_gelu, grad_gate = pull_gelu(grad_mixed)
-    grad_hidden = jnp.concatenate([grad_gelu, grad_gate], axis=1).astype(bf16)
-    grad_normed_mid = scatter_rows(contract_last(grad_hidden, w_up), row_count)
-    unused, pull_norm = jax.vjp(layer_norm, resid_mid, gain_pair[1])
-    grad_resid, grad_gain = pull_norm(grad_normed_mid)
-    grad_w_down = contract_rows(grad_ffn_all, mixed_rows).astype(bf16)
-    grad_w_up = contract_rows(normed_mid_all, grad_hidden).astype(bf16)
-    grad_w = jnp.concatenate([grad_w_up, grad_w_down], axis=1)
-    return (grad_result + grad_resid, grad_w, grad_gain)
-
-
-def backward_attn(grad_mid, kept, gain_pair, weights, allowed, tables):
-    w_qkv, w_out = weights[0], weights[1]
-    inputs, normed_all = kept[0], kept[2]
-    queries, keys_rot, values_in, log_totals, attended = kept[3:8]
-    row_count = grad_mid.shape[0]
-    full_rows = normed_all.shape[0]
-    grad_att_all = gather_rows(grad_mid.astype(bf16))
-    grad_attended = contract_last(grad_att_all, w_out).astype(bf16).reshape(queries.shape)
-    scores = masked_scores(queries, keys_rot, allowed)
-    soft_exact = jnp.exp(scores - log_totals)
+    soft_exact = jnp.exp(scores - kept["log_totals"])
     soft_weights = soft_exact.astype(bf16)
     grad_values = jnp.einsum(
         "hqk,qhd->khd", soft_weights, grad_attended, preferred_element_type=f32
@@ -212,17 +243,27 @@
         ],
         axis=1,
     )
-    grad_projected = grad_projected.astype(bf16).reshape(full_rows, -1)
-    grad_normed = scatter_rows(contract_last(grad_projected, w_qkv), row_count)
-    unused, pull_norm = jax.vjp(layer_norm, inputs, gain_pair[0])
+    grad_projected = grad_projected.astype(bf16).reshape(4 * row_count, -1)
+
+    def project_back(k):
+        return contract_last(grad_projected[k * row_count : (k + 1) * row_count], w_qkv)
+
+    grad_normed = scatter_parts(project_back)
+    unused, pull_norm = jax.vjp(layer_norm, kept["inputs"], gain_first)
     grad_resid, grad_gain = pull_norm(grad_normed)
-    grad_w_out = contract_rows(grad_att_all, attended).astype(bf16)
-    grad_w_qkv = contract_rows(normed_all, grad_projected).astype(bf16)
-    grad_w = jnp.concatenate([grad_w_qkv, grad_w_out], axis=1)
-    return (grad_mid + grad_resid, grad_w, grad_gain)
-
-
-def other_layer(own, after, pair_x):
+
+    def weight_grads(gate):
+        outer, inner, left, right = (grad_parts, kept["attended"], kept["normed"], grad_projected)
+        if gate is not None:
+            outer, inner, left, right = after_all((outer, inner, left, right), gate)
+        grad_out = contract_rows(joined(outer), joined(inner)).astype(bf16)
+        grad_qkv = contract_rows(joined(left), right).astype(bf16)
+        return joined([grad_qkv, grad_out], 1)
+
+    return (grad_mid + grad_resid, weight_grads, grad_gain)
+
+
+def other_layer(own, after, pair_x, before_core=()):
     core_index = lax.axis_index("core")
     parity = lax.axis_index("x") % 2
     own, unused = lax.optimization_barrier((own, after))
@@ -237,6 +278,7 @@
         piece = rows // 2
         sent = lax.dynamic_slice_in_dim(own, core_index * piece, piece)
         got = half = swap_layer(sent)
+    half = after_all(half, *before_core)
     return in_order(core_index, half, swap_core(half)), got
 
 
@@ -281,24 +323,25 @@
     is_first = section_index == 0
     row_count = tokens.shape[1]
     full_rows = row_count * lax.axis_size("tensor")
+    start_rows = jnp.where(is_first, tokens[0], tokens[1]).astype(f32)
+    end_grads = jnp.where(is_first, cotangent[0], cotangent[1])
+    gains_other = swap_layer(gains[0])
+    gains0 = jnp.where(is_first, gains[0], gains_other)
+    gains1 = jnp.where(is_first, gains_other, gains[0])
+    first_parts = gather_parts(layer_norm(start_rows, gains0[0]).astype(bf16))
     own = (
         w_qkv[0].reshape(w_qkv.shape[1], -1),
         w_out[0],
         w_up[0].reshape(w_up.shape[1], -1),
         w_down[0],
     )
-    other_qkv, after = other_layer(own[0], tokens[0, 0, 0], False)
+    other_qkv, after = other_layer(own[0], tokens[0, 0, 0], False, first_parts)
     other_out, after = other_layer(own[1], after, False)
     other_up, after = other_layer(own[2], after, True)
     other_down, after = other_layer(own[3], after, True)
     others = (other_qkv, other_out, other_up, other_down)
-    gains_other = swap_layer(gains[0])
     layer0 = tuple(jnp.where(is_first, a, b) for a, b in zip(own, others))
     layer1 = tuple(jnp.where(is_first, b, a) for a, b in zip(own, others))
-    gains0 = jnp.where(is_first, gains[0], gains_other)
-    gains1 = jnp.where(is_first, gains_other, gains[0])
-    start_rows = jnp.where(is_first, tokens[0], tokens[1])
-    end_grads = jnp.where(is_first, cotangent[0], cotangent[1])
     doc_lengths = jnp.where(is_first, lengths[0, 0], lengths[1, 0])
     indices = jnp.arange(full_rows, dtype=jnp.int32)
     indices = (indices + lax.axis_index("tensor") * row_count) % full_rows
@@ -310,23 +353,32 @@
     tables0 = rope_tables(positions, 10000.0)
     tables1 = rope_tables(positions, 160000.0)
 
-    out0, kept0 = forward_layer(start_rows.astype(f32), gains0, layer0, allowed0, tables0)
+    out0, kept0 = forward_layer(
+        start_rows, first_parts, gains0[1], layer0, allowed0, tables0
+    )
     out0 = out0.astype(bf16)
-    out1, kept1 = forward_layer(out0.astype(f32), gains1, layer1, allowed1, tables1)
+    second_rows = out0.astype(f32)
+    second_parts = gather_parts(layer_norm(second_rows, gains1[0]).astype(bf16))
+    out1, kept1 = forward_layer(
+        second_rows, second_parts, gains1[1], layer1, allowed1, tables1
+    )
     out1 = out1.astype(bf16)
-    mid1, ffn1, gain_mid1 = backward_ffn(end_grads.astype(f32), kept1, gains1, layer1)
-    in1, attn1, gain_first1 = backward_attn(mid1, kept1, gains1, layer1, allowed1, tables1)
+    mid1, ffn_grads1, gain_mid1 = backward_ffn(end_grads.astype(f32), kept1, gains1[1], layer1)
+    ffn1 = reduce_part(ffn_grads1(mid1))
+    in1, attn_grads1, gain_first1 = backward_attn(
+        mid1, kept1, gains1[0], layer1, allowed1, tables1
+    )
     in1 = in1.astype(bf16)
-    mid0, ffn0, gain_mid0 = backward_ffn(in1.astype(f32), kept0, gains0, layer0)
-    in0, attn0, gain_first0 = backward_attn(mid0, kept0, gains0, layer0, allowed0, tables0)
+    attn1 = reduce_part(attn_grads1(in1))
+    mid0, ffn_grads0, gain_mid0 = backward_ffn(in1.astype(f32), kept0, gains0[1], layer0)
+    ffn0 = reduce_part_now(ffn_grads0(mid0))
+    ffn_sum = spread_part(join_sections(is_first, ffn0, ffn1))
+    in0, attn_grads0, gain_first0 = backward_attn(
+        mid0, kept0, gains0[0], layer0, allowed0, tables0
+    )
     in0 = in0.astype(bf16)
-
-    both1 = reduce_part(jnp.concatenate([attn1, ffn1], axis=1))
-    attn_width = attn1.shape[1]
-    part_ffn0 = reduce_part(ffn0)
-    ffn_sum = spread_part(join_sections(is_first, part_ffn0, both1[:, attn_width:]))
-    part_attn0 = reduce_part_now(attn0)
-    attn_sum = spread_part(join_sections(is_first, part_attn0, both1[:, :attn_width]))
+    attn0 = reduce_part_now(attn_grads0(None))
+    attn_sum = spread_part(join_sections(is_first, attn0, attn1))
     up_width = own[2].shape[1]
     qkv_width = own[0].shape[1]
 

time: 531 us -> 534 us (level)
  waiting for transfers between devices: 212 us -> 148 us
  matrix products: 49.1 us -> 83.7 us
  starting transfers between devices: 122 us -> 149 us
  local copies, waits for them, and re-layouts: 48 us -> 56.3 us
    ppermute x55, waiting for transfers between devices: 157 us -> 69.7 us  [around(): lax.ppermute(block, axis, [(i, (i + distance) % count) for i in range(cou...]
    all_to_all x1 -> x2, waiting for transfers between devices: 0.01 us -> 15.3 us  [reduce_part_now(): pieces = lax.all_to_all(add_core(grads), ('zlo', 'x'), 0, 0, tiled=True)]
    ppermute x10 -> x11, starting transfers between devices: 16.8 us -> 30.6 us  [swap_core(): return lax.ppermute(block, 'core', [(0, 1), (1, 0)])]
    dot_general x8 -> x32, matrix products: 11 us -> 23.3 us  [times(): return jnp.dot(left_rows, weight, preferred_element_type=f32)]
    ppermute x55, starting transfers between devices: 70.2 us -> 77.6 us  [around(): lax.ppermute(block, axis, [(i, (i + distance) % count) for i in range(cou...]
    dot_general x2 -> x10, matrix products: 1.84 us -> 9.05 us  [masked_scores(): jnp.einsum('qhd,khd->hqk', queries, keys_rot, preferred_element_type=f32)]
    all_to_all x1 -> x2, starting transfers between devices: 4.45 us -> 11.6 us  [reduce_part_now(): pieces = lax.all_to_all(add_core(grads), ('zlo', 'x'), 0, 0, tiled=True)]
    reduce_sum x6 -> x2, other arithmetic: 6.55 us -> 0.67 us  [layer_norm(): return centered * lax.rsqrt(variance + epsilon) * gain_scale]
  transfers between devices with their start and end apart: 82 -> 84, of which waited for: 43 -> 30; matrix products, arithmetic and copies ran while one was open for 21% -> 35% of each run, Pallas kernels for 0% -> 0%
where the time goes in v3:
time: 534 us; the launch traced here: 528 us
  starting transfers between devices  149 us (28%)
  waiting for transfers between devices  148 us (28%)
  matrix products  83.7 us (16%)
  other arithmetic  71.8 us (13%)
  local copies, waits for them, and re-layouts  56.3 us (11%)
  between operations  18.2 us (3%)
    ppermute x55, starting transfers between devices, around(): lax.ppermute(block, axis, [(i, (i + distance) % count) for i in range(cou...  77.6 us
    ppermute x55, waiting for transfers between devices, around(): lax.ppermute(block, axis, [(i, (i + distance) % count) for i in range(cou...  69.7 us
    ppermute x11, starting transfers between devices, swap_core(): return lax.ppermute(block, 'core', [(0, 1), (1, 0)])  30.6 us
    unnamed x441, local copies, waits for them, and re-layouts  29.5 us
    reduce_scatter x2, waiting for transfers between devices, reduce_part(): lax.psum_scatter(add_core(grads), ('zlo', 'x'), scatter_dimension=0, tile...  23.3 us
    dot_general x32, matrix products, times(): return jnp.dot(left_rows, weight, preferred_element_type=f32)  23.3 us
    dot_general x32, matrix products, contract_last(): lax.dot_general(left_rows, weight, (((1,), (1,)), ((), ())), preferred_el...  22.3 us
    ppermute x5, waiting for transfers between devices, swap_layer(): lax.ppermute(block, ('section', 'zlo'), [(0, 3), (1, 2), (2, 1), (3, 0)])  18.5 us
  transfers between devices with their start and end apart: 84, of which 30 were waited for; matrix products, arithmetic and copies ran while one was open for 35% of the time, Pallas kernels for 0%

profile of v3, /device:TPU:1, one launch (start us, length us, event | category | flops | bytes accessed | tf_op | source)
XLA Modules:
  0.0 527.7 jit_solution(6841450178841334059)
XLA Ops:
  7.2 4.7 collective-permute-start
  21.9 12.3 %collective-permute-done.1 = bf16[512,768]{0,1:T(8,128)(2,1)} collective-permute-done((bf16[512,768]{0,1:T(8,128)(2,1)}, bf16[512,768]{0,1:T(8,128)(2,1)}, u32[]{:S(2)}, u32[]{:S(2)}) %collective-permute-start.1) | collective-permute-done | bytes 786464 | tf_op jit(solution)/shard_map/ppermute | solution.py:31
  41.6 2.8 collective-permute-start.7
  47.2 2.8 collective-permute-done.3
  50.0 2.7 collective-permute-start.5
  81.5 2.8 fusion.339
  88.1 5.8 %collective-permute-done.14 = bf16[164,1024]{1,0:T(8,128)(2,1)S(1)} collective-permute-done((bf16[164,1024]{1,0:T(8,128)(2,1)S(1)}, bf16[164,1024]{1,0:T(8,128)(2,1)S(1)}, u32[]{:S(2)}, u32[]{:S(2)}) %collective-permute-start.14) | collective-permute-done | bytes 335904 | tf_op jit(solution)/shard_map/ppermute | solution.py:31
  98.3 3.9 collective-permute-done.15
  102.4 3.1 collective-permute-start.16
  113.8 4.9 collective-permute-done.17
  136.0 3.2 collective-permute-done.22
  140.7 2.9 collective-permute-start.24
  145.2 8.8 %collective-permute-done.23 = bf16[128,1024]{1,0:T(8,128)(2,1)S(1)} collective-permute-done((bf16[128,1024]{1,0:T(8,128)(2,1)S(1)}, bf16[128,1024]{1,0:T(8,128)(2,1)S(1)}, u32[]{:S(2)}, u32[]{:S(2)}) %collective-permute-start.23) | collective-permute-done | bytes 262176 | tf_op jit(solution)/shard_map/ppermute | solution.py:19
  162.1 3.5 collective-permute-start.28
  167.4 2.8 fusion.340
  173.5 10.0 %collective-permute-done.27 = bf16[128,1024]{1,0:T(8,128)(2,1)S(1)} collective-permute-done((bf16[128,1024]{1,0:T(8,128)(2,1)S(1)}, bf16[128,1024]{1,0:T(8,128)(2,1)S(1)}, u32[]{:S(2)}, u32[]{:S(2)}) %collective-permute-start.27) | collective-permute-done | bytes 262176 | tf_op jit(solution)/shard_map/ppermute | solution.py:19
  184.3 2.9 collective-permute-start.31
  189.4 4.7 collective-permute-done.33
  197.9 3.3 collective-permute-start.41
  211.7 4.2 collective-permute-done.37
  222.1 3.1 convolution_convert_fusion
  229.7 2.7 collective-permute-done.43
  236.0 3.6 fusion.45
  253.5 2.9 collective-permute-done.46
  270.7 5.0 collective-permute-done.48
  284.0 6.3 %collective-permute-start.75 = (bf16[512,1968]{0,1:T(8,128)(2,1)}, bf16[512,1968]{0,1:T(8,128)(2,1)}, u32[]{:S(2)}, u32[]{:S(2)}) collective-permute-start(bf16[512,1968]{0,1:T(8,128)(2,1)} %fusion.9), channel_id=1, source_target_pairs={{0,4},{4,0},{1,5},{5,1},{2,6},{6,2},{3,7},{7,3},{8,12},{12,8},{9,1... | collective-permute-start | bytes 6045704 | tf_op jit(solution)/shard_map/ppermute | solution.py:23
  305.4 4.1 collective-permute-start.71
  312.8 3.9 multiply_reduce_fusion
  318.9 3.7 add_convert_fusion
  322.6 3.8 copy.166
  338.9 4.5 all-to-all-start.2
  360.2 2.8 add_convert_fusion.3
  365.2 15.3 %all-to-all-done.2 = bf16[8,64,1968]{2,1,0:T(8,128)(2,1)} async-done(((bf16[8,64,1968]{2,1,0:T(8,128)(2,1)}), bf16[8,64,1968]{2,1,0:T(8,128)(2,1)}, u32[]{:S(2)}, u32[]{:S(2)}) %all-to-all-start.2) | async-done | bytes 2015264 | tf_op jit(solution)/shard_map/all_to_all | solution.py:304
  380.5 7.1 %all-to-all-start = ((bf16[8,64,1024]{2,1,0:T(8,128)(2,1)}), bf16[8,64,1024]{2,1,0:T(8,128)(2,1)}, u32[]{:S(2)}, u32[]{:S(2)}) async-start(bf16[8,64,1024]{2,1,0:T(8,128)(2,1)} %bitcast.501), calls=%async_computation | async-start | bytes 2097152 | tf_op jit(solution)/shard_map/all_to_all | solution.py:304
  387.7 2.7 reduce_sum.365
  395.4 13.0 %collective-permute-done.76 = bf16[64,1968]{1,0:T(8,128)(2,1)S(1)} collective-permute-done((bf16[64,1968]{1,0:T(8,128)(2,1)S(1)}, bf16[64,1968]{1,0:T(8,128)(2,1)S(1)}, u32[]{:S(2)}, u32[]{:S(2)}) %collective-permute-start.76) | collective-permute-done | bytes 251936 | tf_op jit(solution)/shard_map/ppermute | solution.py:27
  412.8 4.4 all-to-all-start.3
  430.1 23.3 %reduce-scatter.7.cloned.1.call-done = bf16[64,1024]{1,0:T(8,128)(2,1)} async-done(((bf16[512,1024]{1,0:T(8,128)(2,1)}), bf16[64,1024]{1,0:T(8,128)(2,1)}) %reduce-scatter.7.cloned.1.call-update) | async-done | bytes 131088 | tf_op jit(solution)/shard_map/reduce_scatter | solution.py:300
  461.3 4.5 all-to-all-start.1
  466.5 3.6 collective-permute-start.64
  471.3 2.8 collective-permute-done.62
  474.1 5.4 %collective-permute-start.65 = (f32[2,1024]{1,0:T(2,128)S(1)}, f32[2,1024]{1,0:T(2,128)S(1)}, u32[]{:S(2)}, u32[]{:S(2)}) collective-permute-start(f32[2,1024]{1,0:T(2,128)S(1)} %add_add_fusion.7), channel_id=1, source_target_pairs={{0,4},{4,0},{1,5},{5,1},{2,6},{6,2},{3,7},{7,3},{8,12},{12,8},{9,1... | collective-permute-start | bytes 24584 | tf_op jit(solution)/shard_map/ppermute | solution.py:23
  479.5 3.9 copy.146
  483.4 3.1 collective-permute-start.68
  489.3 3.1 collective-permute-start.60
  494.0 5.4 %collective-permute-done.69 = f32[2,1024]{1,0:T(2,128)S(1)} collective-permute-done((f32[2,1024]{1,0:T(2,128)S(1)}, f32[2,1024]{1,0:T(2,128)S(1)}, u32[]{:S(2)}, u32[]{:S(2)}) %collective-permute-start.69) | collective-permute-done | bytes 8224 | tf_op jit(solution)/shard_map/ppermute | solution.py:19
  509.4 3.5 copy.148
  517.6 3.1 convert.104
  (864 shorter events, 267.0 us)
Async XLA Ops:
  7.2 383.2 %reduce-scatter.9.cloned.1.call-start = ((), (), s32[]{:S(2)}) async-start(), calls=%async_computation.7 | async-start | bytes 2359296 | tf_op jit(solution)/shard_map/reduce_scatter | solution.py:300
  7.2 14.1 %collective-permute-start = (f32[2,1024]{1,0:T(2,128)}, f32[2,1024]{1,0:T(2,128)S(1)}, u32[]{:S(2)}, u32[]{:S(2)}) collective-permute-start(f32[2,1024]{1,0:T(2,128)} %bitcast.565), channel_id=1, source_target_pairs={{0,96},{32,64},{64,32},{96,0},{1,97},{33,65},{65,33},{97,1},{2,98}... | collective-permute-start | bytes 24584 | tf_op jit(solution)/shard_map/ppermute | solution.py:31
  14.6 19.6 %collective-permute-start.1 = (bf16[512,768]{0,1:T(8,128)(2,1)}, bf16[512,768]{0,1:T(8,128)(2,1)}, u32[]{:S(2)}, u32[]{:S(2)}) collective-permute-start(bf16[512,768]{0,1:T(8,128)(2,1)} %constant_dynamic-slice_fusion.3), channel_id=1, source_target_pairs={{0,96},{32,64},{64,32},{96,0},{1,97},{33,65},{65,33},{97,1},{2,98}... | collective-permute-start | bytes 2359304 | tf_op jit(solution)/shard_map/ppermute | solution.py:31
  35.7 11.5 %collective-permute-start.4 = (bf16[128,1024]{1,0:T(8,128)(2,1)}, bf16[128,1024]{1,0:T(8,128)(2,1)S(1)}, u32[]{:S(2)}, u32[]{:S(2)}) collective-permute-start(bf16[128,1024]{1,0:T(8,128)(2,1)} %fusion.160), channel_id=1, source_target_pairs={{0,1},{1,2},{2,3},{3,0},{4,5},{5,6},{6,7},{7,4},{8,9},{9,10},{10,1... | collective-permute-start | bytes 786440 | tf_op jit(solution)/shard_map/ppermute | solution.py:19
  37.0 13.1 %collective-permute-start.3 = (bf16[128,1024]{1,0:T(8,128)(2,1)}, bf16[128,1024]{1,0:T(8,128)(2,1)}, u32[]{:S(2)}, u32[]{:S(2)}) collective-permute-start(bf16[128,1024]{1,0:T(8,128)(2,1)} %fusion.160), channel_id=1, source_target_pairs={{0,2},{1,3},{2,0},{3,1},{4,6},{5,7},{6,4},{7,5},{8,10},{9,11},{10,... | collective-permute-start | bytes 786440 | tf_op jit(solution)/shard_map/ppermute | solution.py:19
  41.6 15.0 %collective-permute-start.7 = (bf16[128,1024]{1,0:T(8,128)(2,1)}, bf16[128,1024]{1,0:T(8,128)(2,1)}, u32[]{:S(2)}, u32[]{:S(2)}) collective-permute-start(bf16[128,1024]{1,0:T(8,128)(2,1)} %collective-permute-done.6), channel_id=1, source_target_pairs={{0,4},{4,0},{1,5},{5,1},{2,6},{6,2},{3,7},{7,3},{8,12},{12,8},{9,1... | collective-permute-start | bytes 786440 | tf_op jit(solution)/shard_map/ppermute | solution.py:23
  53.9 26.3 %collective-permute-start.11 = (bf16[256,1312]{0,1:T(8,128)(2,1)S(1)}, bf16[256,1312]{0,1:T(8,128)(2,1)S(1)}, u32[]{:S(2)}, u32[]{:S(2)}) collective-permute-start(bf16[256,1312]{0,1:T(8,128)(2,1)S(1)} %constant_dynamic-slice_fusion.1), channel_id=1, source_target_pairs={{0,96},{32,64},{64,32},{96,0},{1,97},{33,65},{65,33},{97,1},{2,98}... | collective-permute-start | bytes 2015240 | tf_op jit(solution)/shard_map/ppermute | solution.py:31
  71.3 13.6 %collective-permute-start.9 = (bf16[128,1024]{1,0:T(8,128)(2,1)S(1)}, bf16[128,1024]{1,0:T(8,128)(2,1)S(1)}, u32[]{:S(2)}, u32[]{:S(2)}) collective-permute-start(bf16[128,1024]{1,0:T(8,128)(2,1)S(1)} %convolution_convert_fusion.24), channel_id=1, source_target_pairs={{0,1},{1,2},{2,3},{3,0},{4,5},{5,6},{6,7},{7,4},{8,9},{9,10},{10,1... | collective-permute-start | bytes 786440 | tf_op jit(solution)/shard_map/ppermute | solution.py:19
  72.5 13.6 %collective-permute-start.8 = (bf16[128,1024]{1,0:T(8,128)(2,1)S(1)}, bf16[128,1024]{1,0:T(8,128)(2,1)S(1)}, u32[]{:S(2)}, u32[]{:S(2)}) collective-permute-start(bf16[128,1024]{1,0:T(8,128)(2,1)S(1)} %convolution_convert_fusion.25), channel_id=1, source_target_pairs={{0,2},{1,3},{2,0},{3,1},{4,6},{5,7},{6,4},{7,5},{8,10},{9,11},{10,... | collective-permute-start | bytes 786440 | tf_op jit(solution)/shard_map/ppermute | solution.py:19
  74.9 12.7 %collective-permute-start.10 = (bf16[128,1024]{1,0:T(8,128)(2,1)S(1)}, bf16[128,1024]{1,0:T(8,128)(2,1)S(1)}, u32[]{:S(2)}, u32[]{:S(2)}) collective-permute-start(bf16[128,1024]{1,0:T(8,128)(2,1)S(1)} %convolution_convert_fusion.23), channel_id=1, source_target_pairs={{0,3},{1,0},{2,1},{3,2},{4,7},{5,4},{6,5},{7,6},{8,11},{9,8},{10,9... | collective-permute-start | bytes 786440 | tf_op jit(solution)/shard_map/ppermute | solution.py:19
  80.2 15.5 %collective-permute-start.12 = (bf16[256,1312]{0,1:T(8,128)(2,1)S(1)}, bf16[256,1312]{0,1:T(8,128)(2,1)S(1)}, u32[]{:S(2)}, u32[]{:S(2)}) collective-permute-start(bf16[256,1312]{0,1:T(8,128)(2,1)S(1)} %collective-permute-done.11), channel_id=1, source_target_pairs={{0,8},{8,0},{16,24},{24,16},{1,9},{9,1},{17,25},{25,17},{2,10},{10... | collective-permute-start | bytes 2015240 | tf_op jit(solution)/shard_map/ppermute | solution.py:275
  84.9 110.1 %collective-permute-start.40 = (bf16[128,1024]{1,0:T(8,128)(2,1)S(1)}, bf16[128,1024]{1,0:T(8,128)(2,1)S(1)}, u32[]{:S(2)}, u32[]{:S(2)}) collective-permute-start(bf16[128,1024]{1,0:T(8,128)(2,1)S(1)} %copy-done.155), channel_id=1, source_target_pairs={{0,1},{1,2},{2,3},{3,0},{4,5},{5,6},{6,7},{7,4},{8,9},{9,10},{10,1... | collective-permute-start | bytes 786440 | tf_op jit(solution)/shard_map/ppermute | solution.py:19
  86.1 116.0 %collective-permute-start.38 = (bf16[128,1024]{1,0:T(8,128)(2,1)S(1)}, bf16[128,1024]{1,0:T(8,128)(2,1)S(1)}, u32[]{:S(2)}, u32[]{:S(2)}) collective-permute-start(bf16[128,1024]{1,0:T(8,128)(2,1)S(1)} %copy-done.155), channel_id=1, source_target_pairs={{0,3},{1,0},{2,1},{3,2},{4,7},{5,4},{6,5},{7,6},{8,11},{9,8},{10,9... | collective-permute-start | bytes 786440 | tf_op jit(solution)/shard_map/ppermute | solution.py:19
  96.0 13.5 %collective-permute-start.13 = (bf16[512,1312]{0,1:T(8,128)(2,1)S(1)}, bf16[512,1312]{0,1:T(8,128)(2,1)S(1)}, u32[]{:S(2)}, u32[]{:S(2)}) collective-permute-start(bf16[512,1312]{0,1:T(8,128)(2,1)S(1)} %pad_maximum_fusion.4), channel_id=1, source_target_pairs={{0,4},{4,0},{1,5},{5,1},{2,6},{6,2},{3,7},{7,3},{8,12},{12,8},{9,1... | collective-permute-start | bytes 4030472 | tf_op jit(solution)/shard_map/ppermute | solution.py:23
  105.8 24.3 %collective-permute-start.21 = (bf16[128,1024]{1,0:T(8,128)(2,1)S(1)}, bf16[128,1024]{1,0:T(8,128)(2,1)S(1)}, u32[]{:S(2)}, u32[]{:S(2)}) collective-permute-start(bf16[128,1024]{1,0:T(8,128)(2,1)S(1)} %multiply_convert_fusion.3), channel_id=1, source_target_pairs={{0,1},{1,2},{2,3},{3,0},{4,5},{5,6},{6,7},{7,4},{8,9},{9,10},{10,1... | collective-permute-start | bytes 786440 | tf_op jit(solution)/shard_map/ppermute | solution.py:19
  107.2 16.7 %collective-permute-start.19 = (bf16[128,1024]{1,0:T(8,128)(2,1)S(1)}, bf16[128,1024]{1,0:T(8,128)(2,1)S(1)}, u32[]{:S(2)}, u32[]{:S(2)}) collective-permute-start(bf16[128,1024]{1,0:T(8,128)(2,1)S(1)} %multiply_convert_fusion.3), channel_id=1, source_target_pairs={{0,3},{1,0},{2,1},{3,2},{4,7},{5,4},{6,5},{7,6},{8,11},{9,8},{10,9... | collective-permute-start | bytes 786440 | tf_op jit(solution)/shard_map/ppermute | solution.py:19
  121.5 13.6 %collective-permute-start.18 = (bf16[128,1024]{1,0:T(8,128)(2,1)S(1)}, bf16[128,1024]{1,0:T(8,128)(2,1)S(1)}, u32[]{:S(2)}, u32[]{:S(2)}) collective-permute-start(bf16[128,1024]{1,0:T(8,128)(2,1)S(1)} %convolution_convert_fusion.22), channel_id=1, source_target_pairs={{0,2},{1,3},{2,0},{3,1},{4,6},{5,7},{6,4},{7,5},{8,10},{9,11},{10,... | collective-permute-start | bytes 786440 | tf_op jit(solution)/shard_map/ppermute | solution.py:19
  140.3 15.0 %collective-permute-start.25 = (bf16[128,1024]{1,0:T(8,128)(2,1)S(1)}, bf16[128,1024]{1,0:T(8,128)(2,1)S(1)}, u32[]{:S(2)}, u32[]{:S(2)}) collective-permute-start(bf16[128,1024]{1,0:T(8,128)(2,1)S(1)} %fusion.158), channel_id=1, source_target_pairs={{0,1},{1,2},{2,3},{3,0},{4,5},{5,6},{6,7},{7,4},{8,9},{9,10},{10,1... | collective-permute-start | bytes 786440 | tf_op jit(solution)/shard_map/ppermute | solution.py:19
  140.7 14.0 %collective-permute-start.24 = (bf16[128,1024]{1,0:T(8,128)(2,1)S(1)}, bf16[128,1024]{1,0:T(8,128)(2,1)S(1)}, u32[]{:S(2)}, u32[]{:S(2)}) collective-permute-start(bf16[128,1024]{1,0:T(8,128)(2,1)S(1)} %fusion.158), channel_id=1, source_target_pairs={{0,2},{1,3},{2,0},{3,1},{4,6},{5,7},{6,4},{7,5},{8,10},{9,11},{10,... | collective-permute-start | bytes 786440 | tf_op jit(solution)/shard_map/ppermute | solution.py:19
  167.2 16.2 %collective-permute-start.27 = (bf16[128,1024]{1,0:T(8,128)(2,1)S(1)}, bf16[128,1024]{1,0:T(8,128)(2,1)S(1)}, u32[]{:S(2)}, u32[]{:S(2)}) collective-permute-start(bf16[128,1024]{1,0:T(8,128)(2,1)S(1)} %convolution_convert_fusion.18), channel_id=1, source_target_pairs={{0,1},{1,2},{2,3},{3,0},{4,5},{5,6},{6,7},{7,4},{8,9},{9,10},{10,1... | collective-permute-start | bytes 786440 | tf_op jit(solution)/shard_map/ppermute | solution.py:19
  171.5 33.5 %collective-permute-start.36 = (bf16[128,1024]{1,0:T(8,128)(2,1)S(1)}, bf16[128,1024]{1,0:T(8,128)(2,1)S(1)}, u32[]{:S(2)}, u32[]{:S(2)}) collective-permute-start(bf16[128,1024]{1,0:T(8,128)(2,1)S(1)} %copy-done.155), channel_id=1, source_target_pairs={{0,2},{1,3},{2,0},{3,1},{4,6},{5,7},{6,4},{7,5},{8,10},{9,11},{10,... | collective-permute-start | bytes 786440 | tf_op jit(solution)/shard_map/ppermute | solution.py:19
  184.3 13.6 %collective-permute-start.31 = (bf16[128,1024]{1,0:T(8,128)(2,1)S(1)}, bf16[128,1024]{1,0:T(8,128)(2,1)S(1)}, u32[]{:S(2)}, u32[]{:S(2)}) collective-permute-start(bf16[128,1024]{1,0:T(8,128)(2,1)S(1)} %multiply_convert_fusion.2), channel_id=1, source_target_pairs={{0,3},{1,0},{2,1},{3,2},{4,7},{5,4},{6,5},{7,6},{8,11},{9,8},{10,9... | collective-permute-start | bytes 786440 | tf_op jit(solution)/shard_map/ppermute | solution.py:19
  197.3 221.4 %collective-permute-start.34 = (bf16[128,1024]{1,0:T(8,128)(2,1)}, bf16[128,1024]{1,0:T(8,128)(2,1)}, u32[]{:S(2)}, u32[]{:S(2)}) collective-permute-start(bf16[128,1024]{1,0:T(8,128)(2,1)} %convolution_convert_fusion.14), channel_id=1, source_target_pairs={{0,3},{1,0},{2,1},{3,2},{4,7},{5,4},{6,5},{7,6},{8,11},{9,8},{10,9... | collective-permute-start | bytes 786440 | tf_op jit(solution)/shard_map/ppermute | solution.py:19
  197.9 13.8 %collective-permute-start.41 = (bf16[128,1024]{1,0:T(8,128)(2,1)S(1)}, bf16[128,1024]{1,0:T(8,128)(2,1)S(1)}, u32[]{:S(2)}, u32[]{:S(2)}) collective-permute-start(bf16[128,1024]{1,0:T(8,128)(2,1)S(1)} %convolution_convert_fusion.29), channel_id=1, source_target_pairs={{0,3},{1,0},{2,1},{3,2},{4,7},{5,4},{6,5},{7,6},{8,11},{9,8},{10,9... | collective-permute-start | bytes 786440 | tf_op jit(solution)/shard_map/ppermute | solution.py:19
  209.2 212.0 %collective-permute-start.32 = (bf16[128,1024]{1,0:T(8,128)(2,1)}, bf16[128,1024]{1,0:T(8,128)(2,1)}, u32[]{:S(2)}, u32[]{:S(2)}) collective-permute-start(bf16[128,1024]{1,0:T(8,128)(2,1)} %convolution_convert_fusion.15), channel_id=1, source_target_pairs={{0,1},{1,2},{2,3},{3,0},{4,5},{5,6},{6,7},{7,4},{8,9},{9,10},{10,1... | collective-permute-start | bytes 786440 | tf_op jit(solution)/shard_map/ppermute | solution.py:19
  217.9 11.5 %collective-permute-start.44 = (bf16[128,1024]{1,0:T(8,128)(2,1)S(1)}, bf16[128,1024]{1,0:T(8,128)(2,1)S(1)}, u32[]{:S(2)}, u32[]{:S(2)}) collective-permute-start(bf16[128,1024]{1,0:T(8,128)(2,1)S(1)} %get-tuple-element.65), channel_id=1, source_target_pairs={{0,1},{1,2},{2,3},{3,0},{4,5},{5,6},{6,7},{7,4},{8,9},{9,10},{10,1... | collective-permute-start | bytes 786440 | tf_op jit(solution)/shard_map/ppermute | solution.py:19
  219.7 12.7 %collective-permute-start.43 = (bf16[128,1024]{1,0:T(8,128)(2,1)S(1)}, bf16[128,1024]{1,0:T(8,128)(2,1)S(1)}, u32[]{:S(2)}, u32[]{:S(2)}) collective-permute-start(bf16[128,1024]{1,0:T(8,128)(2,1)S(1)} %get-tuple-element.65), channel_id=1, source_target_pairs={{0,2},{1,3},{2,0},{3,1},{4,6},{5,7},{6,4},{7,5},{8,10},{9,11},{10,... | collective-permute-start | bytes 786440 | tf_op jit(solution)/shard_map/ppermute | solution.py:19
  221.0 11.8 %collective-permute-start.42 = (bf16[128,1024]{1,0:T(8,128)(2,1)S(1)}, bf16[128,1024]{1,0:T(8,128)(2,1)S(1)}, u32[]{:S(2)}, u32[]{:S(2)}) collective-permute-start(bf16[128,1024]{1,0:T(8,128)(2,1)S(1)} %get-tuple-element.65), channel_id=1, source_target_pairs={{0,3},{1,0},{2,1},{3,2},{4,7},{5,4},{6,5},{7,6},{8,11},{9,8},{10,9... | collective-permute-start | bytes 786440 | tf_op jit(solution)/shard_map/ppermute | solution.py:19
  261.8 18.7 %collective-permute-start.52 = (bf16[128,1024]{1,0:T(8,128)(2,1)S(1)}, bf16[128,1024]{1,0:T(8,128)(2,1)S(1)}, u32[]{:S(2)}, u32[]{:S(2)}) collective-permute-start(bf16[128,1024]{1,0:T(8,128)(2,1)S(1)} %add_convert_fusion.6), channel_id=1, source_target_pairs={{0,1},{1,2},{2,3},{3,0},{4,5},{5,6},{6,7},{7,4},{8,9},{9,10},{10,1... | collective-permute-start | bytes 786440 | tf_op jit(solution)/shard_map/ppermute | solution.py:19
  264.2 13.6 %collective-permute-start.50 = (bf16[128,1024]{1,0:T(8,128)(2,1)S(1)}, bf16[128,1024]{1,0:T(8,128)(2,1)S(1)}, u32[]{:S(2)}, u32[]{:S(2)}) collective-permute-start(bf16[128,1024]{1,0:T(8,128)(2,1)S(1)} %add_convert_fusion.6), channel_id=1, source_target_pairs={{0,3},{1,0},{2,1},{3,2},{4,7},{5,4},{6,5},{7,6},{8,11},{9,8},{10,9... | collective-permute-start | bytes 786440 | tf_op jit(solution)/shard_map/ppermute | solution.py:19
  279.2 11.1 %collective-permute-start.51 = (bf16[128,1024]{1,0:T(8,128)(2,1)S(1)}, bf16[128,1024]{1,0:T(8,128)(2,1)S(1)}, u32[]{:S(2)}, u32[]{:S(2)}) collective-permute-start(bf16[128,1024]{1,0:T(8,128)(2,1)S(1)} %convolution_convert_fusion.27), channel_id=1, source_target_pairs={{0,1},{1,2},{2,3},{3,0},{4,5},{5,6},{6,7},{7,4},{8,9},{9,10},{10,1... | collective-permute-start | bytes 786440 | tf_op jit(solution)/shard_map/ppermute | solution.py:19
  284.0 34.1 %collective-permute-start.75 = (bf16[512,1968]{0,1:T(8,128)(2,1)}, bf16[512,1968]{0,1:T(8,128)(2,1)}, u32[]{:S(2)}, u32[]{:S(2)}) collective-permute-start(bf16[512,1968]{0,1:T(8,128)(2,1)} %fusion.9), channel_id=1, source_target_pairs={{0,4},{4,0},{1,5},{5,1},{2,6},{6,2},{3,7},{7,3},{8,12},{12,8},{9,1... | collective-permute-start | bytes 6045704 | tf_op jit(solution)/shard_map/ppermute | solution.py:23
  294.6 10.7 %collective-permute-start.55 = (bf16[128,1024]{1,0:T(8,128)(2,1)S(1)}, bf16[128,1024]{1,0:T(8,128)(2,1)S(1)}, u32[]{:S(2)}, u32[]{:S(2)}) collective-permute-start(bf16[128,1024]{1,0:T(8,128)(2,1)S(1)} %get-tuple-element.154), channel_id=1, source_target_pairs={{0,2},{1,3},{2,0},{3,1},{4,6},{5,7},{6,4},{7,5},{8,10},{9,11},{10,... | collective-permute-start | bytes 786440 | tf_op jit(solution)/shard_map/ppermute | solution.py:19
  305.4 47.5 %collective-permute-start.71 = (bf16[512,1024]{0,1:T(8,128)(2,1)}, bf16[512,1024]{0,1:T(8,128)(2,1)}, u32[]{:S(2)}, u32[]{:S(2)}) collective-permute-start(bf16[512,1024]{0,1:T(8,128)(2,1)} %fusion.61), channel_id=1, source_target_pairs={{0,4},{4,0},{1,5},{5,1},{2,6},{6,2},{3,7},{7,3},{8,12},{12,8},{9,1... | collective-permute-start | bytes 3145736 | tf_op jit(solution)/shard_map/ppermute | solution.py:23
  309.8 22.6 %collective-permute-start.74 = (bf16[512,1968]{0,1:T(8,128)(2,1)}, bf16[512,1968]{0,1:T(8,128)(2,1)}, u32[]{:S(2)}, u32[]{:S(2)}) collective-permute-start(bf16[512,1968]{0,1:T(8,128)(2,1)} %fusion.11), channel_id=1, source_target_pairs={{0,4},{4,0},{1,5},{5,1},{2,6},{6,2},{3,7},{7,3},{8,12},{12,8},{9,1... | collective-permute-start | bytes 6045704 | tf_op jit(solution)/shard_map/ppermute | solution.py:23
  338.9 41.6 %all-to-all-start.2 = ((bf16[8,64,1968]{2,1,0:T(8,128)(2,1)}), bf16[8,64,1968]{2,1,0:T(8,128)(2,1)}, u32[]{:S(2)}, u32[]{:S(2)}) async-start(bf16[8,64,1968]{2,1,0:T(8,128)(2,1)} %bitcast.146), calls=%async_computation.2 | async-start | bytes 4194304 | tf_op jit(solution)/shard_map/all_to_all | solution.py:304
  343.4 110.0 %reduce-scatter.7.cloned.1.call-start = ((), (), s32[]{:S(2)}) async-start(), calls=%async_computation.6 | async-start | bytes 1179648 | tf_op jit(solution)/shard_map/reduce_scatter | solution.py:300
  348.5 11.7 %collective-permute-start.70 = (bf16[512,1024]{0,1:T(8,128)(2,1)}, bf16[512,1024]{0,1:T(8,128)(2,1)}, u32[]{:S(2)}, u32[]{:S(2)}) collective-permute-start(bf16[512,1024]{0,1:T(8,128)(2,1)} %fusion.63), channel_id=1, source_target_pairs={{0,4},{4,0},{1,5},{5,1},{2,6},{6,2},{3,7},{7,3},{8,12},{12,8},{9,1... | collective-permute-start | bytes 3145736 | tf_op jit(solution)/shard_map/ppermute | solution.py:23
  350.4 70.8 %collective-permute-start.30 = (bf16[128,1024]{1,0:T(8,128)(2,1)}, bf16[128,1024]{1,0:T(8,128)(2,1)}, u32[]{:S(2)}, u32[]{:S(2)}) collective-permute-start(bf16[128,1024]{1,0:T(8,128)(2,1)} %convolution_convert_fusion.16), channel_id=1, source_target_pairs={{0,2},{1,3},{2,0},{3,1},{4,6},{5,7},{6,4},{7,5},{8,10},{9,11},{10,... | collective-permute-start | bytes 786440 | tf_op jit(solution)/shard_map/ppermute | solution.py:19
  352.8 72.6 %collective-permute-start.58 = (bf16[128,1024]{1,0:T(8,128)(2,1)}, bf16[128,1024]{1,0:T(8,128)(2,1)}, u32[]{:S(2)}, u32[]{:S(2)}) collective-permute-start(bf16[128,1024]{1,0:T(8,128)(2,1)} %convolution_convert_fusion.9), channel_id=1, source_target_pairs={{0,1},{1,2},{2,3},{3,0},{4,5},{5,6},{6,7},{7,4},{8,9},{9,10},{10,1... | collective-permute-start | bytes 786440 | tf_op jit(solution)/shard_map/ppermute | solution.py:19
  380.5 29.8 %all-to-all-start = ((bf16[8,64,1024]{2,1,0:T(8,128)(2,1)}), bf16[8,64,1024]{2,1,0:T(8,128)(2,1)}, u32[]{:S(2)}, u32[]{:S(2)}) async-start(bf16[8,64,1024]{2,1,0:T(8,128)(2,1)} %bitcast.501), calls=%async_computation | async-start | bytes 2097152 | tf_op jit(solution)/shard_map/all_to_all | solution.py:304
  391.4 16.9 %collective-permute-start.76 = (bf16[64,1968]{1,0:T(8,128)(2,1)S(1)}, bf16[64,1968]{1,0:T(8,128)(2,1)S(1)}, u32[]{:S(2)}, u32[]{:S(2)}) collective-permute-start(bf16[64,1968]{1,0:T(8,128)(2,1)S(1)} %broadcast_select_fusion.26), channel_id=1, source_target_pairs={{0,64},{64,0},{1,65},{65,1},{2,66},{66,2},{3,67},{67,3},{4,68},{68... | collective-permute-start | bytes 755720 | tf_op jit(solution)/shard_map/ppermute | solution.py:27
  408.4 17.1 %collective-permute-start.57 = (bf16[128,1024]{1,0:T(8,128)(2,1)}, bf16[128,1024]{1,0:T(8,128)(2,1)}, u32[]{:S(2)}, u32[]{:S(2)}) collective-permute-start(bf16[128,1024]{1,0:T(8,128)(2,1)} %convolution_convert_fusion.10), channel_id=1, source_target_pairs={{0,2},{1,3},{2,0},{3,1},{4,6},{5,7},{6,4},{7,5},{8,10},{9,11},{10,... | collective-permute-start | bytes 786440 | tf_op jit(solution)/shard_map/ppermute | solution.py:19
  412.8 47.3 %all-to-all-start.3 = ((bf16[8,64,1968]{2,1,0:T(8,128)(2,1)}), bf16[8,64,1968]{2,1,0:T(8,128)(2,1)}, u32[]{:S(2)}, u32[]{:S(2)}) async-start(bf16[8,64,1968]{2,1,0:T(8,128)(2,1)} %broadcast_in_dim.264), calls=%async_computation.3 | async-start | bytes 4194304 | tf_op jit(solution)/shard_map/all_to_all | solution.py:311
  423.7 47.5 %collective-permute-start.35 = (bf16[128,1024]{1,0:T(8,128)(2,1)}, bf16[128,1024]{1,0:T(8,128)(2,1)S(1)}, u32[]{:S(2)}, u32[]{:S(2)}) collective-permute-start(bf16[128,1024]{1,0:T(8,128)(2,1)} %get-tuple-element.386), channel_id=1, source_target_pairs={{0,64},{64,0},{1,65},{65,1},{2,66},{66,2},{3,67},{67,3},{4,68},{68... | collective-permute-start | bytes 786440 | tf_op jit(solution)/shard_map/ppermute | solution.py:27
  461.3 26.4 %all-to-all-start.1 = ((bf16[8,64,1024]{2,1,0:T(8,128)(2,1)}), bf16[8,64,1024]{2,1,0:T(8,128)(2,1)S(1)}, u32[]{:S(2)}, u32[]{:S(2)}) async-start(bf16[8,64,1024]{2,1,0:T(8,128)(2,1)} %broadcast_in_dim.261), calls=%async_computation.1 | async-start | bytes 2097152 | tf_op jit(solution)/shard_map/all_to_all | solution.py:311
  483.4 29.5 %collective-permute-start.77 = (bf16[512,1968]{0,1:T(8,128)(2,1)}, bf16[512,1968]{0,1:T(8,128)(2,1)}, u32[]{:S(2)}, u32[]{:S(2)}) collective-permute-start(bf16[512,1968]{0,1:T(8,128)(2,1)} %copy.146), channel_id=1, source_target_pairs={{0,4},{4,0},{1,5},{5,1},{2,6},{6,2},{3,7},{7,3},{8,12},{12,8},{9,1... | collective-permute-start | bytes 6045704 | tf_op jit(solution)/shard_map/ppermute | solution.py:23
  487.7 13.2 %collective-permute-start.73 = (bf16[512,1024]{1,0:T(8,128)(2,1)S(1)}, bf16[512,1024]{1,0:T(8,128)(2,1)S(1)}, u32[]{:S(2)}, u32[]{:S(2)}) collective-permute-start(bf16[512,1024]{1,0:T(8,128)(2,1)S(1)} %bitcast.500), channel_id=1, source_target_pairs={{0,4},{4,0},{1,5},{5,1},{2,6},{6,2},{3,7},{7,3},{8,12},{12,8},{9,1... | collective-permute-start | bytes 3145736 | tf_op jit(solution)/shard_map/ppermute | solution.py:23
  (254 other events, 1950.0 us)
Sparse Core Ops, SparseCore 0:
  326.5 59.3 reduce-scatter.8
  388.4 65.0 reduce-scatter.6

commit v4 on v3

--- a/solution.py
+++ b/solution.py
@@ -161,7 +161,7 @@
     mixed_rows = [None] * 4
 
     def feed(k):
-        hidden = times(mid_parts[k], w_up)
+        hidden = contract_last(mid_parts[k], w_up)
         local_hidden = hidden.shape[1] // 2
         gelu_in[k] = hidden[:, :local_hidden]
         gate_mult[k] = hidden[:, local_hidden:]
@@ -186,7 +186,7 @@
     return (result, kept)
 
 
-def backward_ffn(grad_result, kept, gain_mid, weights):
+def backward_ffn(grad_result, kept, gain_mid, weights, before):
     w_up, w_down = weights[2], weights[3]
     grad_parts = gather_parts(grad_result.astype(bf16))
     grad_hidden = [None] * 4
@@ -194,10 +194,10 @@
     def feed_back(k):
         grad_mixed = contract_last(grad_parts[k], w_down)
         unused, pull_gelu = jax.vjp(gelu_product, kept["gelu_in"][k], kept["gate_mult"][k])
-        grad_hidden[k] = joined(pull_gelu(grad_mixed), 1).astype(bf16)
-        return contract_last(grad_hidden[k], w_up)
-
-    grad_normed_mid = scatter_parts(feed_back)
+        grad_hidden[k] = tuple(term.astype(bf16) for term in pull_gelu(grad_mixed))
+        return times(joined(grad_hidden[k], 1), w_up)
+
+    grad_normed_mid = after_all(scatter_parts(feed_back), *before)
     unused, pull_norm = jax.vjp(layer_norm, kept["resid_mid"], gain_mid)
     grad_resid, grad_gain = pull_norm(grad_normed_mid)
     grad_mid = grad_result + grad_resid
@@ -206,18 +206,25 @@
         outer, inner, left, right = after_all(
             (grad_parts, kept["mixed"], kept["normed_mid"], grad_hidden), gate
         )
-        grad_down = contract_rows(joined(outer), joined(inner)).astype(bf16)
-        grad_up = contract_rows(joined(left), joined(right)).astype(bf16)
-        return joined([grad_up, grad_down], 1)
+        outer, inner, left = joined(outer), joined(inner), joined(left)
+        first = joined([term[0] for term in right])
+        second = joined([term[1] for term in right])
+        half = inner.shape[1] // 2
+        front, back = inner[:, :half], inner[:, half:]
+        up = add_core(lambda core: contract_rows(core(first, second), left))
+        down = add_core(lambda core: contract_rows(core(front, back), outer))
+        rows = up.shape[0] + down.shape[0]
+        blank = jnp.zeros((-rows % 128, up.shape[1]), bf16)
+        return joined([up, down, blank])
 
     return (grad_mid, weight_grads, grad_gain)
 
 
-def backward_attn(grad_mid, kept, gain_first, weights, allowed, tables):
+def backward_attn(grad_mid, kept, gain_first, weights, allowed, tables, before, before_end):
     w_qkv, w_out = weights[0], weights[1]
     queries, keys_rot, values_in = kept["queries"], kept["keys"], kept["values"]
     row_count = grad_mid.shape[0]
-    grad_parts = gather_parts(grad_mid.astype(bf16))
+    grad_parts = after_all(gather_parts(grad_mid.astype(bf16)), *before)
     grad_attended = joined([contract_last(part, w_out).astype(bf16) for part in grad_parts])
     grad_attended = grad_attended.reshape(queries.shape)
     scores = masked_scores(queries, keys_rot, allowed)
@@ -248,7 +255,7 @@
     def project_back(k):
         return contract_last(grad_projected[k * row_count : (k + 1) * row_count], w_qkv)
 
-    grad_normed = scatter_parts(project_back)
+    grad_normed = after_all(scatter_parts(project_back), *before_end)
     unused, pull_norm = jax.vjp(layer_norm, kept["inputs"], gain_first)
     grad_resid, grad_gain = pull_norm(grad_normed)
 
@@ -256,9 +263,12 @@
         outer, inner, left, right = (grad_parts, kept["attended"], kept["normed"], grad_projected)
         if gate is not None:
             outer, inner, left, right = after_all((outer, inner, left, right), gate)
-        grad_out = contract_rows(joined(outer), joined(inner)).astype(bf16)
-        grad_qkv = contract_rows(joined(left), right).astype(bf16)
-        return joined([grad_qkv, grad_out], 1)
+        outer, inner, left = joined(outer), joined(inner), joined(left)
+        width = inner.shape[1]
+        of_q, of_k, of_v = (right[:, i * width : (i + 1) * width] for i in range(3))
+        one = add_core(lambda core: contract_rows(left, core(of_q, of_v)))
+        two = add_core(lambda core: contract_rows(core(left, outer), core(of_k, inner)))
+        return joined([one, two])
 
     return (grad_mid + grad_resid, weight_grads, grad_gain)
 
@@ -288,20 +298,15 @@
     return jnp.concatenate([low, high], axis=0)
 
 
-def add_core(grads):
-    core_index = lax.axis_index("core")
-    half = grads.shape[0] // 2
-    sent = lax.dynamic_slice_in_dim(grads, (1 - core_index) * half, half)
-    held = lax.dynamic_slice_in_dim(grads, core_index * half, half)
-    return (held.astype(f32) + swap_core(sent).astype(f32)).astype(bf16)
+def add_core(product):
+    is_core0 = lax.axis_index("core") == 0
+    sent = product(lambda one, two: jnp.where(is_core0, two, one)).astype(bf16)
+    held = product(lambda one, two: jnp.where(is_core0, one, two))
+    return (held + swap_core(sent).astype(f32)).astype(bf16)
 
 
 def reduce_part(grads):
-    return lax.psum_scatter(add_core(grads), ("zlo", "x"), scatter_dimension=0, tiled=True)
-
-
-def reduce_part_now(grads):
-    pieces = lax.all_to_all(add_core(grads), ("zlo", "x"), 0, 0, tiled=True)
+    pieces = lax.all_to_all(grads, ("zlo", "x"), 0, 0, tiled=True)
     pieces = pieces.reshape(8, -1, pieces.shape[1])
     return jnp.sum(pieces.astype(f32), axis=0).astype(bf16)
 
@@ -309,7 +314,9 @@
 def spread_part(part):
     copies = jnp.broadcast_to(part[None], (8,) + part.shape).reshape(-1, part.shape[1])
     half = lax.all_to_all(copies, ("zlo", "x"), 0, 0, tiled=True)
-    return in_order(lax.axis_index("core"), half, swap_core(half))
+    beside = swap_core(half)
+    is_core0 = lax.axis_index("core") == 0
+    return jnp.where(is_core0, half, beside), jnp.where(is_core0, beside, half)
 
 
 def join_sections(is_first, part_first, part_second):
@@ -323,25 +330,29 @@
     is_first = section_index == 0
     row_count = tokens.shape[1]
     full_rows = row_count * lax.axis_size("tensor")
-    start_rows = jnp.where(is_first, tokens[0], tokens[1]).astype(f32)
+    start_rows = jnp.where(is_first, tokens[0], tokens[1])
     end_grads = jnp.where(is_first, cotangent[0], cotangent[1])
+    start_parts = gather_parts(start_rows)
     gains_other = swap_layer(gains[0])
     gains0 = jnp.where(is_first, gains[0], gains_other)
     gains1 = jnp.where(is_first, gains_other, gains[0])
-    first_parts = gather_parts(layer_norm(start_rows, gains0[0]).astype(bf16))
+    first_parts = [layer_norm(part.astype(f32), gains0[0]).astype(bf16) for part in start_parts]
+    start_rows = start_rows.astype(f32)
     own = (
-        w_qkv[0].reshape(w_qkv.shape[1], -1),
+        jnp.transpose(w_qkv[0], (1, 0, 2)).reshape(-1, w_qkv.shape[3]),
         w_out[0],
-        w_up[0].reshape(w_up.shape[1], -1),
+        jnp.transpose(w_up[0], (1, 2, 0)).reshape(-1, w_up.shape[1]),
         w_down[0],
     )
-    other_qkv, after = other_layer(own[0], tokens[0, 0, 0], False, first_parts)
+    other_qkv, after = other_layer(own[0], tokens[0, 0, 0], False, start_parts)
     other_out, after = other_layer(own[1], after, False)
     other_up, after = other_layer(own[2], after, True)
-    other_down, after = other_layer(own[3], after, True)
+    other_down, after = other_layer(own[3], after, False)
     others = (other_qkv, other_out, other_up, other_down)
-    layer0 = tuple(jnp.where(is_first, a, b) for a, b in zip(own, others))
-    layer1 = tuple(jnp.where(is_first, b, a) for a, b in zip(own, others))
+    layer0 = [jnp.where(is_first, a, b) for a, b in zip(own, others)]
+    layer1 = [jnp.where(is_first, b, a) for a, b in zip(own, others)]
+    layer0[0] = joined(jnp.split(layer0[0], 3), 1)
+    layer1[0] = joined(jnp.split(layer1[0], 3), 1)
     doc_lengths = jnp.where(is_first, lengths[0, 0], lengths[1, 0])
     indices = jnp.arange(full_rows, dtype=jnp.int32)
     indices = (indices + lax.axis_index("tensor") * row_count) % full_rows
@@ -363,24 +374,39 @@
         second_rows, second_parts, gains1[1], layer1, allowed1, tables1
     )
     out1 = out1.astype(bf16)
-    mid1, ffn_grads1, gain_mid1 = backward_ffn(end_grads.astype(f32), kept1, gains1[1], layer1)
+    mid1, ffn_grads1, gain_mid1 = backward_ffn(
+        end_grads.astype(f32), kept1, gains1[1], layer1, ()
+    )
     ffn1 = reduce_part(ffn_grads1(mid1))
     in1, attn_grads1, gain_first1 = backward_attn(
-        mid1, kept1, gains1[0], layer1, allowed1, tables1
+        mid1, kept1, gains1[0], layer1, allowed1, tables1, (), ()
     )
     in1 = in1.astype(bf16)
     attn1 = reduce_part(attn_grads1(in1))
-    mid0, ffn_grads0, gain_mid0 = backward_ffn(in1.astype(f32), kept0, gains0[1], layer0)
-    ffn0 = reduce_part_now(ffn_grads0(mid0))
-    ffn_sum = spread_part(join_sections(is_first, ffn0, ffn1))
+    mid0, ffn_grads0, gain_mid0 = backward_ffn(
+        in1.astype(f32), kept0, gains0[1], layer0, (ffn1,)
+    )
+    ffn0 = reduce_part(ffn_grads0(mid0))
     in0, attn_grads0, gain_first0 = backward_attn(
-        mid0, kept0, gains0[0], layer0, allowed0, tables0
+        mid0, kept0, gains0[0], layer0, allowed0, tables0, (attn1,), (ffn0,)
     )
     in0 = in0.astype(bf16)
-    attn0 = reduce_part_now(attn_grads0(None))
-    attn_sum = spread_part(join_sections(is_first, attn0, attn1))
-    up_width = own[2].shape[1]
-    qkv_width = own[0].shape[1]
+    attn0 = reduce_part(attn_grads0(None))
+    ffn_halves = spread_part(join_sections(is_first, ffn0, ffn1))
+    attn_halves = spread_part(join_sections(is_first, attn0, attn1))
+    hidden_width = w_up.shape[3]
+    grad_up = jnp.stack([half[:hidden_width] for half in ffn_halves])
+    down_rows = w_down.shape[1] // 2
+    grad_down = joined([half[hidden_width : hidden_width + down_rows] for half in ffn_halves])
+    model_width = w_qkv.shape[1]
+    grad_qkv = jnp.stack(
+        [
+            attn_halves[0][:model_width],
+            attn_halves[0][model_width:],
+            attn_halves[1][:model_width],
+        ]
+    )
+    grad_out = attn_halves[1][model_width:].T
 
     gain0 = jnp.stack([gain_first0, gain_mid0])
     gain1 = jnp.stack([gain_first1, gain_mid1])
@@ -409,10 +435,10 @@
         section_out[None],
         input_grads[None],
         gain_total[None],
-        attn_sum[:, :qkv_width].astype(f32).reshape(w_qkv.shape),
-        attn_sum[:, qkv_width:].T.astype(f32)[None],
-        ffn_sum[:, :up_width].astype(f32).reshape(w_up.shape),
-        ffn_sum[:, up_width:].T.astype(f32)[None],
+        jnp.transpose(grad_qkv.astype(f32), (1, 0, 2))[None],
+        grad_out.astype(f32)[None],
+        jnp.transpose(grad_up.astype(f32), (2, 0, 1))[None],
+        grad_down.astype(f32)[None],
     )
 
 

time: 534 us -> 544 us (1.019)
  waiting for transfers between devices: 148 us -> 179 us
  local copies, waits for them, and re-layouts: 56.3 us -> 33 us
  blocking collectives: 0 us -> 19.2 us
  between operations: 18.2 us -> 5.91 us
  starting transfers between devices: 149 us -> 139 us
  matrix products: 83.7 us -> 92.7 us
    reduce_scatter x2 -> x0, waiting for transfers between devices: 23.3 us -> none  [reduce_part(): lax.psum_scatter(add_core(grads), ('zlo', 'x'), scatter_dimension=0, tile...]
    ppermute x5, waiting for transfers between devices: 15.2 us -> 38.2 us  [swap_section(): return lax.ppermute(block, 'section', [(0, 1), (1, 0)])]
    all_to_all x0 -> x1, blocking collectives: none -> 19.2 us  [reduce_part(): pieces = lax.all_to_all(grads, ('zlo', 'x'), 0, 0, tiled=True)]
    ppermute x55, waiting for transfers between devices: 69.7 us -> 88.6 us  [around(): lax.ppermute(block, axis, [(i, (i + distance) % count) for i in range(cou...]
    unnamed x441 -> x558, local copies, waits for them, and re-layouts: 29.5 us -> 16.9 us
    all_to_all x2 -> x3, waiting for transfers between devices: 15.3 us -> 27.2 us  [reduce_part(): pieces = lax.all_to_all(grads, ('zlo', 'x'), 0, 0, tiled=True)]
    dot_general x8 -> x16, matrix products: 11.6 us -> 21.2 us  [contract_rows(): lax.dot_general(left_rows, right_rows, (((0,), (0,)), ((), ())), preferre...]
    ppermute x11 -> x15, starting transfers between devices: 30.6 us -> 22.2 us  [swap_core(): return lax.ppermute(block, 'core', [(0, 1), (1, 0)])]
  transfers between devices with their start and end apart: 84 -> 86, of which waited for: 30 -> 37; matrix products, arithmetic and copies ran while one was open for 35% -> 29% of each run, Pallas kernels for 0% -> 0%
where the time goes in v4:
time: 544 us; the launch traced here: 537 us
  waiting for transfers between devices  179 us (33%)
  starting transfers between devices  139 us (26%)
  matrix products  92.7 us (17%)
  other arithmetic  68.3 us (13%)
  local copies, waits for them, and re-layouts  33 us (6%)
  blocking collectives  19.2 us (4%)
  between operations  5.91 us (1%)
    ppermute x55, waiting for transfers between devices, around(): lax.ppermute(block, axis, [(i, (i + distance) % count) for i in range(cou...  88.6 us
    ppermute x55, starting transfers between devices, around(): lax.ppermute(block, axis, [(i, (i + distance) % count) for i in range(cou...  81 us
    ppermute x5, waiting for transfers between devices, swap_section(): return lax.ppermute(block, 'section', [(0, 1), (1, 0)])  38.2 us
    all_to_all x3, waiting for transfers between devices, reduce_part(): pieces = lax.all_to_all(grads, ('zlo', 'x'), 0, 0, tiled=True)  27.2 us
    dot_general x32, matrix products, contract_last(): lax.dot_general(left_rows, weight, (((1,), (1,)), ((), ())), preferred_el...  23.8 us
    ppermute x5, waiting for transfers between devices, swap_layer(): lax.ppermute(block, ('section', 'zlo'), [(0, 3), (1, 2), (2, 1), (3, 0)])  22.3 us
    dot_general x32, matrix products, times(): return jnp.dot(left_rows, weight, preferred_element_type=f32)  22.2 us
    ppermute x15, starting transfers between devices, swap_core(): return lax.ppermute(block, 'core', [(0, 1), (1, 0)])  22.2 us
  transfers between devices with their start and end apart: 86, of which 37 were waited for; matrix products, arithmetic and copies ran while one was open for 29% of the time, Pallas kernels for 0%

profile of v4, /device:TPU:1, one launch (start us, length us, event | category | flops | bytes accessed | tf_op | source)
XLA Modules:
  0.0 536.8 jit_solution(11526637922389635734)
XLA Ops:
  7.8 3.8 collective-permute-start
  25.2 7.5 %collective-permute-done.1 = bf16[1536,256]{0,1:T(8,128)(2,1)} collective-permute-done((bf16[1536,256]{0,1:T(8,128)(2,1)}, bf16[1536,256]{0,1:T(8,128)(2,1)}, u32[]{:S(2)}, u32[]{:S(2)}) %collective-permute-start.1) | collective-permute-done | bytes 786464 | tf_op jit(solution)/shard_map/ppermute | solution.py:31
  33.3 5.9 %collective-permute-done.6 = bf16[128,1024]{1,0:T(8,128)(2,1)S(1)} collective-permute-done((bf16[128,1024]{1,0:T(8,128)(2,1)S(1)}, bf16[128,1024]{1,0:T(8,128)(2,1)S(1)}, u32[]{:S(2)}, u32[]{:S(2)}) %collective-permute-start.6) | collective-permute-done | bytes 262176 | tf_op jit(solution)/shard_map/ppermute | solution.py:31
  39.2 3.9 collective-permute-start.7
  60.4 2.8 fusion.322
  70.2 2.7 collective-permute-start.37
  73.3 8.9 %collective-permute-done.14 = bf16[328,1024]{1,0:T(8,128)(2,1)S(1)} collective-permute-done((bf16[328,1024]{1,0:T(8,128)(2,1)S(1)}, bf16[328,1024]{1,0:T(8,128)(2,1)S(1)}, u32[]{:S(2)}, u32[]{:S(2)}) %collective-permute-start.14) | collective-permute-done | bytes 671776 | tf_op jit(solution)/shard_map/ppermute | solution.py:31
  92.7 2.7 collective-permute-done.20
  105.7 4.9 collective-permute-start.19
  115.0 6.5 %collective-permute-done.21 = bf16[128,1024]{1,0:T(8,128)(2,1)S(1)} collective-permute-done((bf16[128,1024]{1,0:T(8,128)(2,1)S(1)}, bf16[128,1024]{1,0:T(8,128)(2,1)S(1)}, u32[]{:S(2)}, u32[]{:S(2)}) %collective-permute-start.21) | collective-permute-done | bytes 262176 | tf_op jit(solution)/shard_map/ppermute | solution.py:19
  123.1 3.8 collective-permute-start.23
  127.8 10.0 %collective-permute-done.22 = bf16[128,1024]{1,0:T(8,128)(2,1)S(1)} collective-permute-done((bf16[128,1024]{1,0:T(8,128)(2,1)S(1)}, bf16[128,1024]{1,0:T(8,128)(2,1)S(1)}, u32[]{:S(2)}, u32[]{:S(2)}) %collective-permute-start.22) | collective-permute-done | bytes 262176 | tf_op jit(solution)/shard_map/ppermute | solution.py:19
  145.3 2.8 fusion.323
  149.8 3.8 collective-permute-start.26
  157.1 9.5 %collective-permute-done.26 = bf16[128,1024]{1,0:T(8,128)(2,1)S(1)} collective-permute-done((bf16[128,1024]{1,0:T(8,128)(2,1)S(1)}, bf16[128,1024]{1,0:T(8,128)(2,1)S(1)}, u32[]{:S(2)}, u32[]{:S(2)}) %collective-permute-start.26) | collective-permute-done | bytes 262176 | tf_op jit(solution)/shard_map/ppermute | solution.py:19
  167.4 2.8 collective-permute-start.30
  171.1 4.8 collective-permute-done.32
  191.0 5.4 %collective-permute-done.36 = bf16[128,1024]{1,0:T(8,128)(2,1)S(1)} collective-permute-done((bf16[128,1024]{1,0:T(8,128)(2,1)S(1)}, bf16[128,1024]{1,0:T(8,128)(2,1)S(1)}, u32[]{:S(2)}, u32[]{:S(2)}) %collective-permute-start.36) | collective-permute-done | bytes 262176 | tf_op jit(solution)/shard_map/ppermute | solution.py:19
  204.9 3.1 collective-permute-start.54
  208.4 5.5 %collective-permute-done.43 = bf16[128,1024]{1,0:T(8,128)(2,1)S(1)} collective-permute-done((bf16[128,1024]{1,0:T(8,128)(2,1)S(1)}, bf16[128,1024]{1,0:T(8,128)(2,1)S(1)}, u32[]{:S(2)}, u32[]{:S(2)}) %collective-permute-start.43) | collective-permute-done | bytes 262176 | tf_op jit(solution)/shard_map/ppermute | solution.py:19
  217.9 3.6 fusion.27
  229.9 4.0 collective-permute-start.44
  237.6 7.4 %collective-permute-done.44 = bf16[128,1024]{1,0:T(8,128)(2,1)S(1)} collective-permute-done((bf16[128,1024]{1,0:T(8,128)(2,1)S(1)}, bf16[128,1024]{1,0:T(8,128)(2,1)S(1)}, u32[]{:S(2)}, u32[]{:S(2)}) %collective-permute-start.44) | collective-permute-done | bytes 262176 | tf_op jit(solution)/shard_map/ppermute | solution.py:19
  257.8 6.1 %collective-permute-done.47 = bf16[128,1024]{1,0:T(8,128)(2,1)S(1)} collective-permute-done((bf16[128,1024]{1,0:T(8,128)(2,1)}, bf16[128,1024]{1,0:T(8,128)(2,1)S(1)}, u32[]{:S(2)}, u32[]{:S(2)}) %collective-permute-start.47) | collective-permute-done | bytes 262176 | tf_op jit(solution)/shard_map/ppermute | solution.py:19
  268.9 4.2 all-to-all-start.1
  281.9 7.2 %all-to-all-done.1 = bf16[8,256,256]{2,1,0:T(8,128)(2,1)} async-done(((bf16[8,256,256]{2,1,0:T(8,128)(2,1)}), bf16[8,256,256]{2,1,0:T(8,128)(2,1)}, u32[]{:S(2)}, u32[]{:S(2)}) %all-to-all-start.1) | async-done | bytes 1048608 | tf_op jit(solution)/shard_map/all_to_all | solution.py:309
  289.1 4.4 all-to-all-start
  310.5 10.1 %all-to-all-done = bf16[8,128,1024]{2,1,0:T(8,128)(2,1)} async-done(((bf16[8,128,1024]{2,1,0:T(8,128)(2,1)}), bf16[8,128,1024]{2,1,0:T(8,128)(2,1)}, u32[]{:S(2)}, u32[]{:S(2)}) %all-to-all-start) | async-done | bytes 2097184 | tf_op jit(solution)/shard_map/all_to_all | solution.py:309
  320.6 2.7 reduce_sum.499
  342.6 3.9 multiply_reduce_fusion
  358.0 5.9 %all-to-all-start.2 = ((bf16[8,128,1024]{2,1,0:T(8,128)(2,1)}), bf16[8,128,1024]{2,1,0:T(8,128)(2,1)}, u32[]{:S(2)}, u32[]{:S(2)}) async-start(bf16[8,128,1024]{2,1,0:T(8,128)(2,1)} %bitcast.445), calls=%async_computation.2 | async-start | bytes 4194304 | tf_op jit(solution)/shard_map/all_to_all | solution.py:309
  366.7 3.0 collective-permute-start.60
  370.4 3.0 collective-permute-done.61
  373.4 7.2 %collective-permute-done.60 = bf16[128,1024]{1,0:T(8,128)(2,1)S(1)} collective-permute-done((bf16[128,1024]{1,0:T(8,128)(2,1)S(1)}, bf16[128,1024]{1,0:T(8,128)(2,1)S(1)}, u32[]{:S(2)}, u32[]{:S(2)}) %collective-permute-start.60) | collective-permute-done | bytes 262176 | tf_op jit(solution)/shard_map/ppermute | solution.py:19
  381.1 10.0 %all-to-all-done.2 = bf16[8,128,1024]{2,1,0:T(8,128)(2,1)} async-done(((bf16[8,128,1024]{2,1,0:T(8,128)(2,1)}), bf16[8,128,1024]{2,1,0:T(8,128)(2,1)}, u32[]{:S(2)}, u32[]{:S(2)}) %all-to-all-start.2) | async-done | bytes 2097184 | tf_op jit(solution)/shard_map/all_to_all | solution.py:309
  391.0 2.7 reduce_sum.504
  400.7 19.2 %all_to_all.54 = bf16[8,256,256]{2,1,0:T(8,128)(2,1)} all-to-all(bf16[8,256,256]{2,1,0:T(8,128)(2,1)S(1)} %bitcast.448), channel_id=1, replica_groups=mesh['section'=2,'zlo'=2,'x'=4,'core'=2,'tensor'=4] {'zlo','x'}, dimensions={0} | all-to-all | bytes 2097152 | tf_op jit(solution)/shard_map/all_to_all | solution.py:309
  422.5 6.5 %collective-permute-start.33 = (bf16[128,1024]{1,0:T(8,128)(2,1)}, bf16[128,1024]{1,0:T(8,128)(2,1)}, u32[]{:S(2)}, u32[]{:S(2)}) collective-permute-start(bf16[128,1024]{1,0:T(8,128)(2,1)} %convolution_convert_fusion.14), channel_id=1, source_target_pairs={{0,3},{1,0},{2,1},{3,2},{4,7},{5,4},{6,5},{7,6},{8,11},{9,8},{10,9... | collective-permute-start | bytes 786440 | tf_op jit(solution)/shard_map/ppermute | solution.py:19
  430.1 4.4 all-to-all-start.4
  435.6 2.9 collective-permute-start.31
  441.0 2.9 collective-permute-start.29
  443.9 11.7 %collective-permute-done.79 = bf16[128,1024]{1,0:T(8,128)(2,1)S(1)} collective-permute-done((bf16[128,1024]{1,0:T(8,128)(2,1)S(1)}, bf16[128,1024]{1,0:T(8,128)(2,1)S(1)}, u32[]{:S(2)}, u32[]{:S(2)}) %collective-permute-start.79) | collective-permute-done | bytes 262176 | tf_op jit(solution)/shard_map/ppermute | solution.py:27
  458.9 4.5 all-to-all-start.5
  468.3 25.2 %collective-permute-done.66 = f32[2,1024]{1,0:T(2,128)S(1)} collective-permute-done((f32[2,1024]{1,0:T(2,128)S(1)}, f32[2,1024]{1,0:T(2,128)S(1)}, u32[]{:S(2)}, u32[]{:S(2)}) %collective-permute-start.66) | collective-permute-done | bytes 8224 | tf_op jit(solution)/shard_map/ppermute | solution.py:27
  498.4 2.8 collective-permute-done.67
  501.3 3.4 collective-permute-start.70
  514.0 5.2 collective-permute-done.74
  533.9 2.7 convert_bitcast_fusion
  (1014 shorter events, 253.2 us)
Async XLA Ops:
  1.9 22.4 %collective-permute-start.4 = (bf16[128,1024]{1,0:T(8,128)(2,1)S(1)}, bf16[128,1024]{1,0:T(8,128)(2,1)S(1)}, u32[]{:S(2)}, u32[]{:S(2)}) collective-permute-start(bf16[128,1024]{1,0:T(8,128)(2,1)S(1)} %get-tuple-element.192), channel_id=1, source_target_pairs={{0,1},{1,2},{2,3},{3,0},{4,5},{5,6},{6,7},{7,4},{8,9},{9,10},{10,1... | collective-permute-start | bytes 786440 | tf_op jit(solution)/shard_map/ppermute | solution.py:19
  4.1 20.3 %collective-permute-start.3 = (bf16[128,1024]{1,0:T(8,128)(2,1)S(1)}, bf16[128,1024]{1,0:T(8,128)(2,1)S(1)}, u32[]{:S(2)}, u32[]{:S(2)}) collective-permute-start(bf16[128,1024]{1,0:T(8,128)(2,1)S(1)} %get-tuple-element.192), channel_id=1, source_target_pairs={{0,2},{1,3},{2,0},{3,1},{4,6},{5,7},{6,4},{7,5},{8,10},{9,11},{10,... | collective-permute-start | bytes 786440 | tf_op jit(solution)/shard_map/ppermute | solution.py:19
  6.7 18.3 %collective-permute-start.2 = (bf16[128,1024]{1,0:T(8,128)(2,1)S(1)}, bf16[128,1024]{1,0:T(8,128)(2,1)S(1)}, u32[]{:S(2)}, u32[]{:S(2)}) collective-permute-start(bf16[128,1024]{1,0:T(8,128)(2,1)S(1)} %get-tuple-element.192), channel_id=1, source_target_pairs={{0,3},{1,0},{2,1},{3,2},{4,7},{5,4},{6,5},{7,6},{8,11},{9,8},{10,9... | collective-permute-start | bytes 786440 | tf_op jit(solution)/shard_map/ppermute | solution.py:19
  7.8 16.5 %collective-permute-start = (f32[2,1024]{1,0:T(2,128)}, f32[2,1024]{1,0:T(2,128)S(1)}, u32[]{:S(2)}, u32[]{:S(2)}) collective-permute-start(f32[2,1024]{1,0:T(2,128)} %bitcast.545), channel_id=1, source_target_pairs={{0,96},{32,64},{64,32},{96,0},{1,97},{33,65},{65,33},{97,1},{2,98}... | collective-permute-start | bytes 24584 | tf_op jit(solution)/shard_map/ppermute | solution.py:31
  13.9 18.8 %collective-permute-start.1 = (bf16[1536,256]{0,1:T(8,128)(2,1)}, bf16[1536,256]{0,1:T(8,128)(2,1)}, u32[]{:S(2)}, u32[]{:S(2)}) collective-permute-start(bf16[1536,256]{0,1:T(8,128)(2,1)} %copy.101), channel_id=1, source_target_pairs={{0,96},{32,64},{64,32},{96,0},{1,97},{33,65},{65,33},{97,1},{2,98}... | collective-permute-start | bytes 2359304 | tf_op jit(solution)/shard_map/ppermute | solution.py:31
  43.6 20.6 %collective-permute-start.11 = (bf16[328,1024]{1,0:T(8,128)(2,1)S(1)}, bf16[328,1024]{1,0:T(8,128)(2,1)S(1)}, u32[]{:S(2)}, u32[]{:S(2)}) collective-permute-start(bf16[328,1024]{1,0:T(8,128)(2,1)S(1)} %constant_dynamic-slice_fusion), channel_id=1, source_target_pairs={{0,96},{32,64},{64,32},{96,0},{1,97},{33,65},{65,33},{97,1},{2,98}... | collective-permute-start | bytes 2015240 | tf_op jit(solution)/shard_map/ppermute | solution.py:31
  55.6 14.7 %collective-permute-start.9 = (bf16[128,1024]{1,0:T(8,128)(2,1)S(1)}, bf16[128,1024]{1,0:T(8,128)(2,1)S(1)}, u32[]{:S(2)}, u32[]{:S(2)}) collective-permute-start(bf16[128,1024]{1,0:T(8,128)(2,1)S(1)} %convolution_convert_fusion.24), channel_id=1, source_target_pairs={{0,1},{1,2},{2,3},{3,0},{4,5},{5,6},{6,7},{7,4},{8,9},{9,10},{10,1... | collective-permute-start | bytes 786440 | tf_op jit(solution)/shard_map/ppermute | solution.py:19
  56.3 14.0 %collective-permute-start.8 = (bf16[128,1024]{1,0:T(8,128)(2,1)S(1)}, bf16[128,1024]{1,0:T(8,128)(2,1)S(1)}, u32[]{:S(2)}, u32[]{:S(2)}) collective-permute-start(bf16[128,1024]{1,0:T(8,128)(2,1)S(1)} %convolution_convert_fusion.25), channel_id=1, source_target_pairs={{0,2},{1,3},{2,0},{3,1},{4,6},{5,7},{6,4},{7,5},{8,10},{9,11},{10,... | collective-permute-start | bytes 786440 | tf_op jit(solution)/shard_map/ppermute | solution.py:19
  58.7 14.2 %collective-permute-start.10 = (bf16[128,1024]{1,0:T(8,128)(2,1)S(1)}, bf16[128,1024]{1,0:T(8,128)(2,1)S(1)}, u32[]{:S(2)}, u32[]{:S(2)}) collective-permute-start(bf16[128,1024]{1,0:T(8,128)(2,1)S(1)} %convolution_convert_fusion.23), channel_id=1, source_target_pairs={{0,3},{1,0},{2,1},{3,2},{4,7},{5,4},{6,5},{7,6},{8,11},{9,8},{10,9... | collective-permute-start | bytes 786440 | tf_op jit(solution)/shard_map/ppermute | solution.py:19
  65.0 17.2 %collective-permute-start.14 = (bf16[328,1024]{1,0:T(8,128)(2,1)S(1)}, bf16[328,1024]{1,0:T(8,128)(2,1)S(1)}, u32[]{:S(2)}, u32[]{:S(2)}) collective-permute-start(bf16[328,1024]{1,0:T(8,128)(2,1)S(1)} %constant_dynamic-slice_fusion.2), channel_id=1, source_target_pairs={{0,96},{32,64},{64,32},{96,0},{1,97},{33,65},{65,33},{97,1},{2,98}... | collective-permute-start | bytes 2015240 | tf_op jit(solution)/shard_map/ppermute | solution.py:31
  67.0 16.8 %collective-permute-start.12 = (bf16[328,1024]{1,0:T(8,128)(2,1)S(1)}, bf16[328,1024]{1,0:T(8,128)(2,1)S(1)}, u32[]{:S(2)}, u32[]{:S(2)}) collective-permute-start(bf16[328,1024]{1,0:T(8,128)(2,1)S(1)} %collective-permute-done.11), channel_id=1, source_target_pairs={{0,8},{8,0},{16,24},{24,16},{1,9},{9,1},{17,25},{25,17},{2,10},{10... | collective-permute-start | bytes 2015240 | tf_op jit(solution)/shard_map/ppermute | solution.py:285
  70.2 106.6 %collective-permute-start.39 = (bf16[128,1024]{1,0:T(8,128)(2,1)}, bf16[128,1024]{1,0:T(8,128)(2,1)S(1)}, u32[]{:S(2)}, u32[]{:S(2)}) collective-permute-start(bf16[128,1024]{1,0:T(8,128)(2,1)} %select_bitcast_fusion.2), channel_id=1, source_target_pairs={{0,1},{1,2},{2,3},{3,0},{4,5},{5,6},{6,7},{7,4},{8,9},{9,10},{10,1... | collective-permute-start | bytes 786440 | tf_op jit(solution)/shard_map/ppermute | solution.py:19
  70.2 110.7 %collective-permute-start.37 = (bf16[128,1024]{1,0:T(8,128)(2,1)}, bf16[128,1024]{1,0:T(8,128)(2,1)S(1)}, u32[]{:S(2)}, u32[]{:S(2)}) collective-permute-start(bf16[128,1024]{1,0:T(8,128)(2,1)} %select_bitcast_fusion.2), channel_id=1, source_target_pairs={{0,3},{1,0},{2,1},{3,2},{4,7},{5,4},{6,5},{7,6},{8,11},{9,8},{10,9... | collective-permute-start | bytes 786440 | tf_op jit(solution)/shard_map/ppermute | solution.py:19
  122.6 16.7 %collective-permute-start.24 = (bf16[128,1024]{1,0:T(8,128)(2,1)S(1)}, bf16[128,1024]{1,0:T(8,128)(2,1)S(1)}, u32[]{:S(2)}, u32[]{:S(2)}) collective-permute-start(bf16[128,1024]{1,0:T(8,128)(2,1)S(1)} %fusion.92), channel_id=1, source_target_pairs={{0,1},{1,2},{2,3},{3,0},{4,5},{5,6},{6,7},{7,4},{8,9},{9,10},{10,1... | collective-permute-start | bytes 786440 | tf_op jit(solution)/shard_map/ppermute | solution.py:19
  123.1 15.5 %collective-permute-start.23 = (bf16[128,1024]{1,0:T(8,128)(2,1)S(1)}, bf16[128,1024]{1,0:T(8,128)(2,1)S(1)}, u32[]{:S(2)}, u32[]{:S(2)}) collective-permute-start(bf16[128,1024]{1,0:T(8,128)(2,1)S(1)} %fusion.92), channel_id=1, source_target_pairs={{0,2},{1,3},{2,0},{3,1},{4,6},{5,7},{6,4},{7,5},{8,10},{9,11},{10,... | collective-permute-start | bytes 786440 | tf_op jit(solution)/shard_map/ppermute | solution.py:19
  149.8 16.8 %collective-permute-start.26 = (bf16[128,1024]{1,0:T(8,128)(2,1)S(1)}, bf16[128,1024]{1,0:T(8,128)(2,1)S(1)}, u32[]{:S(2)}, u32[]{:S(2)}) collective-permute-start(bf16[128,1024]{1,0:T(8,128)(2,1)S(1)} %convolution_convert_fusion.18), channel_id=1, source_target_pairs={{0,1},{1,2},{2,3},{3,0},{4,5},{5,6},{6,7},{7,4},{8,9},{9,10},{10,1... | collective-permute-start | bytes 786440 | tf_op jit(solution)/shard_map/ppermute | solution.py:19
  153.9 12.7 %collective-permute-start.27 = (bf16[128,1024]{1,0:T(8,128)(2,1)S(1)}, bf16[128,1024]{1,0:T(8,128)(2,1)S(1)}, u32[]{:S(2)}, u32[]{:S(2)}) collective-permute-start(bf16[128,1024]{1,0:T(8,128)(2,1)S(1)} %convolution_convert_fusion.17), channel_id=1, source_target_pairs={{0,3},{1,0},{2,1},{3,2},{4,7},{5,4},{6,5},{7,6},{8,11},{9,8},{10,9... | collective-permute-start | bytes 786440 | tf_op jit(solution)/shard_map/ppermute | solution.py:19
  157.1 27.6 %collective-permute-start.35 = (bf16[128,1024]{1,0:T(8,128)(2,1)}, bf16[128,1024]{1,0:T(8,128)(2,1)S(1)}, u32[]{:S(2)}, u32[]{:S(2)}) collective-permute-start(bf16[128,1024]{1,0:T(8,128)(2,1)} %select_bitcast_fusion.2), channel_id=1, source_target_pairs={{0,2},{1,3},{2,0},{3,1},{4,6},{5,7},{6,4},{7,5},{8,10},{9,11},{10,... | collective-permute-start | bytes 786440 | tf_op jit(solution)/shard_map/ppermute | solution.py:19
  167.4 12.6 %collective-permute-start.30 = (bf16[128,1024]{1,0:T(8,128)(2,1)S(1)}, bf16[128,1024]{1,0:T(8,128)(2,1)S(1)}, u32[]{:S(2)}, u32[]{:S(2)}) collective-permute-start(bf16[128,1024]{1,0:T(8,128)(2,1)S(1)} %multiply_convert_fusion.2), channel_id=1, source_target_pairs={{0,3},{1,0},{2,1},{3,2},{4,7},{5,4},{6,5},{7,6},{8,11},{9,8},{10,9... | collective-permute-start | bytes 786440 | tf_op jit(solution)/shard_map/ppermute | solution.py:19
  199.1 14.9 %collective-permute-start.43 = (bf16[128,1024]{1,0:T(8,128)(2,1)S(1)}, bf16[128,1024]{1,0:T(8,128)(2,1)S(1)}, u32[]{:S(2)}, u32[]{:S(2)}) collective-permute-start(bf16[128,1024]{1,0:T(8,128)(2,1)S(1)} %get-tuple-element.108), channel_id=1, source_target_pairs={{0,1},{1,2},{2,3},{3,0},{4,5},{5,6},{6,7},{7,4},{8,9},{9,10},{10,1... | collective-permute-start | bytes 786440 | tf_op jit(solution)/shard_map/ppermute | solution.py:19
  199.5 14.5 %collective-permute-start.42 = (bf16[128,1024]{1,0:T(8,128)(2,1)S(1)}, bf16[128,1024]{1,0:T(8,128)(2,1)S(1)}, u32[]{:S(2)}, u32[]{:S(2)}) collective-permute-start(bf16[128,1024]{1,0:T(8,128)(2,1)S(1)} %get-tuple-element.108), channel_id=1, source_target_pairs={{0,2},{1,3},{2,0},{3,1},{4,6},{5,7},{6,4},{7,5},{8,10},{9,11},{10,... | collective-permute-start | bytes 786440 | tf_op jit(solution)/shard_map/ppermute | solution.py:19
  199.6 14.4 %collective-permute-start.41 = (bf16[128,1024]{1,0:T(8,128)(2,1)S(1)}, bf16[128,1024]{1,0:T(8,128)(2,1)S(1)}, u32[]{:S(2)}, u32[]{:S(2)}) collective-permute-start(bf16[128,1024]{1,0:T(8,128)(2,1)S(1)} %get-tuple-element.108), channel_id=1, source_target_pairs={{0,3},{1,0},{2,1},{3,2},{4,7},{5,4},{6,5},{7,6},{8,11},{9,8},{10,9... | collective-permute-start | bytes 786440 | tf_op jit(solution)/shard_map/ppermute | solution.py:19
  204.9 49.3 %collective-permute-start.54 = (bf16[328,1024]{1,0:T(8,128)(2,1)}, bf16[328,1024]{1,0:T(8,128)(2,1)}, u32[]{:S(2)}, u32[]{:S(2)}) collective-permute-start(bf16[328,1024]{1,0:T(8,128)(2,1)} %convolution_convert_fusion.3), channel_id=1, source_target_pairs={{0,4},{4,0},{1,5},{5,1},{2,6},{6,2},{3,7},{7,3},{8,12},{12,8},{9,1... | collective-permute-start | bytes 2015240 | tf_op jit(solution)/shard_map/ppermute | solution.py:23
  229.9 15.1 %collective-permute-start.44 = (bf16[128,1024]{1,0:T(8,128)(2,1)S(1)}, bf16[128,1024]{1,0:T(8,128)(2,1)S(1)}, u32[]{:S(2)}, u32[]{:S(2)}) collective-permute-start(bf16[128,1024]{1,0:T(8,128)(2,1)S(1)} %convolution_convert_fusion.13), channel_id=1, source_target_pairs={{0,2},{1,3},{2,0},{3,1},{4,6},{5,7},{6,4},{7,5},{8,10},{9,11},{10,... | collective-permute-start | bytes 786440 | tf_op jit(solution)/shard_map/ppermute | solution.py:19
  235.9 42.0 %collective-permute-start.53 = (bf16[656,1024]{1,0:T(8,128)(2,1)}, bf16[656,1024]{1,0:T(8,128)(2,1)}, u32[]{:S(2)}, u32[]{:S(2)}) collective-permute-start(bf16[656,1024]{1,0:T(8,128)(2,1)} %convolution_convert_fusion.1), channel_id=1, source_target_pairs={{0,4},{4,0},{1,5},{5,1},{2,6},{6,2},{3,7},{7,3},{8,12},{12,8},{9,1... | collective-permute-start | bytes 4030472 | tf_op jit(solution)/shard_map/ppermute | solution.py:23
  247.7 48.9 %collective-permute-start.51 = (bf16[128,1024]{1,0:T(8,128)(2,1)}, bf16[128,1024]{1,0:T(8,128)(2,1)}, u32[]{:S(2)}, u32[]{:S(2)}) collective-permute-start(bf16[128,1024]{1,0:T(8,128)(2,1)} %add_convert_fusion.7), channel_id=1, source_target_pairs={{0,1},{1,2},{2,3},{3,0},{4,5},{5,6},{6,7},{7,4},{8,9},{9,10},{10,1... | collective-permute-start | bytes 786440 | tf_op jit(solution)/shard_map/ppermute | solution.py:19
  248.4 27.3 %collective-permute-start.49 = (bf16[128,1024]{1,0:T(8,128)(2,1)}, bf16[128,1024]{1,0:T(8,128)(2,1)}, u32[]{:S(2)}, u32[]{:S(2)}) collective-permute-start(bf16[128,1024]{1,0:T(8,128)(2,1)} %add_convert_fusion.7), channel_id=1, source_target_pairs={{0,3},{1,0},{2,1},{3,2},{4,7},{5,4},{6,5},{7,6},{8,11},{9,8},{10,9... | collective-permute-start | bytes 786440 | tf_op jit(solution)/shard_map/ppermute | solution.py:19
  250.9 12.9 %collective-permute-start.47 = (bf16[128,1024]{1,0:T(8,128)(2,1)}, bf16[128,1024]{1,0:T(8,128)(2,1)S(1)}, u32[]{:S(2)}, u32[]{:S(2)}) collective-permute-start(bf16[128,1024]{1,0:T(8,128)(2,1)} %add_convert_fusion.7), channel_id=1, source_target_pairs={{0,2},{1,3},{2,0},{3,1},{4,6},{5,7},{6,4},{7,5},{8,10},{9,11},{10,... | collective-permute-start | bytes 786440 | tf_op jit(solution)/shard_map/ppermute | solution.py:19
  254.2 12.5 %collective-permute-start.58 = (bf16[1024,256]{1,0:T(8,128)(2,1)S(1)}, bf16[1024,256]{1,0:T(8,128)(2,1)S(1)}, u32[]{:S(2)}, u32[]{:S(2)}) collective-permute-start(bf16[1024,256]{1,0:T(8,128)(2,1)S(1)} %convolution_convert_fusion.7), channel_id=1, source_target_pairs={{0,4},{4,0},{1,5},{5,1},{2,6},{6,2},{3,7},{7,3},{8,12},{12,8},{9,1... | collective-permute-start | bytes 1572872 | tf_op jit(solution)/shard_map/ppermute | solution.py:23
  268.9 20.2 %all-to-all-start.1 = ((bf16[8,256,256]{2,1,0:T(8,128)(2,1)}), bf16[8,256,256]{2,1,0:T(8,128)(2,1)}, u32[]{:S(2)}, u32[]{:S(2)}) async-start(bf16[8,256,256]{2,1,0:T(8,128)(2,1)} %bitcast.447), calls=%async_computation.1 | async-start | bytes 2097152 | tf_op jit(solution)/shard_map/all_to_all | solution.py:309
  275.7 26.8 %collective-permute-start.48 = (bf16[128,1024]{1,0:T(8,128)(2,1)}, bf16[128,1024]{1,0:T(8,128)(2,1)}, u32[]{:S(2)}, u32[]{:S(2)}) collective-permute-start(bf16[128,1024]{1,0:T(8,128)(2,1)} %convolution_convert_fusion.28), channel_id=1, source_target_pairs={{0,2},{1,3},{2,0},{3,1},{4,6},{5,7},{6,4},{7,5},{8,10},{9,11},{10,... | collective-permute-start | bytes 786440 | tf_op jit(solution)/shard_map/ppermute | solution.py:19
  289.1 31.5 %all-to-all-start = ((bf16[8,128,1024]{2,1,0:T(8,128)(2,1)}), bf16[8,128,1024]{2,1,0:T(8,128)(2,1)}, u32[]{:S(2)}, u32[]{:S(2)}) async-start(bf16[8,128,1024]{2,1,0:T(8,128)(2,1)} %bitcast.444), calls=%async_computation | async-start | bytes 4194304 | tf_op jit(solution)/shard_map/all_to_all | solution.py:309
  326.4 13.2 %collective-permute-start.57 = (bf16[128,1024]{1,0:T(8,128)(2,1)S(1)}, bf16[128,1024]{1,0:T(8,128)(2,1)S(1)}, u32[]{:S(2)}, u32[]{:S(2)}) collective-permute-start(bf16[128,1024]{1,0:T(8,128)(2,1)S(1)} %get-tuple-element.116), channel_id=1, source_target_pairs={{0,1},{1,2},{2,3},{3,0},{4,5},{5,6},{6,7},{7,4},{8,9},{9,10},{10,1... | collective-permute-start | bytes 786440 | tf_op jit(solution)/shard_map/ppermute | solution.py:19
  327.8 13.2 %collective-permute-start.55 = (bf16[128,1024]{1,0:T(8,128)(2,1)S(1)}, bf16[128,1024]{1,0:T(8,128)(2,1)S(1)}, u32[]{:S(2)}, u32[]{:S(2)}) collective-permute-start(bf16[128,1024]{1,0:T(8,128)(2,1)S(1)} %get-tuple-element.116), channel_id=1, source_target_pairs={{0,3},{1,0},{2,1},{3,2},{4,7},{5,4},{6,5},{7,6},{8,11},{9,8},{10,9... | collective-permute-start | bytes 786440 | tf_op jit(solution)/shard_map/ppermute | solution.py:19
  334.8 17.2 %collective-permute-start.64 = (bf16[328,1024]{1,0:T(8,128)(2,1)}, bf16[328,1024]{1,0:T(8,128)(2,1)}, u32[]{:S(2)}, u32[]{:S(2)}) collective-permute-start(bf16[328,1024]{1,0:T(8,128)(2,1)} %convolution_convert_fusion.2), channel_id=1, source_target_pairs={{0,4},{4,0},{1,5},{5,1},{2,6},{6,2},{3,7},{7,3},{8,12},{12,8},{9,1... | collective-permute-start | bytes 2015240 | tf_op jit(solution)/shard_map/ppermute | solution.py:23
  338.7 15.4 %collective-permute-start.63 = (bf16[656,1024]{1,0:T(8,128)(2,1)}, bf16[656,1024]{1,0:T(8,128)(2,1)}, u32[]{:S(2)}, u32[]{:S(2)}) collective-permute-start(bf16[656,1024]{1,0:T(8,128)(2,1)} %convolution_convert_fusion), channel_id=1, source_target_pairs={{0,4},{4,0},{1,5},{5,1},{2,6},{6,2},{3,7},{7,3},{8,12},{12,8},{9,1... | collective-permute-start | bytes 4030472 | tf_op jit(solution)/shard_map/ppermute | solution.py:23
  358.0 33.0 %all-to-all-start.2 = ((bf16[8,128,1024]{2,1,0:T(8,128)(2,1)}), bf16[8,128,1024]{2,1,0:T(8,128)(2,1)}, u32[]{:S(2)}, u32[]{:S(2)}) async-start(bf16[8,128,1024]{2,1,0:T(8,128)(2,1)} %bitcast.445), calls=%async_computation.2 | async-start | bytes 4194304 | tf_op jit(solution)/shard_map/all_to_all | solution.py:309
  366.7 13.8 %collective-permute-start.60 = (bf16[128,1024]{1,0:T(8,128)(2,1)S(1)}, bf16[128,1024]{1,0:T(8,128)(2,1)S(1)}, u32[]{:S(2)}, u32[]{:S(2)}) collective-permute-start(bf16[128,1024]{1,0:T(8,128)(2,1)S(1)} %convolution_convert_fusion.10), channel_id=1, source_target_pairs={{0,2},{1,3},{2,0},{3,1},{4,6},{5,7},{6,4},{7,5},{8,10},{9,11},{10,... | collective-permute-start | bytes 786440 | tf_op jit(solution)/shard_map/ppermute | solution.py:19
  422.5 41.0 %collective-permute-start.33 = (bf16[128,1024]{1,0:T(8,128)(2,1)}, bf16[128,1024]{1,0:T(8,128)(2,1)}, u32[]{:S(2)}, u32[]{:S(2)}) collective-permute-start(bf16[128,1024]{1,0:T(8,128)(2,1)} %convolution_convert_fusion.14), channel_id=1, source_target_pairs={{0,3},{1,0},{2,1},{3,2},{4,7},{5,4},{6,5},{7,6},{8,11},{9,8},{10,9... | collective-permute-start | bytes 786440 | tf_op jit(solution)/shard_map/ppermute | solution.py:19
  430.1 26.3 %all-to-all-start.4 = ((bf16[8,256,256]{2,1,0:T(8,128)(2,1)}), bf16[8,256,256]{2,1,0:T(8,128)(2,1)}, u32[]{:S(2)}, u32[]{:S(2)}) async-start(bf16[8,256,256]{2,1,0:T(8,128)(2,1)} %broadcast_in_dim.274), calls=%async_computation.4 | async-start | bytes 2097152 | tf_op jit(solution)/shard_map/all_to_all | solution.py:316
  435.6 27.8 %collective-permute-start.31 = (bf16[128,1024]{1,0:T(8,128)(2,1)}, bf16[128,1024]{1,0:T(8,128)(2,1)}, u32[]{:S(2)}, u32[]{:S(2)}) collective-permute-start(bf16[128,1024]{1,0:T(8,128)(2,1)} %convolution_convert_fusion.15), channel_id=1, source_target_pairs={{0,1},{1,2},{2,3},{3,0},{4,5},{5,6},{6,7},{7,4},{8,9},{9,10},{10,1... | collective-permute-start | bytes 786440 | tf_op jit(solution)/shard_map/ppermute | solution.py:19
  438.5 17.0 %collective-permute-start.79 = (bf16[128,1024]{1,0:T(8,128)(2,1)S(1)}, bf16[128,1024]{1,0:T(8,128)(2,1)S(1)}, u32[]{:S(2)}, u32[]{:S(2)}) collective-permute-start(bf16[128,1024]{1,0:T(8,128)(2,1)S(1)} %broadcast_select_fusion.24), channel_id=1, source_target_pairs={{0,64},{64,0},{1,65},{65,1},{2,66},{66,2},{3,67},{67,3},{4,68},{68... | collective-permute-start | bytes 786440 | tf_op jit(solution)/shard_map/ppermute | solution.py:27
  441.0 22.5 %collective-permute-start.29 = (bf16[128,1024]{1,0:T(8,128)(2,1)}, bf16[128,1024]{1,0:T(8,128)(2,1)}, u32[]{:S(2)}, u32[]{:S(2)}) collective-permute-start(bf16[128,1024]{1,0:T(8,128)(2,1)} %convolution_convert_fusion.16), channel_id=1, source_target_pairs={{0,2},{1,3},{2,0},{3,1},{4,6},{5,7},{6,4},{7,5},{8,10},{9,11},{10,... | collective-permute-start | bytes 786440 | tf_op jit(solution)/shard_map/ppermute | solution.py:19
  458.9 52.7 %all-to-all-start.5 = ((bf16[8,128,1024]{2,1,0:T(8,128)(2,1)}), bf16[8,128,1024]{2,1,0:T(8,128)(2,1)}, u32[]{:S(2)}, u32[]{:S(2)}) async-start(bf16[8,128,1024]{2,1,0:T(8,128)(2,1)} %broadcast_in_dim.279), calls=%async_computation.5 | async-start | bytes 4194304 | tf_op jit(solution)/shard_map/all_to_all | solution.py:316
  465.2 33.2 %collective-permute-start.34 = (bf16[128,1024]{1,0:T(8,128)(2,1)S(1)}, bf16[128,1024]{1,0:T(8,128)(2,1)S(1)}, u32[]{:S(2)}, u32[]{:S(2)}) collective-permute-start(bf16[128,1024]{1,0:T(8,128)(2,1)S(1)} %get-tuple-element.407), channel_id=1, source_target_pairs={{0,64},{64,0},{1,65},{65,1},{2,66},{66,2},{3,67},{67,3},{4,68},{68... | collective-permute-start | bytes 786440 | tf_op jit(solution)/shard_map/ppermute | solution.py:27
  466.7 26.9 %collective-permute-start.66 = (f32[2,1024]{1,0:T(2,128)S(1)}, f32[2,1024]{1,0:T(2,128)S(1)}, u32[]{:S(2)}, u32[]{:S(2)}) collective-permute-start(f32[2,1024]{1,0:T(2,128)S(1)} %broadcast_select_fusion.28), channel_id=1, source_target_pairs={{0,64},{64,0},{1,65},{65,1},{2,66},{66,2},{3,67},{67,3},{4,68},{68... | collective-permute-start | bytes 24584 | tf_op jit(solution)/shard_map/ppermute | solution.py:27
  509.1 12.9 %collective-permute-start.78 = (bf16[2048,256]{1,0:T(8,128)(2,1)}, bf16[2048,256]{1,0:T(8,128)(2,1)}, u32[]{:S(2)}, u32[]{:S(2)}) collective-permute-start(bf16[2048,256]{1,0:T(8,128)(2,1)} %bitcast.138), channel_id=1, source_target_pairs={{0,4},{4,0},{1,5},{5,1},{2,6},{6,2},{3,7},{7,3},{8,12},{12,8},{9,1... | collective-permute-start | bytes 3145736 | tf_op jit(solution)/shard_map/ppermute | solution.py:23
  511.7 17.6 %collective-permute-start.80 = (bf16[1024,1024]{1,0:T(8,128)(2,1)}, bf16[1024,1024]{1,0:T(8,128)(2,1)}, u32[]{:S(2)}, u32[]{:S(2)}) collective-permute-start(bf16[1024,1024]{1,0:T(8,128)(2,1)} %bitcast.146), channel_id=1, source_target_pairs={{0,4},{4,0},{1,5},{5,1},{2,6},{6,2},{3,7},{7,3},{8,12},{12,8},{9,1... | collective-permute-start | bytes 6291464 | tf_op jit(solution)/shard_map/ppermute | solution.py:23
  (295 other events, 2376.1 us)

commit v5 on v4

--- a/solution.py
+++ b/solution.py
@@ -38,11 +38,13 @@
     return [block, ahead1, ahead2, ahead3]
 
 
-def scatter_parts(term_of):
+def scatter_parts(term_of, beside=None):
     sent2 = around(term_of(2).astype(bf16), "tensor", 2)
     sent1 = around(term_of(1).astype(bf16), "tensor", 1)
     sent3 = around(term_of(3).astype(bf16), "tensor", -1)
     kept = term_of(0).astype(f32)
+    if beside is not None:
+        kept = after_all(kept, beside(kept))
     return kept + sent2.astype(f32) + sent1.astype(f32) + sent3.astype(f32)
 
 
@@ -125,8 +127,8 @@
     return jax.nn.gelu(first_half, approximate=False) * second_half
 
 
-def forward_layer(inputs, normed_parts, gain_mid, weights, allowed, tables):
-    w_qkv, w_out, w_up, w_down = weights
+def forward_layer(inputs, normed_parts, gain_mid, weights, allowed, tables, late, points):
+    w_qkv, w_out = weights[0], weights[1]
     row_count = inputs.shape[0]
     local_width = w_out.shape[0]
     queries, keys_rot, values_in = [], [], []
@@ -155,6 +157,8 @@
         return times(attended[k], w_out)
 
     resid_mid = inputs + scatter_parts(attend)
+    points(attended[0], resid_mid)
+    w_up, w_down = weights[2], weights[3]
     mid_parts = gather_parts(layer_norm(resid_mid, gain_mid).astype(bf16))
     gelu_in = [None] * 4
     gate_mult = [None] * 4
@@ -168,7 +172,16 @@
         mixed_rows[k] = gelu_product(gelu_in[k], gate_mult[k]).astype(bf16)
         return times(mixed_rows[k], w_down)
 
-    result = resid_mid + scatter_parts(feed)
+    if late:
+        for k in range(4):
+            feed(k)
+
+        def result(gate):
+            held = after_all(mixed_rows, gate)
+            return resid_mid + scatter_parts(lambda k: times(held[k], w_down))
+
+    else:
+        result = resid_mid + scatter_parts(feed)
     kept = dict(
         inputs=inputs,
         resid_mid=resid_mid,
@@ -186,21 +199,19 @@
     return (result, kept)
 
 
-def backward_ffn(grad_result, kept, gain_mid, weights, before):
+def backward_ffn(grad_result, kept, gain_mid, weights, gather_gate):
     w_up, w_down = weights[2], weights[3]
     grad_parts = gather_parts(grad_result.astype(bf16))
+    if gather_gate is not None:
+        grad_parts = after_all(grad_parts, gather_gate)
     grad_hidden = [None] * 4
+    finish = []
 
     def feed_back(k):
         grad_mixed = contract_last(grad_parts[k], w_down)
         unused, pull_gelu = jax.vjp(gelu_product, kept["gelu_in"][k], kept["gate_mult"][k])
         grad_hidden[k] = tuple(term.astype(bf16) for term in pull_gelu(grad_mixed))
         return times(joined(grad_hidden[k], 1), w_up)
-
-    grad_normed_mid = after_all(scatter_parts(feed_back), *before)
-    unused, pull_norm = jax.vjp(layer_norm, kept["resid_mid"], gain_mid)
-    grad_resid, grad_gain = pull_norm(grad_normed_mid)
-    grad_mid = grad_result + grad_resid
 
     def weight_grads(gate):
         outer, inner, left, right = after_all(
@@ -211,20 +222,31 @@
         second = joined([term[1] for term in right])
         half = inner.shape[1] // 2
         front, back = inner[:, :half], inner[:, half:]
-        up = add_core(lambda core: contract_rows(core(first, second), left))
-        down = add_core(lambda core: contract_rows(core(front, back), outer))
-        rows = up.shape[0] + down.shape[0]
-        blank = jnp.zeros((-rows % 128, up.shape[1]), bf16)
-        return joined([up, down, blank])
-
-    return (grad_mid, weight_grads, grad_gain)
-
-
-def backward_attn(grad_mid, kept, gain_first, weights, allowed, tables, before, before_end):
+        sent_up, add_up = add_core(lambda core: contract_rows(core(first, second), left))
+        sent_down, add_down = add_core(lambda core: contract_rows(core(front, back), outer))
+
+        def add(gate):
+            up, down = add_up(gate), add_down(gate)
+            rows = up.shape[0] + down.shape[0]
+            blank = jnp.zeros((-rows % 128, up.shape[1]), bf16)
+            return joined([up, down, blank])
+
+        finish.append(add)
+        return (sent_up, sent_down)
+
+    grad_normed_mid = scatter_parts(feed_back, weight_grads)
+    unused, pull_norm = jax.vjp(layer_norm, kept["resid_mid"], gain_mid)
+    grad_resid, grad_gain = pull_norm(grad_normed_mid)
+    grad_mid = grad_result + grad_resid
+    return (grad_mid, finish[0], grad_gain)
+
+
+def backward_attn(grad_mid, kept, gain_first, weights, allowed, tables, gather_gate, last):
     w_qkv, w_out = weights[0], weights[1]
     queries, keys_rot, values_in = kept["queries"], kept["keys"], kept["values"]
     row_count = grad_mid.shape[0]
-    grad_parts = after_all(gather_parts(grad_mid.astype(bf16)), *before)
+    grad_parts = after_all(gather_parts(grad_mid.astype(bf16)), gather_gate)
+    finish = []
     grad_attended = joined([contract_last(part, w_out).astype(bf16) for part in grad_parts])
     grad_attended = grad_attended.reshape(queries.shape)
     scores = masked_scores(queries, keys_rot, allowed)
@@ -255,40 +277,47 @@
     def project_back(k):
         return contract_last(grad_projected[k * row_count : (k + 1) * row_count], w_qkv)
 
-    grad_normed = after_all(scatter_parts(project_back), *before_end)
-    unused, pull_norm = jax.vjp(layer_norm, kept["inputs"], gain_first)
-    grad_resid, grad_gain = pull_norm(grad_normed)
-
     def weight_grads(gate):
-        outer, inner, left, right = (grad_parts, kept["attended"], kept["normed"], grad_projected)
-        if gate is not None:
-            outer, inner, left, right = after_all((outer, inner, left, right), gate)
+        outer, inner, left, right = after_all(
+            (grad_parts, kept["attended"], kept["normed"], grad_projected), gate
+        )
         outer, inner, left = joined(outer), joined(inner), joined(left)
         width = inner.shape[1]
         of_q, of_k, of_v = (right[:, i * width : (i + 1) * width] for i in range(3))
-        one = add_core(lambda core: contract_rows(left, core(of_q, of_v)))
-        two = add_core(lambda core: contract_rows(core(left, outer), core(of_k, inner)))
-        return joined([one, two])
-
-    return (grad_mid + grad_resid, weight_grads, grad_gain)
-
-
-def other_layer(own, after, pair_x, before_core=()):
+        sent_one, add_one = add_core(lambda core: contract_rows(left, core(of_q, of_v)))
+        sent_two, add_two = add_core(
+            lambda core: contract_rows(core(left, outer), core(of_k, inner))
+        )
+
+        def add(gate):
+            return joined([add_one(gate), add_two(gate)])
+
+        finish.append(add)
+        return add(()) if last else (sent_one, sent_two)
+
+    grad_normed = scatter_parts(project_back, weight_grads)
+    unused, pull_norm = jax.vjp(layer_norm, kept["inputs"], gain_first)
+    grad_resid, grad_gain = pull_norm(grad_normed)
+    return (grad_mid + grad_resid, finish[0], grad_gain)
+
+
+def other_layer(own, after, pair_x, before_x, before_core):
     core_index = lax.axis_index("core")
     parity = lax.axis_index("x") % 2
-    own, unused = lax.optimization_barrier((own, after))
+    own = after_all(own, after)
     rows = own.shape[0]
     if pair_x:
         piece = rows // 4
         sent = lax.dynamic_slice_in_dim(own, (core_index * 2 + parity) * piece, piece)
         got = swap_layer(sent)
-        beside = lax.ppermute(got, "x", [(0, 1), (1, 0), (2, 3), (3, 2)])
-        half = in_order(parity, got, beside)
+        kept = after_all(got, before_x)
+        beside = lax.ppermute(kept, "x", [(0, 1), (1, 0), (2, 3), (3, 2)])
+        half = in_order(parity, kept, beside)
     else:
         piece = rows // 2
         sent = lax.dynamic_slice_in_dim(own, core_index * piece, piece)
         got = half = swap_layer(sent)
-    half = after_all(half, *before_core)
+    half = after_all(half, before_core)
     return in_order(core_index, half, swap_core(half)), got
 
 
@@ -301,11 +330,20 @@
 def add_core(product):
     is_core0 = lax.axis_index("core") == 0
     sent = product(lambda one, two: jnp.where(is_core0, two, one)).astype(bf16)
-    held = product(lambda one, two: jnp.where(is_core0, one, two))
-    return (held + swap_core(sent).astype(f32)).astype(bf16)
+    got = swap_core(sent)
+
+    def add(gate):
+        held = product(lambda one, two: after_all(jnp.where(is_core0, one, two), gate))
+        return (held + got.astype(f32)).astype(bf16)
+
+    return sent, add
 
 
 def reduce_part(grads):
+    return lax.psum_scatter(grads, ("zlo", "x"), scatter_dimension=0, tiled=True)
+
+
+def reduce_part_now(grads):
     pieces = lax.all_to_all(grads, ("zlo", "x"), 0, 0, tiled=True)
     pieces = pieces.reshape(8, -1, pieces.shape[1])
     return jnp.sum(pieces.astype(f32), axis=0).astype(bf16)
@@ -344,15 +382,19 @@
         jnp.transpose(w_up[0], (1, 2, 0)).reshape(-1, w_up.shape[1]),
         w_down[0],
     )
-    other_qkv, after = other_layer(own[0], tokens[0, 0, 0], False, start_parts)
-    other_out, after = other_layer(own[1], after, False)
-    other_up, after = other_layer(own[2], after, True)
-    other_down, after = other_layer(own[3], after, False)
-    others = (other_qkv, other_out, other_up, other_down)
-    layer0 = [jnp.where(is_first, a, b) for a, b in zip(own, others)]
-    layer1 = [jnp.where(is_first, b, a) for a, b in zip(own, others)]
+    other_qkv, after = other_layer(own[0], (), False, (), start_parts)
+    other_out, after_out = other_layer(own[1], after, False, (), ())
+    layer0 = [jnp.where(is_first, own[0], other_qkv), jnp.where(is_first, own[1], other_out)]
+    layer1 = [jnp.where(is_first, other_qkv, own[0]), jnp.where(is_first, other_out, own[1])]
     layer0[0] = joined(jnp.split(layer0[0], 3), 1)
     layer1[0] = joined(jnp.split(layer1[0], 3), 1)
+
+    def feed_weights(attended, resid_mid):
+        other_up, after = other_layer(own[2], after_out, True, attended, resid_mid)
+        other_down, unused = other_layer(own[3], after, False, (), resid_mid)
+        layer0.extend([jnp.where(is_first, own[2], other_up), jnp.where(is_first, own[3], other_down)])
+        layer1.extend([jnp.where(is_first, other_up, own[2]), jnp.where(is_first, other_down, own[3])])
+
     doc_lengths = jnp.where(is_first, lengths[0, 0], lengths[1, 0])
     indices = jnp.arange(full_rows, dtype=jnp.int32)
     indices = (indices + lax.axis_index("tensor") * row_count) % full_rows
@@ -365,34 +407,39 @@
     tables1 = rope_tables(positions, 160000.0)
 
     out0, kept0 = forward_layer(
-        start_rows, first_parts, gains0[1], layer0, allowed0, tables0
+        start_rows, first_parts, gains0[1], layer0, allowed0, tables0, False, feed_weights
     )
     out0 = out0.astype(bf16)
     second_rows = out0.astype(f32)
     second_parts = gather_parts(layer_norm(second_rows, gains1[0]).astype(bf16))
-    out1, kept1 = forward_layer(
-        second_rows, second_parts, gains1[1], layer1, allowed1, tables1
-    )
-    out1 = out1.astype(bf16)
-    mid1, ffn_grads1, gain_mid1 = backward_ffn(
-        end_grads.astype(f32), kept1, gains1[1], layer1, ()
-    )
-    ffn1 = reduce_part(ffn_grads1(mid1))
-    in1, attn_grads1, gain_first1 = backward_attn(
-        mid1, kept1, gains1[0], layer1, allowed1, tables1, (), ()
-    )
+    out1_of, kept1 = forward_layer(
+        second_rows, second_parts, gains1[1], layer1, allowed1, tables1, True, lambda *points: None
+    )
+    mid1, add_ffn1, gain_mid1 = backward_ffn(
+        end_grads.astype(f32), kept1, gains1[1], layer1, None
+    )
+    ffn1 = add_ffn1(mid1)
+    in1, add_attn1, gain_first1 = backward_attn(
+        mid1, kept1, gains1[0], layer1, allowed1, tables1, ffn1, False
+    )
+    ffn1 = reduce_part(ffn1)
     in1 = in1.astype(bf16)
-    attn1 = reduce_part(attn_grads1(in1))
-    mid0, ffn_grads0, gain_mid0 = backward_ffn(
-        in1.astype(f32), kept0, gains0[1], layer0, (ffn1,)
-    )
-    ffn0 = reduce_part(ffn_grads0(mid0))
-    in0, attn_grads0, gain_first0 = backward_attn(
-        mid0, kept0, gains0[0], layer0, allowed0, tables0, (attn1,), (ffn0,)
-    )
+    attn1 = add_attn1(in1)
+    mid0, add_ffn0, gain_mid0 = backward_ffn(
+        in1.astype(f32), kept0, gains0[1], layer0, attn1
+    )
+    attn1 = reduce_part(attn1)
+    mid0 = after_all(mid0, ffn1)
+    ffn0 = add_ffn0(mid0)
+    in0, add_attn0, gain_first0 = backward_attn(
+        mid0, kept0, gains0[0], layer0, allowed0, tables0, (ffn0, attn1), True
+    )
+    ffn0 = reduce_part_now(ffn0)
     in0 = in0.astype(bf16)
-    attn0 = reduce_part(attn_grads0(None))
-    ffn_halves = spread_part(join_sections(is_first, ffn0, ffn1))
+    attn0 = reduce_part_now(add_attn0(()))
+    out1 = out1_of(attn0).astype(bf16)
+    ffn_sum = after_all(join_sections(is_first, ffn0, ffn1), attn0)
+    ffn_halves = spread_part(ffn_sum)
     attn_halves = spread_part(join_sections(is_first, attn0, attn1))
     hidden_width = w_up.shape[3]
     grad_up = jnp.stack([half[:hidden_width] for half in ffn_halves])

time: 544 us -> 542 us (level)
  waiting for transfers between devices: 179 us -> 155 us
  between operations: 5.91 us -> 18.7 us
  local copies, waits for them, and re-layouts: 33 us -> 40 us
    all_to_all x3 -> x1, waiting for transfers between devices: 27.2 us -> 0.01 us  [reduce_part_now(): pieces = lax.all_to_all(grads, ('zlo', 'x'), 0, 0, tiled=True)]
    ppermute x55, waiting for transfers between devices: 88.6 us -> 108 us  [around(): lax.ppermute(block, axis, [(i, (i + distance) % count) for i in range(cou...]
    ppermute x5, waiting for transfers between devices: 38.2 us -> 26.1 us  [swap_section(): return lax.ppermute(block, 'section', [(0, 1), (1, 0)])]
    all_to_all x3 -> x1, starting transfers between devices: 14.5 us -> 4.69 us  [reduce_part_now(): pieces = lax.all_to_all(grads, ('zlo', 'x'), 0, 0, tiled=True)]
    ppermute x5, waiting for transfers between devices: 22.3 us -> 12.8 us  [swap_layer(): lax.ppermute(block, ('section', 'zlo'), [(0, 3), (1, 2), (2, 1), (3, 0)])]
    dot_general x32, matrix products: 23.8 us -> 30.6 us  [contract_last(): lax.dot_general(left_rows, weight, (((1,), (1,)), ((), ())), preferred_el...]
    ppermute x5, starting transfers between devices: 4.64 us -> 10.8 us  [swap_section(): return lax.ppermute(block, 'section', [(0, 1), (1, 0)])]
    dot_general x16, matrix products: 21.2 us -> 15 us  [contract_rows(): lax.dot_general(left_rows, right_rows, (((0,), (0,)), ((), ())), preferre...]
  transfers between devices with their start and end apart: 86 -> 86, of which waited for: 37 -> 39; matrix products, arithmetic and copies ran while one was open for 29% -> 31% of each run, Pallas kernels for 0% -> 0%
where the time goes in v5:
time: 542 us; the launch traced here: 531 us
  waiting for transfers between devices  155 us (29%)
  starting transfers between devices  134 us (25%)
  matrix products  91.9 us (17%)
  other arithmetic  72.3 us (13%)
  local copies, waits for them, and re-layouts  40 us (7%)
  blocking collectives  19 us (4%)
  between operations  18.7 us (3%)
    ppermute x55, waiting for transfers between devices, around(): lax.ppermute(block, axis, [(i, (i + distance) % count) for i in range(cou...  108 us
    ppermute x55, starting transfers between devices, around(): lax.ppermute(block, axis, [(i, (i + distance) % count) for i in range(cou...  78.5 us
    dot_general x32, matrix products, contract_last(): lax.dot_general(left_rows, weight, (((1,), (1,)), ((), ())), preferred_el...  30.6 us
    ppermute x5, waiting for transfers between devices, swap_section(): return lax.ppermute(block, 'section', [(0, 1), (1, 0)])  26.1 us
    ppermute x15, starting transfers between devices, swap_core(): return lax.ppermute(block, 'core', [(0, 1), (1, 0)])  23.1 us
    unnamed x472, local copies, waits for them, and re-layouts  21.7 us
    dot_general x32, matrix products, times(): return jnp.dot(left_rows, weight, preferred_element_type=f32)  20.8 us
    all_to_all x1, blocking collectives, reduce_part_now(): pieces = lax.all_to_all(grads, ('zlo', 'x'), 0, 0, tiled=True)  19 us
  transfers between devices with their start and end apart: 86, of which 39 were waited for; matrix products, arithmetic and copies ran while one was open for 31% of the time, Pallas kernels for 0%

profile of v5, /device:TPU:1, one launch (start us, length us, event | category | flops | bytes accessed | tf_op | source)
XLA Modules:
  0.0 530.9 jit_solution(7490328910311764538)
XLA Ops:
  10.7 2.6 collective-permute-start.3
  14.4 3.8 collective-permute-start
  42.0 4.7 collective-permute-done.6
  46.7 3.9 collective-permute-start.7
  68.3 2.7 fusion.281
  80.9 2.6 collective-permute-done.10
  83.9 6.0 %collective-permute-done.14 = bf16[328,1024]{1,0:T(8,128)(2,1)S(1)} collective-permute-done((bf16[328,1024]{1,0:T(8,128)(2,1)S(1)}, bf16[328,1024]{1,0:T(8,128)(2,1)S(1)}, u32[]{:S(2)}, u32[]{:S(2)}) %collective-permute-start.14) | collective-permute-done | bytes 671776 | tf_op jit(solution)/shard_map/ppermute | solution.py:31
  90.3 2.6 collective-permute-start.15
  120.4 7.5 %collective-permute-done.19 = bf16[128,1024]{1,0:T(8,128)(2,1)S(1)} collective-permute-done((bf16[128,1024]{1,0:T(8,128)(2,1)S(1)}, bf16[128,1024]{1,0:T(8,128)(2,1)S(1)}, u32[]{:S(2)}, u32[]{:S(2)}) %collective-permute-start.19) | collective-permute-done | bytes 262176 | tf_op jit(solution)/shard_map/ppermute | solution.py:19
  129.6 3.2 collective-permute-start.23
  134.1 9.6 %collective-permute-done.22 = bf16[128,1024]{1,0:T(8,128)(2,1)S(1)} collective-permute-done((bf16[128,1024]{1,0:T(8,128)(2,1)S(1)}, bf16[128,1024]{1,0:T(8,128)(2,1)S(1)}, u32[]{:S(2)}, u32[]{:S(2)}) %collective-permute-start.22) | collective-permute-done | bytes 262176 | tf_op jit(solution)/shard_map/ppermute | solution.py:19
  151.3 2.8 fusion.282
  163.0 4.6 collective-permute-start.31
  167.6 2.6 collective-permute-done.26
  171.6 2.7 collective-permute-start.30
  179.8 2.7 collective-permute-start.28
  184.5 3.4 collective-permute-done.29
  200.1 5.6 %collective-permute-done.36 = bf16[128,1024]{1,0:T(8,128)(2,1)S(1)} collective-permute-done((bf16[128,1024]{1,0:T(8,128)(2,1)S(1)}, bf16[128,1024]{1,0:T(8,128)(2,1)S(1)}, u32[]{:S(2)}, u32[]{:S(2)}) %collective-permute-start.36) | collective-permute-done | bytes 262176 | tf_op jit(solution)/shard_map/ppermute | solution.py:19
  207.4 6.7 %collective-permute-done.35 = bf16[128,1024]{1,0:T(8,128)(2,1)S(1)} collective-permute-done((bf16[128,1024]{1,0:T(8,128)(2,1)S(1)}, bf16[128,1024]{1,0:T(8,128)(2,1)S(1)}, u32[]{:S(2)}, u32[]{:S(2)}) %collective-permute-start.35) | collective-permute-done | bytes 262176 | tf_op jit(solution)/shard_map/ppermute | solution.py:19
  222.8 7.9 %collective-permute-done.39 = bf16[128,1024]{1,0:T(8,128)(2,1)} collective-permute-done((bf16[128,1024]{1,0:T(8,128)(2,1)}, bf16[128,1024]{1,0:T(8,128)(2,1)}, u32[]{:S(2)}, u32[]{:S(2)}) %collective-permute-start.39) | collective-permute-done | bytes 262176 | tf_op jit(solution)/shard_map/ppermute | solution.py:19
  239.3 3.7 fusion.27
  253.4 2.8 collective-permute-start.42
  263.4 4.0 collective-permute-done.42
  271.0 2.8 collective-permute-start.46
  278.0 7.7 %collective-permute-done.46 = bf16[128,1024]{1,0:T(8,128)(2,1)} collective-permute-done((bf16[128,1024]{1,0:T(8,128)(2,1)}, bf16[128,1024]{1,0:T(8,128)(2,1)}, u32[]{:S(2)}, u32[]{:S(2)}) %collective-permute-start.46) | collective-permute-done | bytes 262176 | tf_op jit(solution)/shard_map/ppermute | solution.py:19
  315.1 4.1 collective-permute-done.50
  319.3 5.9 %collective-permute-done.51 = bf16[128,1024]{1,0:T(8,128)(2,1)S(1)} collective-permute-done((bf16[128,1024]{1,0:T(8,128)(2,1)}, bf16[128,1024]{1,0:T(8,128)(2,1)S(1)}, u32[]{:S(2)}, u32[]{:S(2)}) %collective-permute-start.51) | collective-permute-done | bytes 262176 | tf_op jit(solution)/shard_map/ppermute | solution.py:19
  327.3 2.8 collective-permute-start.54
  332.2 2.7 add_convert_fusion
  337.4 4.7 reduce-scatter.5.cloned.1.call-done
  345.5 3.5 fusion.30
  359.1 5.5 %collective-permute-start.58 = (bf16[1024,256]{1,0:T(8,128)(2,1)S(1)}, bf16[1024,256]{1,0:T(8,128)(2,1)S(1)}, u32[]{:S(2)}, u32[]{:S(2)}) collective-permute-start(bf16[1024,256]{1,0:T(8,128)(2,1)S(1)} %convolution_convert_fusion.5), channel_id=1, source_target_pairs={{0,4},{4,0},{1,5},{5,1},{2,6},{6,2},{3,7},{7,3},{8,12},{12,8},{9,1... | collective-permute-start | bytes 1572872 | tf_op jit(solution)/shard_map/ppermute | solution.py:23
  369.7 19.0 %all_to_all.36 = bf16[8,256,256]{2,1,0:T(8,128)(2,1)} all-to-all(bf16[8,256,256]{2,1,0:T(8,128)(2,1)S(1)} %bitcast.462), channel_id=1, replica_groups=mesh['section'=2,'zlo'=2,'x'=4,'core'=2,'tensor'=4] {'zlo','x'}, dimensions={0} | all-to-all | bytes 2097152 | tf_op jit(solution)/shard_map/all_to_all | solution.py:347
  388.8 4.7 all-to-all-start.2
  396.1 2.5 collective-permute-start.64
  399.7 3.7 collective-permute-done.65
  403.3 6.6 %collective-permute-done.64 = bf16[128,1024]{1,0:T(8,128)(2,1)S(1)} collective-permute-done((bf16[128,1024]{1,0:T(8,128)(2,1)S(1)}, bf16[128,1024]{1,0:T(8,128)(2,1)S(1)}, u32[]{:S(2)}, u32[]{:S(2)}) %collective-permute-start.64) | collective-permute-done | bytes 262176 | tf_op jit(solution)/shard_map/ppermute | solution.py:19
  411.9 2.6 collective-permute-start.77
  414.5 9.5 %collective-permute-done.77 = bf16[256,256]{1,0:T(8,128)(2,1)S(1)} collective-permute-done((bf16[256,256]{1,0:T(8,128)(2,1)S(1)}, bf16[256,256]{1,0:T(8,128)(2,1)S(1)}, u32[]{:S(2)}, u32[]{:S(2)}) %collective-permute-start.77) | collective-permute-done | bytes 131104 | tf_op jit(solution)/shard_map/ppermute | solution.py:27
  425.1 4.2 all-to-all-start.1
  434.9 14.3 %collective-permute-done.68 = f32[2,1024]{1,0:T(2,128)S(1)} collective-permute-done((f32[2,1024]{1,0:T(2,128)S(1)}, f32[2,1024]{1,0:T(2,128)S(1)}, u32[]{:S(2)}, u32[]{:S(2)}) %collective-permute-start.68) | collective-permute-done | bytes 8224 | tf_op jit(solution)/shard_map/ppermute | solution.py:27
  454.9 4.7 all-to-all-start.3
  462.3 2.9 collective-permute-start.75
  466.4 17.5 %collective-permute-done.75 = f32[2,1024]{1,0:T(2,128)S(1)} collective-permute-done((f32[2,1024]{1,0:T(2,128)S(1)}, f32[2,1024]{1,0:T(2,128)S(1)}, u32[]{:S(2)}, u32[]{:S(2)}) %collective-permute-start.75) | collective-permute-done | bytes 8224 | tf_op jit(solution)/shard_map/ppermute | solution.py:19
  498.2 3.4 collective-permute-start.78
  503.8 2.7 collective-permute-start.63
  516.4 2.5 broadcast_select_fusion.3
  521.1 2.7 convert_bitcast_fusion
  (939 shorter events, 270.2 us)
Async XLA Ops:
  7.2 319.8 %reduce-scatter.3.cloned.1.call-start = ((), (), s32[]{:S(2)}) async-start(), calls=%async_computation.6 | async-start | bytes 2359296 | tf_op jit(solution)/shard_map/reduce_scatter | solution.py:343
  8.5 22.8 %collective-permute-start.4 = (bf16[128,1024]{1,0:T(8,128)(2,1)S(1)}, bf16[128,1024]{1,0:T(8,128)(2,1)}, u32[]{:S(2)}, u32[]{:S(2)}) collective-permute-start(bf16[128,1024]{1,0:T(8,128)(2,1)S(1)} %get-tuple-element.266), channel_id=1, source_target_pairs={{0,1},{1,2},{2,3},{3,0},{4,5},{5,6},{6,7},{7,4},{8,9},{9,10},{10,1... | collective-permute-start | bytes 786440 | tf_op jit(solution)/shard_map/ppermute | solution.py:19
  10.7 21.9 %collective-permute-start.3 = (bf16[128,1024]{1,0:T(8,128)(2,1)S(1)}, bf16[128,1024]{1,0:T(8,128)(2,1)}, u32[]{:S(2)}, u32[]{:S(2)}) collective-permute-start(bf16[128,1024]{1,0:T(8,128)(2,1)S(1)} %get-tuple-element.266), channel_id=1, source_target_pairs={{0,2},{1,3},{2,0},{3,1},{4,6},{5,7},{6,4},{7,5},{8,10},{9,11},{10,... | collective-permute-start | bytes 786440 | tf_op jit(solution)/shard_map/ppermute | solution.py:19
  13.3 22.7 %collective-permute-start.2 = (bf16[128,1024]{1,0:T(8,128)(2,1)S(1)}, bf16[128,1024]{1,0:T(8,128)(2,1)}, u32[]{:S(2)}, u32[]{:S(2)}) collective-permute-start(bf16[128,1024]{1,0:T(8,128)(2,1)S(1)} %get-tuple-element.266), channel_id=1, source_target_pairs={{0,3},{1,0},{2,1},{3,2},{4,7},{5,4},{6,5},{7,6},{8,11},{9,8},{10,9... | collective-permute-start | bytes 786440 | tf_op jit(solution)/shard_map/ppermute | solution.py:19
  14.4 16.9 %collective-permute-start = (f32[2,1024]{1,0:T(2,128)}, f32[2,1024]{1,0:T(2,128)S(1)}, u32[]{:S(2)}, u32[]{:S(2)}) collective-permute-start(f32[2,1024]{1,0:T(2,128)} %bitcast.547), channel_id=1, source_target_pairs={{0,96},{32,64},{64,32},{96,0},{1,97},{33,65},{65,33},{97,1},{2,98}... | collective-permute-start | bytes 24584 | tf_op jit(solution)/shard_map/ppermute | solution.py:31
  20.5 18.8 %collective-permute-start.1 = (bf16[1536,256]{0,1:T(8,128)(2,1)}, bf16[1536,256]{0,1:T(8,128)(2,1)}, u32[]{:S(2)}, u32[]{:S(2)}) collective-permute-start(bf16[1536,256]{0,1:T(8,128)(2,1)} %copy.102), channel_id=1, source_target_pairs={{0,96},{32,64},{64,32},{96,0},{1,97},{33,65},{65,33},{97,1},{2,98}... | collective-permute-start | bytes 2359304 | tf_op jit(solution)/shard_map/ppermute | solution.py:31
  52.9 19.1 %collective-permute-start.11 = (bf16[328,1024]{1,0:T(8,128)(2,1)S(1)}, bf16[328,1024]{1,0:T(8,128)(2,1)S(1)}, u32[]{:S(2)}, u32[]{:S(2)}) collective-permute-start(bf16[328,1024]{1,0:T(8,128)(2,1)S(1)} %constant_dynamic-slice_fusion), channel_id=1, source_target_pairs={{0,96},{32,64},{64,32},{96,0},{1,97},{33,65},{65,33},{97,1},{2,98}... | collective-permute-start | bytes 2015240 | tf_op jit(solution)/shard_map/ppermute | solution.py:31
  65.0 14.4 %collective-permute-start.9 = (bf16[128,1024]{1,0:T(8,128)(2,1)S(1)}, bf16[128,1024]{1,0:T(8,128)(2,1)S(1)}, u32[]{:S(2)}, u32[]{:S(2)}) collective-permute-start(bf16[128,1024]{1,0:T(8,128)(2,1)S(1)} %convolution_convert_fusion.24), channel_id=1, source_target_pairs={{0,1},{1,2},{2,3},{3,0},{4,5},{5,6},{6,7},{7,4},{8,9},{9,10},{10,1... | collective-permute-start | bytes 786440 | tf_op jit(solution)/shard_map/ppermute | solution.py:19
  65.7 13.7 %collective-permute-start.8 = (bf16[128,1024]{1,0:T(8,128)(2,1)S(1)}, bf16[128,1024]{1,0:T(8,128)(2,1)S(1)}, u32[]{:S(2)}, u32[]{:S(2)}) collective-permute-start(bf16[128,1024]{1,0:T(8,128)(2,1)S(1)} %convolution_convert_fusion.25), channel_id=1, source_target_pairs={{0,2},{1,3},{2,0},{3,1},{4,6},{5,7},{6,4},{7,5},{8,10},{9,11},{10,... | collective-permute-start | bytes 786440 | tf_op jit(solution)/shard_map/ppermute | solution.py:19
  72.9 16.9 %collective-permute-start.14 = (bf16[328,1024]{1,0:T(8,128)(2,1)S(1)}, bf16[328,1024]{1,0:T(8,128)(2,1)S(1)}, u32[]{:S(2)}, u32[]{:S(2)}) collective-permute-start(bf16[328,1024]{1,0:T(8,128)(2,1)S(1)} %constant_dynamic-slice_fusion.2), channel_id=1, source_target_pairs={{0,96},{32,64},{64,32},{96,0},{1,97},{33,65},{65,33},{97,1},{2,98}... | collective-permute-start | bytes 2015240 | tf_op jit(solution)/shard_map/ppermute | solution.py:31
  75.1 15.0 %collective-permute-start.12 = (bf16[328,1024]{1,0:T(8,128)(2,1)S(1)}, bf16[328,1024]{1,0:T(8,128)(2,1)S(1)}, u32[]{:S(2)}, u32[]{:S(2)}) collective-permute-start(bf16[328,1024]{1,0:T(8,128)(2,1)S(1)} %collective-permute-done.11), channel_id=1, source_target_pairs={{0,8},{8,0},{16,24},{24,16},{1,9},{9,1},{17,25},{25,17},{2,10},{10... | collective-permute-start | bytes 2015240 | tf_op jit(solution)/shard_map/ppermute | solution.py:314
  79.4 103.9 %collective-permute-start.33 = (bf16[128,1024]{1,0:T(8,128)(2,1)S(1)}, bf16[128,1024]{1,0:T(8,128)(2,1)S(1)}, u32[]{:S(2)}, u32[]{:S(2)}) collective-permute-start(bf16[128,1024]{1,0:T(8,128)(2,1)S(1)} %copy-done.74), channel_id=1, source_target_pairs={{0,1},{1,2},{2,3},{3,0},{4,5},{5,6},{6,7},{7,4},{8,9},{9,10},{10,1... | collective-permute-start | bytes 786440 | tf_op jit(solution)/shard_map/ppermute | solution.py:19
  79.4 109.4 %collective-permute-start.32 = (bf16[128,1024]{1,0:T(8,128)(2,1)S(1)}, bf16[128,1024]{1,0:T(8,128)(2,1)S(1)}, u32[]{:S(2)}, u32[]{:S(2)}) collective-permute-start(bf16[128,1024]{1,0:T(8,128)(2,1)S(1)} %copy-done.74), channel_id=1, source_target_pairs={{0,2},{1,3},{2,0},{3,1},{4,6},{5,7},{6,4},{7,5},{8,10},{9,11},{10,... | collective-permute-start | bytes 786440 | tf_op jit(solution)/shard_map/ppermute | solution.py:19
  114.8 13.2 %collective-permute-start.19 = (bf16[128,1024]{1,0:T(8,128)(2,1)S(1)}, bf16[128,1024]{1,0:T(8,128)(2,1)S(1)}, u32[]{:S(2)}, u32[]{:S(2)}) collective-permute-start(bf16[128,1024]{1,0:T(8,128)(2,1)S(1)} %convolution_convert_fusion.21), channel_id=1, source_target_pairs={{0,1},{1,2},{2,3},{3,0},{4,5},{5,6},{6,7},{7,4},{8,9},{9,10},{10,1... | collective-permute-start | bytes 786440 | tf_op jit(solution)/shard_map/ppermute | solution.py:19
  129.1 16.2 %collective-permute-start.24 = (bf16[128,1024]{1,0:T(8,128)(2,1)S(1)}, bf16[128,1024]{1,0:T(8,128)(2,1)S(1)}, u32[]{:S(2)}, u32[]{:S(2)}) collective-permute-start(bf16[128,1024]{1,0:T(8,128)(2,1)S(1)} %fusion.74), channel_id=1, source_target_pairs={{0,1},{1,2},{2,3},{3,0},{4,5},{5,6},{6,7},{7,4},{8,9},{9,10},{10,1... | collective-permute-start | bytes 786440 | tf_op jit(solution)/shard_map/ppermute | solution.py:19
  129.6 14.9 %collective-permute-start.23 = (bf16[128,1024]{1,0:T(8,128)(2,1)S(1)}, bf16[128,1024]{1,0:T(8,128)(2,1)S(1)}, u32[]{:S(2)}, u32[]{:S(2)}) collective-permute-start(bf16[128,1024]{1,0:T(8,128)(2,1)S(1)} %fusion.74), channel_id=1, source_target_pairs={{0,2},{1,3},{2,0},{3,1},{4,6},{5,7},{6,4},{7,5},{8,10},{9,11},{10,... | collective-permute-start | bytes 786440 | tf_op jit(solution)/shard_map/ppermute | solution.py:19
  157.5 12.6 %collective-permute-start.26 = (bf16[128,1024]{1,0:T(8,128)(2,1)S(1)}, bf16[128,1024]{1,0:T(8,128)(2,1)S(1)}, u32[]{:S(2)}, u32[]{:S(2)}) collective-permute-start(bf16[128,1024]{1,0:T(8,128)(2,1)S(1)} %convolution_convert_fusion.18), channel_id=1, source_target_pairs={{0,1},{1,2},{2,3},{3,0},{4,5},{5,6},{6,7},{7,4},{8,9},{9,10},{10,1... | collective-permute-start | bytes 786440 | tf_op jit(solution)/shard_map/ppermute | solution.py:19
  163.0 29.3 %collective-permute-start.31 = (bf16[128,1024]{1,0:T(8,128)(2,1)S(1)}, bf16[128,1024]{1,0:T(8,128)(2,1)S(1)}, u32[]{:S(2)}, u32[]{:S(2)}) collective-permute-start(bf16[128,1024]{1,0:T(8,128)(2,1)S(1)} %copy-done.74), channel_id=1, source_target_pairs={{0,3},{1,0},{2,1},{3,2},{4,7},{5,4},{6,5},{7,6},{8,11},{9,8},{10,9... | collective-permute-start | bytes 786440 | tf_op jit(solution)/shard_map/ppermute | solution.py:19
  174.3 13.5 %collective-permute-start.29 = (bf16[128,1024]{1,0:T(8,128)(2,1)S(1)}, bf16[128,1024]{1,0:T(8,128)(2,1)S(1)}, u32[]{:S(2)}, u32[]{:S(2)}) collective-permute-start(bf16[128,1024]{1,0:T(8,128)(2,1)S(1)} %multiply_convert_fusion.2), channel_id=1, source_target_pairs={{0,2},{1,3},{2,0},{3,1},{4,6},{5,7},{6,4},{7,5},{8,10},{9,11},{10,... | collective-permute-start | bytes 786440 | tf_op jit(solution)/shard_map/ppermute | solution.py:19
  195.1 23.7 %collective-permute-start.41 = (bf16[328,1024]{1,0:T(8,128)(2,1)S(1)}, bf16[328,1024]{1,0:T(8,128)(2,1)S(1)}, u32[]{:S(2)}, u32[]{:S(2)}) collective-permute-start(bf16[328,1024]{1,0:T(8,128)(2,1)S(1)} %convolution_convert_fusion.3), channel_id=1, source_target_pairs={{0,4},{4,0},{1,5},{5,1},{2,6},{6,2},{3,7},{7,3},{8,12},{12,8},{9,1... | collective-permute-start | bytes 2015240 | tf_op jit(solution)/shard_map/ppermute | solution.py:23
  198.1 21.3 %collective-permute-start.40 = (bf16[656,1024]{1,0:T(8,128)(2,1)S(1)}, bf16[656,1024]{1,0:T(8,128)(2,1)S(1)}, u32[]{:S(2)}, u32[]{:S(2)}) collective-permute-start(bf16[656,1024]{1,0:T(8,128)(2,1)S(1)} %convolution_convert_fusion.1), channel_id=1, source_target_pairs={{0,4},{4,0},{1,5},{5,1},{2,6},{6,2},{3,7},{7,3},{8,12},{12,8},{9,1... | collective-permute-start | bytes 4030472 | tf_op jit(solution)/shard_map/ppermute | solution.py:23
  199.2 14.8 %collective-permute-start.35 = (bf16[128,1024]{1,0:T(8,128)(2,1)S(1)}, bf16[128,1024]{1,0:T(8,128)(2,1)S(1)}, u32[]{:S(2)}, u32[]{:S(2)}) collective-permute-start(bf16[128,1024]{1,0:T(8,128)(2,1)S(1)} %convolution_convert_fusion.30), channel_id=1, source_target_pairs={{0,1},{1,2},{2,3},{3,0},{4,5},{5,6},{6,7},{7,4},{8,9},{9,10},{10,1... | collective-permute-start | bytes 786440 | tf_op jit(solution)/shard_map/ppermute | solution.py:19
  216.2 14.5 %collective-permute-start.39 = (bf16[128,1024]{1,0:T(8,128)(2,1)}, bf16[128,1024]{1,0:T(8,128)(2,1)}, u32[]{:S(2)}, u32[]{:S(2)}) collective-permute-start(bf16[128,1024]{1,0:T(8,128)(2,1)} %get-tuple-element.148), channel_id=1, source_target_pairs={{0,1},{1,2},{2,3},{3,0},{4,5},{5,6},{6,7},{7,4},{8,9},{9,10},{10,1... | collective-permute-start | bytes 786440 | tf_op jit(solution)/shard_map/ppermute | solution.py:19
  216.2 14.5 %collective-permute-start.38 = (bf16[128,1024]{1,0:T(8,128)(2,1)}, bf16[128,1024]{1,0:T(8,128)(2,1)}, u32[]{:S(2)}, u32[]{:S(2)}) collective-permute-start(bf16[128,1024]{1,0:T(8,128)(2,1)} %get-tuple-element.148), channel_id=1, source_target_pairs={{0,2},{1,3},{2,0},{3,1},{4,6},{5,7},{6,4},{7,5},{8,10},{9,11},{10,... | collective-permute-start | bytes 786440 | tf_op jit(solution)/shard_map/ppermute | solution.py:19
  217.1 14.0 %collective-permute-start.37 = (bf16[128,1024]{1,0:T(8,128)(2,1)}, bf16[128,1024]{1,0:T(8,128)(2,1)}, u32[]{:S(2)}, u32[]{:S(2)}) collective-permute-start(bf16[128,1024]{1,0:T(8,128)(2,1)} %get-tuple-element.148), channel_id=1, source_target_pairs={{0,3},{1,0},{2,1},{3,2},{4,7},{5,4},{6,5},{7,6},{8,11},{9,8},{10,9... | collective-permute-start | bytes 786440 | tf_op jit(solution)/shard_map/ppermute | solution.py:19
  222.8 119.3 %reduce-scatter.5.cloned.1.call-start = ((), (), s32[]{:S(2)}) async-start(), calls=%async_computation.7 | async-start | bytes 1179648 | tf_op jit(solution)/shard_map/reduce_scatter | solution.py:343
  253.4 13.9 %collective-permute-start.42 = (bf16[128,1024]{1,0:T(8,128)(2,1)S(1)}, bf16[128,1024]{1,0:T(8,128)(2,1)S(1)}, u32[]{:S(2)}, u32[]{:S(2)}) collective-permute-start(bf16[128,1024]{1,0:T(8,128)(2,1)S(1)} %convolution_convert_fusion.16), channel_id=1, source_target_pairs={{0,2},{1,3},{2,0},{3,1},{4,6},{5,7},{6,4},{7,5},{8,10},{9,11},{10,... | collective-permute-start | bytes 786440 | tf_op jit(solution)/shard_map/ppermute | solution.py:19
  256.8 17.8 %collective-permute-start.48 = (bf16[1024,256]{1,0:T(8,128)(2,1)S(1)}, bf16[1024,256]{1,0:T(8,128)(2,1)S(1)}, u32[]{:S(2)}, u32[]{:S(2)}) collective-permute-start(bf16[1024,256]{1,0:T(8,128)(2,1)S(1)} %convolution_convert_fusion.7), channel_id=1, source_target_pairs={{0,4},{4,0},{1,5},{5,1},{2,6},{6,2},{3,7},{7,3},{8,12},{12,8},{9,1... | collective-permute-start | bytes 1572872 | tf_op jit(solution)/shard_map/ppermute | solution.py:23
  271.0 14.6 %collective-permute-start.46 = (bf16[128,1024]{1,0:T(8,128)(2,1)}, bf16[128,1024]{1,0:T(8,128)(2,1)}, u32[]{:S(2)}, u32[]{:S(2)}) collective-permute-start(bf16[128,1024]{1,0:T(8,128)(2,1)} %add_convert_fusion.7), channel_id=1, source_target_pairs={{0,2},{1,3},{2,0},{3,1},{4,6},{5,7},{6,4},{7,5},{8,10},{9,11},{10,... | collective-permute-start | bytes 786440 | tf_op jit(solution)/shard_map/ppermute | solution.py:19
  300.3 30.0 %collective-permute-start.57 = (bf16[328,1024]{1,0:T(8,128)(2,1)}, bf16[328,1024]{1,0:T(8,128)(2,1)}, u32[]{:S(2)}, u32[]{:S(2)}) collective-permute-start(bf16[328,1024]{1,0:T(8,128)(2,1)} %convolution_convert_fusion.2), channel_id=1, source_target_pairs={{0,4},{4,0},{1,5},{5,1},{2,6},{6,2},{3,7},{7,3},{8,12},{12,8},{9,1... | collective-permute-start | bytes 2015240 | tf_op jit(solution)/shard_map/ppermute | solution.py:23
  304.1 28.1 %collective-permute-start.56 = (bf16[656,1024]{1,0:T(8,128)(2,1)}, bf16[656,1024]{1,0:T(8,128)(2,1)}, u32[]{:S(2)}, u32[]{:S(2)}) collective-permute-start(bf16[656,1024]{1,0:T(8,128)(2,1)} %convolution_convert_fusion), channel_id=1, source_target_pairs={{0,4},{4,0},{1,5},{5,1},{2,6},{6,2},{3,7},{7,3},{8,12},{12,8},{9,1... | collective-permute-start | bytes 4030472 | tf_op jit(solution)/shard_map/ppermute | solution.py:23
  310.4 14.8 %collective-permute-start.51 = (bf16[128,1024]{1,0:T(8,128)(2,1)}, bf16[128,1024]{1,0:T(8,128)(2,1)S(1)}, u32[]{:S(2)}, u32[]{:S(2)}) collective-permute-start(bf16[128,1024]{1,0:T(8,128)(2,1)} %convolution_convert_fusion.27), channel_id=1, source_target_pairs={{0,1},{1,2},{2,3},{3,0},{4,5},{5,6},{6,7},{7,4},{8,9},{9,10},{10,1... | collective-permute-start | bytes 786440 | tf_op jit(solution)/shard_map/ppermute | solution.py:19
  312.0 13.2 %collective-permute-start.52 = (bf16[128,1024]{1,0:T(8,128)(2,1)}, bf16[128,1024]{1,0:T(8,128)(2,1)S(1)}, u32[]{:S(2)}, u32[]{:S(2)}) collective-permute-start(bf16[128,1024]{1,0:T(8,128)(2,1)} %convolution_convert_fusion.26), channel_id=1, source_target_pairs={{0,3},{1,0},{2,1},{3,2},{4,7},{5,4},{6,5},{7,6},{8,11},{9,8},{10,9... | collective-permute-start | bytes 786440 | tf_op jit(solution)/shard_map/ppermute | solution.py:19
  327.0 15.1 %collective-permute-start.55 = (bf16[128,1024]{1,0:T(8,128)(2,1)S(1)}, bf16[128,1024]{1,0:T(8,128)(2,1)S(1)}, u32[]{:S(2)}, u32[]{:S(2)}) collective-permute-start(bf16[128,1024]{1,0:T(8,128)(2,1)S(1)} %convert_element_type.813), channel_id=1, source_target_pairs={{0,1},{1,2},{2,3},{3,0},{4,5},{5,6},{6,7},{7,4},{8,9},{9,10},{10,1... | collective-permute-start | bytes 786440 | tf_op jit(solution)/shard_map/ppermute | solution.py:19
  327.3 14.8 %collective-permute-start.54 = (bf16[128,1024]{1,0:T(8,128)(2,1)S(1)}, bf16[128,1024]{1,0:T(8,128)(2,1)}, u32[]{:S(2)}, u32[]{:S(2)}) collective-permute-start(bf16[128,1024]{1,0:T(8,128)(2,1)S(1)} %convert_element_type.813), channel_id=1, source_target_pairs={{0,2},{1,3},{2,0},{3,1},{4,6},{5,7},{6,4},{7,5},{8,10},{9,11},{10,... | collective-permute-start | bytes 786440 | tf_op jit(solution)/shard_map/ppermute | solution.py:19
  388.8 35.3 %all-to-all-start.2 = ((bf16[8,128,1024]{2,1,0:T(8,128)(2,1)}), bf16[8,128,1024]{2,1,0:T(8,128)(2,1)}, u32[]{:S(2)}, u32[]{:S(2)}) async-start(bf16[8,128,1024]{2,1,0:T(8,128)(2,1)} %bitcast.454), calls=%async_computation.4 | async-start | bytes 4194304 | tf_op jit(solution)/shard_map/all_to_all | solution.py:347
  396.1 13.8 %collective-permute-start.64 = (bf16[128,1024]{1,0:T(8,128)(2,1)S(1)}, bf16[128,1024]{1,0:T(8,128)(2,1)S(1)}, u32[]{:S(2)}, u32[]{:S(2)}) collective-permute-start(bf16[128,1024]{1,0:T(8,128)(2,1)S(1)} %convolution_convert_fusion.10), channel_id=1, source_target_pairs={{0,2},{1,3},{2,0},{3,1},{4,6},{5,7},{6,4},{7,5},{8,10},{9,11},{10,... | collective-permute-start | bytes 786440 | tf_op jit(solution)/shard_map/ppermute | solution.py:19
  411.9 12.1 %collective-permute-start.77 = (bf16[256,256]{1,0:T(8,128)(2,1)S(1)}, bf16[256,256]{1,0:T(8,128)(2,1)S(1)}, u32[]{:S(2)}, u32[]{:S(2)}) collective-permute-start(bf16[256,256]{1,0:T(8,128)(2,1)S(1)} %broadcast_select_fusion.37), channel_id=1, source_target_pairs={{0,64},{64,0},{1,65},{65,1},{2,66},{66,2},{3,67},{67,3},{4,68},{68... | collective-permute-start | bytes 393224 | tf_op jit(solution)/shard_map/ppermute | solution.py:27
  425.1 28.2 %all-to-all-start.1 = ((bf16[8,256,256]{2,1,0:T(8,128)(2,1)}), bf16[8,256,256]{2,1,0:T(8,128)(2,1)}, u32[]{:S(2)}, u32[]{:S(2)}) async-start(bf16[8,256,256]{2,1,0:T(8,128)(2,1)} %broadcast_in_dim.274), calls=%async_computation.3 | async-start | bytes 2097152 | tf_op jit(solution)/shard_map/all_to_all | solution.py:354
  431.8 21.4 %collective-permute-start.79 = (bf16[128,1024]{1,0:T(8,128)(2,1)S(1)}, bf16[128,1024]{1,0:T(8,128)(2,1)S(1)}, u32[]{:S(2)}, u32[]{:S(2)}) collective-permute-start(bf16[128,1024]{1,0:T(8,128)(2,1)S(1)} %broadcast_select_fusion.34), channel_id=1, source_target_pairs={{0,64},{64,0},{1,65},{65,1},{2,66},{66,2},{3,67},{67,3},{4,68},{68... | collective-permute-start | bytes 786440 | tf_op jit(solution)/shard_map/ppermute | solution.py:27
  433.3 16.0 %collective-permute-start.68 = (f32[2,1024]{1,0:T(2,128)S(1)}, f32[2,1024]{1,0:T(2,128)S(1)}, u32[]{:S(2)}, u32[]{:S(2)}) collective-permute-start(f32[2,1024]{1,0:T(2,128)S(1)} %broadcast_select_fusion.38), channel_id=1, source_target_pairs={{0,64},{64,0},{1,65},{65,1},{2,66},{66,2},{3,67},{67,3},{4,68},{68... | collective-permute-start | bytes 24584 | tf_op jit(solution)/shard_map/ppermute | solution.py:27
  454.9 46.7 %all-to-all-start.3 = ((bf16[8,128,1024]{2,1,0:T(8,128)(2,1)}), bf16[8,128,1024]{2,1,0:T(8,128)(2,1)}, u32[]{:S(2)}, u32[]{:S(2)}) async-start(bf16[8,128,1024]{2,1,0:T(8,128)(2,1)} %broadcast_in_dim.279), calls=%async_computation.5 | async-start | bytes 4194304 | tf_op jit(solution)/shard_map/all_to_all | solution.py:354
  462.3 21.6 %collective-permute-start.75 = (f32[2,1024]{1,0:T(2,128)S(1)}, f32[2,1024]{1,0:T(2,128)S(1)}, u32[]{:S(2)}, u32[]{:S(2)}) collective-permute-start(f32[2,1024]{1,0:T(2,128)S(1)} %add.548), channel_id=1, source_target_pairs={{0,24},{8,0},{16,8},{24,16},{1,25},{9,1},{17,9},{25,17},{2,26},{10... | collective-permute-start | bytes 24584 | tf_op jit(solution)/shard_map/ppermute | solution.py:19
  465.2 20.0 %collective-permute-start.74 = (f32[2,1024]{1,0:T(2,128)S(1)}, f32[2,1024]{1,0:T(2,128)S(1)}, u32[]{:S(2)}, u32[]{:S(2)}) collective-permute-start(f32[2,1024]{1,0:T(2,128)S(1)} %add.548), channel_id=1, source_target_pairs={{0,16},{8,24},{16,0},{24,8},{1,17},{9,25},{17,1},{25,9},{2,18},{10... | collective-permute-start | bytes 24584 | tf_op jit(solution)/shard_map/ppermute | solution.py:19
  465.8 20.4 %collective-permute-start.73 = (f32[2,1024]{1,0:T(2,128)S(1)}, f32[2,1024]{1,0:T(2,128)S(1)}, u32[]{:S(2)}, u32[]{:S(2)}) collective-permute-start(f32[2,1024]{1,0:T(2,128)S(1)} %add.548), channel_id=1, source_target_pairs={{0,8},{8,16},{16,24},{24,0},{1,9},{9,17},{17,25},{25,1},{2,10},{10... | collective-permute-start | bytes 24584 | tf_op jit(solution)/shard_map/ppermute | solution.py:19
  487.9 13.8 %collective-permute-start.62 = (bf16[128,1024]{1,0:T(8,128)(2,1)S(1)}, bf16[128,1024]{1,0:T(8,128)(2,1)}, u32[]{:S(2)}, u32[]{:S(2)}) collective-permute-start(bf16[128,1024]{1,0:T(8,128)(2,1)S(1)} %convolution_convert_fusion.11), channel_id=1, source_target_pairs={{0,3},{1,0},{2,1},{3,2},{4,7},{5,4},{6,5},{7,6},{8,11},{9,8},{10,9... | collective-permute-start | bytes 786440 | tf_op jit(solution)/shard_map/ppermute | solution.py:19
  498.2 13.3 %collective-permute-start.78 = (bf16[2048,256]{1,0:T(8,128)(2,1)}, bf16[2048,256]{1,0:T(8,128)(2,1)S(1)}, u32[]{:S(2)}, u32[]{:S(2)}) collective-permute-start(bf16[2048,256]{1,0:T(8,128)(2,1)} %bitcast.135), channel_id=1, source_target_pairs={{0,4},{4,0},{1,5},{5,1},{2,6},{6,2},{3,7},{7,3},{8,12},{12,8},{9,1... | collective-permute-start | bytes 3145736 | tf_op jit(solution)/shard_map/ppermute | solution.py:23
  501.6 14.8 %collective-permute-start.80 = (bf16[1024,1024]{1,0:T(8,128)(2,1)}, bf16[1024,1024]{1,0:T(8,128)(2,1)}, u32[]{:S(2)}, u32[]{:S(2)}) collective-permute-start(bf16[1024,1024]{1,0:T(8,128)(2,1)} %bitcast.144), channel_id=1, source_target_pairs={{0,4},{4,0},{1,5},{5,1},{2,6},{6,2},{3,7},{7,3},{8,12},{12,8},{9,1... | collective-permute-start | bytes 6291464 | tf_op jit(solution)/shard_map/ppermute | solution.py:23
  (249 other events, 2045.0 us)
Sparse Core Ops, SparseCore 0:
  222.9 37.2 reduce-scatter.2
  309.6 32.4 reduce-scatter.4

commit v6 on v4

v6 whole, which is shorter than its diff:
```python
import jax
import jax.numpy as jnp
from jax import lax
from jax.sharding import Mesh
from jax.sharding import PartitionSpec as P

HEAD_DIM = 64
WINDOW = 128

epsilon = 1e-05
bf16 = jnp.bfloat16
f32 = jnp.float32

DP = ("zlo", "x", "core")


def around(block, axis, distance):
    count = lax.axis_size(axis)
    return lax.ppermute(block, axis, [(i, (i + distance) % count) for i in range(count)])


def swap_core(block):
    return lax.ppermute(block, "core", [(0, 1), (1, 0)])


def swap_section(block):
    return lax.ppermute(block, "section", [(0, 1), (1, 0)])


def swap_layer(block):
    return lax.ppermute(block, ("section", "zlo"), [(0, 3), (1, 2), (2, 1), (3, 0)])


def gather_parts(block):
    far = around(block, "tensor", 2)
    ahead = around(block, "tensor", -1)
    behind = around(block, "tensor", 1)
    return [joined([block, ahead, behind]), far]


def scatter_parts(near, far):
    rows = far.shape[0]
    sent_far = around(far.astype(bf16), "tensor", 2)
    sent_ahead = around(near[rows : 2 * rows].astype(bf16), "tensor", 1)
    sent_behind = around(near[2 * rows :].astype(bf16), "tensor", -1)
    kept = near[:rows].astype(f32)
    return kept + sent_far.astype(f32) + sent_ahead.astype(f32) + sent_behind.astype(f32)


def joined(parts, axis=0):
    return jnp.concatenate(parts, axis=axis)


def after_all(values, *others):
    return lax.optimization_barrier((values,) + others)[0]


def sum_tensor(block):
    return (
        block
        + around(block, "tensor", 2)
        + around(block, "tensor", 1)
        + around(block, "tensor", -1)
    )


def layer_norm(values, gain_scale):
    centered = values - jnp.mean(values, axis=-1, keepdims=True)
    variance = jnp.mean(centered * centered, axis=-1, keepdims=True)
    return centered * lax.rsqrt(variance + epsilon) * gain_scale


def doc_layout(doc_lengths, indices):
    doc_ends = jnp.cumsum(doc_lengths)
    passed = indices[:, None] >= doc_ends[None, :]
    doc_ids = jnp.sum(passed.astype(jnp.int32), axis=1)
    starts = jnp.sum(jnp.where(passed, doc_lengths[None, :], 0), axis=1)
    return (doc_ids, indices - starts)


def rope_tables(positions, rope_base):
    half_dim = HEAD_DIM // 2
    inverse = rope_base ** (-2.0 * jnp.arange(half_dim, dtype=f32) / HEAD_DIM)
    angles = positions.astype(f32)[..., None] * inverse
    angles = jnp.concatenate([angles, angles], axis=-1)
    return (jnp.cos(angles), jnp.sin(angles))


def rotate(values, cosine_table, sine_table):
    half_dim = values.shape[-1] // 2
    turned = jnp.concatenate([-values[..., half_dim:], values[..., :half_dim]], axis=-1)
    return values * cosine_table[..., None, :] + turned * sine_table[..., None, :]


def rotate_back(gradients, cosine_table, sine_table):
    half_dim = gradients.shape[-1] // 2
    scaled = gradients * sine_table[..., None, :]
    turned = jnp.concatenate([scaled[..., half_dim:], -scaled[..., :half_dim]], axis=-1)
    return gradients * cosine_table[..., None, :] + turned


def masked_scores(queries, keys_rot, allowed):
    scores = jnp.einsum(
        "qhd,khd->hqk", queries, keys_rot, preferred_element_type=f32
    ) * HEAD_DIM ** (-0.5)
    return jnp.where(allowed[None], scores, -1e30)


def contract_rows(left_rows, right_rows):
    return lax.dot_general(
        left_rows, right_rows, (((0,), (0,)), ((), ())), preferred_element_type=f32
    )


def contract_last(left_rows, weight):
    return lax.dot_general(
        left_rows, weight, (((1,), (1,)), ((), ())), preferred_element_type=f32
    )


def times(left_rows, weight):
    return jnp.dot(left_rows, weight, preferred_element_type=f32)


def gelu_product(first_half, second_half):
    return jax.nn.gelu(first_half, approximate=False) * second_half


def in_turn(work, parts):
    first = work(0, parts[0])
    return first, work(1, after_all(parts[1], first))


def forward_layer(inputs, normed_parts, gain_mid, weights, allowed, tables, late, points):
    w_qkv, w_out = weights[0], weights[1]
    row_count = inputs.shape[0]
    local_width = w_out.shape[0]
    spans = (slice(0, 3 * row_count), slice(3 * row_count, 4 * row_count))

    def project(k, part):
        projected = times(part, w_qkv).reshape(part.shape[0], 3, -1, HEAD_DIM)
        turns = (tables[0][spans[k]], tables[1][spans[k]])
        return (
            rotate(projected[:, 0], *turns).astype(bf16),
            rotate(projected[:, 1], *turns).astype(bf16),
            projected[:, 2].astype(bf16),
        )

    near, far = in_turn(project, normed_parts)
    queries = (near[0], far[0])
    keys_all = joined([near[1], far[1]])
    values_all = joined([near[2], far[2]])

    def attend(k, own_queries):
        scores = masked_scores(own_queries, keys_all, allowed[spans[k]])
        largest = jnp.max(scores, axis=2, keepdims=True)
        exp_scores = jnp.exp(scores - largest)
        totals = jnp.sum(exp_scores, axis=2, keepdims=True)
        soft_weights = (exp_scores / totals).astype(bf16)
        mixed = jnp.einsum("hqk,khd->qhd", soft_weights, values_all, preferred_element_type=f32)
        mixed = mixed.reshape(own_queries.shape[0], local_width).astype(bf16)
        return largest + jnp.log(totals), mixed, times(mixed, w_out).astype(bf16)

    far_logs, far_mixed, far_term = attend(1, queries[1])
    near_logs, near_mixed, near_term = attend(0, after_all(queries[0], far_term))
    resid_mid = inputs + scatter_parts(near_term, far_term)
    points(near_mixed, resid_mid)
    w_up, w_down = weights[2], weights[3]
    mid_parts = gather_parts(layer_norm(resid_mid, gain_mid).astype(bf16))

    def feed(k, part):
        hidden = contract_last(part, w_up)
        local_hidden = hidden.shape[1] // 2
        gelu_in = hidden[:, :local_hidden]
        gate_mult = hidden[:, local_hidden:]
        mixed = gelu_product(gelu_in, gate_mult).astype(bf16)
        return gelu_in, gate_mult, mixed, None if late else times(mixed, w_down).astype(bf16)

    fed = in_turn(feed, mid_parts)
    if late:

        def result(gate):
            held = after_all((fed[0][2], fed[1][2]), gate)
            return [times(mixed, w_down).astype(bf16) for mixed in held]

    else:
        result = resid_mid + scatter_parts(fed[0][3], fed[1][3])
    kept = dict(
        inputs=inputs,
        resid_mid=resid_mid,
        normed=normed_parts,
        queries=joined(queries),
        keys=keys_all,
        values=values_all,
        log_totals=joined([near_logs, far_logs], 1),
        attended=(near_mixed, far_mixed),
        normed_mid=mid_parts,
        gelu_in=(fed[0][0], fed[1][0]),
        gate_mult=(fed[0][1], fed[1][1]),
        mixed=(fed[0][2], fed[1][2]),
    )
    return (result, kept)


def backward_ffn(grad_result, kept, gain_mid, weights):
    w_up, w_down = weights[2], weights[3]
    grad_parts = gather_parts(grad_result.astype(bf16))

    def feed_back(k, part):
        grad_mixed = contract_last(part, w_down)
        unused, pull_gelu = jax.vjp(gelu_product, kept["gelu_in"][k], kept["gate_mult"][k])
        terms = tuple(term.astype(bf16) for term in pull_gelu(grad_mixed))
        return terms[0], terms[1], times(joined(terms, 1), w_up).astype(bf16)

    near, far = in_turn(feed_back, grad_parts)
    grad_normed_mid = scatter_parts(near[2], far[2])
    unused, pull_norm = jax.vjp(layer_norm, kept["resid_mid"], gain_mid)
    grad_resid, grad_gain = pull_norm(grad_normed_mid)

    def weight_grads(gate):
        outer, inner, left, first, second = after_all(
            (grad_parts, kept["mixed"], kept["normed_mid"], (near[0], far[0]), (near[1], far[1])),
            gate,
        )
        outer, inner, left = joined(outer), joined(inner), joined(left)
        first, second = joined(first), joined(second)
        half = inner.shape[1] // 2
        front, back = inner[:, :half], inner[:, half:]
        up = add_core(lambda core: contract_rows(core(first, second), left))
        down = add_core(lambda core: contract_rows(core(front, back), outer))
        rows = up.shape[0] + down.shape[0]
        blank = jnp.zeros((-rows % 128, up.shape[1]), bf16)
        return joined([up, down, blank])

    return (grad_result + grad_resid, weight_grads, grad_gain)


def backward_attn(grad_mid, kept, gain_first, weights, allowed, tables):
    w_qkv, w_out = weights[0], weights[1]
    queries, keys_rot, values_in = kept["queries"], kept["keys"], kept["values"]
    row_count = grad_mid.shape[0]
    grad_parts = gather_parts(grad_mid.astype(bf16))
    near, far = in_turn(lambda k, part: contract_last(part, w_out).astype(bf16), grad_parts)
    grad_attended = joined([near, far]).reshape(queries.shape)
    scores = masked_scores(queries, keys_rot, allowed)
    soft_exact = jnp.exp(scores - kept["log_totals"])
    soft_weights = soft_exact.astype(bf16)
    grad_values = jnp.einsum(
        "hqk,qhd->khd", soft_weights, grad_attended, preferred_element_type=f32
    )
    grad_soft = jnp.einsum("qhd,khd->hqk", grad_attended, values_in, preferred_element_type=f32)
    row_dots = jnp.sum(soft_exact * grad_soft, axis=2, keepdims=True)
    grad_scores = (soft_exact * (grad_soft - row_dots)).astype(bf16)
    grad_queries = jnp.einsum(
        "hqk,khd->qhd", grad_scores, keys_rot, preferred_element_type=f32
    ) * HEAD_DIM ** (-0.5)
    grad_keys = jnp.einsum(
        "hqk,qhd->khd", grad_scores, queries, preferred_element_type=f32
    ) * HEAD_DIM ** (-0.5)
    grad_projected = jnp.stack(
        [
            rotate_back(grad_queries, *tables),
            rotate_back(grad_keys, *tables),
            grad_values,
        ],
        axis=1,
    )
    grad_projected = grad_projected.astype(bf16).reshape(4 * row_count, -1)
    far_term = contract_last(grad_projected[3 * row_count :], w_qkv).astype(bf16)
    near_term = contract_last(grad_projected[: 3 * row_count], w_qkv).astype(bf16)
    grad_normed = scatter_parts(near_term, far_term)
    unused, pull_norm = jax.vjp(layer_norm, kept["inputs"], gain_first)
    grad_resid, grad_gain = pull_norm(grad_normed)

    def gain_before():
        total = 0.0
        for term, normed in zip((near_term, far_term), kept["normed"]):
            total = total + jnp.sum(term.astype(f32) * normed.astype(f32), axis=0)
        return total / gain_first

    def weight_grads(gate, gains):
        outer, inner, left, right = after_all(
            (grad_parts, kept["attended"], kept["normed"], grad_projected), gate
        )
        outer, inner, left = joined(outer), joined(inner), joined(left)
        width = inner.shape[1]
        of_q, of_k, of_v = (right[:, i * width : (i + 1) * width] for i in range(3))
        one = add_core(lambda core: contract_rows(left, core(of_q, of_v)))
        two = add_core(lambda core: contract_rows(core(left, outer), core(of_k, inner)))
        extra = jnp.stack(gains).astype(bf16).reshape(-1, width)
        blank = jnp.zeros((-extra.shape[0] % 128, width), bf16)
        return joined([one, two, extra, blank])

    return (grad_mid + grad_resid, weight_grads, grad_gain, gain_before)


def other_layer(own, after, pair_x, before_x, before_core):
    core_index = lax.axis_index("core")
    parity = lax.axis_index("x") % 2
    own = after_all(own, after)
    rows = own.shape[0]
    if pair_x:
        piece = rows // 4
        sent = lax.dynamic_slice_in_dim(own, (core_index * 2 + parity) * piece, piece)
        got = swap_layer(sent)
        kept = after_all(got, before_x)
        beside = lax.ppermute(kept, "x", [(0, 1), (1, 0), (2, 3), (3, 2)])
        half = in_order(parity, kept, beside)
    else:
        piece = rows // 2
        sent = lax.dynamic_slice_in_dim(own, core_index * piece, piece)
        got = half = swap_layer(sent)
    half = after_all(half, before_core)
    return in_order(core_index, half, swap_core(half)), got


def in_order(index, mine, other):
    low = jnp.where(index == 0, mine, other)
    high = jnp.where(index == 0, other, mine)
    return jnp.concatenate([low, high], axis=0)


def add_core(product):
    is_core0 = lax.axis_index("core") == 0
    sent = product(lambda one, two: jnp.where(is_core0, two, one)).astype(bf16)
    held = product(lambda one, two: jnp.where(is_core0, one, two))
    return (held + swap_core(sent).astype(f32)).astype(bf16)


def reduce_part(grads):
    return lax.psum_scatter(grads, ("zlo", "x"), scatter_dimension=0, tiled=True)


def reduce_part_now(grads):
    pieces = lax.all_to_all(grads, ("zlo", "x"), 0, 0, tiled=True)
    pieces = pieces.reshape(8, -1, pieces.shape[1])
    return jnp.sum(pieces.astype(f32), axis=0).astype(bf16)


def spread_part(part):
    copies = jnp.broadcast_to(part[None], (8,) + part.shape).reshape(-1, part.shape[1])
    half = lax.all_to_all(copies, ("zlo", "x"), 0, 0, tiled=True)
    beside = swap_core(half)
    is_core0 = lax.axis_index("core") == 0
    return jnp.where(is_core0, half, beside), jnp.where(is_core0, beside, half)


def pick_sections(is_first, part_first, part_second):
    own = jnp.where(is_first, part_first, part_second)
    sent = jnp.where(is_first, part_second, part_first)
    return own, sent


def local(tokens, cotangent, lengths, gains, w_qkv, w_out, w_up, w_down):
    section_index = lax.axis_index("section")
    is_first = section_index == 0
    row_count = tokens.shape[1]
    full_rows = row_count * lax.axis_size("tensor")
    start_rows = jnp.where(is_first, tokens[0], tokens[1])
    end_grads = jnp.where(is_first, cotangent[0], cotangent[1])
    start_parts = gather_parts(start_rows)
    gains_other = swap_layer(gains[0])
    gains0 = jnp.where(is_first, gains[0], gains_other)
    gains1 = jnp.where(is_first, gains_other, gains[0])
    first_parts = in_turn(
        lambda k, part: layer_norm(part.astype(f32), gains0[0]).astype(bf16), start_parts
    )
    start_rows = start_rows.astype(f32)
    own = (
        jnp.transpose(w_qkv[0], (1, 0, 2)).reshape(-1, w_qkv.shape[3]),
        w_out[0],
        jnp.transpose(w_up[0], (1, 2, 0)).reshape(-1, w_up.shape[1]),
        w_down[0],
    )
    other_qkv, after = other_layer(own[0], (), False, (), start_parts)
    other_out, after_out = other_layer(own[1], after, False, (), ())
    layer0 = [jnp.where(is_first, own[0], other_qkv), jnp.where(is_first, own[1], other_out)]
    layer1 = [jnp.where(is_first, other_qkv, own[0]), jnp.where(is_first, other_out, own[1])]
    layer0[0] = joined(jnp.split(layer0[0], 3), 1)
    layer1[0] = joined(jnp.split(layer1[0], 3), 1)

    def feed_weights(attended, resid_mid):
        other_up, after = other_layer(own[2], after_out, True, attended, resid_mid)
        other_down, unused = other_layer(own[3], after, False, (), resid_mid)
        layer0.extend([jnp.where(is_first, own[2], other_up), jnp.where(is_first, own[3], other_down)])
        layer1.extend([jnp.where(is_first, other_up, own[2]), jnp.where(is_first, other_down, own[3])])

    doc_lengths = jnp.where(is_first, lengths[0, 0], lengths[1, 0])
    indices = jnp.arange(full_rows, dtype=jnp.int32)
    blocks = jnp.array([0, 1, 3, 2], jnp.int32) + lax.axis_index("tensor")
    indices = (jnp.repeat(blocks, row_count) * row_count + indices % row_count) % full_rows
    doc_ids, positions = doc_layout(doc_lengths, indices)
    same_doc = doc_ids[:, None] == doc_ids[None, :]
    near = jnp.abs(indices[:, None] - indices[None, :]) <= WINDOW // 2
    allowed0 = same_doc & near
    allowed1 = same_doc
    tables0 = rope_tables(positions, 10000.0)
    tables1 = rope_tables(positions, 160000.0)

    out0, kept0 = forward_layer(
        start_rows, first_parts, gains0[1], layer0, allowed0, tables0, False, feed_weights
    )
    out0 = out0.astype(bf16)
    second_rows = out0.astype(f32)
    second_parts = gather_parts(layer_norm(second_rows, gains1[0]).astype(bf16))
    out1_of, kept1 = forward_layer(
        second_rows, second_parts, gains1[1], layer1, allowed1, tables1, True, lambda *points: None
    )
    mid1, ffn_grads1, gain_mid1 = backward_ffn(
        end_grads.astype(f32), kept1, gains1[1], layer1
    )
    in1, attn_grads1, gain_first1, unused = backward_attn(
        mid1, kept1, gains1[0], layer1, allowed1, tables1
    )
    in1 = in1.astype(bf16)
    ffn1 = ffn_grads1(mid1)
    in1, ffn1 = lax.optimization_barrier((in1, ffn1))
    ffn1 = reduce_part(ffn1)
    mid0, ffn_grads0, gain_mid0 = backward_ffn(in1.astype(f32), kept0, gains0[1], layer0)
    attn1 = reduce_part_now(attn_grads1(in1, [gain_first1, gain_mid1]))
    mid0 = after_all(mid0, ffn1, attn1)
    in0, attn_grads0, unused, gain_before = backward_attn(
        mid0, kept0, gains0[0], layer0, allowed0, tables0
    )
    in0 = in0.astype(bf16)
    ffn0 = reduce_part(ffn_grads0(mid0))
    attn_pack0 = attn_grads0((), [gain_before(), gain_mid0])
    attn0 = reduce_part_now(attn_pack0)
    out1_terms = out1_of(attn_pack0)
    attn0, in0 = lax.optimization_barrier((attn0, in0))
    attn_own, attn_sent = pick_sections(is_first, attn0, attn1)
    attn_sent = after_all(attn_sent, out1_terms)
    attn_sum = (attn_own.astype(f32) + swap_section(attn_sent).astype(f32)).astype(bf16)
    out1 = (kept1["resid_mid"] + scatter_parts(*out1_terms)).astype(bf16)
    ffn_own, ffn_sent = pick_sections(is_first, ffn0, ffn1)
    ffn_sum = (ffn_own.astype(f32) + swap_section(ffn_sent).astype(f32)).astype(bf16)
    attn_sum, out1 = lax.optimization_barrier((attn_sum, out1))
    attn_halves = spread_part(attn_sum)
    ffn_halves = spread_part(ffn_sum)
    gain_rows = sum(half[2 * w_qkv.shape[1] :][:8].astype(f32) for half in attn_halves)
    gain_total = sum_tensor(gain_rows).reshape(2, -1)
    hidden_width = w_up.shape[3]
    grad_up = jnp.stack([half[:hidden_width] for half in ffn_halves])
    down_rows = w_down.shape[1] // 2
    grad_down = joined([half[hidden_width : hidden_width + down_rows] for half in ffn_halves])
    model_width = w_qkv.shape[1]
    grad_qkv = jnp.stack(
        [
            attn_halves[0][:model_width],
            attn_halves[0][model_width : 2 * model_width],
            attn_halves[1][:model_width],
        ]
    )
    grad_out = attn_halves[1][model_width : 2 * model_width].T

    got_out = swap_section(jnp.where(is_first, out1, out0))
    section_out = jnp.stack(
        [jnp.where(is_first, out0, got_out), jnp.where(is_first, got_out, out1)]
    )
    got_in = swap_section(jnp.where(is_first, in1, in0))
    input_grads = jnp.stack(
        [jnp.where(is_first, in0, got_in), jnp.where(is_first, got_in, in1)]
    )
    return (
        section_out[None],
        input_grads[None],
        gain_total[None],
        jnp.transpose(grad_qkv.astype(f32), (1, 0, 2))[None],
        grad_out.astype(f32)[None],
        jnp.transpose(grad_up.astype(f32), (2, 0, 1))[None],
        grad_down.astype(f32)[None],
    )


def solution(mesh):
    sizes = dict(zip(mesh.axis_names, mesh.devices.shape))
    fine = Mesh(
        mesh.devices.reshape(sizes["section"], 2, sizes["dp"] // 4, 2, sizes["tensor"]),
        ("section", "zlo", "x", "core", "tensor"),
    )
    rows = ("zlo", "x", "core", "tensor")
    in_specs = (
        P(None, rows, None),
        P(None, rows, None),
        P(None, DP, None),
        P("section", None, None),
        P("section", None, None, "tensor"),
        P("section", "tensor", None),
        P("section", None, None, "tensor"),
        P("section", "tensor", None),
    )
    out_specs = (
        P("section", None, rows, None),
        P("section", None, rows, None),
        P("section", None, None),
        P("section", None, None, "tensor"),
        P("section", "tensor", None),
        P("section", None, None, "tensor"),
        P("section", "tensor", None),
    )
    return jax.shard_map(local, mesh=fine, in_specs=in_specs, out_specs=out_specs, check_vma=False)
```

time: 544 us -> 538 us (0.989)
  blocking collectives: 19.2 us -> 0 us
  waiting for transfers between devices: 179 us -> 166 us
  between operations: 5.91 us -> 18.3 us
  matrix products: 92.7 us -> 86.4 us
  other arithmetic: 68.3 us -> 74.6 us
  local copies, waits for them, and re-layouts: 33 us -> 39.1 us
    ppermute x55 -> x51, waiting for transfers between devices: 88.6 us -> 45.1 us  [around(): lax.ppermute(block, axis, [(i, (i + distance) % count) for i in range(cou...]
    all_to_all x1 -> x0, blocking collectives: 19.2 us -> none  [reduce_part(): pieces = lax.all_to_all(grads, ('zlo', 'x'), 0, 0, tiled=True)]
    ppermute x5 -> x4, waiting for transfers between devices: 38.2 us -> 54.5 us  [swap_section(): return lax.ppermute(block, 'section', [(0, 1), (1, 0)])]
    ppermute x15 -> x14, starting transfers between devices: 22.2 us -> 38.1 us  [swap_core(): return lax.ppermute(block, 'core', [(0, 1), (1, 0)])]
    ppermute x5, waiting for transfers between devices: 22.3 us -> 34.9 us  [swap_layer(): lax.ppermute(block, ('section', 'zlo'), [(0, 3), (1, 2), (2, 1), (3, 0)])]
    ppermute x55 -> x51, starting transfers between devices: 81 us -> 72.7 us  [around(): lax.ppermute(block, axis, [(i, (i + distance) % count) for i in range(cou...]
    reduce_sum x4 -> x2, other arithmetic: 8.95 us -> 2.24 us  [reduce_part_now(): return jnp.sum(pieces.astype(f32), axis=0).astype(bf16)]
    concatenate x7 -> x12, other arithmetic: 5.43 us -> 11.8 us  [joined(): return jnp.concatenate(parts, axis=axis)]
  transfers between devices with their start and end apart: 86 -> 81, of which waited for: 37 -> 25; matrix products, arithmetic and copies ran while one was open for 29% -> 33% of each run, Pallas kernels for 0% -> 0%
where the time goes in v6:
time: 538 us; the launch traced here: 527 us
  waiting for transfers between devices  166 us (31%)
  starting transfers between devices  142 us (26%)
  matrix products  86.4 us (16%)
  other arithmetic  74.6 us (14%)
  local copies, waits for them, and re-layouts  39.1 us (7%)
  between operations  18.3 us (3%)
    ppermute x51, starting transfers between devices, around(): lax.ppermute(block, axis, [(i, (i + distance) % count) for i in range(cou...  72.7 us
    ppermute x4, waiting for transfers between devices, swap_section(): return lax.ppermute(block, 'section', [(0, 1), (1, 0)])  54.5 us
    ppermute x51, waiting for transfers between devices, around(): lax.ppermute(block, axis, [(i, (i + distance) % count) for i in range(cou...  45.1 us
    ppermute x14, starting transfers between devices, swap_core(): return lax.ppermute(block, 'core', [(0, 1), (1, 0)])  38.1 us
    ppermute x5, waiting for transfers between devices, swap_layer(): lax.ppermute(block, ('section', 'zlo'), [(0, 3), (1, 2), (2, 1), (3, 0)])  34.9 us
    all_to_all x2, waiting for transfers between devices, reduce_part_now(): pieces = lax.all_to_all(grads, ('zlo', 'x'), 0, 0, tiled=True)  31 us
    dot_general x16, matrix products, contract_rows(): lax.dot_general(left_rows, right_rows, (((0,), (0,)), ((), ())), preferre...  24.4 us
    dot_general x16, matrix products, contract_last(): lax.dot_general(left_rows, weight, (((1,), (1,)), ((), ())), preferred_el...  20.3 us
  transfers between devices with their start and end apart: 81, of which 25 were waited for; matrix products, arithmetic and copies ran while one was open for 33% of the time, Pallas kernels for 0%

profile of v6, /device:TPU:1, one launch (start us, length us, event | category | flops | bytes accessed | tf_op | source)
XLA Modules:
  0.0 527.0 jit_solution(3817513072395137384)
XLA Ops:
  8.5 3.8 collective-permute-start.4
  15.0 3.8 collective-permute-start.2
  34.1 2.7 collective-permute-start.30
  39.1 16.0 %collective-permute-done.3 = bf16[1536,256]{1,0:T(8,128)(2,1)S(1)} collective-permute-done((bf16[1536,256]{1,0:T(8,128)(2,1)}, bf16[1536,256]{1,0:T(8,128)(2,1)S(1)}, u32[]{:S(2)}, u32[]{:S(2)}) %collective-permute-start.3) | collective-permute-done | bytes 786464 | tf_op jit(solution)/shard_map/ppermute | solution.py:31
  55.7 3.4 collective-permute-start.5
  59.0 2.6 collective-permute-done.6
  61.6 4.4 collective-permute-start.7
  81.7 3.9 collective-permute-done.13
  90.2 12.5 %collective-permute-done.16 = bf16[328,1024]{1,0:T(8,128)(2,1)S(1)} collective-permute-done((bf16[328,1024]{1,0:T(8,128)(2,1)S(1)}, bf16[328,1024]{1,0:T(8,128)(2,1)S(1)}, u32[]{:S(2)}, u32[]{:S(2)}) %collective-permute-start.16) | collective-permute-done | bytes 671776 | tf_op jit(solution)/shard_map/ppermute | solution.py:31
  111.3 8.8 %collective-permute-done.12 = bf16[128,1024]{1,0:T(8,128)(2,1)S(1)} collective-permute-done((bf16[128,1024]{1,0:T(8,128)(2,1)S(1)}, bf16[128,1024]{1,0:T(8,128)(2,1)S(1)}, u32[]{:S(2)}, u32[]{:S(2)}) %collective-permute-start.12) | collective-permute-done | bytes 262176 | tf_op jit(solution)/shard_map/ppermute | solution.py:19
  121.8 3.0 multiply_convert_fusion.5
  125.8 2.7 collective-permute-start.21
  131.3 2.8 fusion.178
  135.1 4.2 collective-permute-done.19
  149.2 4.9 collective-permute-done.24
  165.2 7.1 %collective-permute-done.26 = bf16[128,1024]{1,0:T(8,128)(2,1)S(1)} collective-permute-done((bf16[128,1024]{1,0:T(8,128)(2,1)S(1)}, bf16[128,1024]{1,0:T(8,128)(2,1)S(1)}, u32[]{:S(2)}, u32[]{:S(2)}) %collective-permute-start.26) | collective-permute-done | bytes 262176 | tf_op jit(solution)/shard_map/ppermute | solution.py:19
  173.1 2.8 collective-permute-start.28
  176.5 2.8 fusion.179
  184.4 2.4 collective-permute-done.32
  198.6 2.7 collective-permute-done.35
  205.4 2.7 collective-permute-start.37
  210.9 12.7 %collective-permute-start.44 = (bf16[328,1024]{1,0:T(8,128)(2,1)}, bf16[328,1024]{1,0:T(8,128)(2,1)}, u32[]{:S(2)}, u32[]{:S(2)}) collective-permute-start(bf16[328,1024]{1,0:T(8,128)(2,1)} %convolution_convert_fusion.11), channel_id=1, source_target_pairs={{0,4},{4,0},{1,5},{5,1},{2,6},{6,2},{3,7},{7,3},{8,12},{12,8},{9,1... | collective-permute-start | bytes 2015240 | tf_op jit(solution)/shard_map/ppermute | solution.py:23
  230.0 3.6 fusion.25
  244.5 2.7 collective-permute-start.42
  248.0 3.1 collective-permute-start.43
  252.1 3.0 collective-permute-done.41
  261.6 2.6 collective-permute-start.47
  272.5 3.0 collective-permute-start.51
  285.2 3.7 collective-permute-start.48
  290.3 2.5 collective-permute-start.50
  296.5 4.6 collective-permute-done.49
  308.6 4.1 all-to-all-start
  315.1 14.1 %all-to-all-done = bf16[8,272,256]{2,1,0:T(8,128)(2,1)S(1)} async-done(((bf16[8,272,256]{2,1,0:T(8,128)(2,1)}), bf16[8,272,256]{2,1,0:T(8,128)(2,1)S(1)}, u32[]{:S(2)}, u32[]{:S(2)}) %all-to-all-start) | async-done | bytes 1114144 | tf_op jit(solution)/shard_map/all_to_all | solution.py:335
  330.1 3.7 collective-permute-start.55
  349.5 3.5 fusion.28
  362.1 2.7 collective-permute-start.58
  369.0 2.5 collective-permute-start.60
  391.5 4.4 all-to-all-start.1
  402.2 16.9 %all-to-all-done.1 = bf16[8,272,256]{2,1,0:T(8,128)(2,1)} async-done(((bf16[8,272,256]{2,1,0:T(8,128)(2,1)}), bf16[8,272,256]{2,1,0:T(8,128)(2,1)}, u32[]{:S(2)}, u32[]{:S(2)}) %all-to-all-start.1) | async-done | bytes 1114144 | tf_op jit(solution)/shard_map/all_to_all | solution.py:335
  420.5 2.5 collective-permute-start.61
  425.0 7.5 %collective-permute-done.61 = bf16[272,256]{1,0:T(8,128)(2,1)S(1)} collective-permute-done((bf16[272,256]{1,0:T(8,128)(2,1)S(1)}, bf16[272,256]{1,0:T(8,128)(2,1)S(1)}, u32[]{:S(2)}, u32[]{:S(2)}) %collective-permute-start.61) | collective-permute-done | bytes 139296 | tf_op jit(solution)/shard_map/ppermute | solution.py:27
  433.6 3.6 all-to-all-start.2
  439.6 16.0 %collective-permute-done.73 = bf16[128,1024]{1,0:T(8,128)(2,1)S(1)} collective-permute-done((bf16[128,1024]{1,0:T(8,128)(2,1)S(1)}, bf16[128,1024]{1,0:T(8,128)(2,1)S(1)}, u32[]{:S(2)}, u32[]{:S(2)}) %collective-permute-start.73) | collective-permute-done | bytes 262176 | tf_op jit(solution)/shard_map/ppermute | solution.py:27
  458.4 5.8 %all-to-all-start.3 = ((bf16[8,128,1024]{2,1,0:T(8,128)(2,1)}), bf16[8,128,1024]{2,1,0:T(8,128)(2,1)S(1)}, u32[]{:S(2)}, u32[]{:S(2)}) async-start(bf16[8,128,1024]{2,1,0:T(8,128)(2,1)} %broadcast_in_dim.226), calls=%async_computation.5 | async-start | bytes 4194304 | tf_op jit(solution)/shard_map/all_to_all | solution.py:342
  468.8 26.3 %collective-permute-done.66 = bf16[128,1024]{1,0:T(8,128)(2,1)S(1)} collective-permute-done((bf16[128,1024]{1,0:T(8,128)(2,1)S(1)}, bf16[128,1024]{1,0:T(8,128)(2,1)S(1)}, u32[]{:S(2)}, u32[]{:S(2)}) %collective-permute-start.66) | collective-permute-done | bytes 262176 | tf_op jit(solution)/shard_map/ppermute | solution.py:27
  495.9 4.7 collective-permute-done.65
  505.0 2.7 collective-permute-start.70
  517.0 2.7 convert_bitcast_fusion
  (812 shorter events, 243.5 us)
Async XLA Ops:
  7.2 322.9 %reduce-scatter.3.cloned.1.call-start = ((), (), s32[]{:S(2)}) async-start(), calls=%async_computation.6 | async-start | bytes 2359296 | tf_op jit(solution)/shard_map/reduce_scatter | solution.py:331
  8.5 30.4 %collective-permute-start.4 = (bf16[128,1024]{1,0:T(8,128)(2,1)S(1)}, bf16[128,1024]{1,0:T(8,128)(2,1)S(1)}, u32[]{:S(2)}, u32[]{:S(2)}) collective-permute-start(bf16[128,1024]{1,0:T(8,128)(2,1)S(1)} %get-tuple-element.158), channel_id=1, source_target_pairs={{0,2},{1,3},{2,0},{3,1},{4,6},{5,7},{6,4},{7,5},{8,10},{9,11},{10,... | collective-permute-start | bytes 786440 | tf_op jit(solution)/shard_map/ppermute | solution.py:19
  12.4 24.5 %collective-permute-start.1 = (bf16[128,1024]{1,0:T(8,128)(2,1)S(1)}, bf16[128,1024]{1,0:T(8,128)(2,1)}, u32[]{:S(2)}, u32[]{:S(2)}) collective-permute-start(bf16[128,1024]{1,0:T(8,128)(2,1)S(1)} %get-tuple-element.158), channel_id=1, source_target_pairs={{0,1},{1,2},{2,3},{3,0},{4,5},{5,6},{6,7},{7,4},{8,9},{9,10},{10,1... | collective-permute-start | bytes 786440 | tf_op jit(solution)/shard_map/ppermute | solution.py:19
  12.8 24.2 %collective-permute-start = (bf16[128,1024]{1,0:T(8,128)(2,1)S(1)}, bf16[128,1024]{1,0:T(8,128)(2,1)}, u32[]{:S(2)}, u32[]{:S(2)}) collective-permute-start(bf16[128,1024]{1,0:T(8,128)(2,1)S(1)} %get-tuple-element.158), channel_id=1, source_target_pairs={{0,3},{1,0},{2,1},{3,2},{4,7},{5,4},{6,5},{7,6},{8,11},{9,8},{10,9... | collective-permute-start | bytes 786440 | tf_op jit(solution)/shard_map/ppermute | solution.py:19
  15.0 19.1 %collective-permute-start.2 = (f32[2,1024]{1,0:T(2,128)}, f32[2,1024]{1,0:T(2,128)S(1)}, u32[]{:S(2)}, u32[]{:S(2)}) collective-permute-start(f32[2,1024]{1,0:T(2,128)} %bitcast.342), channel_id=1, source_target_pairs={{0,96},{32,64},{64,32},{96,0},{1,97},{33,65},{65,33},{97,1},{2,98}... | collective-permute-start | bytes 24584 | tf_op jit(solution)/shard_map/ppermute | solution.py:31
  20.5 45.7 %collective-permute-start.31 = (bf16[128,1024]{1,0:T(8,128)(2,1)}, bf16[128,1024]{1,0:T(8,128)(2,1)}, u32[]{:S(2)}, u32[]{:S(2)}) collective-permute-start(bf16[128,1024]{1,0:T(8,128)(2,1)} %select_bitcast_fusion.4), channel_id=1, source_target_pairs={{0,1},{1,2},{2,3},{3,0},{4,5},{5,6},{6,7},{7,4},{8,9},{9,10},{10,1... | collective-permute-start | bytes 786440 | tf_op jit(solution)/shard_map/ppermute | solution.py:19
  34.1 32.1 %collective-permute-start.30 = (bf16[128,1024]{1,0:T(8,128)(2,1)}, bf16[128,1024]{1,0:T(8,128)(2,1)S(1)}, u32[]{:S(2)}, u32[]{:S(2)}) collective-permute-start(bf16[128,1024]{1,0:T(8,128)(2,1)} %select_bitcast_fusion.4), channel_id=1, source_target_pairs={{0,3},{1,0},{2,1},{3,2},{4,7},{5,4},{6,5},{7,6},{8,11},{9,8},{10,9... | collective-permute-start | bytes 786440 | tf_op jit(solution)/shard_map/ppermute | solution.py:19
  36.9 18.2 %collective-permute-start.3 = (bf16[1536,256]{1,0:T(8,128)(2,1)}, bf16[1536,256]{1,0:T(8,128)(2,1)S(1)}, u32[]{:S(2)}, u32[]{:S(2)}) collective-permute-start(bf16[1536,256]{1,0:T(8,128)(2,1)} %constant_dynamic-slice_fusion.3), channel_id=1, source_target_pairs={{0,96},{32,64},{64,32},{96,0},{1,97},{33,65},{65,33},{97,1},{2,98}... | collective-permute-start | bytes 2359304 | tf_op jit(solution)/shard_map/ppermute | solution.py:31
  55.7 12.7 %collective-permute-start.5 = (bf16[1536,256]{1,0:T(8,128)(2,1)S(1)}, bf16[1536,256]{1,0:T(8,128)(2,1)S(1)}, u32[]{:S(2)}, u32[]{:S(2)}) collective-permute-start(bf16[1536,256]{1,0:T(8,128)(2,1)S(1)} %collective-permute-done.3), channel_id=1, source_target_pairs={{0,4},{4,0},{1,5},{5,1},{2,6},{6,2},{3,7},{7,3},{8,12},{12,8},{9,1... | collective-permute-start | bytes 2359304 | tf_op jit(solution)/shard_map/ppermute | solution.py:23
  67.5 18.0 %collective-permute-start.13 = (bf16[328,1024]{1,0:T(8,128)(2,1)S(1)}, bf16[328,1024]{1,0:T(8,128)(2,1)S(1)}, u32[]{:S(2)}, u32[]{:S(2)}) collective-permute-start(bf16[328,1024]{1,0:T(8,128)(2,1)S(1)} %constant_dynamic-slice_fusion), channel_id=1, source_target_pairs={{0,96},{32,64},{64,32},{96,0},{1,97},{33,65},{65,33},{97,1},{2,98}... | collective-permute-start | bytes 2015240 | tf_op jit(solution)/shard_map/ppermute | solution.py:31
  74.2 12.9 %collective-permute-start.8 = (bf16[128,1024]{1,0:T(8,128)(2,1)S(1)}, bf16[128,1024]{1,0:T(8,128)(2,1)S(1)}, u32[]{:S(2)}, u32[]{:S(2)}) collective-permute-start(bf16[128,1024]{1,0:T(8,128)(2,1)S(1)} %convolution_convert_fusion.21), channel_id=1, source_target_pairs={{0,2},{1,3},{2,0},{3,1},{4,6},{5,7},{6,4},{7,5},{8,10},{9,11},{10,... | collective-permute-start | bytes 786440 | tf_op jit(solution)/shard_map/ppermute | solution.py:19
  85.6 17.1 %collective-permute-start.16 = (bf16[328,1024]{1,0:T(8,128)(2,1)S(1)}, bf16[328,1024]{1,0:T(8,128)(2,1)S(1)}, u32[]{:S(2)}, u32[]{:S(2)}) collective-permute-start(bf16[328,1024]{1,0:T(8,128)(2,1)S(1)} %constant_dynamic-slice_fusion.2), channel_id=1, source_target_pairs={{0,96},{32,64},{64,32},{96,0},{1,97},{33,65},{65,33},{97,1},{2,98}... | collective-permute-start | bytes 2015240 | tf_op jit(solution)/shard_map/ppermute | solution.py:31
  85.7 17.0 %collective-permute-start.14 = (bf16[328,1024]{1,0:T(8,128)(2,1)S(1)}, bf16[328,1024]{1,0:T(8,128)(2,1)S(1)}, u32[]{:S(2)}, u32[]{:S(2)}) collective-permute-start(bf16[328,1024]{1,0:T(8,128)(2,1)S(1)} %collective-permute-done.13), channel_id=1, source_target_pairs={{0,8},{8,0},{16,24},{24,16},{1,9},{9,1},{17,25},{25,17},{2,10},{10... | collective-permute-start | bytes 2015240 | tf_op jit(solution)/shard_map/ppermute | solution.py:307
  87.1 103.4 %collective-permute-start.33 = (bf16[128,1024]{1,0:T(8,128)(2,1)}, bf16[128,1024]{1,0:T(8,128)(2,1)S(1)}, u32[]{:S(2)}, u32[]{:S(2)}) collective-permute-start(bf16[128,1024]{1,0:T(8,128)(2,1)} %select_bitcast_fusion.4), channel_id=1, source_target_pairs={{0,2},{1,3},{2,0},{3,1},{4,6},{5,7},{6,4},{7,5},{8,10},{9,11},{10,... | collective-permute-start | bytes 786440 | tf_op jit(solution)/shard_map/ppermute | solution.py:19
  105.1 20.5 %collective-permute-start.18 = (bf16[128,1024]{1,0:T(8,128)(2,1)S(1)}, bf16[128,1024]{1,0:T(8,128)(2,1)S(1)}, u32[]{:S(2)}, u32[]{:S(2)}) collective-permute-start(bf16[128,1024]{1,0:T(8,128)(2,1)S(1)} %multiply_convert_fusion.7), channel_id=1, source_target_pairs={{0,2},{1,3},{2,0},{3,1},{4,6},{5,7},{6,4},{7,5},{8,10},{9,11},{10,... | collective-permute-start | bytes 786440 | tf_op jit(solution)/shard_map/ppermute | solution.py:19
  105.2 14.9 %collective-permute-start.12 = (bf16[128,1024]{1,0:T(8,128)(2,1)S(1)}, bf16[128,1024]{1,0:T(8,128)(2,1)S(1)}, u32[]{:S(2)}, u32[]{:S(2)}) collective-permute-start(bf16[128,1024]{1,0:T(8,128)(2,1)S(1)} %multiply_convert_fusion.7), channel_id=1, source_target_pairs={{0,1},{1,2},{2,3},{3,0},{4,5},{5,6},{6,7},{7,4},{8,9},{9,10},{10,1... | collective-permute-start | bytes 786440 | tf_op jit(solution)/shard_map/ppermute | solution.py:19
  106.4 13.7 %collective-permute-start.11 = (bf16[128,1024]{1,0:T(8,128)(2,1)S(1)}, bf16[128,1024]{1,0:T(8,128)(2,1)S(1)}, u32[]{:S(2)}, u32[]{:S(2)}) collective-permute-start(bf16[128,1024]{1,0:T(8,128)(2,1)S(1)} %multiply_convert_fusion.7), channel_id=1, source_target_pairs={{0,3},{1,0},{2,1},{3,2},{4,7},{5,4},{6,5},{7,6},{8,11},{9,8},{10,9... | collective-permute-start | bytes 786440 | tf_op jit(solution)/shard_map/ppermute | solution.py:19
  203.0 22.5 %collective-permute-start.39 = (bf16[128,1024]{1,0:T(8,128)(2,1)S(1)}, bf16[128,1024]{1,0:T(8,128)(2,1)S(1)}, u32[]{:S(2)}, u32[]{:S(2)}) collective-permute-start(bf16[128,1024]{1,0:T(8,128)(2,1)S(1)} %get-tuple-element.165), channel_id=1, source_target_pairs={{0,2},{1,3},{2,0},{3,1},{4,6},{5,7},{6,4},{7,5},{8,10},{9,11},{10,... | collective-permute-start | bytes 786440 | tf_op jit(solution)/shard_map/ppermute | solution.py:19
  205.4 18.4 %collective-permute-start.38 = (bf16[128,1024]{1,0:T(8,128)(2,1)S(1)}, bf16[128,1024]{1,0:T(8,128)(2,1)S(1)}, u32[]{:S(2)}, u32[]{:S(2)}) collective-permute-start(bf16[128,1024]{1,0:T(8,128)(2,1)S(1)} %get-tuple-element.165), channel_id=1, source_target_pairs={{0,1},{1,2},{2,3},{3,0},{4,5},{5,6},{6,7},{7,4},{8,9},{9,10},{10,1... | collective-permute-start | bytes 786440 | tf_op jit(solution)/shard_map/ppermute | solution.py:19
  205.4 18.4 %collective-permute-start.37 = (bf16[128,1024]{1,0:T(8,128)(2,1)S(1)}, bf16[128,1024]{1,0:T(8,128)(2,1)S(1)}, u32[]{:S(2)}, u32[]{:S(2)}) collective-permute-start(bf16[128,1024]{1,0:T(8,128)(2,1)S(1)} %get-tuple-element.165), channel_id=1, source_target_pairs={{0,3},{1,0},{2,1},{3,2},{4,7},{5,4},{6,5},{7,6},{8,11},{9,8},{10,9... | collective-permute-start | bytes 786440 | tf_op jit(solution)/shard_map/ppermute | solution.py:19
  210.9 46.4 %collective-permute-start.44 = (bf16[328,1024]{1,0:T(8,128)(2,1)}, bf16[328,1024]{1,0:T(8,128)(2,1)}, u32[]{:S(2)}, u32[]{:S(2)}) collective-permute-start(bf16[328,1024]{1,0:T(8,128)(2,1)} %convolution_convert_fusion.11), channel_id=1, source_target_pairs={{0,4},{4,0},{1,5},{5,1},{2,6},{6,2},{3,7},{7,3},{8,12},{12,8},{9,1... | collective-permute-start | bytes 2015240 | tf_op jit(solution)/shard_map/ppermute | solution.py:23
  261.6 20.5 %collective-permute-start.47 = (bf16[128,1024]{1,0:T(8,128)(2,1)}, bf16[128,1024]{1,0:T(8,128)(2,1)}, u32[]{:S(2)}, u32[]{:S(2)}) collective-permute-start(bf16[128,1024]{1,0:T(8,128)(2,1)} %add_convert_fusion.9), channel_id=1, source_target_pairs={{0,2},{1,3},{2,0},{3,1},{4,6},{5,7},{6,4},{7,5},{8,10},{9,11},{10,... | collective-permute-start | bytes 786440 | tf_op jit(solution)/shard_map/ppermute | solution.py:19
  264.2 12.6 %collective-permute-start.46 = (bf16[128,1024]{1,0:T(8,128)(2,1)}, bf16[128,1024]{1,0:T(8,128)(2,1)}, u32[]{:S(2)}, u32[]{:S(2)}) collective-permute-start(bf16[128,1024]{1,0:T(8,128)(2,1)} %add_convert_fusion.9), channel_id=1, source_target_pairs={{0,1},{1,2},{2,3},{3,0},{4,5},{5,6},{6,7},{7,4},{8,9},{9,10},{10,1... | collective-permute-start | bytes 786440 | tf_op jit(solution)/shard_map/ppermute | solution.py:19
  272.5 31.1 %collective-permute-start.51 = (bf16[1024,256]{1,0:T(8,128)(2,1)}, bf16[1024,256]{1,0:T(8,128)(2,1)}, u32[]{:S(2)}, u32[]{:S(2)}) collective-permute-start(bf16[1024,256]{1,0:T(8,128)(2,1)} %convolution_convert_fusion.15), channel_id=1, source_target_pairs={{0,4},{4,0},{1,5},{5,1},{2,6},{6,2},{3,7},{7,3},{8,12},{12,8},{9,1... | collective-permute-start | bytes 1572872 | tf_op jit(solution)/shard_map/ppermute | solution.py:23
  294.2 11.3 %collective-permute-start.52 = (bf16[1024,256]{1,0:T(8,128)(2,1)}, bf16[1024,256]{1,0:T(8,128)(2,1)}, u32[]{:S(2)}, u32[]{:S(2)}) collective-permute-start(bf16[1024,256]{1,0:T(8,128)(2,1)} %convolution_convert_fusion.14), channel_id=1, source_target_pairs={{0,4},{4,0},{1,5},{5,1},{2,6},{6,2},{3,7},{7,3},{8,12},{12,8},{9,1... | collective-permute-start | bytes 1572872 | tf_op jit(solution)/shard_map/ppermute | solution.py:23
  308.6 20.6 %all-to-all-start = ((bf16[8,272,256]{2,1,0:T(8,128)(2,1)}), bf16[8,272,256]{2,1,0:T(8,128)(2,1)S(1)}, u32[]{:S(2)}, u32[]{:S(2)}) async-start(bf16[8,272,256]{2,1,0:T(8,128)(2,1)} %bitcast.67), calls=%async_computation.1 | async-start | bytes 2228224 | tf_op jit(solution)/shard_map/all_to_all | solution.py:335
  312.7 124.5 %reduce-scatter.5.cloned.1.call-start = ((), (), s32[]{:S(2)}) async-start(), calls=%async_computation.7 | async-start | bytes 2359296 | tf_op jit(solution)/shard_map/reduce_scatter | solution.py:331
  330.1 17.7 %collective-permute-start.55 = (bf16[128,1024]{1,0:T(8,128)(2,1)S(1)}, bf16[128,1024]{1,0:T(8,128)(2,1)S(1)}, u32[]{:S(2)}, u32[]{:S(2)}) collective-permute-start(bf16[128,1024]{1,0:T(8,128)(2,1)S(1)} %convert_element_type.627), channel_id=1, source_target_pairs={{0,2},{1,3},{2,0},{3,1},{4,6},{5,7},{6,4},{7,5},{8,10},{9,11},{10,... | collective-permute-start | bytes 786440 | tf_op jit(solution)/shard_map/ppermute | solution.py:19
  333.9 12.4 %collective-permute-start.54 = (bf16[128,1024]{1,0:T(8,128)(2,1)S(1)}, bf16[128,1024]{1,0:T(8,128)(2,1)S(1)}, u32[]{:S(2)}, u32[]{:S(2)}) collective-permute-start(bf16[128,1024]{1,0:T(8,128)(2,1)S(1)} %convert_element_type.627), channel_id=1, source_target_pairs={{0,1},{1,2},{2,3},{3,0},{4,5},{5,6},{6,7},{7,4},{8,9},{9,10},{10,1... | collective-permute-start | bytes 786440 | tf_op jit(solution)/shard_map/ppermute | solution.py:19
  334.2 12.1 %collective-permute-start.53 = (bf16[128,1024]{1,0:T(8,128)(2,1)S(1)}, bf16[128,1024]{1,0:T(8,128)(2,1)S(1)}, u32[]{:S(2)}, u32[]{:S(2)}) collective-permute-start(bf16[128,1024]{1,0:T(8,128)(2,1)S(1)} %convert_element_type.627), channel_id=1, source_target_pairs={{0,3},{1,0},{2,1},{3,2},{4,7},{5,4},{6,5},{7,6},{8,11},{9,8},{10,9... | collective-permute-start | bytes 786440 | tf_op jit(solution)/shard_map/ppermute | solution.py:19
  341.3 33.1 %collective-permute-start.72 = (bf16[328,1024]{1,0:T(8,128)(2,1)}, bf16[328,1024]{1,0:T(8,128)(2,1)}, u32[]{:S(2)}, u32[]{:S(2)}) collective-permute-start(bf16[328,1024]{1,0:T(8,128)(2,1)} %convolution_convert_fusion.10), channel_id=1, source_target_pairs={{0,4},{4,0},{1,5},{5,1},{2,6},{6,2},{3,7},{7,3},{8,12},{12,8},{9,1... | collective-permute-start | bytes 2015240 | tf_op jit(solution)/shard_map/ppermute | solution.py:23
  345.4 33.0 %collective-permute-start.71 = (bf16[656,1024]{1,0:T(8,128)(2,1)}, bf16[656,1024]{1,0:T(8,128)(2,1)}, u32[]{:S(2)}, u32[]{:S(2)}) collective-permute-start(bf16[656,1024]{1,0:T(8,128)(2,1)} %convolution_convert_fusion), channel_id=1, source_target_pairs={{0,4},{4,0},{1,5},{5,1},{2,6},{6,2},{3,7},{7,3},{8,12},{12,8},{9,1... | collective-permute-start | bytes 4030472 | tf_op jit(solution)/shard_map/ppermute | solution.py:23
  362.1 20.8 %collective-permute-start.58 = (bf16[128,1024]{1,0:T(8,128)(2,1)}, bf16[128,1024]{1,0:T(8,128)(2,1)}, u32[]{:S(2)}, u32[]{:S(2)}) collective-permute-start(bf16[128,1024]{1,0:T(8,128)(2,1)} %get-tuple-element.326), channel_id=1, source_target_pairs={{0,2},{1,3},{2,0},{3,1},{4,6},{5,7},{6,4},{7,5},{8,10},{9,11},{10,... | collective-permute-start | bytes 786440 | tf_op jit(solution)/shard_map/ppermute | solution.py:19
  368.5 14.4 %collective-permute-start.59 = (bf16[128,1024]{1,0:T(8,128)(2,1)}, bf16[128,1024]{1,0:T(8,128)(2,1)}, u32[]{:S(2)}, u32[]{:S(2)}) collective-permute-start(bf16[128,1024]{1,0:T(8,128)(2,1)} %get-tuple-element.229), channel_id=1, source_target_pairs={{0,1},{1,2},{2,3},{3,0},{4,5},{5,6},{6,7},{7,4},{8,9},{9,10},{10,1... | collective-permute-start | bytes 786440 | tf_op jit(solution)/shard_map/ppermute | solution.py:19
  369.0 14.0 %collective-permute-start.60 = (bf16[128,1024]{1,0:T(8,128)(2,1)}, bf16[128,1024]{1,0:T(8,128)(2,1)}, u32[]{:S(2)}, u32[]{:S(2)}) collective-permute-start(bf16[128,1024]{1,0:T(8,128)(2,1)} %get-tuple-element.230), channel_id=1, source_target_pairs={{0,3},{1,0},{2,1},{3,2},{4,7},{5,4},{6,5},{7,6},{8,11},{9,8},{10,9... | collective-permute-start | bytes 786440 | tf_op jit(solution)/shard_map/ppermute | solution.py:19
  374.5 12.5 %collective-permute-start.56 = (bf16[1024,256]{1,0:T(8,128)(2,1)}, bf16[1024,256]{1,0:T(8,128)(2,1)}, u32[]{:S(2)}, u32[]{:S(2)}) collective-permute-start(bf16[1024,256]{1,0:T(8,128)(2,1)} %convolution_convert_fusion.13), channel_id=1, source_target_pairs={{0,4},{4,0},{1,5},{5,1},{2,6},{6,2},{3,7},{7,3},{8,12},{12,8},{9,1... | collective-permute-start | bytes 1572872 | tf_op jit(solution)/shard_map/ppermute | solution.py:23
  391.5 27.6 %all-to-all-start.1 = ((bf16[8,272,256]{2,1,0:T(8,128)(2,1)}), bf16[8,272,256]{2,1,0:T(8,128)(2,1)}, u32[]{:S(2)}, u32[]{:S(2)}) async-start(bf16[8,272,256]{2,1,0:T(8,128)(2,1)} %bitcast.281), calls=%async_computation.2 | async-start | bytes 2228224 | tf_op jit(solution)/shard_map/all_to_all | solution.py:335
  398.0 25.1 %collective-permute-start.62 = (bf16[128,1024]{1,0:T(8,128)(2,1)}, bf16[128,1024]{1,0:T(8,128)(2,1)}, u32[]{:S(2)}, u32[]{:S(2)}) collective-permute-start(bf16[128,1024]{1,0:T(8,128)(2,1)} %convolution_convert_fusion.16), channel_id=1, source_target_pairs={{0,2},{1,3},{2,0},{3,1},{4,6},{5,7},{6,4},{7,5},{8,10},{9,11},{10,... | collective-permute-start | bytes 786440 | tf_op jit(solution)/shard_map/ppermute | solution.py:19
  399.4 23.7 %collective-permute-start.63 = (bf16[128,1024]{1,0:T(8,128)(2,1)S(1)}, bf16[128,1024]{1,0:T(8,128)(2,1)S(1)}, u32[]{:S(2)}, u32[]{:S(2)}) collective-permute-start(bf16[128,1024]{1,0:T(8,128)(2,1)S(1)} %get-tuple-element.227), channel_id=1, source_target_pairs={{0,1},{1,2},{2,3},{3,0},{4,5},{5,6},{6,7},{7,4},{8,9},{9,10},{10,1... | collective-permute-start | bytes 786440 | tf_op jit(solution)/shard_map/ppermute | solution.py:19
  400.0 23.0 %collective-permute-start.64 = (bf16[128,1024]{1,0:T(8,128)(2,1)S(1)}, bf16[128,1024]{1,0:T(8,128)(2,1)S(1)}, u32[]{:S(2)}, u32[]{:S(2)}) collective-permute-start(bf16[128,1024]{1,0:T(8,128)(2,1)S(1)} %get-tuple-element.228), channel_id=1, source_target_pairs={{0,3},{1,0},{2,1},{3,2},{4,7},{5,4},{6,5},{7,6},{8,11},{9,8},{10,9... | collective-permute-start | bytes 786440 | tf_op jit(solution)/shard_map/ppermute | solution.py:19
  420.5 12.0 %collective-permute-start.61 = (bf16[272,256]{1,0:T(8,128)(2,1)S(1)}, bf16[272,256]{1,0:T(8,128)(2,1)S(1)}, u32[]{:S(2)}, u32[]{:S(2)}) collective-permute-start(bf16[272,256]{1,0:T(8,128)(2,1)S(1)} %broadcast_select_fusion.27), channel_id=1, source_target_pairs={{0,64},{64,0},{1,65},{65,1},{2,66},{66,2},{3,67},{67,3},{4,68},{68... | collective-permute-start | bytes 417800 | tf_op jit(solution)/shard_map/ppermute | solution.py:27
  433.6 23.1 %all-to-all-start.2 = ((bf16[8,272,256]{2,1,0:T(8,128)(2,1)}), bf16[8,272,256]{2,1,0:T(8,128)(2,1)S(1)}, u32[]{:S(2)}, u32[]{:S(2)}) async-start(bf16[8,272,256]{2,1,0:T(8,128)(2,1)} %broadcast_in_dim.221), calls=%async_computation.3 | async-start | bytes 2228224 | tf_op jit(solution)/shard_map/all_to_all | solution.py:342
  437.3 18.4 %collective-permute-start.73 = (bf16[128,1024]{1,0:T(8,128)(2,1)S(1)}, bf16[128,1024]{1,0:T(8,128)(2,1)S(1)}, u32[]{:S(2)}, u32[]{:S(2)}) collective-permute-start(bf16[128,1024]{1,0:T(8,128)(2,1)S(1)} %broadcast_select_fusion.24), channel_id=1, source_target_pairs={{0,64},{64,0},{1,65},{65,1},{2,66},{66,2},{3,67},{67,3},{4,68},{68... | collective-permute-start | bytes 786440 | tf_op jit(solution)/shard_map/ppermute | solution.py:27
  458.4 42.3 %all-to-all-start.3 = ((bf16[8,128,1024]{2,1,0:T(8,128)(2,1)}), bf16[8,128,1024]{2,1,0:T(8,128)(2,1)S(1)}, u32[]{:S(2)}, u32[]{:S(2)}) async-start(bf16[8,128,1024]{2,1,0:T(8,128)(2,1)} %broadcast_in_dim.226), calls=%async_computation.5 | async-start | bytes 4194304 | tf_op jit(solution)/shard_map/all_to_all | solution.py:342
  464.3 38.9 %collective-permute-start.67 = (bf16[2176,256]{1,0:T(8,128)(2,1)}, bf16[2176,256]{1,0:T(8,128)(2,1)}, u32[]{:S(2)}, u32[]{:S(2)}) collective-permute-start(bf16[2176,256]{1,0:T(8,128)(2,1)} %bitcast.282), channel_id=1, source_target_pairs={{0,4},{4,0},{1,5},{5,1},{2,6},{6,2},{3,7},{7,3},{8,12},{12,8},{9,1... | collective-permute-start | bytes 3342344 | tf_op jit(solution)/shard_map/ppermute | solution.py:23
  465.6 29.5 %collective-permute-start.66 = (bf16[128,1024]{1,0:T(8,128)(2,1)S(1)}, bf16[128,1024]{1,0:T(8,128)(2,1)S(1)}, u32[]{:S(2)}, u32[]{:S(2)}) collective-permute-start(bf16[128,1024]{1,0:T(8,128)(2,1)S(1)} %broadcast_select_fusion.25), channel_id=1, source_target_pairs={{0,64},{64,0},{1,65},{65,1},{2,66},{66,2},{3,67},{67,3},{4,68},{68... | collective-permute-start | bytes 786440 | tf_op jit(solution)/shard_map/ppermute | solution.py:27
  467.6 33.0 %collective-permute-start.65 = (bf16[128,1024]{1,0:T(8,128)(2,1)S(1)}, bf16[128,1024]{1,0:T(8,128)(2,1)S(1)}, u32[]{:S(2)}, u32[]{:S(2)}) collective-permute-start(bf16[128,1024]{1,0:T(8,128)(2,1)S(1)} %broadcast_select_fusion.26), channel_id=1, source_target_pairs={{0,64},{64,0},{1,65},{65,1},{2,66},{66,2},{3,67},{67,3},{4,68},{68... | collective-permute-start | bytes 786440 | tf_op jit(solution)/shard_map/ppermute | solution.py:27
  500.7 12.2 %collective-permute-start.74 = (bf16[1024,1024]{1,0:T(8,128)(2,1)S(1)}, bf16[1024,1024]{1,0:T(8,128)(2,1)}, u32[]{:S(2)}, u32[]{:S(2)}) collective-permute-start(bf16[1024,1024]{1,0:T(8,128)(2,1)S(1)} %bitcast.280), channel_id=1, source_target_pairs={{0,4},{4,0},{1,5},{5,1},{2,6},{6,2},{3,7},{7,3},{8,12},{12,8},{9,1... | collective-permute-start | bytes 6291464 | tf_op jit(solution)/shard_map/ppermute | solution.py:23
  (227 other events, 2205.5 us)
Sparse Core Ops, SparseCore 0:
  268.9 37.3 reduce-scatter.2
  383.0 46.0 reduce-scatter.4

commit v7 on v6

--- a/solution.py
+++ b/solution.py
@@ -132,9 +132,9 @@
 
 
 def forward_layer(inputs, normed_parts, gain_mid, weights, allowed, tables, late, points):
-    w_qkv, w_out = weights[0], weights[1]
+    w_qkv = weights[0]
     row_count = inputs.shape[0]
-    local_width = w_out.shape[0]
+    local_width = w_qkv.shape[1] // 3
     spans = (slice(0, 3 * row_count), slice(3 * row_count, 4 * row_count))
 
     def project(k, part):
@@ -150,6 +150,8 @@
     queries = (near[0], far[0])
     keys_all = joined([near[1], far[1]])
     values_all = joined([near[2], far[2]])
+    points[0](values_all)
+    w_out = weights[1]
 
     def attend(k, own_queries):
         scores = masked_scores(own_queries, keys_all, allowed[spans[k]])
@@ -162,11 +164,13 @@
         return largest + jnp.log(totals), mixed, times(mixed, w_out).astype(bf16)
 
     far_logs, far_mixed, far_term = attend(1, queries[1])
+    points[1](far_term)
     near_logs, near_mixed, near_term = attend(0, after_all(queries[0], far_term))
     resid_mid = inputs + scatter_parts(near_term, far_term)
-    points(near_mixed, resid_mid)
+    points[2](resid_mid)
+    mid_parts = gather_parts(layer_norm(resid_mid, gain_mid).astype(bf16))
+    points[3](mid_parts)
     w_up, w_down = weights[2], weights[3]
-    mid_parts = gather_parts(layer_norm(resid_mid, gain_mid).astype(bf16))
 
     def feed(k, part):
         hidden = contract_last(part, w_up)
@@ -235,13 +239,13 @@
     return (grad_result + grad_resid, weight_grads, grad_gain)
 
 
-def backward_attn(grad_mid, kept, gain_first, weights, allowed, tables):
+def backward_attn(grad_mid, kept, gain_first, weights, allowed, tables, gate):
     w_qkv, w_out = weights[0], weights[1]
     queries, keys_rot, values_in = kept["queries"], kept["keys"], kept["values"]
     row_count = grad_mid.shape[0]
     grad_parts = gather_parts(grad_mid.astype(bf16))
     near, far = in_turn(lambda k, part: contract_last(part, w_out).astype(bf16), grad_parts)
-    grad_attended = joined([near, far]).reshape(queries.shape)
+    grad_attended = after_all(joined([near, far]).reshape(queries.shape), gate)
     scores = masked_scores(queries, keys_rot, allowed)
     soft_exact = jnp.exp(scores - kept["log_totals"])
     soft_weights = soft_exact.astype(bf16)
@@ -294,24 +298,19 @@
     return (grad_mid + grad_resid, weight_grads, grad_gain, gain_before)
 
 
-def other_layer(own, after, pair_x, before_x, before_core):
-    core_index = lax.axis_index("core")
-    parity = lax.axis_index("x") % 2
-    own = after_all(own, after)
-    rows = own.shape[0]
-    if pair_x:
-        piece = rows // 4
-        sent = lax.dynamic_slice_in_dim(own, (core_index * 2 + parity) * piece, piece)
-        got = swap_layer(sent)
-        kept = after_all(got, before_x)
-        beside = lax.ppermute(kept, "x", [(0, 1), (1, 0), (2, 3), (3, 2)])
-        half = in_order(parity, kept, beside)
-    else:
-        piece = rows // 2
-        sent = lax.dynamic_slice_in_dim(own, core_index * piece, piece)
-        got = half = swap_layer(sent)
-    half = after_all(half, before_core)
-    return in_order(core_index, half, swap_core(half)), got
+def fetch_half(own, after):
+    piece = own.shape[0] // 2
+    start = lax.axis_index("core") * piece
+    return swap_layer(lax.dynamic_slice_in_dim(after_all(own, after), start, piece))
+
+
+def both_halves(half, after=()):
+    half = after_all(half, after)
+    return in_order(lax.axis_index("core"), half, swap_core(half))
+
+
+def by_layer(is_first, own, other):
+    return jnp.where(is_first, own, other), jnp.where(is_first, other, own)
 
 
 def in_order(index, mine, other):
@@ -362,9 +361,6 @@
     gains_other = swap_layer(gains[0])
     gains0 = jnp.where(is_first, gains[0], gains_other)
     gains1 = jnp.where(is_first, gains_other, gains[0])
-    first_parts = in_turn(
-        lambda k, part: layer_norm(part.astype(f32), gains0[0]).astype(bf16), start_parts
-    )
     start_rows = start_rows.astype(f32)
     own = (
         jnp.transpose(w_qkv[0], (1, 0, 2)).reshape(-1, w_qkv.shape[3]),
@@ -372,18 +368,39 @@
         jnp.transpose(w_up[0], (1, 2, 0)).reshape(-1, w_up.shape[1]),
         w_down[0],
     )
-    other_qkv, after = other_layer(own[0], (), False, (), start_parts)
-    other_out, after_out = other_layer(own[1], after, False, (), ())
-    layer0 = [jnp.where(is_first, own[0], other_qkv), jnp.where(is_first, own[1], other_out)]
-    layer1 = [jnp.where(is_first, other_qkv, own[0]), jnp.where(is_first, other_out, own[1])]
-    layer0[0] = joined(jnp.split(layer0[0], 3), 1)
-    layer1[0] = joined(jnp.split(layer1[0], 3), 1)
-
-    def feed_weights(attended, resid_mid):
-        other_up, after = other_layer(own[2], after_out, True, attended, resid_mid)
-        other_down, unused = other_layer(own[3], after, False, (), resid_mid)
-        layer0.extend([jnp.where(is_first, own[2], other_up), jnp.where(is_first, own[3], other_down)])
-        layer1.extend([jnp.where(is_first, other_up, own[2]), jnp.where(is_first, other_down, own[3])])
+    half_qkv = fetch_half(own[0], ())
+    start_parts, lengths = after_all((start_parts, lengths), half_qkv)
+    first_parts = in_turn(
+        lambda k, part: layer_norm(part.astype(f32), gains0[0]).astype(bf16), start_parts
+    )
+    half_out = fetch_half(own[1], half_qkv)
+    qkv0, qkv1 = by_layer(is_first, own[0], both_halves(half_qkv))
+    layer0 = [joined(jnp.split(qkv0, 3), 1)]
+    layer1 = [joined(jnp.split(qkv1, 3), 1)]
+    hidden_width = w_up.shape[3]
+    moving = []
+
+    def at_projected(values):
+        out0, out1 = by_layer(is_first, own[1], both_halves(half_out, values))
+        layer0.append(out0)
+        layer1.append(out1)
+        moving.append(fetch_half(own[2][:hidden_width], (half_out, values)))
+
+    def at_far_term(far_term):
+        moving.append(both_halves(moving[0], far_term))
+        moving.append(fetch_half(own[2][hidden_width:], (moving[0], far_term)))
+
+    def at_mid(resid_mid):
+        moving.append(both_halves(moving[2], resid_mid))
+        moving.append(fetch_half(own[3], (moving[2], resid_mid)))
+
+    def at_gathered(parts):
+        up0, up1 = by_layer(is_first, own[2], joined([moving[1], moving[3]]))
+        down0, down1 = by_layer(is_first, own[3], both_halves(moving[4], parts))
+        layer0.extend([up0, down0])
+        layer1.extend([up1, down1])
+
+    points = (at_projected, at_far_term, at_mid, at_gathered)
 
     doc_lengths = jnp.where(is_first, lengths[0, 0], lengths[1, 0])
     indices = jnp.arange(full_rows, dtype=jnp.int32)
@@ -398,19 +415,19 @@
     tables1 = rope_tables(positions, 160000.0)
 
     out0, kept0 = forward_layer(
-        start_rows, first_parts, gains0[1], layer0, allowed0, tables0, False, feed_weights
+        start_rows, first_parts, gains0[1], layer0, allowed0, tables0, False, points
     )
     out0 = out0.astype(bf16)
     second_rows = out0.astype(f32)
     second_parts = gather_parts(layer_norm(second_rows, gains1[0]).astype(bf16))
     out1_of, kept1 = forward_layer(
-        second_rows, second_parts, gains1[1], layer1, allowed1, tables1, True, lambda *points: None
+        second_rows, second_parts, gains1[1], layer1, allowed1, tables1, True, (lambda value: None,) * 4
     )
     mid1, ffn_grads1, gain_mid1 = backward_ffn(
         end_grads.astype(f32), kept1, gains1[1], layer1
     )
     in1, attn_grads1, gain_first1, unused = backward_attn(
-        mid1, kept1, gains1[0], layer1, allowed1, tables1
+        mid1, kept1, gains1[0], layer1, allowed1, tables1, ()
     )
     in1 = in1.astype(bf16)
     ffn1 = ffn_grads1(mid1)
@@ -419,11 +436,12 @@
     mid0, ffn_grads0, gain_mid0 = backward_ffn(in1.astype(f32), kept0, gains0[1], layer0)
     attn1 = reduce_part_now(attn_grads1(in1, [gain_first1, gain_mid1]))
     mid0 = after_all(mid0, ffn1, attn1)
+    ffn_pack0 = ffn_grads0(mid0)
     in0, attn_grads0, unused, gain_before = backward_attn(
-        mid0, kept0, gains0[0], layer0, allowed0, tables0
+        mid0, kept0, gains0[0], layer0, allowed0, tables0, ffn_pack0
     )
     in0 = in0.astype(bf16)
-    ffn0 = reduce_part(ffn_grads0(mid0))
+    ffn0 = reduce_part(ffn_pack0)
     attn_pack0 = attn_grads0((), [gain_before(), gain_mid0])
     attn0 = reduce_part_now(attn_pack0)
     out1_terms = out1_of(attn_pack0)
@@ -439,7 +457,6 @@
     ffn_halves = spread_part(ffn_sum)
     gain_rows = sum(half[2 * w_qkv.shape[1] :][:8].astype(f32) for half in attn_halves)
     gain_total = sum_tensor(gain_rows).reshape(2, -1)
-    hidden_width = w_up.shape[3]
     grad_up = jnp.stack([half[:hidden_width] for half in ffn_halves])
     down_rows = w_down.shape[1] // 2
     grad_down = joined([half[hidden_width : hidden_width + down_rows] for half in ffn_halves])

time: 538 us -> 524 us (0.974)
  matrix products: 86.4 us -> 74.7 us
  waiting for transfers between devices: 166 us -> 160 us
    ppermute x51, waiting for transfers between devices: 45.1 us -> 71.1 us  [around(): lax.ppermute(block, axis, [(i, (i + distance) % count) for i in range(cou...]
    ppermute x5 -> x6, waiting for transfers between devices: 34.9 us -> 13.5 us  [swap_layer(): lax.ppermute(block, ('section', 'zlo'), [(0, 3), (1, 2), (2, 1), (3, 0)])]
    ppermute x51, starting transfers between devices: 72.7 us -> 88.4 us  [around(): lax.ppermute(block, axis, [(i, (i + distance) % count) for i in range(cou...]
    ppermute x14 -> x15, starting transfers between devices: 38.1 us -> 28.2 us  [swap_core(): return lax.ppermute(block, 'core', [(0, 1), (1, 0)])]
    all_to_all x2, waiting for transfers between devices: 31 us -> 21.3 us  [reduce_part_now(): pieces = lax.all_to_all(grads, ('zlo', 'x'), 0, 0, tiled=True)]
    unnamed x407 -> x413, local copies, waits for them, and re-layouts: 15.9 us -> 18.1 us
    concatenate x12 -> x13, other arithmetic: 11.8 us -> 13.9 us  [joined(): return jnp.concatenate(parts, axis=axis)]
  transfers between devices with their start and end apart: 81 -> 82, of which waited for: 25 -> 30; matrix products, arithmetic and copies ran while one was open for 33% -> 30% of each run, Pallas kernels for 0% -> 0%
where the time goes in v7:
time: 524 us; the launch traced here: 514 us
  waiting for transfers between devices  160 us (31%)
  starting transfers between devices  147 us (28%)
  matrix products  74.7 us (14%)
  other arithmetic  73.3 us (14%)
  local copies, waits for them, and re-layouts  41.2 us (8%)
  between operations  18 us (3%)
    ppermute x51, starting transfers between devices, around(): lax.ppermute(block, axis, [(i, (i + distance) % count) for i in range(cou...  88.4 us
    ppermute x51, waiting for transfers between devices, around(): lax.ppermute(block, axis, [(i, (i + distance) % count) for i in range(cou...  71.1 us
    ppermute x4, waiting for transfers between devices, swap_section(): return lax.ppermute(block, 'section', [(0, 1), (1, 0)])  52.6 us
    ppermute x15, starting transfers between devices, swap_core(): return lax.ppermute(block, 'core', [(0, 1), (1, 0)])  28.2 us
    all_to_all x2, waiting for transfers between devices, reduce_part_now(): pieces = lax.all_to_all(grads, ('zlo', 'x'), 0, 0, tiled=True)  21.3 us
    dot_general x16, matrix products, contract_rows(): lax.dot_general(left_rows, right_rows, (((0,), (0,)), ((), ())), preferre...  21.1 us
    unnamed x413, local copies, waits for them, and re-layouts  18.1 us
    dot_general x16, matrix products, contract_last(): lax.dot_general(left_rows, weight, (((1,), (1,)), ((), ())), preferred_el...  16 us
  transfers between devices with their start and end apart: 82, of which 30 were waited for; matrix products, arithmetic and copies ran while one was open for 30% of the time, Pallas kernels for 0%

profile of v7, /device:TPU:1, one launch (start us, length us, event | category | flops | bytes accessed | tf_op | source)
XLA Modules:
  0.0 514.3 jit_solution(12272457470833444891)
XLA Ops:
  12.3 3.8 collective-permute-start.4
  23.7 2.7 collective-permute-start.31
  28.4 3.6 collective-permute-done.31
  34.4 4.4 collective-permute-done.3
  46.4 4.8 collective-permute-start.5
  60.6 2.9 collective-permute-start.8
  69.9 5.2 %collective-permute-done.9 = bf16[128,1024]{1,0:T(8,128)(2,1)S(1)} collective-permute-done((bf16[128,1024]{1,0:T(8,128)(2,1)S(1)}, bf16[128,1024]{1,0:T(8,128)(2,1)S(1)}, u32[]{:S(2)}, u32[]{:S(2)}) %collective-permute-start.9) | collective-permute-done | bytes 262176 | tf_op jit(solution)/shard_map/ppermute | solution.py:19
  79.5 3.2 collective-permute-start.11
  84.2 9.1 %collective-permute-done.15 = bf16[328,1024]{1,0:T(8,128)(2,1)S(1)} collective-permute-done((bf16[328,1024]{1,0:T(8,128)(2,1)S(1)}, bf16[328,1024]{1,0:T(8,128)(2,1)S(1)}, u32[]{:S(2)}, u32[]{:S(2)}) %collective-permute-start.15) | collective-permute-done | bytes 671776 | tf_op jit(solution)/shard_map/ppermute | solution.py:31
  95.4 2.6 collective-permute-start.16
  98.0 2.7 fusion.178
  104.9 11.2 %collective-permute-done.18 = bf16[128,1024]{1,0:T(8,128)(2,1)S(1)} collective-permute-done((bf16[128,1024]{1,0:T(8,128)(2,1)S(1)}, bf16[128,1024]{1,0:T(8,128)(2,1)S(1)}, u32[]{:S(2)}, u32[]{:S(2)}) %collective-permute-start.18) | collective-permute-done | bytes 262176 | tf_op jit(solution)/shard_map/ppermute | solution.py:19
  120.7 3.0 multiply_convert_fusion.5
  132.9 2.6 collective-permute-done.21
  135.5 4.6 collective-permute-done.22
  147.8 3.3 collective-permute-done.24
  152.6 4.3 collective-permute-done.25
  166.6 7.4 %collective-permute-done.27 = bf16[128,1024]{1,0:T(8,128)(2,1)S(1)} collective-permute-done((bf16[128,1024]{1,0:T(8,128)(2,1)S(1)}, bf16[128,1024]{1,0:T(8,128)(2,1)S(1)}, u32[]{:S(2)}, u32[]{:S(2)}) %collective-permute-start.27) | collective-permute-done | bytes 262176 | tf_op jit(solution)/shard_map/ppermute | solution.py:19
  174.8 2.9 collective-permute-start.29
  178.3 2.8 fusion.179
  200.0 6.2 %collective-permute-done.36 = bf16[128,1024]{1,0:T(8,128)(2,1)S(1)} collective-permute-done((bf16[128,1024]{1,0:T(8,128)(2,1)S(1)}, bf16[128,1024]{1,0:T(8,128)(2,1)S(1)}, u32[]{:S(2)}, u32[]{:S(2)}) %collective-permute-start.36) | collective-permute-done | bytes 262176 | tf_op jit(solution)/shard_map/ppermute | solution.py:19
  207.8 2.9 collective-permute-start.40
  216.3 3.5 collective-permute-start.45
  226.3 3.6 fusion.25
  237.9 4.2 collective-permute-start.41
  250.1 3.9 collective-permute-done.42
  260.6 3.6 collective-permute-start.48
  285.5 3.6 collective-permute-start.49
  290.4 2.5 collective-permute-start.51
  296.5 4.9 collective-permute-done.50
  308.9 4.1 all-to-all-start
  315.3 14.2 %all-to-all-done = bf16[8,272,256]{2,1,0:T(8,128)(2,1)S(1)} async-done(((bf16[8,272,256]{2,1,0:T(8,128)(2,1)}), bf16[8,272,256]{2,1,0:T(8,128)(2,1)S(1)}, u32[]{:S(2)}, u32[]{:S(2)}) %all-to-all-start) | async-done | bytes 1114144 | tf_op jit(solution)/shard_map/all_to_all | solution.py:334
  330.3 3.5 collective-permute-start.56
  355.5 3.5 fusion.28
  368.5 2.6 collective-permute-start.61
  377.6 2.5 collective-permute-start.59
  389.2 4.4 all-to-all-start.1
  395.6 3.6 collective-permute-start.65
  403.0 7.1 %all-to-all-done.1 = bf16[8,272,256]{2,1,0:T(8,128)(2,1)} async-done(((bf16[8,272,256]{2,1,0:T(8,128)(2,1)}), bf16[8,272,256]{2,1,0:T(8,128)(2,1)}, u32[]{:S(2)}, u32[]{:S(2)}) %all-to-all-start.1) | async-done | bytes 1114144 | tf_op jit(solution)/shard_map/all_to_all | solution.py:334
  413.6 3.9 collective-permute-done.64
  418.6 3.6 all-to-all-start.2
  423.6 17.5 %collective-permute-done.74 = bf16[128,1024]{1,0:T(8,128)(2,1)S(1)} collective-permute-done((bf16[128,1024]{1,0:T(8,128)(2,1)S(1)}, bf16[128,1024]{1,0:T(8,128)(2,1)S(1)}, u32[]{:S(2)}, u32[]{:S(2)}) %collective-permute-start.74) | collective-permute-done | bytes 262176 | tf_op jit(solution)/shard_map/ppermute | solution.py:27
  443.9 4.7 all-to-all-start.3
  449.6 3.0 collective-permute-start.69
  452.7 26.5 %collective-permute-done.69 = bf16[128,1024]{1,0:T(8,128)(2,1)S(1)} collective-permute-done((bf16[128,1024]{1,0:T(8,128)(2,1)S(1)}, bf16[128,1024]{1,0:T(8,128)(2,1)S(1)}, u32[]{:S(2)}, u32[]{:S(2)}) %collective-permute-start.69) | collective-permute-done | bytes 262176 | tf_op jit(solution)/shard_map/ppermute | solution.py:27
  480.1 4.7 collective-permute-done.68
  489.5 4.1 collective-permute-start.72
  504.3 2.7 convert_bitcast_fusion
  (822 shorter events, 254.2 us)
Async XLA Ops:
  7.2 323.1 %reduce-scatter.3.cloned.1.call-start = ((), (), s32[]{:S(2)}) async-start(), calls=%async_computation.6 | async-start | bytes 2359296 | tf_op jit(solution)/shard_map/reduce_scatter | solution.py:330
  8.6 18.4 %collective-permute-start.1 = (bf16[128,1024]{1,0:T(8,128)(2,1)S(1)}, bf16[128,1024]{1,0:T(8,128)(2,1)S(1)}, u32[]{:S(2)}, u32[]{:S(2)}) collective-permute-start(bf16[128,1024]{1,0:T(8,128)(2,1)S(1)} %get-tuple-element.168), channel_id=1, source_target_pairs={{0,1},{1,2},{2,3},{3,0},{4,5},{5,6},{6,7},{7,4},{8,9},{9,10},{10,1... | collective-permute-start | bytes 786440 | tf_op jit(solution)/shard_map/ppermute | solution.py:19
  10.8 16.6 %collective-permute-start = (bf16[128,1024]{1,0:T(8,128)(2,1)S(1)}, bf16[128,1024]{1,0:T(8,128)(2,1)}, u32[]{:S(2)}, u32[]{:S(2)}) collective-permute-start(bf16[128,1024]{1,0:T(8,128)(2,1)S(1)} %get-tuple-element.168), channel_id=1, source_target_pairs={{0,3},{1,0},{2,1},{3,2},{4,7},{5,4},{6,5},{7,6},{8,11},{9,8},{10,9... | collective-permute-start | bytes 786440 | tf_op jit(solution)/shard_map/ppermute | solution.py:19
  12.3 11.4 %collective-permute-start.4 = (f32[2,1024]{1,0:T(2,128)}, f32[2,1024]{1,0:T(2,128)S(1)}, u32[]{:S(2)}, u32[]{:S(2)}) collective-permute-start(f32[2,1024]{1,0:T(2,128)} %bitcast.350), channel_id=1, source_target_pairs={{0,96},{32,64},{64,32},{96,0},{1,97},{33,65},{65,33},{97,1},{2,98}... | collective-permute-start | bytes 24584 | tf_op jit(solution)/shard_map/ppermute | solution.py:31
  19.9 18.8 %collective-permute-start.3 = (bf16[1536,256]{1,0:T(8,128)(2,1)}, bf16[1536,256]{1,0:T(8,128)(2,1)}, u32[]{:S(2)}, u32[]{:S(2)}) collective-permute-start(bf16[1536,256]{1,0:T(8,128)(2,1)} %constant_dynamic-slice_fusion.4), channel_id=1, source_target_pairs={{0,96},{32,64},{64,32},{96,0},{1,97},{33,65},{65,33},{97,1},{2,98}... | collective-permute-start | bytes 2359304 | tf_op jit(solution)/shard_map/ppermute | solution.py:31
  46.0 11.6 %collective-permute-start.6 = (bf16[128,1024]{1,0:T(8,128)(2,1)S(1)}, bf16[128,1024]{1,0:T(8,128)(2,1)S(1)}, u32[]{:S(2)}, u32[]{:S(2)}) collective-permute-start(bf16[128,1024]{1,0:T(8,128)(2,1)S(1)} %constant_dynamic-slice_fusion.2), channel_id=1, source_target_pairs={{0,96},{32,64},{64,32},{96,0},{1,97},{33,65},{65,33},{97,1},{2,98}... | collective-permute-start | bytes 786440 | tf_op jit(solution)/shard_map/ppermute | solution.py:31
  58.2 18.3 %collective-permute-start.13 = (bf16[328,1024]{1,0:T(8,128)(2,1)S(1)}, bf16[328,1024]{1,0:T(8,128)(2,1)S(1)}, u32[]{:S(2)}, u32[]{:S(2)}) collective-permute-start(bf16[328,1024]{1,0:T(8,128)(2,1)S(1)} %constant_dynamic-slice_fusion.1), channel_id=1, source_target_pairs={{0,96},{32,64},{64,32},{96,0},{1,97},{33,65},{65,33},{97,1},{2,98}... | collective-permute-start | bytes 2015240 | tf_op jit(solution)/shard_map/ppermute | solution.py:31
  76.7 16.7 %collective-permute-start.15 = (bf16[328,1024]{1,0:T(8,128)(2,1)S(1)}, bf16[328,1024]{1,0:T(8,128)(2,1)S(1)}, u32[]{:S(2)}, u32[]{:S(2)}) collective-permute-start(bf16[328,1024]{1,0:T(8,128)(2,1)S(1)} %constant_dynamic-slice_fusion), channel_id=1, source_target_pairs={{0,96},{32,64},{64,32},{96,0},{1,97},{33,65},{65,33},{97,1},{2,98}... | collective-permute-start | bytes 2015240 | tf_op jit(solution)/shard_map/ppermute | solution.py:31
  79.2 21.5 %collective-permute-start.12 = (bf16[128,1024]{1,0:T(8,128)(2,1)S(1)}, bf16[128,1024]{1,0:T(8,128)(2,1)S(1)}, u32[]{:S(2)}, u32[]{:S(2)}) collective-permute-start(bf16[128,1024]{1,0:T(8,128)(2,1)S(1)} %multiply_convert_fusion.7), channel_id=1, source_target_pairs={{0,1},{1,2},{2,3},{3,0},{4,5},{5,6},{6,7},{7,4},{8,9},{9,10},{10,1... | collective-permute-start | bytes 786440 | tf_op jit(solution)/shard_map/ppermute | solution.py:19
  79.5 22.1 %collective-permute-start.11 = (bf16[128,1024]{1,0:T(8,128)(2,1)S(1)}, bf16[128,1024]{1,0:T(8,128)(2,1)S(1)}, u32[]{:S(2)}, u32[]{:S(2)}) collective-permute-start(bf16[128,1024]{1,0:T(8,128)(2,1)S(1)} %multiply_convert_fusion.7), channel_id=1, source_target_pairs={{0,3},{1,0},{2,1},{3,2},{4,7},{5,4},{6,5},{7,6},{8,11},{9,8},{10,9... | collective-permute-start | bytes 786440 | tf_op jit(solution)/shard_map/ppermute | solution.py:19
  82.7 22.1 %collective-permute-start.14 = (bf16[328,1024]{1,0:T(8,128)(2,1)S(1)}, bf16[328,1024]{1,0:T(8,128)(2,1)S(1)}, u32[]{:S(2)}, u32[]{:S(2)}) collective-permute-start(bf16[328,1024]{1,0:T(8,128)(2,1)S(1)} %collective-permute-done.13), channel_id=1, source_target_pairs={{0,4},{4,0},{1,5},{5,1},{2,6},{6,2},{3,7},{7,3},{8,12},{12,8},{9,1... | collective-permute-start | bytes 2015240 | tf_op jit(solution)/shard_map/ppermute | solution.py:23
  93.4 22.7 %collective-permute-start.17 = (bf16[328,1024]{1,0:T(8,128)(2,1)S(1)}, bf16[328,1024]{1,0:T(8,128)(2,1)S(1)}, u32[]{:S(2)}, u32[]{:S(2)}) collective-permute-start(bf16[328,1024]{1,0:T(8,128)(2,1)S(1)} %constant_dynamic-slice_fusion.3), channel_id=1, source_target_pairs={{0,96},{32,64},{64,32},{96,0},{1,97},{33,65},{65,33},{97,1},{2,98}... | collective-permute-start | bytes 2015240 | tf_op jit(solution)/shard_map/ppermute | solution.py:31
  95.4 21.9 %collective-permute-start.16 = (bf16[328,1024]{1,0:T(8,128)(2,1)S(1)}, bf16[328,1024]{1,0:T(8,128)(2,1)S(1)}, u32[]{:S(2)}, u32[]{:S(2)}) collective-permute-start(bf16[328,1024]{1,0:T(8,128)(2,1)S(1)} %collective-permute-done.15), channel_id=1, source_target_pairs={{0,4},{4,0},{1,5},{5,1},{2,6},{6,2},{3,7},{7,3},{8,12},{12,8},{9,1... | collective-permute-start | bytes 2015240 | tf_op jit(solution)/shard_map/ppermute | solution.py:23
  100.7 91.1 %collective-permute-start.34 = (bf16[128,1024]{1,0:T(8,128)(2,1)}, bf16[128,1024]{1,0:T(8,128)(2,1)S(1)}, u32[]{:S(2)}, u32[]{:S(2)}) collective-permute-start(bf16[128,1024]{1,0:T(8,128)(2,1)} %select_bitcast_fusion.4), channel_id=1, source_target_pairs={{0,2},{1,3},{2,0},{3,1},{4,6},{5,7},{6,4},{7,5},{8,10},{9,11},{10,... | collective-permute-start | bytes 786440 | tf_op jit(solution)/shard_map/ppermute | solution.py:19
  101.6 14.5 %collective-permute-start.18 = (bf16[128,1024]{1,0:T(8,128)(2,1)S(1)}, bf16[128,1024]{1,0:T(8,128)(2,1)S(1)}, u32[]{:S(2)}, u32[]{:S(2)}) collective-permute-start(bf16[128,1024]{1,0:T(8,128)(2,1)S(1)} %multiply_convert_fusion.7), channel_id=1, source_target_pairs={{0,2},{1,3},{2,0},{3,1},{4,6},{5,7},{6,4},{7,5},{8,10},{9,11},{10,... | collective-permute-start | bytes 786440 | tf_op jit(solution)/shard_map/ppermute | solution.py:19
  126.5 13.7 %collective-permute-start.22 = (bf16[128,1024]{1,0:T(8,128)(2,1)S(1)}, bf16[128,1024]{1,0:T(8,128)(2,1)S(1)}, u32[]{:S(2)}, u32[]{:S(2)}) collective-permute-start(bf16[128,1024]{1,0:T(8,128)(2,1)S(1)} %get-tuple-element.250), channel_id=1, source_target_pairs={{0,3},{1,0},{2,1},{3,2},{4,7},{5,4},{6,5},{7,6},{8,11},{9,8},{10,9... | collective-permute-start | bytes 786440 | tf_op jit(solution)/shard_map/ppermute | solution.py:19
  194.1 12.1 %collective-permute-start.36 = (bf16[128,1024]{1,0:T(8,128)(2,1)S(1)}, bf16[128,1024]{1,0:T(8,128)(2,1)S(1)}, u32[]{:S(2)}, u32[]{:S(2)}) collective-permute-start(bf16[128,1024]{1,0:T(8,128)(2,1)S(1)} %get-tuple-element.245), channel_id=1, source_target_pairs={{0,1},{1,2},{2,3},{3,0},{4,5},{5,6},{6,7},{7,4},{8,9},{9,10},{10,1... | collective-permute-start | bytes 786440 | tf_op jit(solution)/shard_map/ppermute | solution.py:19
  195.1 11.1 %collective-permute-start.37 = (bf16[128,1024]{1,0:T(8,128)(2,1)S(1)}, bf16[128,1024]{1,0:T(8,128)(2,1)S(1)}, u32[]{:S(2)}, u32[]{:S(2)}) collective-permute-start(bf16[128,1024]{1,0:T(8,128)(2,1)S(1)} %get-tuple-element.246), channel_id=1, source_target_pairs={{0,3},{1,0},{2,1},{3,2},{4,7},{5,4},{6,5},{7,6},{8,11},{9,8},{10,9... | collective-permute-start | bytes 786440 | tf_op jit(solution)/shard_map/ppermute | solution.py:19
  207.8 14.8 %collective-permute-start.40 = (bf16[128,1024]{1,0:T(8,128)(2,1)S(1)}, bf16[128,1024]{1,0:T(8,128)(2,1)S(1)}, u32[]{:S(2)}, u32[]{:S(2)}) collective-permute-start(bf16[128,1024]{1,0:T(8,128)(2,1)S(1)} %get-tuple-element.175), channel_id=1, source_target_pairs={{0,2},{1,3},{2,0},{3,1},{4,6},{5,7},{6,4},{7,5},{8,10},{9,11},{10,... | collective-permute-start | bytes 786440 | tf_op jit(solution)/shard_map/ppermute | solution.py:19
  210.8 11.1 %collective-permute-start.39 = (bf16[128,1024]{1,0:T(8,128)(2,1)S(1)}, bf16[128,1024]{1,0:T(8,128)(2,1)S(1)}, u32[]{:S(2)}, u32[]{:S(2)}) collective-permute-start(bf16[128,1024]{1,0:T(8,128)(2,1)S(1)} %get-tuple-element.175), channel_id=1, source_target_pairs={{0,1},{1,2},{2,3},{3,0},{4,5},{5,6},{6,7},{7,4},{8,9},{9,10},{10,1... | collective-permute-start | bytes 786440 | tf_op jit(solution)/shard_map/ppermute | solution.py:19
  216.3 40.0 %collective-permute-start.45 = (bf16[328,1024]{1,0:T(8,128)(2,1)}, bf16[328,1024]{1,0:T(8,128)(2,1)}, u32[]{:S(2)}, u32[]{:S(2)}) collective-permute-start(bf16[328,1024]{1,0:T(8,128)(2,1)} %convolution_convert_fusion.11), channel_id=1, source_target_pairs={{0,4},{4,0},{1,5},{5,1},{2,6},{6,2},{3,7},{7,3},{8,12},{12,8},{9,1... | collective-permute-start | bytes 2015240 | tf_op jit(solution)/shard_map/ppermute | solution.py:23
  237.9 12.2 %collective-permute-start.41 = (bf16[128,1024]{1,0:T(8,128)(2,1)S(1)}, bf16[128,1024]{1,0:T(8,128)(2,1)S(1)}, u32[]{:S(2)}, u32[]{:S(2)}) collective-permute-start(bf16[128,1024]{1,0:T(8,128)(2,1)S(1)} %convolution_convert_fusion.18), channel_id=1, source_target_pairs={{0,2},{1,3},{2,0},{3,1},{4,6},{5,7},{6,4},{7,5},{8,10},{9,11},{10,... | collective-permute-start | bytes 786440 | tf_op jit(solution)/shard_map/ppermute | solution.py:19
  243.0 11.0 %collective-permute-start.42 = (bf16[128,1024]{1,0:T(8,128)(2,1)S(1)}, bf16[128,1024]{1,0:T(8,128)(2,1)S(1)}, u32[]{:S(2)}, u32[]{:S(2)}) collective-permute-start(bf16[128,1024]{1,0:T(8,128)(2,1)S(1)} %get-tuple-element.243), channel_id=1, source_target_pairs={{0,1},{1,2},{2,3},{3,0},{4,5},{5,6},{6,7},{7,4},{8,9},{9,10},{10,1... | collective-permute-start | bytes 786440 | tf_op jit(solution)/shard_map/ppermute | solution.py:19
  246.9 11.1 %collective-permute-start.44 = (bf16[656,1024]{1,0:T(8,128)(2,1)S(1)}, bf16[656,1024]{1,0:T(8,128)(2,1)S(1)}, u32[]{:S(2)}, u32[]{:S(2)}) collective-permute-start(bf16[656,1024]{1,0:T(8,128)(2,1)S(1)} %convolution_convert_fusion.1), channel_id=1, source_target_pairs={{0,4},{4,0},{1,5},{5,1},{2,6},{6,2},{3,7},{7,3},{8,12},{12,8},{9,1... | collective-permute-start | bytes 4030472 | tf_op jit(solution)/shard_map/ppermute | solution.py:23
  260.6 21.8 %collective-permute-start.48 = (bf16[128,1024]{1,0:T(8,128)(2,1)}, bf16[128,1024]{1,0:T(8,128)(2,1)}, u32[]{:S(2)}, u32[]{:S(2)}) collective-permute-start(bf16[128,1024]{1,0:T(8,128)(2,1)} %add_convert_fusion.9), channel_id=1, source_target_pairs={{0,2},{1,3},{2,0},{3,1},{4,6},{5,7},{6,4},{7,5},{8,10},{9,11},{10,... | collective-permute-start | bytes 786440 | tf_op jit(solution)/shard_map/ppermute | solution.py:19
  264.2 13.0 %collective-permute-start.47 = (bf16[128,1024]{1,0:T(8,128)(2,1)}, bf16[128,1024]{1,0:T(8,128)(2,1)}, u32[]{:S(2)}, u32[]{:S(2)}) collective-permute-start(bf16[128,1024]{1,0:T(8,128)(2,1)} %add_convert_fusion.9), channel_id=1, source_target_pairs={{0,1},{1,2},{2,3},{3,0},{4,5},{5,6},{6,7},{7,4},{8,9},{9,10},{10,1... | collective-permute-start | bytes 786440 | tf_op jit(solution)/shard_map/ppermute | solution.py:19
  264.5 11.7 %collective-permute-start.46 = (bf16[128,1024]{1,0:T(8,128)(2,1)}, bf16[128,1024]{1,0:T(8,128)(2,1)}, u32[]{:S(2)}, u32[]{:S(2)}) collective-permute-start(bf16[128,1024]{1,0:T(8,128)(2,1)} %add_convert_fusion.9), channel_id=1, source_target_pairs={{0,3},{1,0},{2,1},{3,2},{4,7},{5,4},{6,5},{7,6},{8,11},{9,8},{10,9... | collective-permute-start | bytes 786440 | tf_op jit(solution)/shard_map/ppermute | solution.py:19
  272.5 31.5 %collective-permute-start.52 = (bf16[1024,256]{1,0:T(8,128)(2,1)}, bf16[1024,256]{1,0:T(8,128)(2,1)}, u32[]{:S(2)}, u32[]{:S(2)}) collective-permute-start(bf16[1024,256]{1,0:T(8,128)(2,1)} %convolution_convert_fusion.15), channel_id=1, source_target_pairs={{0,4},{4,0},{1,5},{5,1},{2,6},{6,2},{3,7},{7,3},{8,12},{12,8},{9,1... | collective-permute-start | bytes 1572872 | tf_op jit(solution)/shard_map/ppermute | solution.py:23
  290.1 11.4 %collective-permute-start.50 = (bf16[128,1024]{1,0:T(8,128)(2,1)}, bf16[128,1024]{1,0:T(8,128)(2,1)S(1)}, u32[]{:S(2)}, u32[]{:S(2)}) collective-permute-start(bf16[128,1024]{1,0:T(8,128)(2,1)} %get-tuple-element.241), channel_id=1, source_target_pairs={{0,1},{1,2},{2,3},{3,0},{4,5},{5,6},{6,7},{7,4},{8,9},{9,10},{10,1... | collective-permute-start | bytes 786440 | tf_op jit(solution)/shard_map/ppermute | solution.py:19
  290.4 11.1 %collective-permute-start.51 = (bf16[128,1024]{1,0:T(8,128)(2,1)}, bf16[128,1024]{1,0:T(8,128)(2,1)}, u32[]{:S(2)}, u32[]{:S(2)}) collective-permute-start(bf16[128,1024]{1,0:T(8,128)(2,1)} %get-tuple-element.242), channel_id=1, source_target_pairs={{0,3},{1,0},{2,1},{3,2},{4,7},{5,4},{6,5},{7,6},{8,11},{9,8},{10,9... | collective-permute-start | bytes 786440 | tf_op jit(solution)/shard_map/ppermute | solution.py:19
  294.3 11.6 %collective-permute-start.53 = (bf16[1024,256]{1,0:T(8,128)(2,1)}, bf16[1024,256]{1,0:T(8,128)(2,1)}, u32[]{:S(2)}, u32[]{:S(2)}) collective-permute-start(bf16[1024,256]{1,0:T(8,128)(2,1)} %convolution_convert_fusion.14), channel_id=1, source_target_pairs={{0,4},{4,0},{1,5},{5,1},{2,6},{6,2},{3,7},{7,3},{8,12},{12,8},{9,1... | collective-permute-start | bytes 1572872 | tf_op jit(solution)/shard_map/ppermute | solution.py:23
  308.9 20.6 %all-to-all-start = ((bf16[8,272,256]{2,1,0:T(8,128)(2,1)}), bf16[8,272,256]{2,1,0:T(8,128)(2,1)S(1)}, u32[]{:S(2)}, u32[]{:S(2)}) async-start(bf16[8,272,256]{2,1,0:T(8,128)(2,1)} %bitcast.68), calls=%async_computation.1 | async-start | bytes 2228224 | tf_op jit(solution)/shard_map/all_to_all | solution.py:334
  313.0 109.2 %reduce-scatter.5.cloned.1.call-start = ((), (), s32[]{:S(2)}) async-start(), calls=%async_computation.7 | async-start | bytes 2359296 | tf_op jit(solution)/shard_map/reduce_scatter | solution.py:330
  330.3 16.7 %collective-permute-start.56 = (bf16[128,1024]{1,0:T(8,128)(2,1)S(1)}, bf16[128,1024]{1,0:T(8,128)(2,1)S(1)}, u32[]{:S(2)}, u32[]{:S(2)}) collective-permute-start(bf16[128,1024]{1,0:T(8,128)(2,1)S(1)} %convert_element_type.627), channel_id=1, source_target_pairs={{0,2},{1,3},{2,0},{3,1},{4,6},{5,7},{6,4},{7,5},{8,10},{9,11},{10,... | collective-permute-start | bytes 786440 | tf_op jit(solution)/shard_map/ppermute | solution.py:19
  333.9 12.4 %collective-permute-start.55 = (bf16[128,1024]{1,0:T(8,128)(2,1)S(1)}, bf16[128,1024]{1,0:T(8,128)(2,1)S(1)}, u32[]{:S(2)}, u32[]{:S(2)}) collective-permute-start(bf16[128,1024]{1,0:T(8,128)(2,1)S(1)} %convert_element_type.627), channel_id=1, source_target_pairs={{0,1},{1,2},{2,3},{3,0},{4,5},{5,6},{6,7},{7,4},{8,9},{9,10},{10,1... | collective-permute-start | bytes 786440 | tf_op jit(solution)/shard_map/ppermute | solution.py:19
  334.1 12.1 %collective-permute-start.54 = (bf16[128,1024]{1,0:T(8,128)(2,1)S(1)}, bf16[128,1024]{1,0:T(8,128)(2,1)S(1)}, u32[]{:S(2)}, u32[]{:S(2)}) collective-permute-start(bf16[128,1024]{1,0:T(8,128)(2,1)S(1)} %convert_element_type.627), channel_id=1, source_target_pairs={{0,3},{1,0},{2,1},{3,2},{4,7},{5,4},{6,5},{7,6},{8,11},{9,8},{10,9... | collective-permute-start | bytes 786440 | tf_op jit(solution)/shard_map/ppermute | solution.py:19
  368.5 12.5 %collective-permute-start.61 = (bf16[128,1024]{1,0:T(8,128)(2,1)}, bf16[128,1024]{1,0:T(8,128)(2,1)}, u32[]{:S(2)}, u32[]{:S(2)}) collective-permute-start(bf16[128,1024]{1,0:T(8,128)(2,1)} %get-tuple-element.336), channel_id=1, source_target_pairs={{0,2},{1,3},{2,0},{3,1},{4,6},{5,7},{6,4},{7,5},{8,10},{9,11},{10,... | collective-permute-start | bytes 786440 | tf_op jit(solution)/shard_map/ppermute | solution.py:19
  389.2 20.9 %all-to-all-start.1 = ((bf16[8,272,256]{2,1,0:T(8,128)(2,1)}), bf16[8,272,256]{2,1,0:T(8,128)(2,1)}, u32[]{:S(2)}, u32[]{:S(2)}) async-start(bf16[8,272,256]{2,1,0:T(8,128)(2,1)} %bitcast.286), calls=%async_computation.2 | async-start | bytes 2228224 | tf_op jit(solution)/shard_map/all_to_all | solution.py:334
  395.6 16.0 %collective-permute-start.65 = (bf16[128,1024]{1,0:T(8,128)(2,1)}, bf16[128,1024]{1,0:T(8,128)(2,1)}, u32[]{:S(2)}, u32[]{:S(2)}) collective-permute-start(bf16[128,1024]{1,0:T(8,128)(2,1)} %convolution_convert_fusion.16), channel_id=1, source_target_pairs={{0,2},{1,3},{2,0},{3,1},{4,6},{5,7},{6,4},{7,5},{8,10},{9,11},{10,... | collective-permute-start | bytes 786440 | tf_op jit(solution)/shard_map/ppermute | solution.py:19
  400.1 11.6 %collective-permute-start.66 = (bf16[128,1024]{1,0:T(8,128)(2,1)S(1)}, bf16[128,1024]{1,0:T(8,128)(2,1)S(1)}, u32[]{:S(2)}, u32[]{:S(2)}) collective-permute-start(bf16[128,1024]{1,0:T(8,128)(2,1)S(1)} %get-tuple-element.237), channel_id=1, source_target_pairs={{0,1},{1,2},{2,3},{3,0},{4,5},{5,6},{6,7},{7,4},{8,9},{9,10},{10,1... | collective-permute-start | bytes 786440 | tf_op jit(solution)/shard_map/ppermute | solution.py:19
  400.4 11.3 %collective-permute-start.67 = (bf16[128,1024]{1,0:T(8,128)(2,1)S(1)}, bf16[128,1024]{1,0:T(8,128)(2,1)S(1)}, u32[]{:S(2)}, u32[]{:S(2)}) collective-permute-start(bf16[128,1024]{1,0:T(8,128)(2,1)S(1)} %get-tuple-element.238), channel_id=1, source_target_pairs={{0,3},{1,0},{2,1},{3,2},{4,7},{5,4},{6,5},{7,6},{8,11},{9,8},{10,9... | collective-permute-start | bytes 786440 | tf_op jit(solution)/shard_map/ppermute | solution.py:19
  418.6 23.6 %all-to-all-start.2 = ((bf16[8,272,256]{2,1,0:T(8,128)(2,1)}), bf16[8,272,256]{2,1,0:T(8,128)(2,1)S(1)}, u32[]{:S(2)}, u32[]{:S(2)}) async-start(bf16[8,272,256]{2,1,0:T(8,128)(2,1)} %broadcast_in_dim.221), calls=%async_computation.3 | async-start | bytes 2228224 | tf_op jit(solution)/shard_map/all_to_all | solution.py:341
  422.3 18.9 %collective-permute-start.74 = (bf16[128,1024]{1,0:T(8,128)(2,1)S(1)}, bf16[128,1024]{1,0:T(8,128)(2,1)S(1)}, u32[]{:S(2)}, u32[]{:S(2)}) collective-permute-start(bf16[128,1024]{1,0:T(8,128)(2,1)S(1)} %broadcast_select_fusion.22), channel_id=1, source_target_pairs={{0,64},{64,0},{1,65},{65,1},{2,66},{66,2},{3,67},{67,3},{4,68},{68... | collective-permute-start | bytes 786440 | tf_op jit(solution)/shard_map/ppermute | solution.py:27
  443.9 41.0 %all-to-all-start.3 = ((bf16[8,128,1024]{2,1,0:T(8,128)(2,1)}), bf16[8,128,1024]{2,1,0:T(8,128)(2,1)S(1)}, u32[]{:S(2)}, u32[]{:S(2)}) async-start(bf16[8,128,1024]{2,1,0:T(8,128)(2,1)} %broadcast_in_dim.226), calls=%async_computation.5 | async-start | bytes 4194304 | tf_op jit(solution)/shard_map/all_to_all | solution.py:341
  448.6 39.2 %collective-permute-start.70 = (bf16[2176,256]{1,0:T(8,128)(2,1)}, bf16[2176,256]{1,0:T(8,128)(2,1)}, u32[]{:S(2)}, u32[]{:S(2)}) collective-permute-start(bf16[2176,256]{1,0:T(8,128)(2,1)} %bitcast.287), channel_id=1, source_target_pairs={{0,4},{4,0},{1,5},{5,1},{2,6},{6,2},{3,7},{7,3},{8,12},{12,8},{9,1... | collective-permute-start | bytes 3342344 | tf_op jit(solution)/shard_map/ppermute | solution.py:23
  449.6 29.6 %collective-permute-start.69 = (bf16[128,1024]{1,0:T(8,128)(2,1)S(1)}, bf16[128,1024]{1,0:T(8,128)(2,1)S(1)}, u32[]{:S(2)}, u32[]{:S(2)}) collective-permute-start(bf16[128,1024]{1,0:T(8,128)(2,1)S(1)} %broadcast_select_fusion.23), channel_id=1, source_target_pairs={{0,64},{64,0},{1,65},{65,1},{2,66},{66,2},{3,67},{67,3},{4,68},{68... | collective-permute-start | bytes 786440 | tf_op jit(solution)/shard_map/ppermute | solution.py:27
  452.6 32.2 %collective-permute-start.68 = (bf16[128,1024]{1,0:T(8,128)(2,1)S(1)}, bf16[128,1024]{1,0:T(8,128)(2,1)S(1)}, u32[]{:S(2)}, u32[]{:S(2)}) collective-permute-start(bf16[128,1024]{1,0:T(8,128)(2,1)S(1)} %broadcast_select_fusion.24), channel_id=1, source_target_pairs={{0,64},{64,0},{1,65},{65,1},{2,66},{66,2},{3,67},{67,3},{4,68},{68... | collective-permute-start | bytes 786440 | tf_op jit(solution)/shard_map/ppermute | solution.py:27
  484.9 15.3 %collective-permute-start.75 = (bf16[1024,1024]{1,0:T(8,128)(2,1)S(1)}, bf16[1024,1024]{1,0:T(8,128)(2,1)}, u32[]{:S(2)}, u32[]{:S(2)}) collective-permute-start(bf16[1024,1024]{1,0:T(8,128)(2,1)S(1)} %bitcast.285), channel_id=1, source_target_pairs={{0,4},{4,0},{1,5},{5,1},{2,6},{6,2},{3,7},{7,3},{8,12},{12,8},{9,1... | collective-permute-start | bytes 6291464 | tf_op jit(solution)/shard_map/ppermute | solution.py:23
  (231 other events, 2390.7 us)
Sparse Core Ops, SparseCore 0:
  268.9 35.3 reduce-scatter.2
  355.6 35.4 reduce-scatter.4

commit v8 on v7

--- a/solution.py
+++ b/solution.py
@@ -338,7 +338,10 @@
 
 def spread_part(part):
     copies = jnp.broadcast_to(part[None], (8,) + part.shape).reshape(-1, part.shape[1])
-    half = lax.all_to_all(copies, ("zlo", "x"), 0, 0, tiled=True)
+    return lax.all_to_all(copies, ("zlo", "x"), 0, 0, tiled=True)
+
+
+def trade_halves(half):
     beside = swap_core(half)
     is_core0 = lax.axis_index("core") == 0
     return jnp.where(is_core0, half, beside), jnp.where(is_core0, beside, half)
@@ -445,16 +448,18 @@
     attn_pack0 = attn_grads0((), [gain_before(), gain_mid0])
     attn0 = reduce_part_now(attn_pack0)
     out1_terms = out1_of(attn_pack0)
-    attn0, in0 = lax.optimization_barrier((attn0, in0))
+    ffn_own, ffn_sent = pick_sections(is_first, ffn0, ffn1)
+    ffn_sum = (ffn_own.astype(f32) + swap_section(ffn_sent).astype(f32)).astype(bf16)
+    attn0, ffn_sum, in0 = lax.optimization_barrier((attn0, ffn_sum, in0))
     attn_own, attn_sent = pick_sections(is_first, attn0, attn1)
     attn_sent = after_all(attn_sent, out1_terms)
     attn_sum = (attn_own.astype(f32) + swap_section(attn_sent).astype(f32)).astype(bf16)
     out1 = (kept1["resid_mid"] + scatter_parts(*out1_terms)).astype(bf16)
-    ffn_own, ffn_sent = pick_sections(is_first, ffn0, ffn1)
-    ffn_sum = (ffn_own.astype(f32) + swap_section(ffn_sent).astype(f32)).astype(bf16)
-    attn_sum, out1 = lax.optimization_barrier((attn_sum, out1))
-    attn_halves = spread_part(attn_sum)
-    ffn_halves = spread_part(ffn_sum)
+    ffn_half = spread_part(ffn_sum)
+    attn_sum, out1, ffn_half = lax.optimization_barrier((attn_sum, out1, ffn_half))
+    attn_half = spread_part(attn_sum)
+    ffn_halves = trade_halves(ffn_half)
+    attn_halves = trade_halves(attn_half)
     gain_rows = sum(half[2 * w_qkv.shape[1] :][:8].astype(f32) for half in attn_halves)
     gain_total = sum_tensor(gain_rows).reshape(2, -1)
     grad_up = jnp.stack([half[:hidden_width] for half in ffn_halves])
@@ -471,10 +476,12 @@
     grad_out = attn_halves[1][model_width : 2 * model_width].T
 
     got_out = swap_section(jnp.where(is_first, out1, out0))
+    got_out = after_all(got_out, attn_half)
     section_out = jnp.stack(
         [jnp.where(is_first, out0, got_out), jnp.where(is_first, got_out, out1)]
     )
     got_in = swap_section(jnp.where(is_first, in1, in0))
+    got_in = after_all(got_in, attn_half)
     input_grads = jnp.stack(
         [jnp.where(is_first, in0, got_in), jnp.where(is_first, got_in, in1)]
     )

time: 524 us -> 525 us (level)
  waiting for transfers between devices: 160 us -> 152 us
    ppermute x4, waiting for transfers between devices: 52.6 us -> 21.5 us  [swap_section(): return lax.ppermute(block, 'section', [(0, 1), (1, 0)])]
    all_to_all x2, waiting for transfers between devices: 0.01 us -> 15.4 us  [spread_part(): return lax.all_to_all(copies, ('zlo', 'x'), 0, 0, tiled=True)]
  transfers between devices with their start and end apart: 82 -> 82, of which waited for: 30 -> 31; matrix products, arithmetic and copies ran while one was open for 30% -> 30% of each run, Pallas kernels for 0% -> 0%
where the time goes in v8:
time: 525 us; the launch traced here: 515 us
  waiting for transfers between devices  152 us (29%)
  starting transfers between devices  148 us (28%)
  matrix products  78.1 us (15%)
  other arithmetic  75.8 us (14%)
  local copies, waits for them, and re-layouts  42.9 us (8%)
  between operations  18 us (3%)
    ppermute x51, starting transfers between devices, around(): lax.ppermute(block, axis, [(i, (i + distance) % count) for i in range(cou...  87.5 us
    ppermute x51, waiting for transfers between devices, around(): lax.ppermute(block, axis, [(i, (i + distance) % count) for i in range(cou...  73.8 us
    all_to_all x2, waiting for transfers between devices, reduce_part_now(): pieces = lax.all_to_all(grads, ('zlo', 'x'), 0, 0, tiled=True)  26.3 us
    ppermute x15, starting transfers between devices, swap_core(): return lax.ppermute(block, 'core', [(0, 1), (1, 0)])  26.3 us
    dot_general x16, matrix products, contract_rows(): lax.dot_general(left_rows, right_rows, (((0,), (0,)), ((), ())), preferre...  24.1 us
    ppermute x4, waiting for transfers between devices, swap_section(): return lax.ppermute(block, 'section', [(0, 1), (1, 0)])  21.5 us
    unnamed x413, local copies, waits for them, and re-layouts  18.9 us
    all_to_all x2, waiting for transfers between devices, spread_part(): return lax.all_to_all(copies, ('zlo', 'x'), 0, 0, tiled=True)  15.4 us
  transfers between devices with their start and end apart: 82, of which 31 were waited for; matrix products, arithmetic and copies ran while one was open for 30% of the time, Pallas kernels for 0%

profile of v8, /device:TPU:1, one launch (start us, length us, event | category | flops | bytes accessed | tf_op | source)
XLA Modules:
  0.0 515.2 jit_solution(10587809001452863686)
XLA Ops:
  12.3 3.8 collective-permute-start.4
  23.7 2.7 collective-permute-start.31
  28.4 3.6 collective-permute-done.31
  34.4 4.4 collective-permute-done.3
  46.4 4.8 collective-permute-start.5
  60.6 2.9 collective-permute-start.8
  69.9 5.2 %collective-permute-done.9 = bf16[128,1024]{1,0:T(8,128)(2,1)S(1)} collective-permute-done((bf16[128,1024]{1,0:T(8,128)(2,1)S(1)}, bf16[128,1024]{1,0:T(8,128)(2,1)S(1)}, u32[]{:S(2)}, u32[]{:S(2)}) %collective-permute-start.9) | collective-permute-done | bytes 262176 | tf_op jit(solution)/shard_map/ppermute | solution.py:19
  79.5 3.2 collective-permute-start.11
  84.2 9.1 %collective-permute-done.15 = bf16[328,1024]{1,0:T(8,128)(2,1)S(1)} collective-permute-done((bf16[328,1024]{1,0:T(8,128)(2,1)S(1)}, bf16[328,1024]{1,0:T(8,128)(2,1)S(1)}, u32[]{:S(2)}, u32[]{:S(2)}) %collective-permute-start.15) | collective-permute-done | bytes 671776 | tf_op jit(solution)/shard_map/ppermute | solution.py:31
  95.4 2.6 collective-permute-start.16
  98.0 2.7 fusion.178
  104.9 11.2 %collective-permute-done.18 = bf16[128,1024]{1,0:T(8,128)(2,1)S(1)} collective-permute-done((bf16[128,1024]{1,0:T(8,128)(2,1)S(1)}, bf16[128,1024]{1,0:T(8,128)(2,1)S(1)}, u32[]{:S(2)}, u32[]{:S(2)}) %collective-permute-start.18) | collective-permute-done | bytes 262176 | tf_op jit(solution)/shard_map/ppermute | solution.py:19
  120.7 3.0 multiply_convert_fusion.5
  132.9 2.6 collective-permute-done.21
  135.5 4.6 collective-permute-done.22
  147.8 3.3 collective-permute-done.24
  152.6 4.3 collective-permute-done.25
  166.6 7.4 %collective-permute-done.27 = bf16[128,1024]{1,0:T(8,128)(2,1)S(1)} collective-permute-done((bf16[128,1024]{1,0:T(8,128)(2,1)S(1)}, bf16[128,1024]{1,0:T(8,128)(2,1)S(1)}, u32[]{:S(2)}, u32[]{:S(2)}) %collective-permute-start.27) | collective-permute-done | bytes 262176 | tf_op jit(solution)/shard_map/ppermute | solution.py:19
  174.8 2.9 collective-permute-start.29
  178.3 2.8 fusion.179
  200.0 6.2 %collective-permute-done.36 = bf16[128,1024]{1,0:T(8,128)(2,1)S(1)} collective-permute-done((bf16[128,1024]{1,0:T(8,128)(2,1)S(1)}, bf16[128,1024]{1,0:T(8,128)(2,1)S(1)}, u32[]{:S(2)}, u32[]{:S(2)}) %collective-permute-start.36) | collective-permute-done | bytes 262176 | tf_op jit(solution)/shard_map/ppermute | solution.py:19
  207.8 2.9 collective-permute-start.40
  216.3 3.5 collective-permute-start.45
  226.3 3.6 fusion.25
  237.9 4.2 collective-permute-start.41
  250.1 4.0 collective-permute-done.42
  260.6 3.6 collective-permute-start.48
  264.5 2.5 collective-permute-start.46
  285.5 3.6 collective-permute-start.49
  289.5 2.5 collective-permute-start.51
  295.7 5.8 %collective-permute-done.50 = bf16[128,1024]{1,0:T(8,128)(2,1)S(1)} collective-permute-done((bf16[128,1024]{1,0:T(8,128)(2,1)S(1)}, bf16[128,1024]{1,0:T(8,128)(2,1)S(1)}, u32[]{:S(2)}, u32[]{:S(2)}) %collective-permute-start.50) | collective-permute-done | bytes 262176 | tf_op jit(solution)/shard_map/ppermute | solution.py:19
  309.0 4.2 all-to-all-start
  315.4 14.3 %all-to-all-done = bf16[8,272,256]{2,1,0:T(8,128)(2,1)S(1)} async-done(((bf16[8,272,256]{2,1,0:T(8,128)(2,1)}), bf16[8,272,256]{2,1,0:T(8,128)(2,1)S(1)}, u32[]{:S(2)}, u32[]{:S(2)}) %all-to-all-start) | async-done | bytes 1114144 | tf_op jit(solution)/shard_map/all_to_all | solution.py:334
  330.6 3.3 collective-permute-start.56
  355.6 3.5 fusion.28
  367.6 2.6 collective-permute-start.62
  388.0 3.7 all-to-all-start.1
  396.1 12.0 %all-to-all-done.1 = bf16[8,272,256]{2,1,0:T(8,128)(2,1)S(1)} async-done(((bf16[8,272,256]{2,1,0:T(8,128)(2,1)}), bf16[8,272,256]{2,1,0:T(8,128)(2,1)S(1)}, u32[]{:S(2)}, u32[]{:S(2)}) %all-to-all-start.1) | async-done | bytes 1114144 | tf_op jit(solution)/shard_map/all_to_all | solution.py:334
  411.1 6.6 %all-to-all-start.2 = ((bf16[8,128,1024]{2,1,0:T(8,128)(2,1)}), bf16[8,128,1024]{2,1,0:T(8,128)(2,1)S(1)}, u32[]{:S(2)}, u32[]{:S(2)}) async-start(bf16[8,128,1024]{2,1,0:T(8,128)(2,1)} %broadcast_in_dim.219), calls=%async_computation.4 | async-start | bytes 4194304 | tf_op jit(solution)/shard_map/all_to_all | solution.py:341
  419.5 3.6 collective-permute-start.66
  428.3 4.5 collective-permute-start.65
  435.8 13.7 %collective-permute-done.65 = bf16[272,256]{1,0:T(8,128)(2,1)S(1)} collective-permute-done((bf16[272,256]{1,0:T(8,128)(2,1)S(1)}, bf16[272,256]{1,0:T(8,128)(2,1)S(1)}, u32[]{:S(2)}, u32[]{:S(2)}) %collective-permute-start.65) | collective-permute-done | bytes 139296 | tf_op jit(solution)/shard_map/ppermute | solution.py:27
  450.7 4.3 all-to-all-start.3
  456.2 15.4 %all-to-all-done.3 = bf16[8,272,256]{2,1,0:T(8,128)(2,1)} async-done(((bf16[8,272,256]{2,1,0:T(8,128)(2,1)}), bf16[8,272,256]{2,1,0:T(8,128)(2,1)}, u32[]{:S(2)}, u32[]{:S(2)}) %all-to-all-start.3) | async-done | bytes 1114144 | tf_op jit(solution)/shard_map/all_to_all | solution.py:341
  474.9 7.0 %collective-permute-done.69 = bf16[128,1024]{1,0:T(8,128)(2,1)S(1)} collective-permute-done((bf16[128,1024]{1,0:T(8,128)(2,1)S(1)}, bf16[128,1024]{1,0:T(8,128)(2,1)S(1)}, u32[]{:S(2)}, u32[]{:S(2)}) %collective-permute-start.69) | collective-permute-done | bytes 262176 | tf_op jit(solution)/shard_map/ppermute | solution.py:27
  487.1 3.5 collective-permute-start.73
  502.2 2.9 maximum_convert_fusion.2
  505.2 2.7 convert_bitcast_fusion
  (822 shorter events, 260.1 us)
Async XLA Ops:
  7.2 323.3 %reduce-scatter.3.cloned.1.call-start = ((), (), s32[]{:S(2)}) async-start(), calls=%async_computation.6 | async-start | bytes 2359296 | tf_op jit(solution)/shard_map/reduce_scatter | solution.py:330
  8.6 18.4 %collective-permute-start.1 = (bf16[128,1024]{1,0:T(8,128)(2,1)S(1)}, bf16[128,1024]{1,0:T(8,128)(2,1)S(1)}, u32[]{:S(2)}, u32[]{:S(2)}) collective-permute-start(bf16[128,1024]{1,0:T(8,128)(2,1)S(1)} %get-tuple-element.176), channel_id=1, source_target_pairs={{0,1},{1,2},{2,3},{3,0},{4,5},{5,6},{6,7},{7,4},{8,9},{9,10},{10,1... | collective-permute-start | bytes 786440 | tf_op jit(solution)/shard_map/ppermute | solution.py:19
  10.8 16.6 %collective-permute-start = (bf16[128,1024]{1,0:T(8,128)(2,1)S(1)}, bf16[128,1024]{1,0:T(8,128)(2,1)}, u32[]{:S(2)}, u32[]{:S(2)}) collective-permute-start(bf16[128,1024]{1,0:T(8,128)(2,1)S(1)} %get-tuple-element.176), channel_id=1, source_target_pairs={{0,3},{1,0},{2,1},{3,2},{4,7},{5,4},{6,5},{7,6},{8,11},{9,8},{10,9... | collective-permute-start | bytes 786440 | tf_op jit(solution)/shard_map/ppermute | solution.py:19
  12.3 11.4 %collective-permute-start.4 = (f32[2,1024]{1,0:T(2,128)}, f32[2,1024]{1,0:T(2,128)S(1)}, u32[]{:S(2)}, u32[]{:S(2)}) collective-permute-start(f32[2,1024]{1,0:T(2,128)} %bitcast.347), channel_id=1, source_target_pairs={{0,96},{32,64},{64,32},{96,0},{1,97},{33,65},{65,33},{97,1},{2,98}... | collective-permute-start | bytes 24584 | tf_op jit(solution)/shard_map/ppermute | solution.py:31
  19.9 18.8 %collective-permute-start.3 = (bf16[1536,256]{1,0:T(8,128)(2,1)}, bf16[1536,256]{1,0:T(8,128)(2,1)}, u32[]{:S(2)}, u32[]{:S(2)}) collective-permute-start(bf16[1536,256]{1,0:T(8,128)(2,1)} %constant_dynamic-slice_fusion.4), channel_id=1, source_target_pairs={{0,96},{32,64},{64,32},{96,0},{1,97},{33,65},{65,33},{97,1},{2,98}... | collective-permute-start | bytes 2359304 | tf_op jit(solution)/shard_map/ppermute | solution.py:31
  46.0 11.6 %collective-permute-start.6 = (bf16[128,1024]{1,0:T(8,128)(2,1)S(1)}, bf16[128,1024]{1,0:T(8,128)(2,1)S(1)}, u32[]{:S(2)}, u32[]{:S(2)}) collective-permute-start(bf16[128,1024]{1,0:T(8,128)(2,1)S(1)} %constant_dynamic-slice_fusion.2), channel_id=1, source_target_pairs={{0,96},{32,64},{64,32},{96,0},{1,97},{33,65},{65,33},{97,1},{2,98}... | collective-permute-start | bytes 786440 | tf_op jit(solution)/shard_map/ppermute | solution.py:31
  58.2 18.3 %collective-permute-start.13 = (bf16[328,1024]{1,0:T(8,128)(2,1)S(1)}, bf16[328,1024]{1,0:T(8,128)(2,1)S(1)}, u32[]{:S(2)}, u32[]{:S(2)}) collective-permute-start(bf16[328,1024]{1,0:T(8,128)(2,1)S(1)} %constant_dynamic-slice_fusion.1), channel_id=1, source_target_pairs={{0,96},{32,64},{64,32},{96,0},{1,97},{33,65},{65,33},{97,1},{2,98}... | collective-permute-start | bytes 2015240 | tf_op jit(solution)/shard_map/ppermute | solution.py:31
  76.7 16.7 %collective-permute-start.15 = (bf16[328,1024]{1,0:T(8,128)(2,1)S(1)}, bf16[328,1024]{1,0:T(8,128)(2,1)S(1)}, u32[]{:S(2)}, u32[]{:S(2)}) collective-permute-start(bf16[328,1024]{1,0:T(8,128)(2,1)S(1)} %constant_dynamic-slice_fusion), channel_id=1, source_target_pairs={{0,96},{32,64},{64,32},{96,0},{1,97},{33,65},{65,33},{97,1},{2,98}... | collective-permute-start | bytes 2015240 | tf_op jit(solution)/shard_map/ppermute | solution.py:31
  79.2 21.5 %collective-permute-start.12 = (bf16[128,1024]{1,0:T(8,128)(2,1)S(1)}, bf16[128,1024]{1,0:T(8,128)(2,1)S(1)}, u32[]{:S(2)}, u32[]{:S(2)}) collective-permute-start(bf16[128,1024]{1,0:T(8,128)(2,1)S(1)} %multiply_convert_fusion.7), channel_id=1, source_target_pairs={{0,1},{1,2},{2,3},{3,0},{4,5},{5,6},{6,7},{7,4},{8,9},{9,10},{10,1... | collective-permute-start | bytes 786440 | tf_op jit(solution)/shard_map/ppermute | solution.py:19
  79.5 22.1 %collective-permute-start.11 = (bf16[128,1024]{1,0:T(8,128)(2,1)S(1)}, bf16[128,1024]{1,0:T(8,128)(2,1)S(1)}, u32[]{:S(2)}, u32[]{:S(2)}) collective-permute-start(bf16[128,1024]{1,0:T(8,128)(2,1)S(1)} %multiply_convert_fusion.7), channel_id=1, source_target_pairs={{0,3},{1,0},{2,1},{3,2},{4,7},{5,4},{6,5},{7,6},{8,11},{9,8},{10,9... | collective-permute-start | bytes 786440 | tf_op jit(solution)/shard_map/ppermute | solution.py:19
  82.7 22.1 %collective-permute-start.14 = (bf16[328,1024]{1,0:T(8,128)(2,1)S(1)}, bf16[328,1024]{1,0:T(8,128)(2,1)S(1)}, u32[]{:S(2)}, u32[]{:S(2)}) collective-permute-start(bf16[328,1024]{1,0:T(8,128)(2,1)S(1)} %collective-permute-done.13), channel_id=1, source_target_pairs={{0,4},{4,0},{1,5},{5,1},{2,6},{6,2},{3,7},{7,3},{8,12},{12,8},{9,1... | collective-permute-start | bytes 2015240 | tf_op jit(solution)/shard_map/ppermute | solution.py:23
  93.4 22.7 %collective-permute-start.17 = (bf16[328,1024]{1,0:T(8,128)(2,1)S(1)}, bf16[328,1024]{1,0:T(8,128)(2,1)S(1)}, u32[]{:S(2)}, u32[]{:S(2)}) collective-permute-start(bf16[328,1024]{1,0:T(8,128)(2,1)S(1)} %constant_dynamic-slice_fusion.3), channel_id=1, source_target_pairs={{0,96},{32,64},{64,32},{96,0},{1,97},{33,65},{65,33},{97,1},{2,98}... | collective-permute-start | bytes 2015240 | tf_op jit(solution)/shard_map/ppermute | solution.py:31
  95.4 21.9 %collective-permute-start.16 = (bf16[328,1024]{1,0:T(8,128)(2,1)S(1)}, bf16[328,1024]{1,0:T(8,128)(2,1)S(1)}, u32[]{:S(2)}, u32[]{:S(2)}) collective-permute-start(bf16[328,1024]{1,0:T(8,128)(2,1)S(1)} %collective-permute-done.15), channel_id=1, source_target_pairs={{0,4},{4,0},{1,5},{5,1},{2,6},{6,2},{3,7},{7,3},{8,12},{12,8},{9,1... | collective-permute-start | bytes 2015240 | tf_op jit(solution)/shard_map/ppermute | solution.py:23
  100.7 91.1 %collective-permute-start.34 = (bf16[128,1024]{1,0:T(8,128)(2,1)}, bf16[128,1024]{1,0:T(8,128)(2,1)S(1)}, u32[]{:S(2)}, u32[]{:S(2)}) collective-permute-start(bf16[128,1024]{1,0:T(8,128)(2,1)} %select_bitcast_fusion.4), channel_id=1, source_target_pairs={{0,2},{1,3},{2,0},{3,1},{4,6},{5,7},{6,4},{7,5},{8,10},{9,11},{10,... | collective-permute-start | bytes 786440 | tf_op jit(solution)/shard_map/ppermute | solution.py:19
  101.6 14.5 %collective-permute-start.18 = (bf16[128,1024]{1,0:T(8,128)(2,1)S(1)}, bf16[128,1024]{1,0:T(8,128)(2,1)S(1)}, u32[]{:S(2)}, u32[]{:S(2)}) collective-permute-start(bf16[128,1024]{1,0:T(8,128)(2,1)S(1)} %multiply_convert_fusion.7), channel_id=1, source_target_pairs={{0,2},{1,3},{2,0},{3,1},{4,6},{5,7},{6,4},{7,5},{8,10},{9,11},{10,... | collective-permute-start | bytes 786440 | tf_op jit(solution)/shard_map/ppermute | solution.py:19
  126.5 13.7 %collective-permute-start.22 = (bf16[128,1024]{1,0:T(8,128)(2,1)S(1)}, bf16[128,1024]{1,0:T(8,128)(2,1)S(1)}, u32[]{:S(2)}, u32[]{:S(2)}) collective-permute-start(bf16[128,1024]{1,0:T(8,128)(2,1)S(1)} %get-tuple-element.258), channel_id=1, source_target_pairs={{0,3},{1,0},{2,1},{3,2},{4,7},{5,4},{6,5},{7,6},{8,11},{9,8},{10,9... | collective-permute-start | bytes 786440 | tf_op jit(solution)/shard_map/ppermute | solution.py:19
  194.1 12.1 %collective-permute-start.36 = (bf16[128,1024]{1,0:T(8,128)(2,1)S(1)}, bf16[128,1024]{1,0:T(8,128)(2,1)S(1)}, u32[]{:S(2)}, u32[]{:S(2)}) collective-permute-start(bf16[128,1024]{1,0:T(8,128)(2,1)S(1)} %get-tuple-element.253), channel_id=1, source_target_pairs={{0,1},{1,2},{2,3},{3,0},{4,5},{5,6},{6,7},{7,4},{8,9},{9,10},{10,1... | collective-permute-start | bytes 786440 | tf_op jit(solution)/shard_map/ppermute | solution.py:19
  195.1 11.1 %collective-permute-start.37 = (bf16[128,1024]{1,0:T(8,128)(2,1)S(1)}, bf16[128,1024]{1,0:T(8,128)(2,1)S(1)}, u32[]{:S(2)}, u32[]{:S(2)}) collective-permute-start(bf16[128,1024]{1,0:T(8,128)(2,1)S(1)} %get-tuple-element.254), channel_id=1, source_target_pairs={{0,3},{1,0},{2,1},{3,2},{4,7},{5,4},{6,5},{7,6},{8,11},{9,8},{10,9... | collective-permute-start | bytes 786440 | tf_op jit(solution)/shard_map/ppermute | solution.py:19
  207.8 14.8 %collective-permute-start.40 = (bf16[128,1024]{1,0:T(8,128)(2,1)S(1)}, bf16[128,1024]{1,0:T(8,128)(2,1)S(1)}, u32[]{:S(2)}, u32[]{:S(2)}) collective-permute-start(bf16[128,1024]{1,0:T(8,128)(2,1)S(1)} %get-tuple-element.183), channel_id=1, source_target_pairs={{0,2},{1,3},{2,0},{3,1},{4,6},{5,7},{6,4},{7,5},{8,10},{9,11},{10,... | collective-permute-start | bytes 786440 | tf_op jit(solution)/shard_map/ppermute | solution.py:19
  210.8 11.1 %collective-permute-start.39 = (bf16[128,1024]{1,0:T(8,128)(2,1)S(1)}, bf16[128,1024]{1,0:T(8,128)(2,1)S(1)}, u32[]{:S(2)}, u32[]{:S(2)}) collective-permute-start(bf16[128,1024]{1,0:T(8,128)(2,1)S(1)} %get-tuple-element.183), channel_id=1, source_target_pairs={{0,1},{1,2},{2,3},{3,0},{4,5},{5,6},{6,7},{7,4},{8,9},{9,10},{10,1... | collective-permute-start | bytes 786440 | tf_op jit(solution)/shard_map/ppermute | solution.py:19
  211.2 10.7 %collective-permute-start.38 = (bf16[128,1024]{1,0:T(8,128)(2,1)S(1)}, bf16[128,1024]{1,0:T(8,128)(2,1)S(1)}, u32[]{:S(2)}, u32[]{:S(2)}) collective-permute-start(bf16[128,1024]{1,0:T(8,128)(2,1)S(1)} %get-tuple-element.183), channel_id=1, source_target_pairs={{0,3},{1,0},{2,1},{3,2},{4,7},{5,4},{6,5},{7,6},{8,11},{9,8},{10,9... | collective-permute-start | bytes 786440 | tf_op jit(solution)/shard_map/ppermute | solution.py:19
  216.3 40.0 %collective-permute-start.45 = (bf16[328,1024]{1,0:T(8,128)(2,1)}, bf16[328,1024]{1,0:T(8,128)(2,1)}, u32[]{:S(2)}, u32[]{:S(2)}) collective-permute-start(bf16[328,1024]{1,0:T(8,128)(2,1)} %convolution_convert_fusion.11), channel_id=1, source_target_pairs={{0,4},{4,0},{1,5},{5,1},{2,6},{6,2},{3,7},{7,3},{8,12},{12,8},{9,1... | collective-permute-start | bytes 2015240 | tf_op jit(solution)/shard_map/ppermute | solution.py:23
  237.9 12.2 %collective-permute-start.41 = (bf16[128,1024]{1,0:T(8,128)(2,1)S(1)}, bf16[128,1024]{1,0:T(8,128)(2,1)S(1)}, u32[]{:S(2)}, u32[]{:S(2)}) collective-permute-start(bf16[128,1024]{1,0:T(8,128)(2,1)S(1)} %convolution_convert_fusion.18), channel_id=1, source_target_pairs={{0,2},{1,3},{2,0},{3,1},{4,6},{5,7},{6,4},{7,5},{8,10},{9,11},{10,... | collective-permute-start | bytes 786440 | tf_op jit(solution)/shard_map/ppermute | solution.py:19
  243.0 11.0 %collective-permute-start.42 = (bf16[128,1024]{1,0:T(8,128)(2,1)S(1)}, bf16[128,1024]{1,0:T(8,128)(2,1)S(1)}, u32[]{:S(2)}, u32[]{:S(2)}) collective-permute-start(bf16[128,1024]{1,0:T(8,128)(2,1)S(1)} %get-tuple-element.251), channel_id=1, source_target_pairs={{0,1},{1,2},{2,3},{3,0},{4,5},{5,6},{6,7},{7,4},{8,9},{9,10},{10,1... | collective-permute-start | bytes 786440 | tf_op jit(solution)/shard_map/ppermute | solution.py:19
  246.9 11.0 %collective-permute-start.44 = (bf16[656,1024]{1,0:T(8,128)(2,1)S(1)}, bf16[656,1024]{1,0:T(8,128)(2,1)S(1)}, u32[]{:S(2)}, u32[]{:S(2)}) collective-permute-start(bf16[656,1024]{1,0:T(8,128)(2,1)S(1)} %convolution_convert_fusion.1), channel_id=1, source_target_pairs={{0,4},{4,0},{1,5},{5,1},{2,6},{6,2},{3,7},{7,3},{8,12},{12,8},{9,1... | collective-permute-start | bytes 4030472 | tf_op jit(solution)/shard_map/ppermute | solution.py:23
  260.6 21.8 %collective-permute-start.48 = (bf16[128,1024]{1,0:T(8,128)(2,1)}, bf16[128,1024]{1,0:T(8,128)(2,1)}, u32[]{:S(2)}, u32[]{:S(2)}) collective-permute-start(bf16[128,1024]{1,0:T(8,128)(2,1)} %add_convert_fusion.9), channel_id=1, source_target_pairs={{0,2},{1,3},{2,0},{3,1},{4,6},{5,7},{6,4},{7,5},{8,10},{9,11},{10,... | collective-permute-start | bytes 786440 | tf_op jit(solution)/shard_map/ppermute | solution.py:19
  264.2 13.0 %collective-permute-start.47 = (bf16[128,1024]{1,0:T(8,128)(2,1)}, bf16[128,1024]{1,0:T(8,128)(2,1)}, u32[]{:S(2)}, u32[]{:S(2)}) collective-permute-start(bf16[128,1024]{1,0:T(8,128)(2,1)} %add_convert_fusion.9), channel_id=1, source_target_pairs={{0,1},{1,2},{2,3},{3,0},{4,5},{5,6},{6,7},{7,4},{8,9},{9,10},{10,1... | collective-permute-start | bytes 786440 | tf_op jit(solution)/shard_map/ppermute | solution.py:19
  264.5 11.7 %collective-permute-start.46 = (bf16[128,1024]{1,0:T(8,128)(2,1)}, bf16[128,1024]{1,0:T(8,128)(2,1)}, u32[]{:S(2)}, u32[]{:S(2)}) collective-permute-start(bf16[128,1024]{1,0:T(8,128)(2,1)} %add_convert_fusion.9), channel_id=1, source_target_pairs={{0,3},{1,0},{2,1},{3,2},{4,7},{5,4},{6,5},{7,6},{8,11},{9,8},{10,9... | collective-permute-start | bytes 786440 | tf_op jit(solution)/shard_map/ppermute | solution.py:19
  272.5 31.6 %collective-permute-start.52 = (bf16[1024,256]{1,0:T(8,128)(2,1)}, bf16[1024,256]{1,0:T(8,128)(2,1)}, u32[]{:S(2)}, u32[]{:S(2)}) collective-permute-start(bf16[1024,256]{1,0:T(8,128)(2,1)} %convolution_convert_fusion.15), channel_id=1, source_target_pairs={{0,4},{4,0},{1,5},{5,1},{2,6},{6,2},{3,7},{7,3},{8,12},{12,8},{9,1... | collective-permute-start | bytes 1572872 | tf_op jit(solution)/shard_map/ppermute | solution.py:23
  289.2 12.2 %collective-permute-start.50 = (bf16[128,1024]{1,0:T(8,128)(2,1)S(1)}, bf16[128,1024]{1,0:T(8,128)(2,1)S(1)}, u32[]{:S(2)}, u32[]{:S(2)}) collective-permute-start(bf16[128,1024]{1,0:T(8,128)(2,1)S(1)} %get-tuple-element.249), channel_id=1, source_target_pairs={{0,1},{1,2},{2,3},{3,0},{4,5},{5,6},{6,7},{7,4},{8,9},{9,10},{10,1... | collective-permute-start | bytes 786440 | tf_op jit(solution)/shard_map/ppermute | solution.py:19
  289.5 11.9 %collective-permute-start.51 = (bf16[128,1024]{1,0:T(8,128)(2,1)S(1)}, bf16[128,1024]{1,0:T(8,128)(2,1)S(1)}, u32[]{:S(2)}, u32[]{:S(2)}) collective-permute-start(bf16[128,1024]{1,0:T(8,128)(2,1)S(1)} %get-tuple-element.250), channel_id=1, source_target_pairs={{0,3},{1,0},{2,1},{3,2},{4,7},{5,4},{6,5},{7,6},{8,11},{9,8},{10,9... | collective-permute-start | bytes 786440 | tf_op jit(solution)/shard_map/ppermute | solution.py:19
  293.4 12.5 %collective-permute-start.53 = (bf16[1024,256]{1,0:T(8,128)(2,1)}, bf16[1024,256]{1,0:T(8,128)(2,1)}, u32[]{:S(2)}, u32[]{:S(2)}) collective-permute-start(bf16[1024,256]{1,0:T(8,128)(2,1)} %convolution_convert_fusion.14), channel_id=1, source_target_pairs={{0,4},{4,0},{1,5},{5,1},{2,6},{6,2},{3,7},{7,3},{8,12},{12,8},{9,1... | collective-permute-start | bytes 1572872 | tf_op jit(solution)/shard_map/ppermute | solution.py:23
  309.0 20.7 %all-to-all-start = ((bf16[8,272,256]{2,1,0:T(8,128)(2,1)}), bf16[8,272,256]{2,1,0:T(8,128)(2,1)S(1)}, u32[]{:S(2)}, u32[]{:S(2)}) async-start(bf16[8,272,256]{2,1,0:T(8,128)(2,1)} %bitcast.68), calls=%async_computation.1 | async-start | bytes 2228224 | tf_op jit(solution)/shard_map/all_to_all | solution.py:334
  313.2 80.8 %reduce-scatter.5.cloned.1.call-start = ((), (), s32[]{:S(2)}) async-start(), calls=%async_computation.7 | async-start | bytes 2359296 | tf_op jit(solution)/shard_map/reduce_scatter | solution.py:330
  330.6 16.5 %collective-permute-start.56 = (bf16[128,1024]{1,0:T(8,128)(2,1)S(1)}, bf16[128,1024]{1,0:T(8,128)(2,1)S(1)}, u32[]{:S(2)}, u32[]{:S(2)}) collective-permute-start(bf16[128,1024]{1,0:T(8,128)(2,1)S(1)} %convert_element_type.627), channel_id=1, source_target_pairs={{0,2},{1,3},{2,0},{3,1},{4,6},{5,7},{6,4},{7,5},{8,10},{9,11},{10,... | collective-permute-start | bytes 786440 | tf_op jit(solution)/shard_map/ppermute | solution.py:19
  333.9 12.4 %collective-permute-start.55 = (bf16[128,1024]{1,0:T(8,128)(2,1)S(1)}, bf16[128,1024]{1,0:T(8,128)(2,1)S(1)}, u32[]{:S(2)}, u32[]{:S(2)}) collective-permute-start(bf16[128,1024]{1,0:T(8,128)(2,1)S(1)} %convert_element_type.627), channel_id=1, source_target_pairs={{0,1},{1,2},{2,3},{3,0},{4,5},{5,6},{6,7},{7,4},{8,9},{9,10},{10,1... | collective-permute-start | bytes 786440 | tf_op jit(solution)/shard_map/ppermute | solution.py:19
  334.2 12.1 %collective-permute-start.54 = (bf16[128,1024]{1,0:T(8,128)(2,1)S(1)}, bf16[128,1024]{1,0:T(8,128)(2,1)S(1)}, u32[]{:S(2)}, u32[]{:S(2)}) collective-permute-start(bf16[128,1024]{1,0:T(8,128)(2,1)S(1)} %convert_element_type.627), channel_id=1, source_target_pairs={{0,3},{1,0},{2,1},{3,2},{4,7},{5,4},{6,5},{7,6},{8,11},{9,8},{10,9... | collective-permute-start | bytes 786440 | tf_op jit(solution)/shard_map/ppermute | solution.py:19
  367.6 12.9 %collective-permute-start.62 = (bf16[128,1024]{1,0:T(8,128)(2,1)}, bf16[128,1024]{1,0:T(8,128)(2,1)}, u32[]{:S(2)}, u32[]{:S(2)}) collective-permute-start(bf16[128,1024]{1,0:T(8,128)(2,1)} %get-tuple-element.344), channel_id=1, source_target_pairs={{0,2},{1,3},{2,0},{3,1},{4,6},{5,7},{6,4},{7,5},{8,10},{9,11},{10,... | collective-permute-start | bytes 786440 | tf_op jit(solution)/shard_map/ppermute | solution.py:19
  388.0 20.1 %all-to-all-start.1 = ((bf16[8,272,256]{2,1,0:T(8,128)(2,1)}), bf16[8,272,256]{2,1,0:T(8,128)(2,1)S(1)}, u32[]{:S(2)}, u32[]{:S(2)}) async-start(bf16[8,272,256]{2,1,0:T(8,128)(2,1)} %bitcast.85), calls=%async_computation.2 | async-start | bytes 2228224 | tf_op jit(solution)/shard_map/all_to_all | solution.py:334
  394.0 14.3 %collective-permute-start.61 = (bf16[128,1024]{1,0:T(8,128)(2,1)S(1)}, bf16[128,1024]{1,0:T(8,128)(2,1)}, u32[]{:S(2)}, u32[]{:S(2)}) collective-permute-start(bf16[128,1024]{1,0:T(8,128)(2,1)S(1)} %broadcast_select_fusion.24), channel_id=1, source_target_pairs={{0,64},{64,0},{1,65},{65,1},{2,66},{66,2},{3,67},{67,3},{4,68},{68... | collective-permute-start | bytes 786440 | tf_op jit(solution)/shard_map/ppermute | solution.py:27
  411.1 38.5 %all-to-all-start.2 = ((bf16[8,128,1024]{2,1,0:T(8,128)(2,1)}), bf16[8,128,1024]{2,1,0:T(8,128)(2,1)S(1)}, u32[]{:S(2)}, u32[]{:S(2)}) async-start(bf16[8,128,1024]{2,1,0:T(8,128)(2,1)} %broadcast_in_dim.219), calls=%async_computation.4 | async-start | bytes 4194304 | tf_op jit(solution)/shard_map/all_to_all | solution.py:341
  419.5 13.3 %collective-permute-start.66 = (bf16[128,1024]{1,0:T(8,128)(2,1)S(1)}, bf16[128,1024]{1,0:T(8,128)(2,1)S(1)}, u32[]{:S(2)}, u32[]{:S(2)}) collective-permute-start(bf16[128,1024]{1,0:T(8,128)(2,1)S(1)} %convolution_convert_fusion.16), channel_id=1, source_target_pairs={{0,2},{1,3},{2,0},{3,1},{4,6},{5,7},{6,4},{7,5},{8,10},{9,11},{10,... | collective-permute-start | bytes 786440 | tf_op jit(solution)/shard_map/ppermute | solution.py:19
  428.3 21.3 %collective-permute-start.65 = (bf16[272,256]{1,0:T(8,128)(2,1)S(1)}, bf16[272,256]{1,0:T(8,128)(2,1)S(1)}, u32[]{:S(2)}, u32[]{:S(2)}) collective-permute-start(bf16[272,256]{1,0:T(8,128)(2,1)S(1)} %broadcast_select_fusion.25), channel_id=1, source_target_pairs={{0,64},{64,0},{1,65},{65,1},{2,66},{66,2},{3,67},{67,3},{4,68},{68... | collective-permute-start | bytes 417800 | tf_op jit(solution)/shard_map/ppermute | solution.py:27
  450.7 20.9 %all-to-all-start.3 = ((bf16[8,272,256]{2,1,0:T(8,128)(2,1)}), bf16[8,272,256]{2,1,0:T(8,128)(2,1)}, u32[]{:S(2)}, u32[]{:S(2)}) async-start(bf16[8,272,256]{2,1,0:T(8,128)(2,1)} %broadcast_in_dim.220), calls=%async_computation.5 | async-start | bytes 2228224 | tf_op jit(solution)/shard_map/all_to_all | solution.py:341
  455.7 18.6 %collective-permute-start.70 = (bf16[128,1024]{1,0:T(8,128)(2,1)}, bf16[128,1024]{1,0:T(8,128)(2,1)S(1)}, u32[]{:S(2)}, u32[]{:S(2)}) collective-permute-start(bf16[128,1024]{1,0:T(8,128)(2,1)} %broadcast_select_fusion.22), channel_id=1, source_target_pairs={{0,64},{64,0},{1,65},{65,1},{2,66},{66,2},{3,67},{67,3},{4,68},{68... | collective-permute-start | bytes 786440 | tf_op jit(solution)/shard_map/ppermute | solution.py:27
  471.6 13.1 %collective-permute-start.71 = (bf16[2176,256]{1,0:T(8,128)(2,1)}, bf16[2176,256]{1,0:T(8,128)(2,1)S(1)}, u32[]{:S(2)}, u32[]{:S(2)}) collective-permute-start(bf16[2176,256]{1,0:T(8,128)(2,1)} %bitcast.87), channel_id=1, source_target_pairs={{0,4},{4,0},{1,5},{5,1},{2,6},{6,2},{3,7},{7,3},{8,12},{12,8},{9,1... | collective-permute-start | bytes 3342344 | tf_op jit(solution)/shard_map/ppermute | solution.py:23
  473.2 24.7 %collective-permute-start.75 = (bf16[1024,1024]{1,0:T(8,128)(2,1)S(1)}, bf16[1024,1024]{1,0:T(8,128)(2,1)}, u32[]{:S(2)}, u32[]{:S(2)}) collective-permute-start(bf16[1024,1024]{1,0:T(8,128)(2,1)S(1)} %bitcast.283), channel_id=1, source_target_pairs={{0,4},{4,0},{1,5},{5,1},{2,6},{6,2},{3,7},{7,3},{8,12},{12,8},{9,1... | collective-permute-start | bytes 6291464 | tf_op jit(solution)/shard_map/ppermute | solution.py:23
  487.1 13.8 %collective-permute-start.73 = (f32[8,256]{1,0:T(8,128)S(1)}, f32[8,256]{1,0:T(8,128)S(1)}, u32[]{:S(2)}, u32[]{:S(2)}) collective-permute-start(f32[8,256]{1,0:T(8,128)S(1)} %convert_add_fusion.5), channel_id=1, source_target_pairs={{0,1},{1,2},{2,3},{3,0},{4,5},{5,6},{6,7},{7,4},{8,9},{9,10},{10,1... | collective-permute-start | bytes 24584 | tf_op jit(solution)/shard_map/ppermute | solution.py:19
  (231 other events, 2411.1 us)
Sparse Core Ops, SparseCore 0:
  268.8 35.4 reduce-scatter.2
  355.6 35.6 reduce-scatter.4

commit v9 on v8

--- a/solution.py
+++ b/solution.py
@@ -1,6 +1,10 @@
+import functools
+
 import jax
 import jax.numpy as jnp
 from jax import lax
+from jax.experimental import pallas as pl
+from jax.experimental.pallas import tpu as pltpu
 from jax.sharding import Mesh
 from jax.sharding import PartitionSpec as P
 
@@ -10,6 +14,8 @@
 epsilon = 1e-05
 bf16 = jnp.bfloat16
 f32 = jnp.float32
+
+BLOCK = 128
 
 DP = ("zlo", "x", "core")
 
@@ -78,32 +84,14 @@
     return (doc_ids, indices - starts)
 
 
-def rope_tables(positions, rope_base):
+def rope_tables(positions, rope_base, heads):
     half_dim = HEAD_DIM // 2
     inverse = rope_base ** (-2.0 * jnp.arange(half_dim, dtype=f32) / HEAD_DIM)
-    angles = positions.astype(f32)[..., None] * inverse
-    angles = jnp.concatenate([angles, angles], axis=-1)
-    return (jnp.cos(angles), jnp.sin(angles))
-
-
-def rotate(values, cosine_table, sine_table):
-    half_dim = values.shape[-1] // 2
-    turned = jnp.concatenate([-values[..., half_dim:], values[..., :half_dim]], axis=-1)
-    return values * cosine_table[..., None, :] + turned * sine_table[..., None, :]
-
-
-def rotate_back(gradients, cosine_table, sine_table):
-    half_dim = gradients.shape[-1] // 2
-    scaled = gradients * sine_table[..., None, :]
-    turned = jnp.concatenate([scaled[..., half_dim:], -scaled[..., :half_dim]], axis=-1)
-    return gradients * cosine_table[..., None, :] + turned
-
-
-def masked_scores(queries, keys_rot, allowed):
-    scores = jnp.einsum(
-        "qhd,khd->hqk", queries, keys_rot, preferred_element_type=f32
-    ) * HEAD_DIM ** (-0.5)
-    return jnp.where(allowed[None], scores, -1e30)
+    angles = positions.astype(f32)[:, None] * inverse
+    cosine, sine = jnp.cos(angles), jnp.sin(angles)
+    cosine = jnp.concatenate([cosine, cosine], axis=-1)
+    sine = jnp.concatenate([-sine, sine], axis=-1)
+    return (jnp.tile(cosine, (1, heads)), jnp.tile(sine, (1, heads)))
 
 
 def contract_rows(left_rows, right_rows):
@@ -126,46 +114,161 @@
     return jax.nn.gelu(first_half, approximate=False) * second_half
 
 
+def dot_nt(left, right):
+    return lax.dot_general(left, right, (((1,), (1,)), ((), ())), preferred_element_type=f32)
+
+
+def dot_tn(left, right):
+    return lax.dot_general(left, right, (((0,), (0,)), ((), ())), preferred_element_type=f32)
+
+
+def swap_halves(values):
+    width = values.shape[1]
+    lanes = lax.broadcasted_iota(jnp.int32, values.shape, 1)
+    up = pltpu.roll(values, width - HEAD_DIM // 2, 1)
+    down = pltpu.roll(values, HEAD_DIM // 2, 1)
+    return jnp.where(lanes % HEAD_DIM < HEAD_DIM // 2, up, down)
+
+
+def excluded_bias(marks_row, marks_col, start, windowed):
+    docs = marks_row[0:1, pl.ds(start, BLOCK)]
+    allowed = marks_col[:, 0:1] == docs
+    if windowed:
+        apart = marks_col[:, 1:2] - marks_row[1:2, pl.ds(start, BLOCK)]
+        allowed = allowed & (jnp.abs(apart) <= WINDOW // 2)
+    return jnp.where(allowed, 0.0, -1e30)
+
+
+def attend_kernel(
+    windowed,
+    near, far, w_qkv, w_out, cosine, sine, marks_row, marks_col,
+    queries, keys, values, logs, attended, near_term, far_term,
+    projected,
+):
+    near_rows = near.shape[0]
+    width = w_out.shape[0]
+    projected[:near_rows] = jnp.dot(near[...], w_qkv[...], preferred_element_type=f32)
+    projected[near_rows:] = jnp.dot(far[...], w_qkv[...], preferred_element_type=f32)
+    for index, target in ((0, queries), (1, keys)):
+        part = projected[:, index * width : (index + 1) * width]
+        turned = part * cosine[...] + swap_halves(part) * sine[...]
+        target[...] = turned.astype(bf16)
+    values[...] = projected[:, 2 * width :].astype(bf16)
+    heads = width // HEAD_DIM
+    lanes = lax.broadcasted_iota(jnp.int32, (BLOCK, width), 1) // HEAD_DIM
+
+    def step(index, carry):
+        start = pl.multiple_of(index * BLOCK, BLOCK)
+        bias = excluded_bias(marks_row, marks_col, start, windowed)
+        block = queries[pl.ds(start, BLOCK)] * jnp.asarray(HEAD_DIM ** (-0.5), bf16)
+        total = jnp.zeros((BLOCK, width), f32)
+        for head in range(heads):
+            own = jnp.where(lanes == head, block, jnp.zeros_like(block))
+            scores = dot_nt(keys[...], own) + bias
+            largest = jnp.max(scores, axis=0, keepdims=True)
+            powers = jnp.exp(scores - largest)
+            sums = jnp.sum(powers, axis=0, keepdims=True)
+            soft = (powers * (1.0 / sums)).astype(bf16)
+            logs[pl.ds(head, 1), pl.ds(start, BLOCK)] = largest + jnp.log(sums)
+            total = jnp.where(lanes == head, dot_tn(soft, values[...]), total)
+        attended[pl.ds(start, BLOCK)] = total.astype(bf16)
+        return carry
+
+    lax.fori_loop(0, queries.shape[0] // BLOCK, step, 0)
+    far_term[...] = jnp.dot(
+        attended[near_rows:], w_out[...], preferred_element_type=f32
+    ).astype(bf16)
+    near_term[...] = jnp.dot(
+        attended[:near_rows], w_out[...], preferred_element_type=f32
+    ).astype(bf16)
+
+
+def attend_back_kernel(
+    windowed,
+    near, far, w_qkv, w_out, cosine, sine, marks_row, marks_col,
+    queries, keys, values, logs,
+    grad_projected, near_term, far_term,
+    grad_attended, grad_queries, grad_keys, grad_values,
+):
+    near_rows = near.shape[0]
+    width = w_out.shape[0]
+    grad_attended[:near_rows] = dot_nt(near[...], w_out[...]).astype(bf16)
+    grad_attended[near_rows:] = dot_nt(far[...], w_out[...]).astype(bf16)
+    grad_keys[...] = jnp.zeros_like(grad_keys)
+    grad_values[...] = jnp.zeros_like(grad_values)
+    heads = width // HEAD_DIM
+    lanes = lax.broadcasted_iota(jnp.int32, (BLOCK, width), 1) // HEAD_DIM
+    all_lanes = lax.broadcasted_iota(jnp.int32, queries.shape, 1) // HEAD_DIM
+
+    def step(index, carry):
+        start = pl.multiple_of(index * BLOCK, BLOCK)
+        bias = excluded_bias(marks_row, marks_col, start, windowed)
+        block = queries[pl.ds(start, BLOCK)] * jnp.asarray(HEAD_DIM ** (-0.5), bf16)
+        grad_block = grad_attended[pl.ds(start, BLOCK)]
+        total = jnp.zeros((BLOCK, width), f32)
+        more_keys = jnp.zeros(queries.shape, f32)
+        more_values = jnp.zeros(queries.shape, f32)
+        for head in range(heads):
+            own = jnp.where(lanes == head, block, jnp.zeros_like(block))
+            own_grad = jnp.where(lanes == head, grad_block, jnp.zeros_like(grad_block))
+            scores = dot_nt(keys[...], own) + bias
+            soft = jnp.exp(scores - logs[pl.ds(head, 1), pl.ds(start, BLOCK)])
+            grad_soft = dot_nt(values[...], own_grad)
+            dots = jnp.sum(soft * grad_soft, axis=0, keepdims=True)
+            grad_scores = (soft * (grad_soft - dots)).astype(bf16)
+            more_values += jnp.dot(soft.astype(bf16), own_grad, preferred_element_type=f32)
+            more_keys += jnp.dot(grad_scores, own, preferred_element_type=f32)
+            total = jnp.where(lanes == head, dot_tn(grad_scores, keys[...]), total)
+        grad_queries[pl.ds(start, BLOCK)] = total * HEAD_DIM ** (-0.5)
+        grad_keys[...] += more_keys
+        grad_values[...] += more_values
+        return carry
+
+    lax.fori_loop(0, queries.shape[0] // BLOCK, step, 0)
+    for index, source in ((0, grad_queries), (1, grad_keys)):
+        part = source[...]
+        back = part * cosine[...] - swap_halves(part) * sine[...]
+        grad_projected[:, index * width : (index + 1) * width] = back.astype(bf16)
+    grad_projected[:, 2 * width :] = grad_values[...].astype(bf16)
+    far_term[...] = dot_nt(grad_projected[near_rows:], w_qkv[...]).astype(bf16)
+    near_term[...] = dot_nt(grad_projected[:near_rows], w_qkv[...]).astype(bf16)
+
+
+def whole_call(kernel, out_shapes, scratch_shapes, flops, *operands):
+    whole = pl.BlockSpec(memory_space=pltpu.VMEM)
+    return pl.pallas_call(
+        kernel,
+        out_shape=[jax.ShapeDtypeStruct(*shape) for shape in out_shapes],
+        in_specs=[whole] * len(operands),
+        out_specs=[whole] * len(out_shapes),
+        scratch_shapes=scratch_shapes,
+        compiler_params=pltpu.CompilerParams(vmem_limit_bytes=40 * 1024 * 1024),
+        cost_estimate=pl.CostEstimate(flops=flops, bytes_accessed=8 << 20, transcendentals=1 << 20),
+    )(*operands)
+
+
 def in_turn(work, parts):
     first = work(0, parts[0])
     return first, work(1, after_all(parts[1], first))
 
 
 def forward_layer(inputs, normed_parts, gain_mid, weights, allowed, tables, late, points):
-    w_qkv = weights[0]
-    row_count = inputs.shape[0]
-    local_width = w_qkv.shape[1] // 3
-    spans = (slice(0, 3 * row_count), slice(3 * row_count, 4 * row_count))
-
-    def project(k, part):
-        projected = times(part, w_qkv).reshape(part.shape[0], 3, -1, HEAD_DIM)
-        turns = (tables[0][spans[k]], tables[1][spans[k]])
-        return (
-            rotate(projected[:, 0], *turns).astype(bf16),
-            rotate(projected[:, 1], *turns).astype(bf16),
-            projected[:, 2].astype(bf16),
-        )
-
-    near, far = in_turn(project, normed_parts)
-    queries = (near[0], far[0])
-    keys_all = joined([near[1], far[1]])
-    values_all = joined([near[2], far[2]])
-    points[0](values_all)
-    w_out = weights[1]
-
-    def attend(k, own_queries):
-        scores = masked_scores(own_queries, keys_all, allowed[spans[k]])
-        largest = jnp.max(scores, axis=2, keepdims=True)
-        exp_scores = jnp.exp(scores - largest)
-        totals = jnp.sum(exp_scores, axis=2, keepdims=True)
-        soft_weights = (exp_scores / totals).astype(bf16)
-        mixed = jnp.einsum("hqk,khd->qhd", soft_weights, values_all, preferred_element_type=f32)
-        mixed = mixed.reshape(own_queries.shape[0], local_width).astype(bf16)
-        return largest + jnp.log(totals), mixed, times(mixed, w_out).astype(bf16)
-
-    far_logs, far_mixed, far_term = attend(1, queries[1])
+    w_qkv, w_out = weights[0], weights[1]
+    near_rows, model_width = normed_parts[0].shape
+    far_rows = normed_parts[1].shape[0]
+    full_rows = near_rows + far_rows
+    width = w_out.shape[0]
+    windowed, marks_row, marks_col = allowed
+    queries, keys, values, logs, attended, near_term, far_term = whole_call(
+        functools.partial(attend_kernel, windowed),
+        [((full_rows, width), bf16)] * 3
+        + [((8, full_rows), f32), ((full_rows, width), bf16)]
+        + [((near_rows, model_width), bf16), ((far_rows, model_width), bf16)],
+        [pltpu.VMEM((full_rows, 3 * width), f32)],
+        3 << 30,
+        *normed_parts, w_qkv, w_out, *tables, marks_row, marks_col,
+    )
     points[1](far_term)
-    near_logs, near_mixed, near_term = attend(0, after_all(queries[0], far_term))
     resid_mid = inputs + scatter_parts(near_term, far_term)
     points[2](resid_mid)
     mid_parts = gather_parts(layer_norm(resid_mid, gain_mid).astype(bf16))
@@ -193,11 +296,11 @@
         inputs=inputs,
         resid_mid=resid_mid,
         normed=normed_parts,
-        queries=joined(queries),
-        keys=keys_all,
-        values=values_all,
-        log_totals=joined([near_logs, far_logs], 1),
-        attended=(near_mixed, far_mixed),
+        queries=queries,
+        keys=keys,
+        values=values,
+        logs=logs,
+        attended=attended,
         normed_mid=mid_parts,
         gelu_in=(fed[0][0], fed[1][0]),
         gate_mult=(fed[0][1], fed[1][1]),
@@ -241,37 +344,18 @@
 
 def backward_attn(grad_mid, kept, gain_first, weights, allowed, tables, gate):
     w_qkv, w_out = weights[0], weights[1]
-    queries, keys_rot, values_in = kept["queries"], kept["keys"], kept["values"]
-    row_count = grad_mid.shape[0]
     grad_parts = gather_parts(grad_mid.astype(bf16))
-    near, far = in_turn(lambda k, part: contract_last(part, w_out).astype(bf16), grad_parts)
-    grad_attended = after_all(joined([near, far]).reshape(queries.shape), gate)
-    scores = masked_scores(queries, keys_rot, allowed)
-    soft_exact = jnp.exp(scores - kept["log_totals"])
-    soft_weights = soft_exact.astype(bf16)
-    grad_values = jnp.einsum(
-        "hqk,qhd->khd", soft_weights, grad_attended, preferred_element_type=f32
-    )
-    grad_soft = jnp.einsum("qhd,khd->hqk", grad_attended, values_in, preferred_element_type=f32)
-    row_dots = jnp.sum(soft_exact * grad_soft, axis=2, keepdims=True)
-    grad_scores = (soft_exact * (grad_soft - row_dots)).astype(bf16)
-    grad_queries = jnp.einsum(
-        "hqk,khd->qhd", grad_scores, keys_rot, preferred_element_type=f32
-    ) * HEAD_DIM ** (-0.5)
-    grad_keys = jnp.einsum(
-        "hqk,qhd->khd", grad_scores, queries, preferred_element_type=f32
-    ) * HEAD_DIM ** (-0.5)
-    grad_projected = jnp.stack(
-        [
-            rotate_back(grad_queries, *tables),
-            rotate_back(grad_keys, *tables),
-            grad_values,
-        ],
-        axis=1,
-    )
-    grad_projected = grad_projected.astype(bf16).reshape(4 * row_count, -1)
-    far_term = contract_last(grad_projected[3 * row_count :], w_qkv).astype(bf16)
-    near_term = contract_last(grad_projected[: 3 * row_count], w_qkv).astype(bf16)
+    near, far = after_all(grad_parts, gate)
+    full_rows, width = kept["queries"].shape
+    windowed, marks_row, marks_col = allowed
+    grad_projected, near_term, far_term = whole_call(
+        functools.partial(attend_back_kernel, windowed),
+        [((full_rows, 3 * width), bf16), (near.shape, bf16), (far.shape, bf16)],
+        [pltpu.VMEM((full_rows, width), bf16)] + [pltpu.VMEM((full_rows, width), f32)] * 3,
+        4 << 30,
+        near, far, w_qkv, w_out, *tables, marks_row, marks_col,
+        kept["queries"], kept["keys"], kept["values"], kept["logs"],
+    )
     grad_normed = scatter_parts(near_term, far_term)
     unused, pull_norm = jax.vjp(layer_norm, kept["inputs"], gain_first)
     grad_resid, grad_gain = pull_norm(grad_normed)
@@ -286,7 +370,7 @@
         outer, inner, left, right = after_all(
             (grad_parts, kept["attended"], kept["normed"], grad_projected), gate
         )
-        outer, inner, left = joined(outer), joined(inner), joined(left)
+        outer, left = joined(outer), joined(left)
         width = inner.shape[1]
         of_q, of_k, of_v = (right[:, i * width : (i + 1) * width] for i in range(3))
         one = add_core(lambda core: contract_rows(left, core(of_q, of_v)))
@@ -383,11 +467,10 @@
     hidden_width = w_up.shape[3]
     moving = []
 
-    def at_projected(values):
-        out0, out1 = by_layer(is_first, own[1], both_halves(half_out, values))
-        layer0.append(out0)
-        layer1.append(out1)
-        moving.append(fetch_half(own[2][:hidden_width], (half_out, values)))
+    out0, out1 = by_layer(is_first, own[1], both_halves(half_out))
+    layer0.append(out0)
+    layer1.append(out1)
+    moving.append(fetch_half(own[2][:hidden_width], half_out))
 
     def at_far_term(far_term):
         moving.append(both_halves(moving[0], far_term))
@@ -403,19 +486,20 @@
         layer0.extend([up0, down0])
         layer1.extend([up1, down1])
 
-    points = (at_projected, at_far_term, at_mid, at_gathered)
+    points = (None, at_far_term, at_mid, at_gathered)
 
     doc_lengths = jnp.where(is_first, lengths[0, 0], lengths[1, 0])
     indices = jnp.arange(full_rows, dtype=jnp.int32)
     blocks = jnp.array([0, 1, 3, 2], jnp.int32) + lax.axis_index("tensor")
     indices = (jnp.repeat(blocks, row_count) * row_count + indices % row_count) % full_rows
     doc_ids, positions = doc_layout(doc_lengths, indices)
-    same_doc = doc_ids[:, None] == doc_ids[None, :]
-    near = jnp.abs(indices[:, None] - indices[None, :]) <= WINDOW // 2
-    allowed0 = same_doc & near
-    allowed1 = same_doc
-    tables0 = rope_tables(positions, 10000.0)
-    tables1 = rope_tables(positions, 160000.0)
+    marks_row = jnp.stack([doc_ids, indices])
+    marks_col = jnp.stack([doc_ids, indices], axis=1)
+    allowed0 = (True, marks_row, marks_col)
+    allowed1 = (False, marks_row, marks_col)
+    heads = w_out.shape[1] // HEAD_DIM
+    tables0 = rope_tables(positions, 10000.0, heads)
+    tables1 = rope_tables(positions, 160000.0, heads)
 
     out0, kept0 = forward_layer(
         start_rows, first_parts, gains0[1], layer0, allowed0, tables0, False, points
@@ -454,17 +538,21 @@
     attn_own, attn_sent = pick_sections(is_first, attn0, attn1)
     attn_sent = after_all(attn_sent, out1_terms)
     attn_sum = (attn_own.astype(f32) + swap_section(attn_sent).astype(f32)).astype(bf16)
+    attn_sum, ffn_sum = lax.optimization_barrier((attn_sum, ffn_sum))
     out1 = (kept1["resid_mid"] + scatter_parts(*out1_terms)).astype(bf16)
     ffn_half = spread_part(ffn_sum)
-    attn_sum, out1, ffn_half = lax.optimization_barrier((attn_sum, out1, ffn_half))
     attn_half = spread_part(attn_sum)
     ffn_halves = trade_halves(ffn_half)
+    grad_up = jnp.stack([half[:hidden_width] for half in ffn_halves]).astype(f32)
+    down_rows = w_down.shape[1] // 2
+    grad_down = joined([half[hidden_width : hidden_width + down_rows] for half in ffn_halves])
+    grad_down = grad_down.astype(f32)
+    attn_half, grad_up, grad_down, out1 = lax.optimization_barrier(
+        (attn_half, grad_up, grad_down, out1)
+    )
     attn_halves = trade_halves(attn_half)
     gain_rows = sum(half[2 * w_qkv.shape[1] :][:8].astype(f32) for half in attn_halves)
     gain_total = sum_tensor(gain_rows).reshape(2, -1)
-    grad_up = jnp.stack([half[:hidden_width] for half in ffn_halves])
-    down_rows = w_down.shape[1] // 2
-    grad_down = joined([half[hidden_width : hidden_width + down_rows] for half in ffn_halves])
     model_width = w_qkv.shape[1]
     grad_qkv = jnp.stack(
         [
@@ -491,8 +579,8 @@
         gain_total[None],
         jnp.transpose(grad_qkv.astype(f32), (1, 0, 2))[None],
         grad_out.astype(f32)[None],
-        jnp.transpose(grad_up.astype(f32), (2, 0, 1))[None],
-        grad_down.astype(f32)[None],
+        jnp.transpose(grad_up, (2, 0, 1))[None],
+        grad_down[None],
     )
 
 

time: 525 us -> 532 us (1.013)
  the two profiles are of different devices: /device:TPU:1 before, /device:TPU:0 now
where the time goes in v9:
time: 532 us; the launch traced here: 522 us
  waiting for transfers between devices  197 us (37%)
  starting transfers between devices  99.1 us (19%)
  other arithmetic  61.4 us (12%)
  local copies, waits for them, and re-layouts  40.1 us (8%)
  Pallas kernels  40 us (8%)
  matrix products  37.1 us (7%)
  blocking collectives  30.5 us (6%)
  between operations  16.7 us (3%)
    ppermute x51, waiting for transfers between devices, around(): lax.ppermute(block, axis, [(i, (i + distance) % count) for i in range(cou...  115 us
    ppermute x51, starting transfers between devices, around(): lax.ppermute(block, axis, [(i, (i + distance) % count) for i in range(cou...  65.8 us
    pallas_call x4, Pallas kernels, whole_call(): pl.pallas_call(kernel, out_shape=[jax.ShapeDtypeStruct(*shape) for shape...  40 us
    all_to_all x1, blocking collectives, spread_part(): return lax.all_to_all(copies, ('zlo', 'x'), 0, 0, tiled=True)  30.5 us
    ppermute x6, waiting for transfers between devices, swap_layer(): lax.ppermute(block, ('section', 'zlo'), [(0, 3), (1, 2), (2, 1), (3, 0)])  25.1 us
    all_to_all x2, waiting for transfers between devices, reduce_part_now(): pieces = lax.all_to_all(grads, ('zlo', 'x'), 0, 0, tiled=True)  24.3 us
    unnamed x255, local copies, waits for them, and re-layouts  23.4 us
    ppermute x4, waiting for transfers between devices, swap_section(): return lax.ppermute(block, 'section', [(0, 1), (1, 0)])  22.2 us
  transfers between devices with their start and end apart: 81, of which 36 were waited for; matrix products, arithmetic and copies ran while one was open for 20% of the time, Pallas kernels for 6%

profile of v9, /device:TPU:0, one launch (start us, length us, event | category | flops | bytes accessed | tf_op | source)
XLA Modules:
  0.0 522.3 jit_solution(1284284630204701966)
XLA Ops:
  15.0 4.1 collective-permute-start.3
  19.4 3.5 slice_bitcast_fusion.3
  22.9 13.1 %collective-permute-done.4 = f32[2,1024]{1,0:T(2,128)S(1)} collective-permute-done((f32[2,1024]{1,0:T(2,128)S(1)}, f32[2,1024]{1,0:T(2,128)S(1)}, u32[]{:S(2)}, u32[]{:S(2)}) %collective-permute-start.4) | collective-permute-done | bytes 8224 | tf_op jit(solution)/shard_map/ppermute | solution.py:37
  37.6 3.0 collective-permute-start.6
  42.4 5.1 collective-permute-done.6
  50.3 3.0 collective-permute-start.13
  58.7 9.7 %shard_map.144 = (bf16[512,256]{1,0:T(8,128)(2,1)S(1)}, bf16[512,256]{1,0:T(8,128)(2,1)S(1)}, bf16[512,256]{1,0:T(8,128)(2,1)S(1)}, f32[8,512]{1,0:T(8,128)S(1)}...) custom-call(bf16[384,1024]{1,0:T(8,128)(2,1)S(1)} %fusion.4.near, ...), custom_call_target="tpu_custom_call" | custom-call | flops 3221225472 | bytes 8388608 | tf_op jit(solution)/shard_map/pallas_call | solution.py:239
  72.9 4.8 collective-permute-done.10
  77.7 6.9 %collective-permute-done.9 = bf16[128,1024]{1,0:T(8,128)(2,1)S(1)} collective-permute-done((bf16[128,1024]{1,0:T(8,128)(2,1)S(1)}, bf16[128,1024]{1,0:T(8,128)(2,1)S(1)}, u32[]{:S(2)}, u32[]{:S(2)}) %collective-permute-start.9) | collective-permute-done | bytes 262176 | tf_op jit(solution)/shard_map/ppermute | solution.py:25
  85.5 3.2 collective-permute-start.11
  90.5 2.9 collective-permute-done.12
  95.0 6.2 %collective-permute-done.18 = bf16[128,1024]{1,0:T(8,128)(2,1)S(1)} collective-permute-done((bf16[128,1024]{1,0:T(8,128)(2,1)S(1)}, bf16[128,1024]{1,0:T(8,128)(2,1)S(1)}, u32[]{:S(2)}, u32[]{:S(2)}) %collective-permute-start.18) | collective-permute-done | bytes 262176 | tf_op jit(solution)/shard_map/ppermute | solution.py:25
  101.3 5.5 %collective-permute-done.17 = bf16[328,1024]{1,0:T(8,128)(2,1)S(1)} collective-permute-done((bf16[328,1024]{1,0:T(8,128)(2,1)S(1)}, bf16[328,1024]{1,0:T(8,128)(2,1)S(1)}, u32[]{:S(2)}, u32[]{:S(2)}) %collective-permute-start.17) | collective-permute-done | bytes 671776 | tf_op jit(solution)/shard_map/ppermute | solution.py:37
  111.2 3.0 multiply_convert_fusion.3
  125.8 8.2 %collective-permute-done.21 = bf16[128,1024]{1,0:T(8,128)(2,1)S(1)} collective-permute-done((bf16[128,1024]{1,0:T(8,128)(2,1)S(1)}, bf16[128,1024]{1,0:T(8,128)(2,1)S(1)}, u32[]{:S(2)}, u32[]{:S(2)}) %collective-permute-start.21) | collective-permute-done | bytes 262176 | tf_op jit(solution)/shard_map/ppermute | solution.py:25
  135.9 3.2 collective-permute-start.23
  143.0 7.7 %collective-permute-done.24 = bf16[128,1024]{1,0:T(8,128)(2,1)} collective-permute-done((bf16[128,1024]{1,0:T(8,128)(2,1)}, bf16[128,1024]{1,0:T(8,128)(2,1)}, u32[]{:S(2)}, u32[]{:S(2)}) %collective-permute-start.24) | collective-permute-done | bytes 262176 | tf_op jit(solution)/shard_map/ppermute | solution.py:25
  151.9 9.8 %shard_map.145 = (bf16[512,256]{1,0:T(8,128)(2,1)S(1)}, bf16[512,256]{1,0:T(8,128)(2,1)S(1)}, bf16[512,256]{1,0:T(8,128)(2,1)S(1)}, f32[8,512]{1,0:T(8,128)S(1)}...) custom-call(bf16[384,1024]{1,0:T(8,128)(2,1)S(1)} %pad_maximum_fusion.7.near, ...), custom_call_target="tpu_custom_call" | custom-call | flops 3221225472 | bytes 8388608 | tf_op jit(solution)/shard_map/pallas_call | solution.py:239
  161.8 3.0 collective-permute-start.28
  169.9 6.7 %collective-permute-done.28 = bf16[128,1024]{1,0:T(8,128)(2,1)S(1)} collective-permute-done((bf16[128,1024]{1,0:T(8,128)(2,1)S(1)}, bf16[128,1024]{1,0:T(8,128)(2,1)S(1)}, u32[]{:S(2)}, u32[]{:S(2)}) %collective-permute-start.28) | collective-permute-done | bytes 262176 | tf_op jit(solution)/shard_map/ppermute | solution.py:25
  176.6 4.3 collective-permute-done.27
  184.9 7.0 %collective-permute-done.32 = bf16[128,1024]{1,0:T(8,128)(2,1)S(1)} collective-permute-done((bf16[128,1024]{1,0:T(8,128)(2,1)S(1)}, bf16[128,1024]{1,0:T(8,128)(2,1)S(1)}, u32[]{:S(2)}, u32[]{:S(2)}) %collective-permute-start.32) | collective-permute-done | bytes 262176 | tf_op jit(solution)/shard_map/ppermute | solution.py:25
  208.5 7.0 %collective-permute-done.36 = bf16[128,1024]{1,0:T(8,128)(2,1)S(1)} collective-permute-done((bf16[128,1024]{1,0:T(8,128)(2,1)S(1)}, bf16[128,1024]{1,0:T(8,128)(2,1)S(1)}, u32[]{:S(2)}, u32[]{:S(2)}) %collective-permute-start.36) | collective-permute-done | bytes 262176 | tf_op jit(solution)/shard_map/ppermute | solution.py:25
  217.1 3.2 collective-permute-start.38
  222.4 7.5 %collective-permute-done.39 = bf16[128,1024]{1,0:T(8,128)(2,1)S(1)} collective-permute-done((bf16[128,1024]{1,0:T(8,128)(2,1)S(1)}, bf16[128,1024]{1,0:T(8,128)(2,1)S(1)}, u32[]{:S(2)}, u32[]{:S(2)}) %collective-permute-start.39) | collective-permute-done | bytes 262176 | tf_op jit(solution)/shard_map/ppermute | solution.py:25
  229.9 10.2 %shard_map.146 = (bf16[512,768]{1,0:T(8,128)(2,1)S(1)}, bf16[384,1024]{1,0:T(8,128)(2,1)S(1)}, bf16[128,1024]{1,0:T(8,128)(2,1)S(1)}) custom-call(bf16[384,1024]{1,0:T(8,128)(2,1)S(1)} %pad_maximum_fusion.10.near, bf16[128,1024]{1,0:T(8,128)(2,1)S(1)} %collective-permute-done.40.far, bf16[1024,768]{1,0:T(8,128)(2,1)S(1)} %pad_maximum_fusion.3.w_qkv, ...), custom_call_target="tpu_custom_call" | custom-call | flops 4294967296 | bytes 8388608 | tf_op jit(solution)/shard_map/pallas_call | solution.py:239
  247.8 5.2 %collective-permute-done.42 = bf16[128,1024]{1,0:T(8,128)(2,1)S(1)} collective-permute-done((bf16[128,1024]{1,0:T(8,128)(2,1)S(1)}, bf16[128,1024]{1,0:T(8,128)(2,1)S(1)}, u32[]{:S(2)}, u32[]{:S(2)}) %collective-permute-start.42) | collective-permute-done | bytes 262176 | tf_op jit(solution)/shard_map/ppermute | solution.py:25
  291.3 4.4 all-to-all-start
  299.3 17.4 %all-to-all-done = bf16[8,272,256]{2,1,0:T(8,128)(2,1)} async-done(((bf16[8,272,256]{2,1,0:T(8,128)(2,1)}), bf16[8,272,256]{2,1,0:T(8,128)(2,1)}, u32[]{:S(2)}, u32[]{:S(2)}) %all-to-all-start) | async-done | bytes 1114144 | tf_op jit(solution)/shard_map/all_to_all | solution.py:418
  332.6 4.9 collective-permute-done.55
  337.6 5.0 collective-permute-done.54
  353.8 10.3 %shard_map.147 = (bf16[512,768]{1,0:T(8,128)(2,1)S(1)}, bf16[384,1024]{1,0:T(8,128)(2,1)S(1)}, bf16[128,1024]{1,0:T(8,128)(2,1)}) custom-call(bf16[384,1024]{1,0:T(8,128)(2,1)S(1)} %pad_maximum_fusion.11.near, bf16[128,1024]{1,0:T(8,128)(2,1)S(1)} %copy-done.15, bf16[1024,768]{1,0:T(8,128)(2,1)S(1)} %copy-done.1, ...), custom_call_target="tpu_custom_call" | custom-call | flops 4294967296 | bytes 8388608 | tf_op jit(solution)/shard_map/pallas_call | solution.py:239
  369.1 3.8 collective-permute-start.64
  374.8 7.1 %collective-permute-done.64 = bf16[128,1024]{1,0:T(8,128)(2,1)S(1)} collective-permute-done((bf16[128,1024]{1,0:T(8,128)(2,1)S(1)}, bf16[128,1024]{1,0:T(8,128)(2,1)S(1)}, u32[]{:S(2)}, u32[]{:S(2)}) %collective-permute-start.64) | collective-permute-done | bytes 262176 | tf_op jit(solution)/shard_map/ppermute | solution.py:25
  386.6 3.7 all-to-all-start.1
  391.5 2.8 convolution_convert_fusion.2
  395.0 3.6 collective-permute-start.61
  399.7 6.9 %all-to-all-done.1 = bf16[8,272,256]{2,1,0:T(8,128)(2,1)S(1)} async-done(((bf16[8,272,256]{2,1,0:T(8,128)(2,1)}), bf16[8,272,256]{2,1,0:T(8,128)(2,1)S(1)}, u32[]{:S(2)}, u32[]{:S(2)}) %all-to-all-start.1) | async-done | bytes 1114144 | tf_op jit(solution)/shard_map/all_to_all | solution.py:418
  406.8 4.7 collective-permute-done.61
  413.7 6.2 %collective-permute-done.65 = bf16[272,256]{1,0:T(8,128)(2,1)S(1)} collective-permute-done((bf16[272,256]{1,0:T(8,128)(2,1)S(1)}, bf16[272,256]{1,0:T(8,128)(2,1)S(1)}, u32[]{:S(2)}, u32[]{:S(2)}) %collective-permute-start.65) | collective-permute-done | bytes 139296 | tf_op jit(solution)/shard_map/ppermute | solution.py:33
  420.2 30.5 %all_to_all.36 = bf16[8,128,1024]{2,1,0:T(8,128)(2,1)S(1)} all-to-all(bf16[8,128,1024]{2,1,0:T(8,128)(2,1)S(1)} %broadcast_in_dim.112), channel_id=1, replica_groups=mesh['section'=2,'zlo'=2,'x'=4,'core'=2,'tensor'=4] {'zlo','x'}, dimensions={0} | all-to-all | bytes 4194304 | tf_op jit(solution)/shard_map/all_to_all | solution.py:425
  454.6 5.3 %collective-permute-done.69 = bf16[128,1024]{1,0:T(8,128)(2,1)S(1)} collective-permute-done((bf16[128,1024]{1,0:T(8,128)(2,1)S(1)}, bf16[128,1024]{1,0:T(8,128)(2,1)S(1)}, u32[]{:S(2)}, u32[]{:S(2)}) %collective-permute-start.69) | collective-permute-done | bytes 262176 | tf_op jit(solution)/shard_map/ppermute | solution.py:25
  459.9 7.9 %collective-permute-done.68 = bf16[128,1024]{1,0:T(8,128)(2,1)S(1)} collective-permute-done((bf16[128,1024]{1,0:T(8,128)(2,1)S(1)}, bf16[128,1024]{1,0:T(8,128)(2,1)S(1)}, u32[]{:S(2)}, u32[]{:S(2)}) %collective-permute-start.68) | collective-permute-done | bytes 262176 | tf_op jit(solution)/shard_map/ppermute | solution.py:25
  469.7 3.6 all-to-all-start.2
  480.1 9.4 %all-to-all-done.2 = bf16[8,272,256]{2,1,0:T(8,128)(2,1)S(1)} async-done(((bf16[8,272,256]{2,1,0:T(8,128)(2,1)}), bf16[8,272,256]{2,1,0:T(8,128)(2,1)S(1)}, u32[]{:S(2)}, u32[]{:S(2)}) %all-to-all-start.2) | async-done | bytes 1114144 | tf_op jit(solution)/shard_map/all_to_all | solution.py:425
  489.5 3.0 collective-permute-start.71
  493.2 7.0 %collective-permute-done.71 = bf16[128,1024]{1,0:T(8,128)(2,1)S(1)} collective-permute-done((bf16[128,1024]{1,0:T(8,128)(2,1)S(1)}, bf16[128,1024]{1,0:T(8,128)(2,1)S(1)}, u32[]{:S(2)}, u32[]{:S(2)}) %collective-permute-start.71) | collective-permute-done | bytes 262176 | tf_op jit(solution)/shard_map/ppermute | solution.py:33
  501.1 4.3 collective-permute-done.70
  (587 shorter events, 196.6 us)
Async XLA Ops:
  7.2 312.6 %reduce-scatter.3.cloned.1.call-start = ((), (), s32[]{:S(2)}) async-start(), calls=%async_computation.6 | async-start | bytes 2359296 | tf_op jit(solution)/shard_map/reduce_scatter | solution.py:414
  8.4 27.6 %collective-permute-start.1 = (bf16[128,1024]{1,0:T(8,128)(2,1)S(1)}, bf16[128,1024]{1,0:T(8,128)(2,1)S(1)}, u32[]{:S(2)}, u32[]{:S(2)}) collective-permute-start(bf16[128,1024]{1,0:T(8,128)(2,1)S(1)} %get-tuple-element.217), channel_id=1, source_target_pairs={{0,1},{1,2},{2,3},{3,0},{4,5},{5,6},{6,7},{7,4},{8,9},{9,10},{10,1... | collective-permute-start | bytes 786440 | tf_op jit(solution)/shard_map/ppermute | solution.py:25
  10.2 25.9 %collective-permute-start = (bf16[128,1024]{1,0:T(8,128)(2,1)S(1)}, bf16[128,1024]{1,0:T(8,128)(2,1)S(1)}, u32[]{:S(2)}, u32[]{:S(2)}) collective-permute-start(bf16[128,1024]{1,0:T(8,128)(2,1)S(1)} %get-tuple-element.217), channel_id=1, source_target_pairs={{0,3},{1,0},{2,1},{3,2},{4,7},{5,4},{6,5},{7,6},{8,11},{9,8},{10,9... | collective-permute-start | bytes 786440 | tf_op jit(solution)/shard_map/ppermute | solution.py:25
  11.7 24.4 %collective-permute-start.2 = (bf16[128,1024]{1,0:T(8,128)(2,1)S(1)}, bf16[128,1024]{1,0:T(8,128)(2,1)S(1)}, u32[]{:S(2)}, u32[]{:S(2)}) collective-permute-start(bf16[128,1024]{1,0:T(8,128)(2,1)S(1)} %get-tuple-element.217), channel_id=1, source_target_pairs={{0,2},{1,3},{2,0},{3,1},{4,6},{5,7},{6,4},{7,5},{8,10},{9,11},{10,... | collective-permute-start | bytes 786440 | tf_op jit(solution)/shard_map/ppermute | solution.py:25
  15.0 21.2 %collective-permute-start.3 = (bf16[1536,256]{1,0:T(8,128)(2,1)S(1)}, bf16[1536,256]{1,0:T(8,128)(2,1)}, u32[]{:S(2)}, u32[]{:S(2)}) collective-permute-start(bf16[1536,256]{1,0:T(8,128)(2,1)S(1)} %constant_dynamic-slice_fusion.4), channel_id=1, source_target_pairs={{0,96},{32,64},{64,32},{96,0},{1,97},{33,65},{65,33},{97,1},{2,98}... | collective-permute-start | bytes 2359304 | tf_op jit(solution)/shard_map/ppermute | solution.py:37
  19.1 16.9 %collective-permute-start.4 = (f32[2,1024]{1,0:T(2,128)S(1)}, f32[2,1024]{1,0:T(2,128)S(1)}, u32[]{:S(2)}, u32[]{:S(2)}) collective-permute-start(f32[2,1024]{1,0:T(2,128)S(1)} %bitcast.170), channel_id=1, source_target_pairs={{0,96},{32,64},{64,32},{96,0},{1,97},{33,65},{65,33},{97,1},{2,98}... | collective-permute-start | bytes 24584 | tf_op jit(solution)/shard_map/ppermute | solution.py:37
  37.4 16.2 %collective-permute-start.5 = (bf16[1536,256]{1,0:T(8,128)(2,1)}, bf16[1536,256]{1,0:T(8,128)(2,1)}, u32[]{:S(2)}, u32[]{:S(2)}) collective-permute-start(bf16[1536,256]{1,0:T(8,128)(2,1)} %collective-permute-done.3), channel_id=1, source_target_pairs={{0,4},{4,0},{1,5},{5,1},{2,6},{6,2},{3,7},{7,3},{8,12},{12,8},{9,1... | collective-permute-start | bytes 2359304 | tf_op jit(solution)/shard_map/ppermute | solution.py:29
  50.3 22.0 %collective-permute-start.13 = (bf16[328,1024]{1,0:T(8,128)(2,1)S(1)}, bf16[328,1024]{1,0:T(8,128)(2,1)S(1)}, u32[]{:S(2)}, u32[]{:S(2)}) collective-permute-start(bf16[328,1024]{1,0:T(8,128)(2,1)S(1)} %constant_dynamic-slice_fusion.2), channel_id=1, source_target_pairs={{0,96},{32,64},{64,32},{96,0},{1,97},{33,65},{65,33},{97,1},{2,98}... | collective-permute-start | bytes 2015240 | tf_op jit(solution)/shard_map/ppermute | solution.py:37
  69.7 15.0 %collective-permute-start.9 = (bf16[128,1024]{1,0:T(8,128)(2,1)S(1)}, bf16[128,1024]{1,0:T(8,128)(2,1)S(1)}, u32[]{:S(2)}, u32[]{:S(2)}) collective-permute-start(bf16[128,1024]{1,0:T(8,128)(2,1)S(1)} %get-tuple-element.294), channel_id=1, source_target_pairs={{0,1},{1,2},{2,3},{3,0},{4,5},{5,6},{6,7},{7,4},{8,9},{9,10},{10,1... | collective-permute-start | bytes 786440 | tf_op jit(solution)/shard_map/ppermute | solution.py:25
  70.6 14.0 %collective-permute-start.8 = (bf16[128,1024]{1,0:T(8,128)(2,1)S(1)}, bf16[128,1024]{1,0:T(8,128)(2,1)S(1)}, u32[]{:S(2)}, u32[]{:S(2)}) collective-permute-start(bf16[128,1024]{1,0:T(8,128)(2,1)S(1)} %get-tuple-element.101), channel_id=1, source_target_pairs={{0,2},{1,3},{2,0},{3,1},{4,6},{5,7},{6,4},{7,5},{8,10},{9,11},{10,... | collective-permute-start | bytes 786440 | tf_op jit(solution)/shard_map/ppermute | solution.py:25
  72.4 17.7 %collective-permute-start.15 = (bf16[328,1024]{1,0:T(8,128)(2,1)S(1)}, bf16[328,1024]{1,0:T(8,128)(2,1)S(1)}, u32[]{:S(2)}, u32[]{:S(2)}) collective-permute-start(bf16[328,1024]{1,0:T(8,128)(2,1)S(1)} %constant_dynamic-slice_fusion.1), channel_id=1, source_target_pairs={{0,96},{32,64},{64,32},{96,0},{1,97},{33,65},{65,33},{97,1},{2,98}... | collective-permute-start | bytes 2015240 | tf_op jit(solution)/shard_map/ppermute | solution.py:37
  72.7 22.2 %collective-permute-start.14 = (bf16[328,1024]{1,0:T(8,128)(2,1)S(1)}, bf16[328,1024]{1,0:T(8,128)(2,1)S(1)}, u32[]{:S(2)}, u32[]{:S(2)}) collective-permute-start(bf16[328,1024]{1,0:T(8,128)(2,1)S(1)} %collective-permute-done.13), channel_id=1, source_target_pairs={{0,4},{4,0},{1,5},{5,1},{2,6},{6,2},{3,7},{7,3},{8,12},{12,8},{9,1... | collective-permute-start | bytes 2015240 | tf_op jit(solution)/shard_map/ppermute | solution.py:29
  90.1 16.7 %collective-permute-start.17 = (bf16[328,1024]{1,0:T(8,128)(2,1)S(1)}, bf16[328,1024]{1,0:T(8,128)(2,1)S(1)}, u32[]{:S(2)}, u32[]{:S(2)}) collective-permute-start(bf16[328,1024]{1,0:T(8,128)(2,1)S(1)} %constant_dynamic-slice_fusion), channel_id=1, source_target_pairs={{0,96},{32,64},{64,32},{96,0},{1,97},{33,65},{65,33},{97,1},{2,98}... | collective-permute-start | bytes 2015240 | tf_op jit(solution)/shard_map/ppermute | solution.py:37
  90.5 16.4 %collective-permute-start.16 = (bf16[328,1024]{1,0:T(8,128)(2,1)S(1)}, bf16[328,1024]{1,0:T(8,128)(2,1)S(1)}, u32[]{:S(2)}, u32[]{:S(2)}) collective-permute-start(bf16[328,1024]{1,0:T(8,128)(2,1)S(1)} %collective-permute-done.15), channel_id=1, source_target_pairs={{0,4},{4,0},{1,5},{5,1},{2,6},{6,2},{3,7},{7,3},{8,12},{12,8},{9,1... | collective-permute-start | bytes 2015240 | tf_op jit(solution)/shard_map/ppermute | solution.py:29
  118.7 15.3 %collective-permute-start.21 = (bf16[128,1024]{1,0:T(8,128)(2,1)S(1)}, bf16[128,1024]{1,0:T(8,128)(2,1)S(1)}, u32[]{:S(2)}, u32[]{:S(2)}) collective-permute-start(bf16[128,1024]{1,0:T(8,128)(2,1)S(1)} %get-tuple-element.292), channel_id=1, source_target_pairs={{0,1},{1,2},{2,3},{3,0},{4,5},{5,6},{6,7},{7,4},{8,9},{9,10},{10,1... | collective-permute-start | bytes 786440 | tf_op jit(solution)/shard_map/ppermute | solution.py:25
  135.9 14.8 %collective-permute-start.24 = (bf16[128,1024]{1,0:T(8,128)(2,1)}, bf16[128,1024]{1,0:T(8,128)(2,1)}, u32[]{:S(2)}, u32[]{:S(2)}) collective-permute-start(bf16[128,1024]{1,0:T(8,128)(2,1)} %fusion.56), channel_id=1, source_target_pairs={{0,1},{1,2},{2,3},{3,0},{4,5},{5,6},{6,7},{7,4},{8,9},{9,10},{10,1... | collective-permute-start | bytes 786440 | tf_op jit(solution)/shard_map/ppermute | solution.py:25
  135.9 14.8 %collective-permute-start.23 = (bf16[128,1024]{1,0:T(8,128)(2,1)}, bf16[128,1024]{1,0:T(8,128)(2,1)}, u32[]{:S(2)}, u32[]{:S(2)}) collective-permute-start(bf16[128,1024]{1,0:T(8,128)(2,1)} %fusion.56), channel_id=1, source_target_pairs={{0,3},{1,0},{2,1},{3,2},{4,7},{5,4},{6,5},{7,6},{8,11},{9,8},{10,9... | collective-permute-start | bytes 786440 | tf_op jit(solution)/shard_map/ppermute | solution.py:25
  161.8 14.8 %collective-permute-start.28 = (bf16[128,1024]{1,0:T(8,128)(2,1)S(1)}, bf16[128,1024]{1,0:T(8,128)(2,1)S(1)}, u32[]{:S(2)}, u32[]{:S(2)}) collective-permute-start(bf16[128,1024]{1,0:T(8,128)(2,1)S(1)} %get-tuple-element.291), channel_id=1, source_target_pairs={{0,3},{1,0},{2,1},{3,2},{4,7},{5,4},{6,5},{7,6},{8,11},{9,8},{10,9... | collective-permute-start | bytes 786440 | tf_op jit(solution)/shard_map/ppermute | solution.py:25
  164.8 16.1 %collective-permute-start.27 = (bf16[128,1024]{1,0:T(8,128)(2,1)S(1)}, bf16[128,1024]{1,0:T(8,128)(2,1)S(1)}, u32[]{:S(2)}, u32[]{:S(2)}) collective-permute-start(bf16[128,1024]{1,0:T(8,128)(2,1)S(1)} %get-tuple-element.290), channel_id=1, source_target_pairs={{0,1},{1,2},{2,3},{3,0},{4,5},{5,6},{6,7},{7,4},{8,9},{9,10},{10,1... | collective-permute-start | bytes 786440 | tf_op jit(solution)/shard_map/ppermute | solution.py:25
  164.8 16.1 %collective-permute-start.26 = (bf16[128,1024]{1,0:T(8,128)(2,1)S(1)}, bf16[128,1024]{1,0:T(8,128)(2,1)S(1)}, u32[]{:S(2)}, u32[]{:S(2)}) collective-permute-start(bf16[128,1024]{1,0:T(8,128)(2,1)S(1)} %get-tuple-element.110), channel_id=1, source_target_pairs={{0,2},{1,3},{2,0},{3,1},{4,6},{5,7},{6,4},{7,5},{8,10},{9,11},{10,... | collective-permute-start | bytes 786440 | tf_op jit(solution)/shard_map/ppermute | solution.py:25
  166.4 25.6 %collective-permute-start.32 = (bf16[128,1024]{1,0:T(8,128)(2,1)S(1)}, bf16[128,1024]{1,0:T(8,128)(2,1)S(1)}, u32[]{:S(2)}, u32[]{:S(2)}) collective-permute-start(bf16[128,1024]{1,0:T(8,128)(2,1)S(1)} %select_bitcast_fusion.4), channel_id=1, source_target_pairs={{0,1},{1,2},{2,3},{3,0},{4,5},{5,6},{6,7},{7,4},{8,9},{9,10},{10,1... | collective-permute-start | bytes 786440 | tf_op jit(solution)/shard_map/ppermute | solution.py:25
  169.0 22.9 %collective-permute-start.31 = (bf16[128,1024]{1,0:T(8,128)(2,1)S(1)}, bf16[128,1024]{1,0:T(8,128)(2,1)S(1)}, u32[]{:S(2)}, u32[]{:S(2)}) collective-permute-start(bf16[128,1024]{1,0:T(8,128)(2,1)S(1)} %select_bitcast_fusion.4), channel_id=1, source_target_pairs={{0,3},{1,0},{2,1},{3,2},{4,7},{5,4},{6,5},{7,6},{8,11},{9,8},{10,9... | collective-permute-start | bytes 786440 | tf_op jit(solution)/shard_map/ppermute | solution.py:25
  176.6 28.6 %collective-permute-start.34 = (bf16[128,1024]{1,0:T(8,128)(2,1)S(1)}, bf16[128,1024]{1,0:T(8,128)(2,1)S(1)}, u32[]{:S(2)}, u32[]{:S(2)}) collective-permute-start(bf16[128,1024]{1,0:T(8,128)(2,1)S(1)} %select_bitcast_fusion.4), channel_id=1, source_target_pairs={{0,2},{1,3},{2,0},{3,1},{4,6},{5,7},{6,4},{7,5},{8,10},{9,11},{10,... | collective-permute-start | bytes 786440 | tf_op jit(solution)/shard_map/ppermute | solution.py:25
  181.6 13.6 %collective-permute-start.30 = (bf16[128,1024]{1,0:T(8,128)(2,1)S(1)}, bf16[128,1024]{1,0:T(8,128)(2,1)S(1)}, u32[]{:S(2)}, u32[]{:S(2)}) collective-permute-start(bf16[128,1024]{1,0:T(8,128)(2,1)S(1)} %multiply_convert_fusion.4), channel_id=1, source_target_pairs={{0,1},{1,2},{2,3},{3,0},{4,5},{5,6},{6,7},{7,4},{8,9},{9,10},{10,1... | collective-permute-start | bytes 786440 | tf_op jit(solution)/shard_map/ppermute | solution.py:25
  201.9 13.6 %collective-permute-start.36 = (bf16[128,1024]{1,0:T(8,128)(2,1)S(1)}, bf16[128,1024]{1,0:T(8,128)(2,1)S(1)}, u32[]{:S(2)}, u32[]{:S(2)}) collective-permute-start(bf16[128,1024]{1,0:T(8,128)(2,1)S(1)} %get-tuple-element.288), channel_id=1, source_target_pairs={{0,1},{1,2},{2,3},{3,0},{4,5},{5,6},{6,7},{7,4},{8,9},{9,10},{10,1... | collective-permute-start | bytes 786440 | tf_op jit(solution)/shard_map/ppermute | solution.py:25
  222.0 34.6 %collective-permute-start.45 = (bf16[328,1024]{1,0:T(8,128)(2,1)}, bf16[328,1024]{1,0:T(8,128)(2,1)}, u32[]{:S(2)}, u32[]{:S(2)}) collective-permute-start(bf16[328,1024]{1,0:T(8,128)(2,1)} %convolution_convert_fusion.7), channel_id=1, source_target_pairs={{0,4},{4,0},{1,5},{5,1},{2,6},{6,2},{3,7},{7,3},{8,12},{12,8},{9,1... | collective-permute-start | bytes 2015240 | tf_op jit(solution)/shard_map/ppermute | solution.py:29
  264.5 19.0 %collective-permute-start.48 = (bf16[128,1024]{1,0:T(8,128)(2,1)}, bf16[128,1024]{1,0:T(8,128)(2,1)}, u32[]{:S(2)}, u32[]{:S(2)}) collective-permute-start(bf16[128,1024]{1,0:T(8,128)(2,1)} %add_convert_fusion.7), channel_id=1, source_target_pairs={{0,2},{1,3},{2,0},{3,1},{4,6},{5,7},{6,4},{7,5},{8,10},{9,11},{10,... | collective-permute-start | bytes 786440 | tf_op jit(solution)/shard_map/ppermute | solution.py:25
  269.4 19.0 %collective-permute-start.53 = (bf16[1024,256]{1,0:T(8,128)(2,1)}, bf16[1024,256]{1,0:T(8,128)(2,1)}, u32[]{:S(2)}, u32[]{:S(2)}) collective-permute-start(bf16[1024,256]{1,0:T(8,128)(2,1)} %convolution_convert_fusion.10), channel_id=1, source_target_pairs={{0,4},{4,0},{1,5},{5,1},{2,6},{6,2},{3,7},{7,3},{8,12},{12,8},{9,1... | collective-permute-start | bytes 1572872 | tf_op jit(solution)/shard_map/ppermute | solution.py:29
  269.4 17.3 %collective-permute-start.52 = (bf16[1024,256]{1,0:T(8,128)(2,1)}, bf16[1024,256]{1,0:T(8,128)(2,1)}, u32[]{:S(2)}, u32[]{:S(2)}) collective-permute-start(bf16[1024,256]{1,0:T(8,128)(2,1)} %convolution_convert_fusion.11), channel_id=1, source_target_pairs={{0,4},{4,0},{1,5},{5,1},{2,6},{6,2},{3,7},{7,3},{8,12},{12,8},{9,1... | collective-permute-start | bytes 1572872 | tf_op jit(solution)/shard_map/ppermute | solution.py:29
  281.5 14.5 %collective-permute-start.51 = (bf16[128,1024]{1,0:T(8,128)(2,1)}, bf16[128,1024]{1,0:T(8,128)(2,1)}, u32[]{:S(2)}, u32[]{:S(2)}) collective-permute-start(bf16[128,1024]{1,0:T(8,128)(2,1)} %get-tuple-element.285), channel_id=1, source_target_pairs={{0,3},{1,0},{2,1},{3,2},{4,7},{5,4},{6,5},{7,6},{8,11},{9,8},{10,9... | collective-permute-start | bytes 786440 | tf_op jit(solution)/shard_map/ppermute | solution.py:25
  281.5 14.5 %collective-permute-start.50 = (bf16[128,1024]{1,0:T(8,128)(2,1)}, bf16[128,1024]{1,0:T(8,128)(2,1)}, u32[]{:S(2)}, u32[]{:S(2)}) collective-permute-start(bf16[128,1024]{1,0:T(8,128)(2,1)} %get-tuple-element.284), channel_id=1, source_target_pairs={{0,1},{1,2},{2,3},{3,0},{4,5},{5,6},{6,7},{7,4},{8,9},{9,10},{10,1... | collective-permute-start | bytes 786440 | tf_op jit(solution)/shard_map/ppermute | solution.py:25
  291.3 25.4 %all-to-all-start = ((bf16[8,272,256]{2,1,0:T(8,128)(2,1)}), bf16[8,272,256]{2,1,0:T(8,128)(2,1)}, u32[]{:S(2)}, u32[]{:S(2)}) async-start(bf16[8,272,256]{2,1,0:T(8,128)(2,1)} %bitcast.138), calls=%async_computation.1 | async-start | bytes 2228224 | tf_op jit(solution)/shard_map/all_to_all | solution.py:418
  295.8 98.5 %reduce-scatter.5.cloned.1.call-start = ((), (), s32[]{:S(2)}) async-start(), calls=%async_computation.7 | async-start | bytes 2359296 | tf_op jit(solution)/shard_map/reduce_scatter | solution.py:414
  324.0 19.1 %collective-permute-start.57 = (bf16[656,1024]{1,0:T(8,128)(2,1)S(1)}, bf16[656,1024]{1,0:T(8,128)(2,1)S(1)}, u32[]{:S(2)}, u32[]{:S(2)}) collective-permute-start(bf16[656,1024]{1,0:T(8,128)(2,1)S(1)} %convolution_convert_fusion), channel_id=1, source_target_pairs={{0,4},{4,0},{1,5},{5,1},{2,6},{6,2},{3,7},{7,3},{8,12},{12,8},{9,1... | collective-permute-start | bytes 4030472 | tf_op jit(solution)/shard_map/ppermute | solution.py:29
  325.7 16.9 %collective-permute-start.58 = (bf16[328,1024]{1,0:T(8,128)(2,1)S(1)}, bf16[328,1024]{1,0:T(8,128)(2,1)S(1)}, u32[]{:S(2)}, u32[]{:S(2)}) collective-permute-start(bf16[328,1024]{1,0:T(8,128)(2,1)S(1)} %convolution_convert_fusion.6), channel_id=1, source_target_pairs={{0,4},{4,0},{1,5},{5,1},{2,6},{6,2},{3,7},{7,3},{8,12},{12,8},{9,1... | collective-permute-start | bytes 2015240 | tf_op jit(solution)/shard_map/ppermute | solution.py:29
  328.6 14.0 %collective-permute-start.54 = (bf16[128,1024]{1,0:T(8,128)(2,1)S(1)}, bf16[128,1024]{1,0:T(8,128)(2,1)S(1)}, u32[]{:S(2)}, u32[]{:S(2)}) collective-permute-start(bf16[128,1024]{1,0:T(8,128)(2,1)S(1)} %convert_element_type.424), channel_id=1, source_target_pairs={{0,3},{1,0},{2,1},{3,2},{4,7},{5,4},{6,5},{7,6},{8,11},{9,8},{10,9... | collective-permute-start | bytes 786440 | tf_op jit(solution)/shard_map/ppermute | solution.py:25
  331.2 14.6 %collective-permute-start.56 = (bf16[128,1024]{1,0:T(8,128)(2,1)S(1)}, bf16[128,1024]{1,0:T(8,128)(2,1)S(1)}, u32[]{:S(2)}, u32[]{:S(2)}) collective-permute-start(bf16[128,1024]{1,0:T(8,128)(2,1)S(1)} %convert_element_type.424), channel_id=1, source_target_pairs={{0,2},{1,3},{2,0},{3,1},{4,6},{5,7},{6,4},{7,5},{8,10},{9,11},{10,... | collective-permute-start | bytes 786440 | tf_op jit(solution)/shard_map/ppermute | solution.py:25
  366.1 16.6 %collective-permute-start.62 = (bf16[128,1024]{1,0:T(8,128)(2,1)}, bf16[128,1024]{1,0:T(8,128)(2,1)S(1)}, u32[]{:S(2)}, u32[]{:S(2)}) collective-permute-start(bf16[128,1024]{1,0:T(8,128)(2,1)} %get-tuple-element.168), channel_id=1, source_target_pairs={{0,2},{1,3},{2,0},{3,1},{4,6},{5,7},{6,4},{7,5},{8,10},{9,11},{10,... | collective-permute-start | bytes 786440 | tf_op jit(solution)/shard_map/ppermute | solution.py:25
  368.9 15.7 %collective-permute-start.60 = (bf16[1024,256]{1,0:T(8,128)(2,1)S(1)}, bf16[1024,256]{1,0:T(8,128)(2,1)S(1)}, u32[]{:S(2)}, u32[]{:S(2)}) collective-permute-start(bf16[1024,256]{1,0:T(8,128)(2,1)S(1)} %convolution_convert_fusion.8), channel_id=1, source_target_pairs={{0,4},{4,0},{1,5},{5,1},{2,6},{6,2},{3,7},{7,3},{8,12},{12,8},{9,1... | collective-permute-start | bytes 1572872 | tf_op jit(solution)/shard_map/ppermute | solution.py:29
  369.1 12.8 %collective-permute-start.64 = (bf16[128,1024]{1,0:T(8,128)(2,1)S(1)}, bf16[128,1024]{1,0:T(8,128)(2,1)S(1)}, u32[]{:S(2)}, u32[]{:S(2)}) collective-permute-start(bf16[128,1024]{1,0:T(8,128)(2,1)S(1)} %get-tuple-element.283), channel_id=1, source_target_pairs={{0,3},{1,0},{2,1},{3,2},{4,7},{5,4},{6,5},{7,6},{8,11},{9,8},{10,9... | collective-permute-start | bytes 786440 | tf_op jit(solution)/shard_map/ppermute | solution.py:25
  386.6 20.0 %all-to-all-start.1 = ((bf16[8,272,256]{2,1,0:T(8,128)(2,1)}), bf16[8,272,256]{2,1,0:T(8,128)(2,1)S(1)}, u32[]{:S(2)}, u32[]{:S(2)}) async-start(bf16[8,272,256]{2,1,0:T(8,128)(2,1)} %bitcast.35), calls=%async_computation.2 | async-start | bytes 2228224 | tf_op jit(solution)/shard_map/all_to_all | solution.py:418
  395.0 16.4 %collective-permute-start.61 = (bf16[128,1024]{1,0:T(8,128)(2,1)}, bf16[128,1024]{1,0:T(8,128)(2,1)}, u32[]{:S(2)}, u32[]{:S(2)}) collective-permute-start(bf16[128,1024]{1,0:T(8,128)(2,1)} %broadcast_select_fusion.22), channel_id=1, source_target_pairs={{0,64},{64,0},{1,65},{65,1},{2,66},{66,2},{3,67},{67,3},{4,68},{68... | collective-permute-start | bytes 786440 | tf_op jit(solution)/shard_map/ppermute | solution.py:33
  450.7 22.6 %collective-permute-start.66 = (bf16[1024,1024]{1,0:T(8,128)(2,1)S(1)}, bf16[1024,1024]{1,0:T(8,128)(2,1)}, u32[]{:S(2)}, u32[]{:S(2)}) collective-permute-start(bf16[1024,1024]{1,0:T(8,128)(2,1)S(1)} %bitcast.136), channel_id=1, source_target_pairs={{0,4},{4,0},{1,5},{5,1},{2,6},{6,2},{3,7},{7,3},{8,12},{12,8},{9,1... | collective-permute-start | bytes 6291464 | tf_op jit(solution)/shard_map/ppermute | solution.py:29
  452.5 15.3 %collective-permute-start.68 = (bf16[128,1024]{1,0:T(8,128)(2,1)S(1)}, bf16[128,1024]{1,0:T(8,128)(2,1)S(1)}, u32[]{:S(2)}, u32[]{:S(2)}) collective-permute-start(bf16[128,1024]{1,0:T(8,128)(2,1)S(1)} %get-tuple-element.280), channel_id=1, source_target_pairs={{0,1},{1,2},{2,3},{3,0},{4,5},{5,6},{6,7},{7,4},{8,9},{9,10},{10,1... | collective-permute-start | bytes 786440 | tf_op jit(solution)/shard_map/ppermute | solution.py:25
  452.8 14.9 %collective-permute-start.67 = (bf16[128,1024]{1,0:T(8,128)(2,1)S(1)}, bf16[128,1024]{1,0:T(8,128)(2,1)S(1)}, u32[]{:S(2)}, u32[]{:S(2)}) collective-permute-start(bf16[128,1024]{1,0:T(8,128)(2,1)S(1)} %copy-done.109), channel_id=1, source_target_pairs={{0,2},{1,3},{2,0},{3,1},{4,6},{5,7},{6,4},{7,5},{8,10},{9,11},{10,... | collective-permute-start | bytes 786440 | tf_op jit(solution)/shard_map/ppermute | solution.py:25
  469.7 19.8 %all-to-all-start.2 = ((bf16[8,272,256]{2,1,0:T(8,128)(2,1)}), bf16[8,272,256]{2,1,0:T(8,128)(2,1)S(1)}, u32[]{:S(2)}, u32[]{:S(2)}) async-start(bf16[8,272,256]{2,1,0:T(8,128)(2,1)} %broadcast_in_dim.111), calls=%async_computation.4 | async-start | bytes 2228224 | tf_op jit(solution)/shard_map/all_to_all | solution.py:425
  489.5 16.9 %collective-permute-start.72 = (bf16[2176,256]{1,0:T(8,128)(2,1)S(1)}, bf16[2176,256]{1,0:T(8,128)(2,1)S(1)}, u32[]{:S(2)}, u32[]{:S(2)}) collective-permute-start(bf16[2176,256]{1,0:T(8,128)(2,1)S(1)} %bitcast.139), channel_id=1, source_target_pairs={{0,4},{4,0},{1,5},{5,1},{2,6},{6,2},{3,7},{7,3},{8,12},{12,8},{9,1... | collective-permute-start | bytes 3342344 | tf_op jit(solution)/shard_map/ppermute | solution.py:29
  492.6 12.8 %collective-permute-start.70 = (bf16[128,1024]{1,0:T(8,128)(2,1)S(1)}, bf16[128,1024]{1,0:T(8,128)(2,1)S(1)}, u32[]{:S(2)}, u32[]{:S(2)}) collective-permute-start(bf16[128,1024]{1,0:T(8,128)(2,1)S(1)} %broadcast_select_fusion.21), channel_id=1, source_target_pairs={{0,64},{64,0},{1,65},{65,1},{2,66},{66,2},{3,67},{67,3},{4,68},{68... | collective-permute-start | bytes 786440 | tf_op jit(solution)/shard_map/ppermute | solution.py:33
  (152 other events, 1443.3 us)
Sparse Core Ops, SparseCore 0:
  270.0 49.7 reduce-scatter.2
  345.9 42.3 reduce-scatter.4
